TPU v7x, 32 devices: a whole 2x2x4 slice. The times are simulated.
32 devices in a mesh: dp: 8 (over y, x, core), seq: 4 (over z).
Axes of the slice: x: 2, y: 2, z: 4, core: 2. Of those that a mesh axis runs over, the one named last changes fastest.
Arguments:
- tokens: bfloat16 [22528, 512], P(('dp', 'seq')), may hold values from -6 to 6
- cotangent: bfloat16 [22528, 512], P(('dp', 'seq')), may hold values from -6 to 6
- w_qkv: bfloat16 [512, 1536], P(('dp', 'seq')), may hold values from -0.25 to 0.25
- w_out: bfloat16 [512, 512], P(('dp', 'seq')), may hold values from -1 to 1
- w_up: bfloat16 [512, 2048], P('dp', 'seq'), may hold values from -0.25 to 0.25
- w_down: bfloat16 [2048, 512], P('seq', 'dp'), may hold values from -0.125 to 0.125
- norm1_gain: bfloat16 [512], P(('dp', 'seq')), may hold values from 0.5 to 1.5
- norm1_shift: bfloat16 [512], P(('dp', 'seq')), may hold values from -3 to 3
- norm2_gain: bfloat16 [512], P(('dp', 'seq')), may hold values from 0.5 to 1.5
- norm2_shift: bfloat16 [512], P(('dp', 'seq')), may hold values from -3 to 3
- clip_steps: int32 [8, 3], P('dp'), may hold values from 76 to 192, as said below
- window_shifts: int32 [8, 3, 2], P('dp'), may hold values from 1 to 3
Outputs:
- output: bfloat16 [22528, 512], P(('dp', 'seq'))
- tokens_grad: bfloat16 [22528, 512], P(('dp', 'seq'))
- w_qkv_grad: float32 [512, 1536], P(('dp', 'seq'))
- w_out_grad: float32 [512, 512], P(('dp', 'seq'))
- w_up_grad: float32 [512, 2048], P('dp', 'seq')
- w_down_grad: float32 [2048, 512], P('seq', 'dp')
- norm1_gain_grad: float32 [512], P(('dp', 'seq'))
- norm1_shift_grad: float32 [512], P(('dp', 'seq'))
- norm2_gain_grad: float32 [512], P(('dp', 'seq'))
- norm2_shift_grad: float32 [512], P(('dp', 'seq'))
Inputs may be any that keep to these rules, and one draw needn't show every extreme that they name: `clip_steps`: A group's row is a leading clip, a clip of 192 time steps, and a trailing clip; the middle clip starts on the group's first device along seq and ends on its last; the leading and trailing lengths are multiples of 4, and every row sums to 352. `window_shifts`: shifts of empty slots are not used.
All inputs are finite; a program needn't handle non-finite values.
Results may differ from a plain program's by a relative error of at most 0.013.
Values may be sent and summed in bfloat16 or wider, within the bound.
No kernel may reach another device: no remote copies, remote signals or barrier semaphores. Data moves between devices by JAX's collectives and lax.ppermute only.
A program may use at most 128 MiB of HBM per device.

v0:
```python
import jax
import jax.numpy as jnp
from jax import lax
from jax.sharding import PartitionSpec as P

D = 512
HEADS = 16
FREQ = 8
STEPS_DEV = 88


epsilon = 1e-06


def padded(cells, sides, width):
    for axis, dim in sides:
        count = lax.axis_size(axis)
        ends = count - 1
        head = lax.slice_in_dim(cells, 0, width, axis=dim)
        tail = lax.slice_in_dim(cells, cells.shape[dim] - width, cells.shape[dim], axis=dim)
        cells = jnp.concatenate(
            [
                lax.ppermute(tail, axis, [(i, (i + 1) % count) for i in range(ends)]),
                cells,
                lax.ppermute(head, axis, [((i + 1) % count, i) for i in range(ends)]),
            ],
            axis=dim,
        )
    return cells


def layer_norm(rows_in, gain, shift):
    row_mean = jnp.mean(rows_in, axis=-1, keepdims=True)
    centered = rows_in - row_mean
    variance = jnp.mean(centered * centered, axis=-1, keepdims=True)
    return centered * lax.rsqrt(variance + epsilon) * gain + shift


def exact_gelu(values_in):
    return jax.nn.gelu(values_in, approximate=False)


def window_ids(step_index, freq_index, steps_row, shifts_row):
    clip_ends = jnp.cumsum(steps_row)
    clip_starts = clip_ends - steps_row
    inside = (step_index[:, None] >= clip_starts[None, :]) & (
        step_index[:, None] < clip_ends[None, :]
    )
    member = inside.astype(jnp.int32)
    slot_index = jnp.arange(steps_row.shape[0], dtype=jnp.int32)
    clip_slot = jnp.sum(member * slot_index[None, :], axis=1)
    clip_start = jnp.sum(member * clip_starts[None, :], axis=1)
    shift_time = jnp.sum(member * shifts_row[None, :, 0], axis=1)
    shift_freq = jnp.sum(member * shifts_row[None, :, 1], axis=1)
    is_valid = jnp.sum(member, axis=1) > 0
    time_group = (step_index - clip_start + 4 - shift_time) // 4
    freq_group = (freq_index + 4 - shift_freq) // 4
    window_key = clip_slot * 65536 + time_group * 4 + freq_group
    return (jnp.where(is_valid, window_key, -1), is_valid)


def block_views(array, blocks, span, rows):
    parts = [
        array[view_index * span : view_index * span + rows].reshape(
            (blocks, span) + array.shape[1:]
        )
        for view_index in range(3)
    ]
    return jnp.concatenate(parts, axis=1)


def right_product(left, right):
    return lax.dot_general(
        left, right, (((1,), (1,)), ((), ())), preferred_element_type=jnp.float32
    )


def left_product(left, right):
    return lax.dot_general(
        left, right, (((0,), (0,)), ((), ())), preferred_element_type=jnp.float32
    )


def per_device(
    tokens,
    cotangent,
    w_qkv,
    w_out,
    w_up,
    w_down,
    norm1_gain,
    norm1_shift,
    norm2_gain,
    norm2_shift,
    clip_steps,
    window_shifts,
):
    rows = tokens.shape[0]
    span = 4 * FREQ
    blocks = rows // span
    rim = 3 * FREQ
    head_dim = D // HEADS
    score_scale = head_dim ** (-0.5)
    w_qkv_all, w_out_all, gain_one, shift_one, gain_two, shift_two = (
        lax.all_gather(w_qkv, ("dp", "seq"), axis=0, tiled=True),
        lax.all_gather(w_out, ("dp", "seq"), axis=0, tiled=True),
        lax.all_gather(norm1_gain, ("dp", "seq"), axis=0, tiled=True),
        lax.all_gather(norm1_shift, ("dp", "seq"), axis=0, tiled=True),
        lax.all_gather(norm2_gain, ("dp", "seq"), axis=0, tiled=True),
        lax.all_gather(norm2_shift, ("dp", "seq"), axis=0, tiled=True),
    )
    up_cols, down_rows = (
        lax.all_gather(w_up, "dp", axis=0, tiled=True),
        lax.all_gather(w_down, "dp", axis=1, tiled=True),
    )
    up_cols, down_rows = (
        lax.all_gather(up_cols, "seq", axis=1, tiled=True),
        lax.all_gather(down_rows, "seq", axis=0, tiled=True),
    )
    base_step = lax.axis_index("seq") * STEPS_DEV
    steps_row = clip_steps[0]
    shifts_row = window_shifts[0]
    row_index = jnp.arange(rows, dtype=jnp.int32)
    query_key, unused = window_ids(
        base_step + row_index // FREQ, row_index % FREQ, steps_row, shifts_row
    )
    ext_index = jnp.arange(rows + 8 * FREQ, dtype=jnp.int32)
    ext_key, ext_valid = window_ids(
        base_step - 3 + ext_index // FREQ, ext_index % FREQ, steps_row, shifts_row
    )
    key_blocks_key = block_views(ext_key, blocks, span, rows)
    key_blocks_valid = block_views(ext_valid, blocks, span, rows)
    allowed = (
        query_key.reshape(blocks, span)[:, :, None] == key_blocks_key[:, None, :]
    ) & key_blocks_valid[:, None, :]
    inputs = tokens.astype(jnp.float32)
    normed, norm_one_back = jax.vjp(
        layer_norm, inputs, gain_one.astype(jnp.float32), shift_one.astype(jnp.float32)
    )
    normed_low = normed.astype(jnp.bfloat16)
    qkv_low = jnp.dot(normed_low, w_qkv_all, preferred_element_type=jnp.float32).astype(
        jnp.bfloat16
    )
    key_value = padded(qkv_low[:, D:], (("seq", 0),), rim)
    key_value = jnp.pad(key_value, ((0, 2 * FREQ), (0, 0)))
    query_blocks = qkv_low[:, :D].reshape(blocks, span, HEADS, head_dim)
    pair_blocks = block_views(key_value, blocks, span, rows)
    key_blocks = pair_blocks[:, :, :D].reshape(blocks, 3 * span, HEADS, head_dim)
    value_blocks = pair_blocks[:, :, D:].reshape(blocks, 3 * span, HEADS, head_dim)
    raw = jnp.einsum(
        "bqhd,bkhd->bhqk", query_blocks, key_blocks, preferred_element_type=jnp.float32
    )
    scores = jnp.where(allowed[:, None], raw * score_scale, -1e30)
    probs = jax.nn.softmax(scores, axis=-1)
    probs_low = probs.astype(jnp.bfloat16)
    mixed_low = (
        jnp.einsum("bhqk,bkhd->bqhd", probs_low, value_blocks, preferred_element_type=jnp.float32)
        .reshape(rows, D)
        .astype(jnp.bfloat16)
    )
    middle = inputs + jnp.dot(mixed_low, w_out_all, preferred_element_type=jnp.float32)
    normed_two, norm_two_back = jax.vjp(
        layer_norm, middle, gain_two.astype(jnp.float32), shift_two.astype(jnp.float32)
    )
    normed_two_low = normed_two.astype(jnp.bfloat16)
    hidden_pre = jnp.dot(normed_two_low, up_cols, preferred_element_type=jnp.float32)
    hidden, gelu_back = jax.vjp(exact_gelu, hidden_pre)
    hidden_low = hidden.astype(jnp.bfloat16)
    branch = jnp.dot(hidden_low, down_rows, preferred_element_type=jnp.float32)
    output = (middle + branch).astype(jnp.bfloat16)
    grad_hidden = right_product(cotangent, down_rows)
    grad_pre_low = gelu_back(grad_hidden)[0].astype(jnp.bfloat16)
    grad_normed_part = right_product(grad_pre_low, up_cols)
    grad_up = left_product(normed_two_low, grad_pre_low)
    grad_down = left_product(hidden_low, cotangent)
    grad_up, grad_down = (
        lax.psum_scatter(
            grad_up.astype(jnp.bfloat16), "seq", scatter_dimension=1, tiled=True
        ).astype(jnp.float32),
        lax.psum_scatter(
            grad_down.astype(jnp.bfloat16), "seq", scatter_dimension=0, tiled=True
        ).astype(jnp.float32),
    )
    grad_up, grad_down = (
        lax.psum_scatter(grad_up, "dp", scatter_dimension=0, tiled=True),
        lax.psum_scatter(grad_down, "dp", scatter_dimension=1, tiled=True),
    )
    grad_middle_norm, grad_gain_two, grad_shift_two = norm_two_back(grad_normed_part)
    grad_middle = cotangent.astype(jnp.float32) + grad_middle_norm
    grad_middle_low = grad_middle.astype(jnp.bfloat16)
    grad_w_out = left_product(mixed_low, grad_middle_low)
    grad_mixed_low = right_product(grad_middle_low, w_out_all).astype(jnp.bfloat16)
    grad_mixed_blocks = grad_mixed_low.reshape(blocks, span, HEADS, head_dim)
    grad_probs = jnp.einsum(
        "bqhd,bkhd->bhqk", grad_mixed_blocks, value_blocks, preferred_element_type=jnp.float32
    )
    delta_sum = jnp.sum(probs * grad_probs, axis=-1, keepdims=True)
    grad_scores_low = (probs * (grad_probs - delta_sum) * score_scale).astype(jnp.bfloat16)
    grad_query = jnp.einsum(
        "bhqk,bkhd->bqhd", grad_scores_low, key_blocks, preferred_element_type=jnp.float32
    ).reshape(rows, D)
    grad_key = jnp.einsum(
        "bhqk,bqhd->bkhd", grad_scores_low, query_blocks, preferred_element_type=jnp.float32
    ).reshape(blocks, 3 * span, D)
    grad_value = jnp.einsum(
        "bhqk,bqhd->bkhd", probs_low, grad_mixed_blocks, preferred_element_type=jnp.float32
    ).reshape(blocks, 3 * span, D)
    grad_pairs = jnp.concatenate((grad_key, grad_value), axis=2)
    grad_ext = jnp.zeros((rows + 8 * FREQ, 2 * D), jnp.float32)
    for view_index in range(3):
        piece = grad_pairs[:, view_index * span : (view_index + 1) * span].reshape(rows, 2 * D)
        grad_ext = grad_ext + jnp.pad(
            piece, ((view_index * span, 8 * FREQ - view_index * span), (0, 0))
        )
    rims_out = jnp.concatenate((grad_ext[:rim], grad_ext[rim + rows : 2 * rim + rows]), axis=0)
    rims_in = padded(rims_out.astype(jnp.bfloat16), (("seq", 0),), rim).astype(rims_out.dtype)
    grad_pair_rows = (
        grad_ext[rim : rim + rows]
        + jnp.pad(rims_in[:rim], ((0, rows - rim), (0, 0)))
        + jnp.pad(rims_in[3 * rim :], ((rows - rim, 0), (0, 0)))
    )
    grad_qkv_low = jnp.concatenate((grad_query, grad_pair_rows), axis=1).astype(jnp.bfloat16)
    grad_w_qkv = left_product(normed_low, grad_qkv_low)
    grad_normed = right_product(grad_qkv_low, w_qkv_all)
    grad_inputs_norm, grad_gain_one, grad_shift_one = norm_one_back(grad_normed)
    tokens_grad = (grad_middle + grad_inputs_norm).astype(jnp.bfloat16)
    owned = (
        lax.psum_scatter(grad_w_qkv, ("dp", "seq"), scatter_dimension=0, tiled=True),
        lax.psum_scatter(grad_w_out, ("dp", "seq"), scatter_dimension=0, tiled=True),
        lax.psum_scatter(grad_gain_one, ("dp", "seq"), scatter_dimension=0, tiled=True),
        lax.psum_scatter(grad_shift_one, ("dp", "seq"), scatter_dimension=0, tiled=True),
        lax.psum_scatter(grad_gain_two, ("dp", "seq"), scatter_dimension=0, tiled=True),
        lax.psum_scatter(grad_shift_two, ("dp", "seq"), scatter_dimension=0, tiled=True),
    )
    return (
        output,
        tokens_grad,
        owned[0],
        owned[1],
        grad_up,
        grad_down,
        owned[2],
        owned[3],
        owned[4],
        owned[5],
    )


def solution(mesh):
    return jax.shard_map(
        per_device,
        mesh=mesh,
        in_specs=(
            P(("dp", "seq"), None),
            P(("dp", "seq"), None),
            P(("dp", "seq"), None),
            P(("dp", "seq"), None),
            P("dp", "seq"),
            P("seq", "dp"),
            P(("dp", "seq")),
            P(("dp", "seq")),
            P(("dp", "seq")),
            P(("dp", "seq")),
            P("dp", None),
            P("dp", None, None),
        ),
        out_specs=(
            P(("dp", "seq"), None),
            P(("dp", "seq"), None),
            P(("dp", "seq"), None),
            P(("dp", "seq"), None),
            P("dp", "seq"),
            P("seq", "dp"),
            P(("dp", "seq")),
            P(("dp", "seq")),
            P(("dp", "seq")),
            P(("dp", "seq")),
        ),
        check_vma=False,
    )
```

profile of v0, /device:TPU:0, one launch (start us, length us, event | category | flops | bytes accessed | tf_op | source)
XLA Modules:
  0.0 658.1 jit_solution(12748756497979494490)
XLA Ops:
  8.0 13.2 %all_gather.36 = bf16[512,512]{1,0:T(8,128)(2,1)} all-gather(bf16[64,512]{1,0:T(8,128)(2,1)} %param.16), channel_id=1, replica_groups=mesh['dp'=8,'seq'=4] {'dp'}, dimensions={0}, use_global_device_ids=true | all-gather | bytes 589824 | tf_op jit(solution)/shard_map/all_gather | solution.py:113
  21.3 10.8 %all_gather.38 = bf16[512,512]{0,1:T(8,128)(2,1)} all-gather(bf16[512,64]{0,1:T(8,128)(2,1)} %param.17), channel_id=1, replica_groups=mesh['dp'=8,'seq'=4] {'dp'}, dimensions={1}, use_global_device_ids=true | all-gather | bytes 589824 | tf_op jit(solution)/shard_map/all_gather | solution.py:114
  38.1 39.8 %all-reduce.15 = (bf16[512]{0:T(512)(128)(2,1)S(1)}, bf16[512]{0:T(512)(128)(2,1)S(1)}, bf16[512]{0:T(512)(128)(2,1)S(1)}, bf16[512]{0:T(512)(128)(2,1)S(1)}) all-reduce(bf16[512]{0:T(512)(128)(2,1)S(1)} %dynamic-update-slice.1, bf16[512]{0:T(512)(128)(2,1)S(1)} %dynamic-update-slice, ...), channel_id=1, replica_groups=mesh['dp'=8,'seq'=4] {'dp','seq'}, use_global_device_ids=true, to_apply=%add.7 | all-reduce | flops 2048 | bytes 8192
  80.2 77.6 %all_gather.33 = bf16[512,512]{1,0:T(8,128)(2,1)S(1)} all-gather(bf16[16,512]{1,0:T(8,128)(2,1)S(1)} %copy-done.16), channel_id=1, replica_groups=mesh['dp'=8,'seq'=4] {'dp','seq'}, dimensions={0}, use_global_device_ids=true | all-gather | bytes 540672 | tf_op jit(solution)/shard_map/all_gather | solution.py:106
  184.6 7.8 %fusion.116 = (f32[22,16,32]{2,1,0:T(8,128)S(1)}, f32[22,16,32,96]{3,2,1,0:T(8,128)}) fusion(pred[22,32,96]{2,1,0:T(8,128)(4,1)S(1)} %compare_and_fusion, bf16[22,32,16,32]{1,3,2,0:T(8,128)(2,1)} %copy.57, bf16[22,96,16,32]{1,3,2,0:T(8,128)(2,1)} %bitcast.76), kind=kOutput, calls=%fused_computation.227 | convolution fusion | flops 73531488 | bytes 7321600 | tf_op jit(solution)/shard_map/sub | solution.py:154
  192.4 5.7 convert_bitcast_fusion.1
  198.1 4.8 copy.54
  208.3 17.6 %multiply_convert_fusion.1 = (bf16[704,2048]{1,0:T(8,128)(2,1)}, f32[704,2048]{1,0:T(8,128)}, f32[704,2048]{1,0:T(8,128)}) fusion(bf16[512,2048]{1,0:T(8,128)(2,1)} %all-gather.6.cloned.1.call-done, f32[704,512]{1,0:T(8,128)S(1)} %get-tuple-element.106, f32[512]{0:T(512)S(1)} %copy-done.20, f32[512]{0:T(512)S(1)} %copy-done.17, f32[704]{0:T(1024)S(1)} %fusion.93, ...), kind=kOutput, calls=%fused_computation.12 | convolution fusion | flops 1571913728 | bytes 17966592 | tf_op jit(solution)/shard_map/dot_general | solution.py:166
  225.8 8.2 %add_convert_fusion = bf16[704,2048]{1,0:T(8,128)(2,1)S(1)} fusion(f32[704,2048]{1,0:T(8,128)} %get-tuple-element.80, f32[704,2048]{1,0:T(8,128)} %get-tuple-element.107, bf16[704,512]{1,0:T(8,128)(2,1)} %param.13, bf16[2048,512]{0,1:T(8,128)(2,1)} %all-gather.8.cloned.1.call-done), kind=kOutput, calls=%fused_computation.11 | convolution fusion | flops 1496580096 | bytes 17235968 | tf_op jit(solution)/shard_map/dot_general | solution.py:73
  239.1 5.1 convolution_convert_fusion.1
  244.5 4.8 multiply_reduce_fusion.1
  257.9 4.8 copy.58
  265.5 6.5 fusion.120
  272.0 5.4 fusion.43
  277.8 72.3 %fusion.22 = f32[22,16,32,96]{3,2,1,0:T(8,128)} fusion(bf16[22,32,16,32]{1,3,2,0:T(8,128)(2,1)} %copy.57, f32[22,16,32,96]{3,2,1,0:T(8,128)} %fusion.120, f32[22,16,32,96]{3,2,1,0:T(8,128)} %get-tuple-element.104, f32[22,16,32]{2,1,0:T(8,128)S(1)} %copy-done.23), kind=kOutput, calls=%fused_computation.49 | convolution fusion | flops 76786784 | bytes 13742080 | tf_op jit(solution)/shard_map/bhqk,bqhd->bkhd/dot_general | solution.py:202
  350.0 6.0 copy.60
  356.0 5.9 copy.59
  374.7 71.8 %convert_bitcast_fusion = bf16[22,32,16,32]{1,3,2,0:T(8,128)(2,1)} fusion(bf16[22,96,16,32]{1,3,2,0:T(8,128)(2,1)} %bitcast.77, f32[22,16,32,96]{3,2,1,0:T(8,128)} %fusion.120, f32[22,16,32,96]{3,2,1,0:T(8,128)} %get-tuple-element.104, f32[22,16,32]{2,1,0:T(8,128)S(1)} %copy-done.23), kind=kOutput, calls=%fused_computation.44 | convolution fusion | flops 77147232 | bytes 11579392 | tf_op jit(solution)/shard_map/bhqk,bkhd->bqhd/dot_general | solution.py:199
  446.5 4.8 copy.56
  467.1 5.2 add_convert_fusion.2
  475.7 40.5 %all-reduce.14 = (f32[512]{0:T(512)S(1)}, f32[512]{0:T(512)S(1)}, f32[512]{0:T(512)S(1)}, f32[512]{0:T(512)S(1)}) all-reduce(f32[512]{0:T(512)S(1)} %get-tuple-element.52, f32[512]{0:T(512)S(1)} %get-tuple-element.55, f32[512]{0:T(512)S(1)} %get-tuple-element.50, ...), channel_id=8, replica_groups=mesh['dp'=8,'seq'=4] {'dp','seq'}, use_global_device_ids=true, to_apply=%region_29.30.clone | all-reduce | flops 2048 | bytes 16384
  521.3 50.8 %reduce-scatter.9.cloned.1.call-done = f32[16,1536]{1,0:T(8,128)} async-done(((f32[512,1536]{1,0:T(8,128)}), f32[16,1536]{1,0:T(8,128)}) %reduce-scatter.9.cloned.1.call-update) | async-done | bytes 98320 | tf_op jit(solution)/shard_map/reduce_scatter | solution.py:228
  572.0 39.1 %reduce-scatter.15.cloned.1.call-done = f32[64,512]{1,0:T(8,128)} async-done(((f32[512,512]{1,0:T(8,128)}), f32[64,512]{1,0:T(8,128)}) %reduce-scatter.15.cloned.1.call-update) | async-done | bytes 131088 | tf_op jit(solution)/shard_map/reduce_scatter | solution.py:185
  611.2 40.2 %reduce-scatter.19.cloned.1.call-done = f32[64,512]{1,0:T(8,128)} async-done(((f32[512,512]{1,0:T(8,128)}), f32[64,512]{1,0:T(8,128)}) %reduce-scatter.19.cloned.1.call-update) | async-done | bytes 131088
  (171 shorter events, 94.8 us)
Async XLA Ops:
  7.2 70.7 %copy-start = (bf16[704,512]{1,0:T(8,128)(2,1)S(1)}, bf16[704,512]{1,0:T(8,128)(2,1)}, u32[]{:S(2)}) copy-start(bf16[704,512]{1,0:T(8,128)(2,1)} %param.12) | copy-start | bytes 2162692
  7.2 73.0 %copy-start.16 = (bf16[16,512]{1,0:T(8,128)(2,1)S(1)}, bf16[16,512]{1,0:T(8,128)(2,1)}, u32[]{:S(2)}) copy-start(bf16[16,512]{1,0:T(8,128)(2,1)} %param.15) | copy-start | bytes 49156
  7.2 150.8 %all-gather.4.cloned.1.call-start = ((), (), s32[]{:S(2)}) async-start(), calls=%async_computation.6 | async-start | bytes 1622016 | tf_op jit(solution)/shard_map/all_gather | solution.py:105
  7.9 200.3 %all-gather.6.cloned.1.call-start = ((), (), s32[]{:S(2)}) async-start(), calls=%async_computation.7 | async-start | bytes 2621440 | tf_op jit(solution)/shard_map/all_gather | solution.py:117
  21.2 204.6 %all-gather.8.cloned.1.call-start = ((), (), s32[]{:S(2)}) async-start(), calls=%async_computation.8 | async-start | bytes 2621440 | tf_op jit(solution)/shard_map/all_gather | solution.py:118
  32.1 430.4 %reduce-scatter.13.cloned.1.call-start = ((), (), s32[]{:S(2)}) async-start(), calls=%async_computation.11 | async-start | bytes 2621440 | tf_op jit(solution)/shard_map/reduce_scatter | solution.py:177
  77.9 82.9 %copy-start.14 = (f32[512]{0:T(512)}, f32[512]{0:T(512)S(1)}, u32[]{:S(2)}) copy-start(f32[512]{0:T(512)S(1)} %convert_element_type.96) | copy-start | bytes 6148
  77.9 82.9 %copy-start.18 = (f32[512]{0:T(512)}, f32[512]{0:T(512)S(1)}, u32[]{:S(2)}) copy-start(f32[512]{0:T(512)S(1)} %convert_element_type.97) | copy-start | bytes 6148
  161.5 12.2 %collective-permute-start = (bf16[24,1024]{1,0:T(8,128)(2,1)}, bf16[24,1024]{1,0:T(8,128)(2,1)S(1)}, u32[]{:S(2)}, u32[]{:S(2)}) collective-permute-start(bf16[24,1024]{1,0:T(8,128)(2,1)} %get-tuple-element.86), channel_id=1, source_target_pairs={{0,1},{1,2},{2,3},{4,5},{5,6},{6,7},{8,9},{9,10},{10,11},{12,13},{... | collective-permute-start | bytes 147464 | tf_op jit(solution)/shard_map/ppermute | solution.py:23
  162.8 10.9 %collective-permute-start.1 = (bf16[24,1024]{1,0:T(8,128)(2,1)}, bf16[24,1024]{1,0:T(8,128)(2,1)}, u32[]{:S(2)}, u32[]{:S(2)}) collective-permute-start(bf16[24,1024]{1,0:T(8,128)(2,1)} %get-tuple-element.87), channel_id=1, source_target_pairs={{1,0},{2,1},{3,2},{5,4},{6,5},{7,6},{9,8},{10,9},{11,10},{13,12},{... | collective-permute-start | bytes 147464 | tf_op jit(solution)/shard_map/ppermute | solution.py:25
  192.4 5.7 copy-start.22
  239.1 225.8 %reduce-scatter.17.cloned.1.call-start = ((), (), s32[]{:S(2)}) async-start(), calls=%async_computation.13 | async-start | bytes 2621440 | tf_op jit(solution)/shard_map/reduce_scatter | solution.py:180
  244.3 277.0 %reduce-scatter.11.cloned.1.call-start = ((), (), s32[]{:S(2)}) async-start(), calls=%async_computation.10 | async-start | bytes 1081344 | tf_op jit(solution)/shard_map/reduce_scatter | solution.py:229
  265.4 6.5 copy-start.3
  265.5 6.5 copy-start.23
  277.5 294.6 %reduce-scatter.9.cloned.1.call-start = ((), (), s32[]{:S(2)}) async-start(), calls=%async_computation.9 | async-start | bytes 3244032 | tf_op jit(solution)/shard_map/reduce_scatter | solution.py:228
  368.6 87.1 %collective-permute-start.2 = (bf16[24,1024]{1,0:T(8,128)(2,1)S(1)}, bf16[24,1024]{1,0:T(8,128)(2,1)S(1)}, u32[]{:S(2)}, u32[]{:S(2)}) collective-permute-start(bf16[24,1024]{1,0:T(8,128)(2,1)S(1)} %get-tuple-element.88), channel_id=1, source_target_pairs={{0,1},{1,2},{2,3},{4,5},{5,6},{6,7},{8,9},{9,10},{10,11},{12,13},{... | collective-permute-start | bytes 147464 | tf_op jit(solution)/shard_map/ppermute | solution.py:23
  373.0 82.7 %collective-permute-start.3 = (bf16[24,1024]{1,0:T(8,128)(2,1)S(1)}, bf16[24,1024]{1,0:T(8,128)(2,1)S(1)}, u32[]{:S(2)}, u32[]{:S(2)}) collective-permute-start(bf16[24,1024]{1,0:T(8,128)(2,1)S(1)} %get-tuple-element.89), channel_id=1, source_target_pairs={{1,0},{2,1},{3,2},{5,4},{6,5},{7,6},{9,8},{10,9},{11,10},{13,12},{... | collective-permute-start | bytes 147464 | tf_op jit(solution)/shard_map/ppermute | solution.py:25
  455.7 6.7 %copy-start.10 = (bf16[704,512]{1,0:T(8,128)(2,1)}, bf16[704,512]{1,0:T(8,128)(2,1)S(1)}, u32[]{:S(2)}) copy-start(bf16[704,512]{1,0:T(8,128)(2,1)S(1)} %reshape.349) | copy-start | bytes 2162692
  462.3 148.8 %reduce-scatter.15.cloned.1.call-start = ((), (), s32[]{:S(2)}) async-start(), calls=%async_computation.12 | async-start | bytes 1179648 | tf_op jit(solution)/shard_map/reduce_scatter | solution.py:185
  464.6 186.7 %reduce-scatter.19.cloned.1.call-start = ((), (), s32[]{:S(2)}) async-start(), calls=%async_computation.14 | async-start | bytes 1179648
  467.1 5.2 copy-start.9
  472.3 46.3 %copy-start.6 = (bf16[704,512]{1,0:T(8,128)(2,1)S(1)}, bf16[704,512]{1,0:T(8,128)(2,1)}, u32[]{:S(2)}) copy-start(bf16[704,512]{1,0:T(8,128)(2,1)} %param.13) | copy-start | bytes 2162692
  473.8 44.8 %copy-start.2 = (f32[704,512]{1,0:T(8,128)S(1)}, f32[704,512]{1,0:T(8,128)}, u32[]{:S(2)}) copy-start(f32[704,512]{1,0:T(8,128)} %copy-done.1) | copy-start | bytes 4325380
  (14 other events, 28.9 us)
Sparse Core Ops, SparseCore 0:
  10.9 57.7 all-gather.3
  70.3 50.3 all-gather.5
  122.2 48.8 all-gather.7
  239.2 43.7 reduce-scatter.12
  285.2 42.9 reduce-scatter.16
  330.9 136.2 reduce-scatter.10
  474.0 97.9 reduce-scatter.8
  576.1 35.0 reduce-scatter.14
  615.3 36.0 reduce-scatter.18
where the time goes:
time: 664 us; the launch traced here: 658 us
  matrix products  226 us (34%)
  blocking collectives  182 us (27%)
  waiting for transfers between devices  131 us (20%)
  local copies, waits for them, and re-layouts  72.7 us (11%)
  other arithmetic  21.5 us (3%)
  between operations  14.6 us (2%)
  starting transfers between devices  10.3 us (2%)
    unnamed x2, blocking collectives  80.3 us
    all_gather x1, blocking collectives, per_device(): lax.all_gather(w_out, ('dp', 'seq'), axis=0, tiled=True)  77.6 us
    dot_general x1, matrix products, per_device(): jnp.einsum('bhqk,bqhd->bkhd', grad_scores_low, query_blocks, preferred_el...  72.3 us
    dot_general x1, matrix products, per_device(): jnp.einsum('bhqk,bkhd->bqhd', grad_scores_low, key_blocks, preferred_elem...  71.8 us
    reduce_scatter x1, waiting for transfers between devices, per_device(): lax.psum_scatter(grad_w_qkv, ('dp', 'seq'), scatter_dimension=0, tiled=True)  50.8 us
    unnamed x10, waiting for transfers between devices  41 us
    reduce_scatter x1, waiting for transfers between devices, per_device(): lax.psum_scatter(grad_up, 'dp', scatter_dimension=0, tiled=True)  39.1 us
    dot_general x1, matrix products, per_device(): jnp.dot(normed_two_low, up_cols, preferred_element_type=jnp.float32)  17.6 us
  transfers between devices with their start and end apart: 13, of which 3 were waited for; matrix products, arithmetic and copies ran while one was open for 46% of the time, Pallas kernels for 0%

commit v1 on v0

v1 whole, which is shorter than its diff:
```python
import functools

import jax
import jax.numpy as jnp
from jax import lax
from jax.experimental import pallas as pl
from jax.experimental.pallas import tpu as pltpu
from jax.sharding import PartitionSpec as P

D = 512
HEADS = 16
HEAD_DIM = D // HEADS
FF = 2048
FREQ = 8
STEPS_DEV = 88
HALO = 4 * FREQ
ROWS = STEPS_DEV * FREQ
WIN = 4 * FREQ
WINDOWS = STEPS_DEV // 4 + 2
WROWS = WINDOWS * WIN
TILE = 256
QUAD = 128
NORMS = 128
CHUNK = 512
CHUNKS = FF // CHUNK
epsilon = 1e-06
F32 = jnp.float32
BF16 = jnp.bfloat16


def mm(left, right):
    return jnp.dot(left, right, preferred_element_type=F32)


def mm_right(left, right):
    return lax.dot_general(left, right, (((1,), (1,)), ((), ())), preferred_element_type=F32)


def mm_left(left, right):
    return lax.dot_general(left, right, (((0,), (0,)), ((), ())), preferred_element_type=F32)


def window_place(info, w):
    lead, mid, trail = info[0], info[1], info[2]
    seq = info[10]
    base = seq * STEPS_DEV
    n_lead = lead // 4 + 1
    n_mid = mid // 4 + 1
    index = jnp.where(seq == 0, 0, base // 4 + 1) + w
    in_mid = index >= n_lead
    in_trail = index >= n_lead + n_mid
    before = jnp.where(in_trail, n_lead + n_mid, jnp.where(in_mid, n_lead, 0))
    start = jnp.where(in_trail, lead + mid, jnp.where(in_mid, lead, 0))
    steps = jnp.where(in_trail, trail, jnp.where(in_mid, mid, lead))
    shift_time = jnp.where(in_trail, info[7], jnp.where(in_mid, info[5], info[3]))
    shift_freq = jnp.where(in_trail, info[8], jnp.where(in_mid, info[6], info[4]))
    first = start - 4 + shift_time + 4 * (index - before)
    here = first < base + STEPS_DEV
    low = jnp.clip(start - first, 0, 4)
    high = jnp.where(here, jnp.clip(start + steps - first, 0, 4), 0)
    own_low = jnp.clip(base - first, 0, 4)
    own_high = jnp.clip(base + STEPS_DEV - first, 0, 4)
    row = jnp.clip(first - base + 4, 0, STEPS_DEV + 4) * FREQ
    row = pl.multiple_of(row, FREQ)
    return (
        row,
        low * FREQ,
        high * FREQ,
        jnp.maximum(low, own_low) * FREQ,
        jnp.minimum(high, own_high) * FREQ,
        shift_freq,
    )


def row_mask(low, high):
    index = lax.broadcasted_iota(jnp.int32, (WIN, 1), 0)
    return (index >= low) & (index < high)


def pad_rows(ext, left, rows, right):
    ext[0:HALO] = left[...].astype(F32)
    ext[HALO : HALO + ROWS] = rows[...].astype(F32)
    ext[HALO + ROWS :] = right[...].astype(F32)


def normalized(values):
    mean = jnp.mean(values, axis=-1, keepdims=True)
    centered = values - mean
    variance = jnp.mean(centered * centered, axis=-1, keepdims=True)
    scale = lax.rsqrt(variance + epsilon)
    return centered * scale, scale


def norm_back(grad, unit, scale):
    mean_one = jnp.mean(grad, axis=-1, keepdims=True)
    mean_two = jnp.mean(grad * unit, axis=-1, keepdims=True)
    return scale * (grad - mean_one - unit * mean_two)


def head_masks():
    lane = lax.broadcasted_iota(jnp.int32, (1, QUAD), 1) // HEAD_DIM
    return [(lane == h).astype(BF16) for h in range(QUAD // HEAD_DIM)]


def spread(block, masks):
    return jnp.concatenate([block * mask for mask in masks], axis=0)


def gathered(product, lane):
    parts = [product[h * WIN : (h + 1) * WIN] for h in range(QUAD // HEAD_DIM)]
    return jnp.where(
        lane < 1, parts[0], jnp.where(lane < 2, parts[1], jnp.where(lane < 3, parts[2], parts[3]))
    )


def place_blocks(info, pieces, order, scratch, rows, first=0):
    for piece, partner in zip(pieces, order):
        for k in range(piece.shape[0]):
            owner = (info[9] ^ partner) * piece.shape[0] + (info[10] ^ k)
            at = pl.multiple_of(owner * rows, rows)
            scratch[pl.ds(at, rows), :] = piece[k, first : first + rows, :]


def attention_kernel(direct, info, left, rows, right, *refs):
    pieces, refs = (refs[:8], refs[8:]) if direct else (refs[:1], refs[1:])
    x_out, qkv_out, mixed_out, probs_out, w_out, norms_out, ext, normed = refs
    if direct:
        place_blocks(info, pieces, ORDER, w_out, pieces[0].shape[1])
    else:
        w_out[...] = pieces[0][...]
    norms_out[...] = jnp.transpose(w_out[:, 3 * D :].astype(F32))[:8]
    gain, shift = norms_out[0:1], norms_out[1:2]
    pad_rows(ext, left, rows, right)

    def place(w, carry):
        row, low, high, _, _, _ = window_place(info, w)
        values = jnp.where(row_mask(low, high), ext[pl.ds(row, WIN), :], 0.0)
        at = pl.ds(pl.multiple_of(w * WIN, WIN), WIN)
        x_out[at, :] = values
        unit, _ = normalized(values)
        normed[at, :] = (unit * gain + shift).astype(BF16)
        return carry

    lax.fori_loop(0, WINDOWS, place, 0)

    def project(i, carry):
        at = pl.ds(pl.multiple_of(i * TILE, TILE), TILE)
        for part in range(3):
            cols = slice(part * D, (part + 1) * D)
            qkv_out[at, cols] = mm(normed[at, :], w_out[:, cols]).astype(BF16)
        return carry

    lax.fori_loop(0, WROWS // TILE, project, 0)
    masks = head_masks()
    lane = lax.broadcasted_iota(jnp.int32, (1, QUAD), 1) // HEAD_DIM
    key_row = lax.broadcasted_iota(jnp.int32, (WIN, QUAD), 0)
    query_row = lax.broadcasted_iota(jnp.int32, (WIN, QUAD), 1) % WIN
    key_freq, query_freq = key_row % FREQ, query_row % FREQ

    def attend(w, carry):
        _, low, high, _, _, shift_freq = window_place(info, w)
        at = pl.ds(pl.multiple_of(w * WIN, WIN), WIN)
        key_group = (key_freq + 4 - shift_freq) >> 2
        query_group = (query_freq + 4 - shift_freq) >> 2
        allowed = (key_group == query_group) & (key_row >= low) & (key_row < high)
        for quad in range(D // QUAD):
            cols = slice(quad * QUAD, (quad + 1) * QUAD)
            query = qkv_out[at, cols]
            key = qkv_out[at, D + quad * QUAD : D + (quad + 1) * QUAD]
            value = qkv_out[at, 2 * D + quad * QUAD : 2 * D + (quad + 1) * QUAD]
            raw = mm_right(key, spread(query, masks))
            scores = jnp.where(allowed, raw * HEAD_DIM**-0.5, -1e30)
            weights = jnp.exp(scores - jnp.max(scores, axis=0, keepdims=True))
            probs = weights / jnp.sum(weights, axis=0, keepdims=True)
            probs_out[at, cols] = probs
            mixed = gathered(mm_left(probs.astype(BF16), value), lane)
            mixed_out[at, cols] = mixed.astype(BF16)
        return carry

    lax.fori_loop(0, WINDOWS, attend, 0)


def gelu_parts(values):
    half_exp = jnp.exp(-0.5 * values * values)
    t = 1.0 / (1.0 + (0.3275911 * 0.7071067811865476) * jnp.abs(values))
    poly = t * (
        0.5 * 0.254829592
        + t
        * (
            0.5 * -0.284496736
            + t * (0.5 * 1.421413741 + t * (0.5 * -1.453152027 + t * (0.5 * 1.061405429)))
        )
    )
    tail = poly * half_exp
    return jnp.where(values >= 0, 1.0 - tail, tail), half_exp * 0.3989422804014327


def feed_kernel(direct, info, left, rows, right, x_in, mixed_in, norms, *refs):
    pieces, refs = (refs[:8], refs[8:]) if direct else (refs[:3], refs[3:])
    out, grad_middle, grad_mixed, grad_norms = refs[:4]
    if direct:
        (keep, send), refs = refs[4:6], refs[6:]
    else:
        (grad_up_out, grad_down_out, grad_w_out), refs = refs[4:7], refs[7:]
    up, down, w_out, ext, cot, cot_own, own, middle, total, normed, normed_own, hidden, pre, grad = refs
    if direct:
        count = pieces[0].shape[0]
        block = D // 8
        for piece, partner in zip(pieces, ORDER):
            dp = info[9] ^ partner
            at = pl.multiple_of(dp * block, block)
            for k in range(count):
                up[k, pl.ds(at, block), :] = piece[k, 0:block, :]
                down[k, pl.ds(at, block), :] = piece[k, block : 2 * block, :]
                row = pl.multiple_of((dp * count + (info[10] ^ k)) * 16, 16)
                w_out[pl.ds(row, 16), :] = piece[k, 2 * block :, :]
    else:
        up[...] = pieces[0][...]
        down[...] = pieces[1][...]
        w_out[...] = pieces[2][...]
    pad_rows(ext, left, rows, right)

    def place(w, carry):
        row, low, high, own_low, own_high, _ = window_place(info, w)
        values = ext[pl.ds(row, WIN), :]
        at = pl.ds(pl.multiple_of(w * WIN, WIN), WIN)
        cot[at, :] = jnp.where(row_mask(low, high), values, 0.0).astype(BF16)
        cot_own[at, :] = jnp.where(row_mask(own_low, own_high), values, 0.0).astype(BF16)
        own[at, :] = jnp.where(row_mask(own_low, own_high), jnp.ones((WIN, QUAD), F32), 0.0)
        return carry

    lax.fori_loop(0, WINDOWS, place, 0)
    gain, shift = norms[2:3], norms[3:4]

    def tile_of(i):
        return pl.ds(pl.multiple_of(i * TILE, TILE), TILE)

    def before(i, carry):
        at = tile_of(i)
        values = x_in[at, :] + mm(mixed_in[at, :], w_out[...])
        middle[at, :] = values
        total[at, :] = values
        unit, _ = normalized(values)
        low = unit * gain + shift
        normed[at, :] = low.astype(BF16)
        normed_own[at, :] = (low * own[at, 0:1]).astype(BF16)
        grad[at, :] = jnp.zeros((TILE, D), F32)
        return carry

    lax.fori_loop(0, WROWS // TILE, before, 0)

    def chunk_step(c, carry):
        up_c, down_c = up[c], down[c]

        def row_step(i, inner):
            at = tile_of(i)
            values = mm(normed[at, :], up_c)
            grad_hidden = mm(cot[at, :], down_c)
            below, density = gelu_parts(values)
            hidden_low = (values * below).astype(BF16)
            grad_low = (grad_hidden * (below + values * density)).astype(BF16)
            hidden[at, :] = hidden_low
            pre[at, :] = grad_low
            total[at, :] += mm_right(hidden_low, down_c)
            grad[at, :] += mm_right(grad_low, up_c)
            return inner

        lax.fori_loop(0, WROWS // TILE, row_step, 0)
        return carry

    for c in range(CHUNKS):
        chunk_step(c, 0)
        grad_up = mm_left(normed_own[...], pre[...])
        grad_down = mm_left(cot_own[...], hidden[...])
        if direct:
            ext[0:D, :] = grad_up
            for partner in range(8):
                target = send if partner & 1 else keep
                row = pl.multiple_of((info[9] ^ partner) * block, block)
                target[partner >> 1, c, 0:block, :] = ext[pl.ds(row, block), :].astype(BF16)
            ext[0:D, :] = grad_down
            for partner in range(8):
                target = send if partner & 1 else keep
                row = pl.multiple_of((info[9] ^ partner) * block, block)
                target[partner >> 1, c, block : 2 * block, :] = ext[pl.ds(row, block), :].astype(
                    BF16
                )
        else:
            grad_up_out[c] = grad_up
            grad_down_out[c] = grad_down
    grad_norms[...] = jnp.zeros(grad_norms.shape, F32)

    def after(i, carry):
        at = tile_of(i)
        unit, scale = normalized(middle[at, :])
        part = grad[at, :]
        masked = part * own[at, 0:1]
        grad_norms[0:1] += jnp.sum(masked * unit, axis=0, keepdims=True)
        grad_norms[1:2] += jnp.sum(masked, axis=0, keepdims=True)
        result = cot[at, :].astype(F32) + norm_back(part * gain, unit, scale)
        grad_middle[at, :] = result
        low = result.astype(BF16)
        grad_mixed[at, :] = mm_right(low, w_out[...]).astype(BF16)
        normed_own[at, :] = (result * own[at, 0:1]).astype(BF16)
        return carry

    lax.fori_loop(0, WROWS // TILE, after, 0)
    grad_out = mm_left(mixed_in[...], normed_own[...])
    if direct:
        ext[0:D, :] = grad_out
        for partner in range(8):
            target = send if partner & 1 else keep
            for k in range(count):
                row = pl.multiple_of(((info[9] ^ partner) * count + (info[10] ^ k)) * 16, 16)
                target[partner >> 1, k, 2 * block :, :] = ext[pl.ds(row, 16), :].astype(BF16)
    else:
        grad_w_out[...] = grad_out
    unplace(info, total, ext, out)


def unplace(info, values, ext, out):
    def back(w, carry):
        row, low, high, _, _, _ = window_place(info, w)
        at = pl.ds(pl.multiple_of(w * WIN, WIN), WIN)
        place = pl.ds(row, WIN)
        ext[place, :] = jnp.where(row_mask(low, high), values[at, :], ext[place, :])
        return carry

    lax.fori_loop(0, WINDOWS, back, 0)
    out[...] = ext[HALO : HALO + ROWS].astype(BF16)


def back_kernel(
    direct, info, x_in, qkv, probs_in, grad_mixed, grad_middle, w_qkv, norms, grad_norms, *refs
):
    out, refs = refs[0], refs[1:]
    if direct:
        (keep, send), refs = refs[:2], refs[2:]
    else:
        w_grad, refs = refs[0], refs[1:]
    ext, normed, grad_qkv, result, gains, grad_w = refs
    masks = head_masks()
    lane = lax.broadcasted_iota(jnp.int32, (1, QUAD), 1) // HEAD_DIM

    def attend_back(w, carry):
        at = pl.ds(pl.multiple_of(w * WIN, WIN), WIN)
        for quad in range(D // QUAD):
            cols = slice(quad * QUAD, (quad + 1) * QUAD)
            cols_key = slice(D + quad * QUAD, D + (quad + 1) * QUAD)
            cols_value = slice(2 * D + quad * QUAD, 2 * D + (quad + 1) * QUAD)
            query = spread(qkv[at, cols], masks)
            key = qkv[at, cols_key]
            value = qkv[at, cols_value]
            grad_out = spread(grad_mixed[at, cols], masks)
            probs = probs_in[at, cols]
            grad_probs = mm_right(value, grad_out)
            delta = jnp.sum(probs * grad_probs, axis=0, keepdims=True)
            grad_scores = (probs * (grad_probs - delta) * HEAD_DIM**-0.5).astype(BF16)
            grad_qkv[at, cols] = gathered(mm_left(grad_scores, key), lane).astype(BF16)
            grad_qkv[at, cols_key] = mm(grad_scores, query).astype(BF16)
            grad_qkv[at, cols_value] = mm(probs.astype(BF16), grad_out).astype(BF16)
        return carry

    lax.fori_loop(0, WINDOWS, attend_back, 0)
    gain, shift = norms[0:1], norms[1:2]
    gains[...] = jnp.zeros(gains.shape, F32)
    index = lax.broadcasted_iota(jnp.int32, (WIN, 1), 0)

    def mask_step(w, carry):
        _, _, _, own_low, own_high, _ = window_place(info, w)
        at = pl.ds(pl.multiple_of(w * WIN, WIN), WIN)
        own = ((index >= own_low) & (index < own_high)).astype(F32)
        unit, scale = normalized(x_in[at, :])
        normed[at, :] = ((unit * gain + shift) * own).astype(BF16)
        part = mm_right(grad_qkv[at, :], w_qkv[:, : 3 * D])
        masked = part * own
        gains[0:1] += jnp.sum(masked * unit, axis=0, keepdims=True)
        gains[1:2] += jnp.sum(masked, axis=0, keepdims=True)
        result[at, :] = grad_middle[at, :] + norm_back(part * gain, unit, scale)
        return carry

    lax.fori_loop(0, WINDOWS, mask_step, 0)
    gains[2:4] = grad_norms[0:2]
    for part in range(3):
        cols = slice(part * D, (part + 1) * D)
        grad_w[:, cols] = mm_left(normed[...], grad_qkv[:, cols])
    grad_w[:, 3 * D :] = jnp.transpose(gains[...])
    if direct:
        count = keep.shape[1]
        for partner in range(8):
            target = send if partner & 1 else keep
            for k in range(count):
                row = pl.multiple_of(((info[9] ^ partner) * count + (info[10] ^ k)) * 16, 16)
                target[partner >> 1, k] = grad_w[pl.ds(row, 16), :].astype(BF16)
    else:
        w_grad[...] = grad_w[...]
    unplace(info, result, ext, out)


ORDER = (0, 2, 4, 6, 1, 3, 5, 7)
SMEM = pl.BlockSpec(memory_space=pltpu.SMEM)
VMEM = pl.BlockSpec(memory_space=pltpu.VMEM)


def run_kernel(body, out_shape, scratch, flops, *operands):
    moved = sum(a.size * a.dtype.itemsize for a in (*operands, *out_shape))
    return pl.pallas_call(
        body,
        out_shape=out_shape,
        in_specs=[SMEM] + [VMEM] * (len(operands) - 1),
        out_specs=[VMEM] * len(out_shape),
        scratch_shapes=scratch,
        cost_estimate=pl.CostEstimate(
            flops=flops, bytes_accessed=moved, transcendentals=flops // 1024
        ),
        compiler_params=pltpu.CompilerParams(vmem_limit_bytes=50 * 1024 * 1024),
    )(*operands)


def swap(array, axis, bit):
    return lax.ppermute(array, axis, [(i, i ^ bit) for i in range(lax.axis_size(axis))])


def spread_out(shard):
    column = jnp.stack([shard] + [swap(shard, "seq", k) for k in range(1, lax.axis_size("seq"))])
    plane = [column] + [swap(column, "dp", partner) for partner in (2, 4, 6)]
    return plane + [swap(piece, "dp", 1) for piece in plane]


def collect(keep, send):
    pair = keep.astype(F32) + swap(send, "dp", 1).astype(F32)
    low = pair.astype(BF16)
    parts = [swap(low[m], "dp", 2 * m) for m in (1, 2, 3)]
    column = pair[0] + sum(part.astype(F32) for part in parts)
    low = column.astype(BF16)
    parts = [swap(low[k], "seq", k) for k in range(1, column.shape[0])]
    return column[0] + sum(part.astype(F32) for part in parts)


def shape(dims, kind):
    return jax.ShapeDtypeStruct(dims, kind)


def per_device(
    tokens,
    cotangent,
    w_qkv,
    w_out,
    w_up,
    w_down,
    norm1_gain,
    norm1_shift,
    norm2_gain,
    norm2_shift,
    clip_steps,
    window_shifts,
):
    n_dp, n_seq = lax.axis_size("dp"), lax.axis_size("seq")
    share = w_qkv.shape[0]
    direct = n_dp == 8 and share % 16 == 0
    info = jnp.concatenate(
        [
            clip_steps.reshape(3),
            window_shifts.reshape(6),
            lax.axis_index("dp").reshape(1).astype(jnp.int32),
            lax.axis_index("seq").reshape(1).astype(jnp.int32),
        ]
    )
    norms = jnp.stack([norm1_gain, norm1_shift, norm2_gain, norm2_shift], axis=1)
    first = jnp.concatenate([w_qkv, jnp.pad(norms, ((0, 0), (0, NORMS - 4)))], axis=1)
    width = first.shape[1]
    if direct:
        second = jnp.concatenate([w_up, w_down.T, w_out], axis=0)
        first_all = spread_out(first)
        second_all = spread_out(second)
    else:
        first_all = [lax.all_gather(first, ("dp", "seq"), axis=0, tiled=True)]
        up_all = lax.all_gather(lax.all_gather(w_up, "dp", axis=0, tiled=True), "seq", axis=0)
        down_all = lax.all_gather(lax.all_gather(w_down.T, "dp", axis=0, tiled=True), "seq", axis=0)
        second_all = [up_all, down_all, lax.all_gather(w_out, ("dp", "seq"), axis=0, tiled=True)]
    both = jnp.stack([tokens, cotangent])
    right_way = [(i, i + 1) for i in range(n_seq - 1)]
    left_way = [(i + 1, i) for i in range(n_seq - 1)]
    left = lax.ppermute(both[:, ROWS - HALO :], "seq", right_way)
    right = lax.ppermute(both[:, :HALO], "seq", left_way)

    x, qkv, mixed, probs, w_qkv_all, norms_all = run_kernel(
        functools.partial(attention_kernel, direct),
        [
            shape((WROWS, D), F32),
            shape((WROWS, 3 * D), BF16),
            shape((WROWS, D), BF16),
            shape((WROWS, D), F32),
            shape((D, width), BF16),
            shape((8, D), F32),
        ],
        [pltpu.VMEM((ROWS + 2 * HALO, D), F32), pltpu.VMEM((WROWS, D), BF16)],
        2 * WROWS * D * 3 * D * 2,
        info,
        left[0],
        tokens,
        right[0],
        *first_all,
    )
    if direct:
        block = (4, n_seq, 2 * (D // 8) + 16, CHUNK)
        grads_shape = [shape(block, BF16)] * 2
    else:
        grads_shape = [shape((CHUNKS, D, CHUNK), F32)] * 2 + [shape((D, D), F32)]
    out, grad_middle, grad_mixed, grad_norms, *grads = run_kernel(
        functools.partial(feed_kernel, direct),
        [
            shape((ROWS, D), BF16),
            shape((WROWS, D), F32),
            shape((WROWS, D), BF16),
            shape((8, D), F32),
            *grads_shape,
        ],
        [
            pltpu.VMEM((CHUNKS, D, CHUNK), BF16),
            pltpu.VMEM((CHUNKS, D, CHUNK), BF16),
            pltpu.VMEM((D, D), BF16),
            pltpu.VMEM((ROWS + 2 * HALO, D), F32),
            pltpu.VMEM((WROWS, D), BF16),
            pltpu.VMEM((WROWS, D), BF16),
            pltpu.VMEM((WROWS, QUAD), F32),
            pltpu.VMEM((WROWS, D), F32),
            pltpu.VMEM((WROWS, D), F32),
            pltpu.VMEM((WROWS, D), BF16),
            pltpu.VMEM((WROWS, D), BF16),
            pltpu.VMEM((WROWS, CHUNK), BF16),
            pltpu.VMEM((WROWS, CHUNK), BF16),
            pltpu.VMEM((WROWS, D), F32),
        ],
        2 * WROWS * D * (6 * FF + 3 * D),
        info,
        left[1],
        cotangent,
        right[1],
        x,
        mixed,
        norms_all,
        *second_all,
    )
    if direct:
        second_sum = collect(*grads)
        grad_up = second_sum[: D // 8]
        grad_down = second_sum[D // 8 : D // 4].T
        grad_out = second_sum[D // 4 :]
        grads_shape = [shape((4, n_seq, share, width), BF16)] * 2
    else:
        grad_up = lax.psum_scatter(grads[0], "seq", scatter_dimension=0)
        grad_up = lax.psum_scatter(grad_up, "dp", scatter_dimension=0, tiled=True)
        grad_down = lax.psum_scatter(grads[1], "seq", scatter_dimension=0)
        grad_down = lax.psum_scatter(grad_down, "dp", scatter_dimension=0, tiled=True).T
        grad_out = lax.psum_scatter(grads[2], ("dp", "seq"), scatter_dimension=0, tiled=True)
        grads_shape = [shape((D, width), F32)]
    tokens_grad, *grads = run_kernel(
        functools.partial(back_kernel, direct),
        [shape((ROWS, D), BF16), *grads_shape],
        [
            pltpu.VMEM((ROWS + 2 * HALO, D), F32),
            pltpu.VMEM((WROWS, D), BF16),
            pltpu.VMEM((WROWS, 3 * D), BF16),
            pltpu.VMEM((WROWS, D), F32),
            pltpu.VMEM((NORMS, D), F32),
            pltpu.VMEM((D, width), F32),
        ],
        2 * WROWS * D * (6 * D + 3 * D),
        info,
        x,
        qkv,
        probs,
        grad_mixed,
        grad_middle,
        w_qkv_all,
        norms_all,
        grad_norms,
    )
    if direct:
        first_sum = collect(*grads)
    else:
        first_sum = lax.psum_scatter(grads[0], ("dp", "seq"), scatter_dimension=0, tiled=True)
    return (
        out,
        tokens_grad,
        first_sum[:, : 3 * D],
        grad_out,
        grad_up,
        grad_down,
        first_sum[:, 3 * D],
        first_sum[:, 3 * D + 1],
        first_sum[:, 3 * D + 2],
        first_sum[:, 3 * D + 3],
    )


def solution(mesh):
    rows = P(("dp", "seq"), None)
    vector = P(("dp", "seq"))
    return jax.shard_map(
        per_device,
        mesh=mesh,
        in_specs=(
            rows,
            rows,
            rows,
            rows,
            P("dp", "seq"),
            P("seq", "dp"),
            vector,
            vector,
            vector,
            vector,
            P("dp", None),
            P("dp", None, None),
        ),
        out_specs=(
            rows,
            rows,
            rows,
            rows,
            P("dp", "seq"),
            P("seq", "dp"),
            vector,
            vector,
            vector,
            vector,
        ),
        check_vma=False,
    )
```

time: 664 us -> 235 us (0.35)
  matrix products: 226 us -> 0 us
  blocking collectives: 182 us -> 0 us
  Pallas kernels: 0 us -> 101 us
  waiting for transfers between devices: 131 us -> 66.1 us
  local copies, waits for them, and re-layouts: 72.7 us -> 10 us
  starting transfers between devices: 10.3 us -> 52.2 us
  other arithmetic: 21.5 us -> 4.53 us
  between operations: 14.6 us -> 0.85 us
    dot_general x17 -> x0, matrix products: 218 us -> none  [the longest x1 72.3 us: per_device(): jnp.einsum('bhqk,bqhd->bkhd', grad_scores_low, query_blocks, preferred_el...]
    all_gather x3 -> x0, blocking collectives: 102 us -> none  [the longest x1 77.6 us: per_device(): lax.all_gather(w_out, ('dp', 'seq'), axis=0, tiled=True)]
    pallas_call x0 -> x3, Pallas kernels: none -> 101 us  [run_kernel(): pl.pallas_call(body, out_shape=out_shape, in_specs=[SMEM] + [VMEM] * (len...]
    reduce_scatter x5 -> x0, waiting for transfers between devices: 89.9 us -> none  [the longest x1 50.8 us: per_device(): lax.psum_scatter(grad_w_qkv, ('dp', 'seq'), scatter_dimension=0, tiled=True)]
    unnamed x2 -> x0, blocking collectives: 80.3 us -> none
    ppermute x4 -> x36, waiting for transfers between devices: 0.01 us -> 66.1 us  [the longest x34 58 us: swap(): lax.ppermute(array, axis, [(i, i ^ bit) for i in range(lax.axis_size(axis...]
    ppermute x4 -> x36, starting transfers between devices: 9.25 us -> 52.2 us  [the longest x34 47 us: swap(): lax.ppermute(array, axis, [(i, i ^ bit) for i in range(lax.axis_size(axis...]
    unnamed x10 -> x0, waiting for transfers between devices: 41 us -> none
  transfers between devices with their start and end apart: 13 -> 36, of which waited for: 3 -> 19; matrix products, arithmetic and copies ran while one was open for 46% -> 3% of each run, Pallas kernels for 0% -> 30%
where the time goes in v1:
time: 235 us; the launch traced here: 234 us
  Pallas kernels  101 us (43%)
  waiting for transfers between devices  66.1 us (28%)
  starting transfers between devices  52.2 us (22%)
  local copies, waits for them, and re-layouts  10 us (4%)
  other arithmetic  4.53 us (2%)
    pallas_call x3, Pallas kernels, run_kernel(): pl.pallas_call(body, out_shape=out_shape, in_specs=[SMEM] + [VMEM] * (len...  101 us
    ppermute x34, waiting for transfers between devices, swap(): lax.ppermute(array, axis, [(i, i ^ bit) for i in range(lax.axis_size(axis...  58 us
    ppermute x34, starting transfers between devices, swap(): lax.ppermute(array, axis, [(i, i ^ bit) for i in range(lax.axis_size(axis...  47 us
    ppermute x1, waiting for transfers between devices, per_device(): right = lax.ppermute(both[:, :HALO], 'seq', left_way)  6.3 us
    unnamed x29, local copies, waits for them, and re-layouts  5.38 us
  transfers between devices with their start and end apart: 36, of which 19 were waited for; matrix products, arithmetic and copies ran while one was open for 3% of the time, Pallas kernels for 30%

profile of v1, /device:TPU:0, one launch (start us, length us, event | category | flops | bytes accessed | tf_op | source)
XLA Modules:
  0.0 234.4 jit_solution(3920645364230746216)
XLA Ops:
  2.4 4.0 %collective-permute-start.3 = (bf16[16,1664]{1,0:T(8,128)(2,1)S(1)}, bf16[16,1664]{1,0:T(8,128)(2,1)S(1)}, u32[]{:S(2)}, u32[]{:S(2)}) collective-permute-start(bf16[16,1664]{1,0:T(8,128)(2,1)S(1)} %get-tuple-element.75), channel_id=1, source_target_pairs={{0,2},{1,3},{2,0},{3,1},{4,6},{5,7},{6,4},{7,5},{8,10},{9,11},{10,... | collective-permute-start | bytes 159752 | tf_op jit(solution)/shard_map/ppermute | solution.py:421
  9.0 2.0 collective-permute-start.13
  10.9 2.5 %collective-permute-start.12 = (bf16[144,512]{1,0:T(8,128)(2,1)S(1)}, bf16[144,512]{1,0:T(8,128)(2,1)S(1)}, u32[]{:S(2)}, u32[]{:S(2)}) collective-permute-start(bf16[144,512]{1,0:T(8,128)(2,1)S(1)} %get-tuple-element.69), channel_id=1, source_target_pairs={{0,1},{1,0},{2,3},{3,2},{4,5},{5,4},{6,7},{7,6},{8,9},{9,8},{10,11... | collective-permute-start | bytes 442376 | tf_op jit(solution)/shard_map/ppermute | solution.py:421
  14.6 8.4 %collective-permute-done.13 = bf16[144,512]{1,0:T(8,128)(2,1)S(1)} collective-permute-done((bf16[144,512]{1,0:T(8,128)(2,1)S(1)}, bf16[144,512]{1,0:T(8,128)(2,1)S(1)}, u32[]{:S(2)}, u32[]{:S(2)}) %collective-permute-start.13) | collective-permute-done | bytes 147488 | tf_op jit(solution)/shard_map/ppermute | solution.py:421
  23.1 2.5 %collective-permute-start.17 = (bf16[4,144,512]{2,1,0:T(8,128)(2,1)S(1)}, bf16[4,144,512]{2,1,0:T(8,128)(2,1)S(1)}, u32[]{:S(2)}, u32[]{:S(2)}) collective-permute-start(bf16[4,144,512]{2,1,0:T(8,128)(2,1)S(1)} %pad_maximum_fusion.refs_0_), channel_id=1, source_target_pairs={{0,24},{4,28},{8,16},{12,20},{16,8},{20,12},{24,0},{28,4},{1,25},{... | collective-permute-start | bytes 1769480 | tf_op jit(solution)/shard_map/ppermute | solution.py:421
  27.9 6.3 %collective-permute-done.1 = bf16[2,32,512]{2,1,0:T(8,128)(2,1)S(1)} collective-permute-done((bf16[2,32,512]{2,1,0:T(8,128)(2,1)S(1)}, bf16[2,32,512]{2,1,0:T(8,128)(2,1)S(1)}, u32[]{:S(2)}, u32[]{:S(2)}) %collective-permute-start.1) | collective-permute-done | bytes 65568 | tf_op jit(solution)/shard_map/ppermute | solution.py:485
  34.9 3.9 %collective-permute-start = (bf16[2,32,512]{2,1,0:T(8,128)(2,1)S(1)}, bf16[2,32,512]{2,1,0:T(8,128)(2,1)S(1)}, u32[]{:S(2)}, u32[]{:S(2)}) collective-permute-start(bf16[2,32,512]{2,1,0:T(8,128)(2,1)S(1)} %get-tuple-element.56), channel_id=1, source_target_pairs={{0,1},{1,2},{2,3},{4,5},{5,6},{6,7},{8,9},{9,10},{10,11},{12,13},{... | collective-permute-start | bytes 196616 | tf_op jit(solution)/shard_map/ppermute | solution.py:484
  38.8 1.9 collective-permute-done
  40.7 2.4 %collective-permute-start.7 = (bf16[4,16,1664]{2,1,0:T(8,128)(2,1)S(1)}, bf16[4,16,1664]{2,1,0:T(8,128)(2,1)}, u32[]{:S(2)}, u32[]{:S(2)}) collective-permute-start(bf16[4,16,1664]{2,1,0:T(8,128)(2,1)S(1)} %pad_maximum_fusion.1.refs_0_), channel_id=1, source_target_pairs={{0,24},{4,28},{8,16},{12,20},{16,8},{20,12},{24,0},{28,4},{1,25},{... | collective-permute-start | bytes 638984 | tf_op jit(solution)/shard_map/ppermute | solution.py:421
  43.6 11.8 %collective-permute-done.7.refs_3_ = bf16[4,16,1664]{2,1,0:T(8,128)(2,1)} collective-permute-done((bf16[4,16,1664]{2,1,0:T(8,128)(2,1)S(1)}, bf16[4,16,1664]{2,1,0:T(8,128)(2,1)}, u32[]{:S(2)}, u32[]{:S(2)}) %collective-permute-start.7) | collective-permute-done | bytes 213024 | tf_op jit(solution)/shard_map/ppermute | solution.py:421
  56.9 2.8 %collective-permute-done.6.refs_2_ = bf16[4,16,1664]{2,1,0:T(8,128)(2,1)S(1)} collective-permute-done((bf16[4,16,1664]{2,1,0:T(8,128)(2,1)S(1)}, bf16[4,16,1664]{2,1,0:T(8,128)(2,1)S(1)}, u32[]{:S(2)}, u32[]{:S(2)}) %collective-permute-start.6) | collective-permute-done | bytes 213024 | tf_op jit(solution)/shard_map/ppermute | solution.py:421
  67.1 36.9 %shard_map.195 = (f32[768,512]{1,0:T(8,128)}, bf16[768,1536]{1,0:T(8,128)(2,1)}, bf16[768,512]{1,0:T(8,128)(2,1)S(1)}, f32[768,512]{1,0:T(8,128)}, bf16[512,1664]{1,0:T(8,128)(2,1)}, /*index=5*/f32[8,512]{1,0:T(8,128)S(1)}) custom-call(s32[11]{0:T(128)S(1)} %pad_add_fusion.info, bf16[32,512]{1,0:T(8,128)(2,1)S(1)} %get-tuple-element.72.left, ...), custom_call_target="tpu_custom_call" | custom-call | flops 2415919104 | bytes 10502188 | tf_op jit(solution)/shard_map/pallas_call | solution.py:407
  106.0 29.3 %shard_map.196 = (bf16[704,512]{1,0:T(8,128)(2,1)}, f32[768,512]{1,0:T(8,128)}, bf16[768,512]{1,0:T(8,128)(2,1)}, f32[8,512]{1,0:T(8,128)S(1)}, bf16[4,4,144,512...) custom-call(s32[11]{0:T(128)S(1)} %pad_add_fusion.info, bf16[32,512]{1,0:T(8,128)(2,1)S(1)} %get-tuple-element.73.left, ...), custom_call_target="tpu_custom_call" | custom-call | flops 10871635968 | bytes 15695916 | tf_op jit(solution)/shard_map/pallas_call | solution.py:407
  136.6 34.4 %shard_map.197 = (bf16[704,512]{1,0:T(8,128)(2,1)}, bf16[4,4,16,1664]{3,2,1,0:T(8,128)(2,1)S(1)}, bf16[4,4,16,1664]{3,2,1,0:T(8,128)(2,1)S(1)}) custom-call(s32[11]{0:T(128)S(1)} %pad_add_fusion.info, f32[768,512]{1,0:T(8,128)S(1)} %copy-done.3, bf16[768,1536]{1,0:T(8,128)(2,1)} %get-tuple-element.29.qkv, f32[768,512]{1,0:T(8,128)} %get-tuple-element.30.probs_in, ...), custom_call_target="tpu_custom_call" | custom-call | flops 3623878656 | bytes 12025900 | tf_op jit(solution)/shard_map/pallas_call | solution.py:407
  171.3 2.1 collective-permute-done.22
  183.3 4.0 %collective-permute-done.25 = bf16[4,16,1664]{2,1,0:T(8,128)(2,1)S(1)} collective-permute-done((bf16[4,16,1664]{2,1,0:T(8,128)(2,1)S(1)}, bf16[4,16,1664]{2,1,0:T(8,128)(2,1)S(1)}, u32[]{:S(2)}, u32[]{:S(2)}) %collective-permute-start.25) | collective-permute-done | bytes 213024 | tf_op jit(solution)/shard_map/ppermute | solution.py:421
  187.4 2.1 collective-permute-done.24
  189.6 5.1 %collective-permute-start.26 = (bf16[16,1664]{1,0:T(8,128)(2,1)S(1)}, bf16[16,1664]{1,0:T(8,128)(2,1)S(1)}, u32[]{:S(2)}, u32[]{:S(2)}) collective-permute-start(bf16[16,1664]{1,0:T(8,128)(2,1)S(1)} %get-tuple-element.65), channel_id=1, source_target_pairs={{0,1},{1,0},{2,3},{3,2},{4,5},{5,4},{6,7},{7,6},{8,9},{9,8},{10,11... | collective-permute-start | bytes 159752 | tf_op jit(solution)/shard_map/ppermute | solution.py:421
  196.1 2.9 %collective-permute-done.30 = bf16[4,144,512]{2,1,0:T(8,128)(2,1)S(1)} collective-permute-done((bf16[4,144,512]{2,1,0:T(8,128)(2,1)S(1)}, bf16[4,144,512]{2,1,0:T(8,128)(2,1)S(1)}, u32[]{:S(2)}, u32[]{:S(2)}) %collective-permute-start.30) | collective-permute-done | bytes 589856 | tf_op jit(solution)/shard_map/ppermute | solution.py:421
  199.1 5.0 %collective-permute-start.27 = (bf16[16,1664]{1,0:T(8,128)(2,1)S(1)}, bf16[16,1664]{1,0:T(8,128)(2,1)S(1)}, u32[]{:S(2)}, u32[]{:S(2)}) collective-permute-start(bf16[16,1664]{1,0:T(8,128)(2,1)S(1)} %get-tuple-element.67), channel_id=1, source_target_pairs={{0,2},{1,3},{2,0},{3,1},{4,6},{5,7},{6,4},{7,5},{8,10},{9,11},{10,... | collective-permute-start | bytes 159752 | tf_op jit(solution)/shard_map/ppermute | solution.py:421
  204.1 8.1 %collective-permute-done.32 = bf16[4,144,512]{2,1,0:T(8,128)(2,1)S(1)} collective-permute-done((bf16[4,144,512]{2,1,0:T(8,128)(2,1)S(1)}, bf16[4,144,512]{2,1,0:T(8,128)(2,1)S(1)}, u32[]{:S(2)}, u32[]{:S(2)}) %collective-permute-start.32) | collective-permute-done | bytes 589856 | tf_op jit(solution)/shard_map/ppermute | solution.py:421
  213.9 5.1 %collective-permute-start.33 = (bf16[144,512]{1,0:T(8,128)(2,1)S(1)}, bf16[144,512]{1,0:T(8,128)(2,1)S(1)}, u32[]{:S(2)}, u32[]{:S(2)}) collective-permute-start(bf16[144,512]{1,0:T(8,128)(2,1)S(1)} %get-tuple-element.60), channel_id=1, source_target_pairs={{0,1},{1,0},{2,3},{3,2},{4,5},{5,4},{6,7},{7,6},{8,9},{9,8},{10,11... | collective-permute-start | bytes 442376 | tf_op jit(solution)/shard_map/ppermute | solution.py:421
  223.3 5.0 %collective-permute-done.35 = bf16[144,512]{1,0:T(8,128)(2,1)S(1)} collective-permute-done((bf16[144,512]{1,0:T(8,128)(2,1)S(1)}, bf16[144,512]{1,0:T(8,128)(2,1)S(1)}, u32[]{:S(2)}, u32[]{:S(2)}) %collective-permute-start.35) | collective-permute-done | bytes 147488 | tf_op jit(solution)/shard_map/ppermute | solution.py:421
  228.3 4.7 %collective-permute-done.34 = bf16[144,512]{1,0:T(8,128)(2,1)S(1)} collective-permute-done((bf16[144,512]{1,0:T(8,128)(2,1)S(1)}, bf16[144,512]{1,0:T(8,128)(2,1)S(1)}, u32[]{:S(2)}, u32[]{:S(2)}) %collective-permute-start.34) | collective-permute-done | bytes 147488 | tf_op jit(solution)/shard_map/ppermute | solution.py:421
  (105 shorter events, 40.3 us)
Async XLA Ops:
  2.4 11.0 %collective-permute-start.3 = (bf16[16,1664]{1,0:T(8,128)(2,1)S(1)}, bf16[16,1664]{1,0:T(8,128)(2,1)S(1)}, u32[]{:S(2)}, u32[]{:S(2)}) collective-permute-start(bf16[16,1664]{1,0:T(8,128)(2,1)S(1)} %get-tuple-element.75), channel_id=1, source_target_pairs={{0,2},{1,3},{2,0},{3,1},{4,6},{5,7},{6,4},{7,5},{8,10},{9,11},{10,... | collective-permute-start | bytes 159752 | tf_op jit(solution)/shard_map/ppermute | solution.py:421
  9.0 14.0 %collective-permute-start.13 = (bf16[144,512]{1,0:T(8,128)(2,1)S(1)}, bf16[144,512]{1,0:T(8,128)(2,1)S(1)}, u32[]{:S(2)}, u32[]{:S(2)}) collective-permute-start(bf16[144,512]{1,0:T(8,128)(2,1)S(1)} %get-tuple-element.69), channel_id=1, source_target_pairs={{0,2},{1,3},{2,0},{3,1},{4,6},{5,7},{6,4},{7,5},{8,10},{9,11},{10,... | collective-permute-start | bytes 442376 | tf_op jit(solution)/shard_map/ppermute | solution.py:421
  10.9 12.0 %collective-permute-start.12 = (bf16[144,512]{1,0:T(8,128)(2,1)S(1)}, bf16[144,512]{1,0:T(8,128)(2,1)S(1)}, u32[]{:S(2)}, u32[]{:S(2)}) collective-permute-start(bf16[144,512]{1,0:T(8,128)(2,1)S(1)} %get-tuple-element.69), channel_id=1, source_target_pairs={{0,1},{1,0},{2,3},{3,2},{4,5},{5,4},{6,7},{7,6},{8,9},{9,8},{10,11... | collective-permute-start | bytes 442376 | tf_op jit(solution)/shard_map/ppermute | solution.py:421
  13.4 9.6 %collective-permute-start.14 = (bf16[144,512]{1,0:T(8,128)(2,1)S(1)}, bf16[144,512]{1,0:T(8,128)(2,1)S(1)}, u32[]{:S(2)}, u32[]{:S(2)}) collective-permute-start(bf16[144,512]{1,0:T(8,128)(2,1)S(1)} %get-tuple-element.69), channel_id=1, source_target_pairs={{0,3},{1,2},{2,1},{3,0},{4,7},{5,6},{6,5},{7,4},{8,11},{9,10},{10,... | collective-permute-start | bytes 442376 | tf_op jit(solution)/shard_map/ppermute | solution.py:421
  14.5 28.6 %collective-permute-start.8 = (bf16[4,16,1664]{2,1,0:T(8,128)(2,1)S(1)}, bf16[4,16,1664]{2,1,0:T(8,128)(2,1)S(1)}, u32[]{:S(2)}, u32[]{:S(2)}) collective-permute-start(bf16[4,16,1664]{2,1,0:T(8,128)(2,1)S(1)} %pad_maximum_fusion.1.refs_0_), channel_id=1, source_target_pairs={{0,4},{4,0},{8,12},{12,8},{16,20},{20,16},{24,28},{28,24},{1,5},{5... | collective-permute-start | bytes 638984 | tf_op jit(solution)/shard_map/ppermute | solution.py:421
  23.1 39.3 %collective-permute-start.17 = (bf16[4,144,512]{2,1,0:T(8,128)(2,1)S(1)}, bf16[4,144,512]{2,1,0:T(8,128)(2,1)S(1)}, u32[]{:S(2)}, u32[]{:S(2)}) collective-permute-start(bf16[4,144,512]{2,1,0:T(8,128)(2,1)S(1)} %pad_maximum_fusion.refs_0_), channel_id=1, source_target_pairs={{0,24},{4,28},{8,16},{12,20},{16,8},{20,12},{24,0},{28,4},{1,25},{... | collective-permute-start | bytes 1769480 | tf_op jit(solution)/shard_map/ppermute | solution.py:421
  25.6 37.1 %collective-permute-start.16 = (bf16[4,144,512]{2,1,0:T(8,128)(2,1)S(1)}, bf16[4,144,512]{2,1,0:T(8,128)(2,1)S(1)}, u32[]{:S(2)}, u32[]{:S(2)}) collective-permute-start(bf16[4,144,512]{2,1,0:T(8,128)(2,1)S(1)} %pad_maximum_fusion.refs_0_), channel_id=1, source_target_pairs={{0,16},{4,20},{8,24},{12,28},{16,0},{20,4},{24,8},{28,12},{1,17},{... | collective-permute-start | bytes 1769480 | tf_op jit(solution)/shard_map/ppermute | solution.py:421
  26.1 36.8 %collective-permute-start.15 = (bf16[4,144,512]{2,1,0:T(8,128)(2,1)S(1)}, bf16[4,144,512]{2,1,0:T(8,128)(2,1)S(1)}, u32[]{:S(2)}, u32[]{:S(2)}) collective-permute-start(bf16[4,144,512]{2,1,0:T(8,128)(2,1)S(1)} %pad_maximum_fusion.refs_0_), channel_id=1, source_target_pairs={{0,8},{4,12},{8,0},{12,4},{16,24},{20,28},{24,16},{28,20},{1,9},{5... | collective-permute-start | bytes 1769480 | tf_op jit(solution)/shard_map/ppermute | solution.py:421
  40.7 14.7 %collective-permute-start.7 = (bf16[4,16,1664]{2,1,0:T(8,128)(2,1)S(1)}, bf16[4,16,1664]{2,1,0:T(8,128)(2,1)}, u32[]{:S(2)}, u32[]{:S(2)}) collective-permute-start(bf16[4,16,1664]{2,1,0:T(8,128)(2,1)S(1)} %pad_maximum_fusion.1.refs_0_), channel_id=1, source_target_pairs={{0,24},{4,28},{8,16},{12,20},{16,8},{20,12},{24,0},{28,4},{1,25},{... | collective-permute-start | bytes 638984 | tf_op jit(solution)/shard_map/ppermute | solution.py:421
  43.1 16.6 %collective-permute-start.6 = (bf16[4,16,1664]{2,1,0:T(8,128)(2,1)S(1)}, bf16[4,16,1664]{2,1,0:T(8,128)(2,1)S(1)}, u32[]{:S(2)}, u32[]{:S(2)}) collective-permute-start(bf16[4,16,1664]{2,1,0:T(8,128)(2,1)S(1)} %pad_maximum_fusion.1.refs_0_), channel_id=1, source_target_pairs={{0,16},{4,20},{8,24},{12,28},{16,0},{20,4},{24,8},{28,12},{1,17},{... | collective-permute-start | bytes 638984 | tf_op jit(solution)/shard_map/ppermute | solution.py:421
  61.3 43.6 %collective-permute-start.18 = (bf16[4,144,512]{2,1,0:T(8,128)(2,1)S(1)}, bf16[4,144,512]{2,1,0:T(8,128)(2,1)S(1)}, u32[]{:S(2)}, u32[]{:S(2)}) collective-permute-start(bf16[4,144,512]{2,1,0:T(8,128)(2,1)S(1)} %pad_maximum_fusion.refs_0_), channel_id=1, source_target_pairs={{0,4},{4,0},{8,12},{12,8},{16,20},{20,16},{24,28},{28,24},{1,5},{5... | collective-permute-start | bytes 1769480 | tf_op jit(solution)/shard_map/ppermute | solution.py:421
  62.3 42.6 %collective-permute-start.21 = (bf16[4,144,512]{2,1,0:T(8,128)(2,1)S(1)}, bf16[4,144,512]{2,1,0:T(8,128)(2,1)S(1)}, u32[]{:S(2)}, u32[]{:S(2)}) collective-permute-start(bf16[4,144,512]{2,1,0:T(8,128)(2,1)S(1)} %collective-permute-done.17.refs_3_), channel_id=1, source_target_pairs={{0,4},{4,0},{8,12},{12,8},{16,20},{20,16},{24,28},{28,24},{1,5},{5... | collective-permute-start | bytes 1769480 | tf_op jit(solution)/shard_map/ppermute | solution.py:421
  62.7 42.2 %collective-permute-start.20 = (bf16[4,144,512]{2,1,0:T(8,128)(2,1)S(1)}, bf16[4,144,512]{2,1,0:T(8,128)(2,1)S(1)}, u32[]{:S(2)}, u32[]{:S(2)}) collective-permute-start(bf16[4,144,512]{2,1,0:T(8,128)(2,1)S(1)} %collective-permute-done.16.refs_2_), channel_id=1, source_target_pairs={{0,4},{4,0},{8,12},{12,8},{16,20},{20,16},{24,28},{28,24},{1,5},{5... | collective-permute-start | bytes 1769480 | tf_op jit(solution)/shard_map/ppermute | solution.py:421
  62.8 42.1 %collective-permute-start.19 = (bf16[4,144,512]{2,1,0:T(8,128)(2,1)S(1)}, bf16[4,144,512]{2,1,0:T(8,128)(2,1)S(1)}, u32[]{:S(2)}, u32[]{:S(2)}) collective-permute-start(bf16[4,144,512]{2,1,0:T(8,128)(2,1)S(1)} %collective-permute-done.15.refs_1_), channel_id=1, source_target_pairs={{0,4},{4,0},{8,12},{12,8},{16,20},{20,16},{24,28},{28,24},{1,5},{5... | collective-permute-start | bytes 1769480 | tf_op jit(solution)/shard_map/ppermute | solution.py:421
  135.3 42.0 %collective-permute-start.29 = (bf16[4,4,144,512]{3,2,1,0:T(8,128)(2,1)}, bf16[4,4,144,512]{3,2,1,0:T(8,128)(2,1)S(1)}, u32[]{:S(2)}, u32[]{:S(2)}) collective-permute-start(bf16[4,4,144,512]{3,2,1,0:T(8,128)(2,1)} %get-tuple-element.39), channel_id=1, source_target_pairs={{0,4},{4,0},{8,12},{12,8},{16,20},{20,16},{24,28},{28,24},{1,5},{5... | collective-permute-start | bytes 7077896 | tf_op jit(solution)/shard_map/ppermute | solution.py:421
  175.2 12.1 %collective-permute-start.25 = (bf16[4,16,1664]{2,1,0:T(8,128)(2,1)S(1)}, bf16[4,16,1664]{2,1,0:T(8,128)(2,1)S(1)}, u32[]{:S(2)}, u32[]{:S(2)}) collective-permute-start(bf16[4,16,1664]{2,1,0:T(8,128)(2,1)S(1)} %get-tuple-element.58), channel_id=1, source_target_pairs={{0,24},{4,28},{8,16},{12,20},{16,8},{20,12},{24,0},{28,4},{1,25},{... | collective-permute-start | bytes 638984 | tf_op jit(solution)/shard_map/ppermute | solution.py:421
  176.7 12.7 %collective-permute-start.24 = (bf16[4,16,1664]{2,1,0:T(8,128)(2,1)S(1)}, bf16[4,16,1664]{2,1,0:T(8,128)(2,1)S(1)}, u32[]{:S(2)}, u32[]{:S(2)}) collective-permute-start(bf16[4,16,1664]{2,1,0:T(8,128)(2,1)S(1)} %get-tuple-element.59), channel_id=1, source_target_pairs={{0,16},{4,20},{8,24},{12,28},{16,0},{20,4},{24,8},{28,12},{1,17},{... | collective-permute-start | bytes 638984 | tf_op jit(solution)/shard_map/ppermute | solution.py:421
  178.3 20.8 %collective-permute-start.30 = (bf16[4,144,512]{2,1,0:T(8,128)(2,1)S(1)}, bf16[4,144,512]{2,1,0:T(8,128)(2,1)S(1)}, u32[]{:S(2)}, u32[]{:S(2)}) collective-permute-start(bf16[4,144,512]{2,1,0:T(8,128)(2,1)S(1)} %get-tuple-element.50), channel_id=1, source_target_pairs={{0,8},{4,12},{8,0},{12,4},{16,24},{20,28},{24,16},{28,20},{1,9},{5... | collective-permute-start | bytes 1769480 | tf_op jit(solution)/shard_map/ppermute | solution.py:421
  179.9 32.3 %collective-permute-start.32 = (bf16[4,144,512]{2,1,0:T(8,128)(2,1)S(1)}, bf16[4,144,512]{2,1,0:T(8,128)(2,1)S(1)}, u32[]{:S(2)}, u32[]{:S(2)}) collective-permute-start(bf16[4,144,512]{2,1,0:T(8,128)(2,1)S(1)} %get-tuple-element.51), channel_id=1, source_target_pairs={{0,24},{4,28},{8,16},{12,20},{16,8},{20,12},{24,0},{28,4},{1,25},{... | collective-permute-start | bytes 1769480 | tf_op jit(solution)/shard_map/ppermute | solution.py:421
  181.8 31.6 %collective-permute-start.31 = (bf16[4,144,512]{2,1,0:T(8,128)(2,1)S(1)}, bf16[4,144,512]{2,1,0:T(8,128)(2,1)S(1)}, u32[]{:S(2)}, u32[]{:S(2)}) collective-permute-start(bf16[4,144,512]{2,1,0:T(8,128)(2,1)S(1)} %get-tuple-element.52), channel_id=1, source_target_pairs={{0,16},{4,20},{8,24},{12,28},{16,0},{20,4},{24,8},{28,12},{1,17},{... | collective-permute-start | bytes 1769480 | tf_op jit(solution)/shard_map/ppermute | solution.py:421
  189.6 30.9 %collective-permute-start.26 = (bf16[16,1664]{1,0:T(8,128)(2,1)S(1)}, bf16[16,1664]{1,0:T(8,128)(2,1)S(1)}, u32[]{:S(2)}, u32[]{:S(2)}) collective-permute-start(bf16[16,1664]{1,0:T(8,128)(2,1)S(1)} %get-tuple-element.65), channel_id=1, source_target_pairs={{0,1},{1,0},{2,3},{3,2},{4,5},{5,4},{6,7},{7,6},{8,9},{9,8},{10,11... | collective-permute-start | bytes 159752 | tf_op jit(solution)/shard_map/ppermute | solution.py:421
  194.7 25.8 %collective-permute-start.28 = (bf16[16,1664]{1,0:T(8,128)(2,1)S(1)}, bf16[16,1664]{1,0:T(8,128)(2,1)S(1)}, u32[]{:S(2)}, u32[]{:S(2)}) collective-permute-start(bf16[16,1664]{1,0:T(8,128)(2,1)S(1)} %get-tuple-element.66), channel_id=1, source_target_pairs={{0,3},{1,2},{2,1},{3,0},{4,7},{5,6},{6,5},{7,4},{8,11},{9,10},{10,... | collective-permute-start | bytes 159752 | tf_op jit(solution)/shard_map/ppermute | solution.py:421
  199.1 21.5 %collective-permute-start.27 = (bf16[16,1664]{1,0:T(8,128)(2,1)S(1)}, bf16[16,1664]{1,0:T(8,128)(2,1)S(1)}, u32[]{:S(2)}, u32[]{:S(2)}) collective-permute-start(bf16[16,1664]{1,0:T(8,128)(2,1)S(1)} %get-tuple-element.67), channel_id=1, source_target_pairs={{0,2},{1,3},{2,0},{3,1},{4,6},{5,7},{6,4},{7,5},{8,10},{9,11},{10,... | collective-permute-start | bytes 159752 | tf_op jit(solution)/shard_map/ppermute | solution.py:421
  220.5 12.5 %collective-permute-start.34 = (bf16[144,512]{1,0:T(8,128)(2,1)S(1)}, bf16[144,512]{1,0:T(8,128)(2,1)S(1)}, u32[]{:S(2)}, u32[]{:S(2)}) collective-permute-start(bf16[144,512]{1,0:T(8,128)(2,1)S(1)} %get-tuple-element.62), channel_id=1, source_target_pairs={{0,2},{1,3},{2,0},{3,1},{4,6},{5,7},{6,4},{7,5},{8,10},{9,11},{10,... | collective-permute-start | bytes 442376 | tf_op jit(solution)/shard_map/ppermute | solution.py:421
  (26 other events, 264.9 us)

commit v2 on v1

--- a/solution.py
+++ b/solution.py
@@ -72,15 +72,49 @@
     )
 
 
+def window_at(w):
+    return pl.ds(pl.multiple_of(w * WIN, WIN), WIN)
+
+
+def tile_at(i):
+    return pl.ds(pl.multiple_of(i * TILE, TILE), TILE)
+
+
 def row_mask(low, high):
     index = lax.broadcasted_iota(jnp.int32, (WIN, 1), 0)
     return (index >= low) & (index < high)
 
 
-def pad_rows(ext, left, rows, right):
-    ext[0:HALO] = left[...].astype(F32)
-    ext[HALO : HALO + ROWS] = rows[...].astype(F32)
-    ext[HALO + ROWS :] = right[...].astype(F32)
+def copy_all(pairs, sems, first=0):
+    copies = [
+        pltpu.make_async_copy(source, target, sems.at[first + i])
+        for i, (source, target) in enumerate(pairs)
+    ]
+    for copy in copies:
+        copy.start()
+    return copies
+
+
+def wait_all(copies):
+    for copy in copies:
+        copy.wait()
+
+
+def row_copies(rows, near, far, column, stage, halos):
+    return [
+        (rows, stage),
+        (near.at[:, column : column + 2 * D], halos.at[0]),
+        (far.at[:, column : column + 2 * D], halos.at[1]),
+    ]
+
+
+def pad_rows(info, ext, stage, halos):
+    ext[HALO : HALO + ROWS] = stage[...].astype(F32)
+    odd = info[10] % 2 == 1
+    for i, is_left in enumerate((odd, jnp.logical_not(odd))):
+        at = pl.multiple_of(jnp.where(is_left, 0, HALO + ROWS), HALO)
+        ext[pl.ds(at, HALO // 2), :] = halos[i, :, 0:D].astype(F32)
+        ext[pl.ds(at + HALO // 2, HALO // 2), :] = halos[i, :, D : 2 * D].astype(F32)
 
 
 def normalized(values):
@@ -113,41 +147,42 @@
     )
 
 
-def place_blocks(info, pieces, order, scratch, rows, first=0):
-    for piece, partner in zip(pieces, order):
-        for k in range(piece.shape[0]):
-            owner = (info[9] ^ partner) * piece.shape[0] + (info[10] ^ k)
-            at = pl.multiple_of(owner * rows, rows)
-            scratch[pl.ds(at, rows), :] = piece[k, first : first + rows, :]
-
-
-def attention_kernel(direct, info, left, rows, right, *refs):
+def attention_kernel(direct, info, rows, near, far, *refs):
     pieces, refs = (refs[:8], refs[8:]) if direct else (refs[:1], refs[1:])
-    x_out, qkv_out, mixed_out, probs_out, w_out, norms_out, ext, normed = refs
-    if direct:
-        place_blocks(info, pieces, ORDER, w_out, pieces[0].shape[1])
-    else:
-        w_out[...] = pieces[0][...]
-    norms_out[...] = jnp.transpose(w_out[:, 3 * D :].astype(F32))[:8]
-    gain, shift = norms_out[0:1], norms_out[1:2]
-    pad_rows(ext, left, rows, right)
+    x_out, qkv_out, mixed_out, probs_out, w_out, norms_out, ext, stage, halos, sems = refs
+    column = w_out.shape[1] if direct else 0
+    row_copy = copy_all(row_copies(rows, near, far, column, stage, halos), sems)
+    if direct:
+        share, pairs = pieces[0].shape[1], []
+        for piece, partner in zip(pieces, ORDER):
+            for k in range(piece.shape[0]):
+                owner = (info[9] ^ partner) * piece.shape[0] + (info[10] ^ k)
+                at = pl.multiple_of(owner * share, share)
+                pairs.append((piece.at[k], w_out.at[pl.ds(at, share), :]))
+    else:
+        pairs = [(pieces[0], w_out)]
+    w_copy = copy_all(pairs, sems, len(row_copy))
+    wait_all(row_copy)
+    pad_rows(info, ext, stage, halos)
 
     def place(w, carry):
         row, low, high, _, _, _ = window_place(info, w)
         values = jnp.where(row_mask(low, high), ext[pl.ds(row, WIN), :], 0.0)
-        at = pl.ds(pl.multiple_of(w * WIN, WIN), WIN)
-        x_out[at, :] = values
-        unit, _ = normalized(values)
-        normed[at, :] = (unit * gain + shift).astype(BF16)
-        return carry
-
-    lax.fori_loop(0, WINDOWS, place, 0)
+        x_out[window_at(w), :] = values.astype(BF16)
+        return carry
+
+    lax.fori_loop(0, WINDOWS, place, 0, unroll=4)
+    wait_all(w_copy)
+    norms_out[...] = jnp.transpose(w_out[:, 3 * D :].astype(F32))[:8]
+    gain, shift = norms_out[0:1], norms_out[1:2]
 
     def project(i, carry):
-        at = pl.ds(pl.multiple_of(i * TILE, TILE), TILE)
+        at = tile_at(i)
+        unit, _ = normalized(x_out[at, :].astype(F32))
+        low = (unit * gain + shift).astype(BF16)
         for part in range(3):
             cols = slice(part * D, (part + 1) * D)
-            qkv_out[at, cols] = mm(normed[at, :], w_out[:, cols]).astype(BF16)
+            qkv_out[at, cols] = mm(low, w_out[:, cols]).astype(BF16)
         return carry
 
     lax.fori_loop(0, WROWS // TILE, project, 0)
@@ -163,21 +198,26 @@
         key_group = (key_freq + 4 - shift_freq) >> 2
         query_group = (query_freq + 4 - shift_freq) >> 2
         allowed = (key_group == query_group) & (key_row >= low) & (key_row < high)
-        for quad in range(D // QUAD):
-            cols = slice(quad * QUAD, (quad + 1) * QUAD)
-            query = qkv_out[at, cols]
+        quads = range(D // QUAD)
+        raw = []
+        for quad in quads:
+            query = qkv_out[at, quad * QUAD : (quad + 1) * QUAD]
             key = qkv_out[at, D + quad * QUAD : D + (quad + 1) * QUAD]
+            raw.append(mm_right(key, spread(query, masks)))
+        scores = [jnp.where(allowed, r * HEAD_DIM**-0.5, -1e30) for r in raw]
+        weights = [jnp.exp(s - jnp.max(s, axis=0, keepdims=True)) for s in scores]
+        probs = [(p / jnp.sum(p, axis=0, keepdims=True)).astype(BF16) for p in weights]
+        products = []
+        for quad in quads:
+            probs_out[at, quad * QUAD : (quad + 1) * QUAD] = probs[quad]
             value = qkv_out[at, 2 * D + quad * QUAD : 2 * D + (quad + 1) * QUAD]
-            raw = mm_right(key, spread(query, masks))
-            scores = jnp.where(allowed, raw * HEAD_DIM**-0.5, -1e30)
-            weights = jnp.exp(scores - jnp.max(scores, axis=0, keepdims=True))
-            probs = weights / jnp.sum(weights, axis=0, keepdims=True)
-            probs_out[at, cols] = probs
-            mixed = gathered(mm_left(probs.astype(BF16), value), lane)
-            mixed_out[at, cols] = mixed.astype(BF16)
-        return carry
-
-    lax.fori_loop(0, WINDOWS, attend, 0)
+            products.append(mm_left(probs[quad], value))
+        for quad in quads:
+            mixed = gathered(products[quad], lane).astype(BF16)
+            mixed_out[at, quad * QUAD : (quad + 1) * QUAD] = mixed
+        return carry
+
+    lax.fori_loop(0, WINDOWS, attend, 0, unroll=4)
 
 
 def gelu_parts(values):
@@ -195,30 +235,42 @@
     return jnp.where(values >= 0, 1.0 - tail, tail), half_exp * 0.3989422804014327
 
 
-def feed_kernel(direct, info, left, rows, right, x_in, mixed_in, norms, *refs):
-    pieces, refs = (refs[:8], refs[8:]) if direct else (refs[:3], refs[3:])
+def feed_kernel(direct, info, rows, near, far, x_in, mixed_in, norms, *refs):
+    pieces, refs = (refs[:16], refs[16:]) if direct else (refs[:3], refs[3:])
     out, grad_middle, grad_mixed, grad_norms = refs[:4]
     if direct:
         (keep, send), refs = refs[4:6], refs[6:]
     else:
         (grad_up_out, grad_down_out, grad_w_out), refs = refs[4:7], refs[7:]
-    up, down, w_out, ext, cot, cot_own, own, middle, total, normed, normed_own, hidden, pre, grad = refs
-    if direct:
-        count = pieces[0].shape[0]
+    up, down, w_out, ext, cot, cot_own, own, middle, total, normed, normed_own, hidden, pre, grad = refs[:14]
+    stage, halos, sems = refs[14:]
+    column = near.shape[1] - 2 * D
+    row_copy = copy_all(row_copies(rows, near, far, column, stage, halos), sems)
+    if direct:
+        count = CHUNKS
         block = D // 8
-        for piece, partner in zip(pieces, ORDER):
+        out_pairs, pairs = [], [[], []]
+        for piece, partner, base in zip(pieces, ORDER * 2, (0,) * 8 + (1,) * 8):
             dp = info[9] ^ partner
-            at = pl.multiple_of(dp * block, block)
-            for k in range(count):
-                up[k, pl.ds(at, block), :] = piece[k, 0:block, :]
-                down[k, pl.ds(at, block), :] = piece[k, block : 2 * block, :]
+            at = pl.ds(pl.multiple_of(dp * block, block), block)
+            ks = slice(base, base + piece.shape[0])
+            pairs[base].append((piece.at[:, 0:block, :], up.at[ks, at, :]))
+            pairs[base].append((piece.at[:, block : 2 * block, :], down.at[ks, at, :]))
+            for k in range(base, base + piece.shape[0]):
                 row = pl.multiple_of((dp * count + (info[10] ^ k)) * 16, 16)
-                w_out[pl.ds(row, 16), :] = piece[k, 2 * block :, :]
-    else:
-        up[...] = pieces[0][...]
-        down[...] = pieces[1][...]
-        w_out[...] = pieces[2][...]
-    pad_rows(ext, left, rows, right)
+                out_pairs.append(
+                    (piece.at[k - base, 2 * block : 2 * block + 16, :], w_out.at[pl.ds(row, 16), :])
+                )
+    else:
+        pairs = [[(pieces[0], up), (pieces[1], down)], []]
+        out_pairs = [(pieces[2], w_out)]
+    at = len(row_copy)
+    out_copy = copy_all(out_pairs, sems, at)
+    at += len(out_pairs)
+    first_copy = copy_all(pairs[0], sems, at)
+    rest_copy = copy_all(pairs[1], sems, at + len(pairs[0]))
+    wait_all(row_copy)
+    pad_rows(info, ext, stage, halos)
 
     def place(w, carry):
         row, low, high, own_low, own_high, _ = window_place(info, w)
@@ -229,15 +281,13 @@
         own[at, :] = jnp.where(row_mask(own_low, own_high), jnp.ones((WIN, QUAD), F32), 0.0)
         return carry
 
-    lax.fori_loop(0, WINDOWS, place, 0)
+    lax.fori_loop(0, WINDOWS, place, 0, unroll=4)
     gain, shift = norms[2:3], norms[3:4]
-
-    def tile_of(i):
-        return pl.ds(pl.multiple_of(i * TILE, TILE), TILE)
+    wait_all(out_copy)
 
     def before(i, carry):
-        at = tile_of(i)
-        values = x_in[at, :] + mm(mixed_in[at, :], w_out[...])
+        at = tile_at(i)
+        values = x_in[at, :].astype(F32) + mm(mixed_in[at, :], w_out[...])
         middle[at, :] = values
         total[at, :] = values
         unit, _ = normalized(values)
@@ -249,27 +299,23 @@
 
     lax.fori_loop(0, WROWS // TILE, before, 0)
 
-    def chunk_step(c, carry):
-        up_c, down_c = up[c], down[c]
-
-        def row_step(i, inner):
-            at = tile_of(i)
-            values = mm(normed[at, :], up_c)
-            grad_hidden = mm(cot[at, :], down_c)
-            below, density = gelu_parts(values)
-            hidden_low = (values * below).astype(BF16)
-            grad_low = (grad_hidden * (below + values * density)).astype(BF16)
-            hidden[at, :] = hidden_low
-            pre[at, :] = grad_low
-            total[at, :] += mm_right(hidden_low, down_c)
-            grad[at, :] += mm_right(grad_low, up_c)
-            return inner
-
-        lax.fori_loop(0, WROWS // TILE, row_step, 0)
-        return carry
+    def row_step(c, i):
+        at = tile_at(i)
+        values = mm(normed[at, :], up[c])
+        grad_hidden = mm(cot[at, :], down[c])
+        below, density = gelu_parts(values)
+        hidden_low = (values * below).astype(BF16)
+        grad_low = (grad_hidden * (below + values * density)).astype(BF16)
+        hidden[at, :] = hidden_low
+        pre[at, :] = grad_low
+        total[at, :] += mm_right(hidden_low, down[c])
+        grad[at, :] += mm_right(grad_low, up[c])
 
     for c in range(CHUNKS):
-        chunk_step(c, 0)
+        if c < 2:
+            wait_all((first_copy, rest_copy)[c])
+        for i in range(WROWS // TILE):
+            row_step(c, i)
         grad_up = mm_left(normed_own[...], pre[...])
         grad_down = mm_left(cot_own[...], hidden[...])
         if direct:
@@ -291,7 +337,7 @@
     grad_norms[...] = jnp.zeros(grad_norms.shape, F32)
 
     def after(i, carry):
-        at = tile_of(i)
+        at = tile_at(i)
         unit, scale = normalized(middle[at, :])
         part = grad[at, :]
         masked = part * own[at, 0:1]
@@ -326,7 +372,7 @@
         ext[place, :] = jnp.where(row_mask(low, high), values[at, :], ext[place, :])
         return carry
 
-    lax.fori_loop(0, WINDOWS, back, 0)
+    lax.fori_loop(0, WINDOWS, back, 0, unroll=4)
     out[...] = ext[HALO : HALO + ROWS].astype(BF16)
 
 
@@ -338,48 +384,54 @@
         (keep, send), refs = refs[:2], refs[2:]
     else:
         w_grad, refs = refs[0], refs[1:]
-    ext, normed, grad_qkv, result, gains, grad_w = refs
+    ext, normed, grad_qkv, result, gains, grad_w, own = refs
     masks = head_masks()
     lane = lax.broadcasted_iota(jnp.int32, (1, QUAD), 1) // HEAD_DIM
 
     def attend_back(w, carry):
-        at = pl.ds(pl.multiple_of(w * WIN, WIN), WIN)
-        for quad in range(D // QUAD):
-            cols = slice(quad * QUAD, (quad + 1) * QUAD)
-            cols_key = slice(D + quad * QUAD, D + (quad + 1) * QUAD)
-            cols_value = slice(2 * D + quad * QUAD, 2 * D + (quad + 1) * QUAD)
-            query = spread(qkv[at, cols], masks)
-            key = qkv[at, cols_key]
-            value = qkv[at, cols_value]
-            grad_out = spread(grad_mixed[at, cols], masks)
-            probs = probs_in[at, cols]
-            grad_probs = mm_right(value, grad_out)
-            delta = jnp.sum(probs * grad_probs, axis=0, keepdims=True)
-            grad_scores = (probs * (grad_probs - delta) * HEAD_DIM**-0.5).astype(BF16)
-            grad_qkv[at, cols] = gathered(mm_left(grad_scores, key), lane).astype(BF16)
-            grad_qkv[at, cols_key] = mm(grad_scores, query).astype(BF16)
-            grad_qkv[at, cols_value] = mm(probs.astype(BF16), grad_out).astype(BF16)
-        return carry
-
-    lax.fori_loop(0, WINDOWS, attend_back, 0)
+        at = window_at(w)
+        own[at, :] = jnp.where(
+            row_mask(*window_place(info, w)[3:5]), jnp.ones((WIN, QUAD), F32), 0.0
+        )
+        quads = range(D // QUAD)
+        cols = [slice(quad * QUAD, (quad + 1) * QUAD) for quad in quads]
+        cols_key = [slice(D + quad * QUAD, D + (quad + 1) * QUAD) for quad in quads]
+        cols_value = [slice(2 * D + quad * QUAD, 2 * D + (quad + 1) * QUAD) for quad in quads]
+        grad_out = [spread(grad_mixed[at, c], masks) for c in cols]
+        grad_probs = [mm_right(qkv[at, c], g) for c, g in zip(cols_value, grad_out)]
+        low = [probs_in[at, c] for c in cols]
+        probs = [p.astype(F32) for p in low]
+        delta = [jnp.sum(p * g, axis=0, keepdims=True) for p, g in zip(probs, grad_probs)]
+        grad_scores = [
+            (p * (g - d) * HEAD_DIM**-0.5).astype(BF16)
+            for p, g, d in zip(probs, grad_probs, delta)
+        ]
+        grad_value = [mm(p, g) for p, g in zip(low, grad_out)]
+        grad_query = [mm_left(g, qkv[at, c]) for g, c in zip(grad_scores, cols_key)]
+        grad_key = [mm(g, spread(qkv[at, c], masks)) for g, c in zip(grad_scores, cols)]
+        for quad in quads:
+            grad_qkv[at, cols_value[quad]] = grad_value[quad].astype(BF16)
+            grad_qkv[at, cols_key[quad]] = grad_key[quad].astype(BF16)
+            grad_qkv[at, cols[quad]] = gathered(grad_query[quad], lane).astype(BF16)
+        return carry
+
+    lax.fori_loop(0, WINDOWS, attend_back, 0, unroll=4)
     gain, shift = norms[0:1], norms[1:2]
     gains[...] = jnp.zeros(gains.shape, F32)
-    index = lax.broadcasted_iota(jnp.int32, (WIN, 1), 0)
-
-    def mask_step(w, carry):
-        _, _, _, own_low, own_high, _ = window_place(info, w)
-        at = pl.ds(pl.multiple_of(w * WIN, WIN), WIN)
-        own = ((index >= own_low) & (index < own_high)).astype(F32)
-        unit, scale = normalized(x_in[at, :])
-        normed[at, :] = ((unit * gain + shift) * own).astype(BF16)
+
+    def after(i, carry):
+        at = tile_at(i)
+        unit, scale = normalized(x_in[at, :].astype(F32))
+        mask = own[at, 0:1]
+        normed[at, :] = ((unit * gain + shift) * mask).astype(BF16)
         part = mm_right(grad_qkv[at, :], w_qkv[:, : 3 * D])
-        masked = part * own
+        masked = part * mask
         gains[0:1] += jnp.sum(masked * unit, axis=0, keepdims=True)
         gains[1:2] += jnp.sum(masked, axis=0, keepdims=True)
         result[at, :] = grad_middle[at, :] + norm_back(part * gain, unit, scale)
         return carry
 
-    lax.fori_loop(0, WINDOWS, mask_step, 0)
+    lax.fori_loop(0, WROWS // TILE, after, 0)
     gains[2:4] = grad_norms[0:2]
     for part in range(3):
         cols = slice(part * D, (part + 1) * D)
@@ -398,47 +450,64 @@
 
 
 ORDER = (0, 2, 4, 6, 1, 3, 5, 7)
+LIMIT = 36 * 1024 * 1024
 SMEM = pl.BlockSpec(memory_space=pltpu.SMEM)
 VMEM = pl.BlockSpec(memory_space=pltpu.VMEM)
-
-
-def run_kernel(body, out_shape, scratch, flops, *operands):
-    moved = sum(a.size * a.dtype.itemsize for a in (*operands, *out_shape))
+ANY = pl.BlockSpec(memory_space=pl.ANY)
+
+
+def near_core(array):
+    return pltpu.with_memory_space_constraint(array, pltpu.VMEM)
+
+
+def far_core(array):
+    return pltpu.with_memory_space_constraint(array, pltpu.HBM)
+
+
+def run_kernel(body, out_shape, scratch, flops, info, vmem, hbm):
+    operands = (*hbm[:3], *vmem, *hbm[3:])
+    specs = [ANY] * len(hbm[:3]) + [VMEM] * len(vmem) + [ANY] * len(hbm[3:])
+    placed = [near_core(a) if s is VMEM else far_core(a) for a, s in zip(operands, specs)]
+    moved = sum(a.size * a.dtype.itemsize for a in operands)
     return pl.pallas_call(
         body,
         out_shape=out_shape,
-        in_specs=[SMEM] + [VMEM] * (len(operands) - 1),
+        in_specs=[SMEM] + specs,
         out_specs=[VMEM] * len(out_shape),
         scratch_shapes=scratch,
         cost_estimate=pl.CostEstimate(
             flops=flops, bytes_accessed=moved, transcendentals=flops // 1024
         ),
-        compiler_params=pltpu.CompilerParams(vmem_limit_bytes=50 * 1024 * 1024),
-    )(*operands)
+        compiler_params=pltpu.CompilerParams(vmem_limit_bytes=LIMIT),
+    )(info, *placed)
 
 
 def swap(array, axis, bit):
     return lax.ppermute(array, axis, [(i, i ^ bit) for i in range(lax.axis_size(axis))])
 
 
-def spread_out(shard):
-    column = jnp.stack([shard] + [swap(shard, "seq", k) for k in range(1, lax.axis_size("seq"))])
-    plane = [column] + [swap(column, "dp", partner) for partner in (2, 4, 6)]
-    return plane + [swap(piece, "dp", 1) for piece in plane]
-
-
-def collect(keep, send):
-    pair = keep.astype(F32) + swap(send, "dp", 1).astype(F32)
-    low = pair.astype(BF16)
-    parts = [swap(low[m], "dp", 2 * m) for m in (1, 2, 3)]
-    column = pair[0] + sum(part.astype(F32) for part in parts)
-    low = column.astype(BF16)
-    parts = [swap(low[k], "seq", k) for k in range(1, column.shape[0])]
-    return column[0] + sum(part.astype(F32) for part in parts)
+def together(*values):
+    return lax.optimization_barrier(values)
+
+
+def along_seq(shard):
+    return [swap(shard, "seq", k) for k in (1, 2, 3)]
+
+
+def along_plane(column):
+    return [swap(column, "dp", partner) for partner in (2, 4, 6)]
+
+
+def along_core(pieces):
+    return [swap(piece, "dp", 1) for piece in pieces]
+
+
+def add_parts(own, parts):
+    return own.astype(F32) + sum(part.astype(F32) for part in parts)
 
 
 def shape(dims, kind):
-    return jax.ShapeDtypeStruct(dims, kind)
+    return pltpu.VMEM(dims, kind)
 
 
 def per_device(
@@ -469,41 +538,66 @@
     norms = jnp.stack([norm1_gain, norm1_shift, norm2_gain, norm2_shift], axis=1)
     first = jnp.concatenate([w_qkv, jnp.pad(norms, ((0, 0), (0, NORMS - 4)))], axis=1)
     width = first.shape[1]
+    head = [a[i : i + HALO // 2] for a in (tokens, cotangent) for i in (0, HALO // 2)]
+    tail = [a[i : i + HALO // 2] for a in (tokens, cotangent) for i in (ROWS - HALO, ROWS - HALO // 2)]
+    head, tail = jnp.concatenate(head, axis=1), jnp.concatenate(tail, axis=1)
+    odd = lax.axis_index("seq") % 2 == 1
+    to_near, to_far = jnp.where(odd, head, tail), jnp.where(odd, tail, head)
     if direct:
         second = jnp.concatenate([w_up, w_down.T, w_out], axis=0)
-        first_all = spread_out(first)
-        second_all = spread_out(second)
+        with_near = jnp.concatenate([first, to_near], axis=1)
+        with_far = jnp.concatenate([first, to_far], axis=1)
+        near, middle, far, *second_own = together(
+            swap(with_near, "seq", 1),
+            swap(first, "seq", 2),
+            swap(with_far, "seq", 3),
+            *along_plane(second),
+        )
+        column = jnp.stack([first, near[:, :width], middle, far[:, :width]])
+        second_own = [second] + second_own
+        column, second = together(column, second)
+        results = together(*along_plane(column), *along_seq(second), *along_core(second_own))
+        first_plane, rest, second_own = [column, *results[:3]], results[3:6], second_own + [*results[6:]]
+        rest = jnp.stack(rest)
+        *first_plane, rest = together(*first_plane, rest)
+        first_all = first_plane + along_core(first_plane)
+        second_plane = along_plane(rest)
     else:
         first_all = [lax.all_gather(first, ("dp", "seq"), axis=0, tiled=True)]
         up_all = lax.all_gather(lax.all_gather(w_up, "dp", axis=0, tiled=True), "seq", axis=0)
         down_all = lax.all_gather(lax.all_gather(w_down.T, "dp", axis=0, tiled=True), "seq", axis=0)
         second_all = [up_all, down_all, lax.all_gather(w_out, ("dp", "seq"), axis=0, tiled=True)]
-    both = jnp.stack([tokens, cotangent])
-    right_way = [(i, i + 1) for i in range(n_seq - 1)]
-    left_way = [(i + 1, i) for i in range(n_seq - 1)]
-    left = lax.ppermute(both[:, ROWS - HALO :], "seq", right_way)
-    right = lax.ppermute(both[:, :HALO], "seq", left_way)
+        from_left = lax.ppermute(tail, "seq", [(i, i + 1) for i in range(n_seq - 1)])
+        from_right = lax.ppermute(head, "seq", [(i + 1, i) for i in range(n_seq - 1)])
+        near, far = jnp.where(odd, from_left, from_right), jnp.where(odd, from_right, from_left)
 
     x, qkv, mixed, probs, w_qkv_all, norms_all = run_kernel(
         functools.partial(attention_kernel, direct),
         [
-            shape((WROWS, D), F32),
+            shape((WROWS, D), BF16),
             shape((WROWS, 3 * D), BF16),
             shape((WROWS, D), BF16),
-            shape((WROWS, D), F32),
+            shape((WROWS, D), BF16),
             shape((D, width), BF16),
             shape((8, D), F32),
         ],
-        [pltpu.VMEM((ROWS + 2 * HALO, D), F32), pltpu.VMEM((WROWS, D), BF16)],
+        [
+            pltpu.VMEM((ROWS + 2 * HALO, D), F32),
+            pltpu.VMEM((ROWS, D), BF16),
+            pltpu.VMEM((2, HALO // 2, 2 * D), BF16),
+            pltpu.SemaphoreType.DMA((35,)),
+        ],
         2 * WROWS * D * 3 * D * 2,
         info,
-        left[0],
-        tokens,
-        right[0],
-        *first_all,
-    )
-    if direct:
-        block = (4, n_seq, 2 * (D // 8) + 16, CHUNK)
+        (),
+        (tokens, near, far, *first_all),
+    )
+    if direct:
+        *second_plane, mixed = together(*second_plane, mixed)
+        second_plane = [rest, *second_plane]
+        second_all = second_own + second_plane + along_core(second_plane)
+        second_all = [a.reshape(-1, *second.shape) for a in second_all]
+        block = (4, n_seq, *second.shape)
         grads_shape = [shape(block, BF16)] * 2
     else:
         grads_shape = [shape((CHUNKS, D, CHUNK), F32)] * 2 + [shape((D, D), F32)]
@@ -531,22 +625,21 @@
             pltpu.VMEM((WROWS, CHUNK), BF16),
             pltpu.VMEM((WROWS, CHUNK), BF16),
             pltpu.VMEM((WROWS, D), F32),
+            pltpu.VMEM((ROWS, D), BF16),
+            pltpu.VMEM((2, HALO // 2, 2 * D), BF16),
+            pltpu.SemaphoreType.DMA((67,)),
         ],
         2 * WROWS * D * (6 * FF + 3 * D),
         info,
-        left[1],
-        cotangent,
-        right[1],
-        x,
-        mixed,
-        norms_all,
-        *second_all,
-    )
-    if direct:
-        second_sum = collect(*grads)
-        grad_up = second_sum[: D // 8]
-        grad_down = second_sum[D // 8 : D // 4].T
-        grad_out = second_sum[D // 4 :]
+        (x, mixed, norms_all),
+        (cotangent, near, far, *second_all),
+    )
+    if direct:
+        pair = add_parts(grads[0], along_core(grads[1:]))
+        second_pair, low_own, low_rest, grad_mixed = together(
+            pair[0], pair[1:, 0].astype(BF16), pair[1:, 1:].astype(BF16), grad_mixed
+        )
+        second_parts = [swap(low_rest[m], "dp", 2 * m + 2) for m in range(3)]
         grads_shape = [shape((4, n_seq, share, width), BF16)] * 2
     else:
         grad_up = lax.psum_scatter(grads[0], "seq", scatter_dimension=0)
@@ -565,20 +658,35 @@
             pltpu.VMEM((WROWS, D), F32),
             pltpu.VMEM((NORMS, D), F32),
             pltpu.VMEM((D, width), F32),
+            pltpu.VMEM((WROWS, QUAD), F32),
         ],
         2 * WROWS * D * (6 * D + 3 * D),
         info,
-        x,
-        qkv,
-        probs,
-        grad_mixed,
-        grad_middle,
-        w_qkv_all,
-        norms_all,
-        grad_norms,
-    )
-    if direct:
-        first_sum = collect(*grads)
+        (x, qkv, probs, grad_mixed, grad_middle, w_qkv_all, norms_all, grad_norms),
+        (),
+    )
+    if direct:
+        keep, send, *second_parts = together(*grads, *second_parts)
+        pair = add_parts(keep, along_core([send]))
+        low, first_own, second_rest = together(
+            pair[1:].astype(BF16), pair[0], add_parts(second_pair[1:], second_parts)
+        )
+        second_low = second_rest.astype(BF16)
+        parts = together(
+            *[swap(low[m], "dp", 2 * m + 2) for m in range(3)],
+            *[swap(second_low[k], "seq", k + 1) for k in range(3)],
+        )
+        first_column = add_parts(first_own, parts[:3])
+        low, low_own, first_own = together(
+            first_column[1:].astype(BF16), low_own, first_column[0]
+        )
+        first_parts = [swap(low[k], "seq", k + 1) for k in range(3)]
+        own_parts = [swap(low_own[m], "dp", 2 * m + 2) for m in range(3)]
+        second_sum = add_parts(second_pair[0], [*parts[3:], *own_parts])
+        first_sum = add_parts(first_own, first_parts)
+        grad_up = second_sum[: D // 8]
+        grad_down = second_sum[D // 8 : D // 4].T
+        grad_out = second_sum[D // 4 :]
     else:
         first_sum = lax.psum_scatter(grads[0], ("dp", "seq"), scatter_dimension=0, tiled=True)
     return (

time: 235 us -> 156 us (0.66)
  Pallas kernels: 101 us -> 48.7 us
  waiting for transfers between devices: 66.1 us -> 43.3 us
  starting transfers between devices: 52.2 us -> 49.3 us
  local copies, waits for them, and re-layouts: 10 us -> 7.21 us
    pallas_call x3, Pallas kernels: 101 us -> 48.7 us  [run_kernel(): pl.pallas_call(body, out_shape=out_shape, in_specs=[SMEM] + specs, out_sp...]
    ppermute x34 -> x44, waiting for transfers between devices: 58 us -> 43.3 us  [swap(): lax.ppermute(array, axis, [(i, i ^ bit) for i in range(lax.axis_size(axis...]
    ppermute x2 -> x0, waiting for transfers between devices: 8.19 us -> none  [the longest x1 6.3 us: per_device(): right = lax.ppermute(both[:, :HALO], 'seq', left_way)]
    ppermute x2 -> x0, starting transfers between devices: 5.2 us -> none  [the longest x1 3.91 us: per_device(): left = lax.ppermute(both[:, ROWS - HALO:], 'seq', right_way)]
    unnamed x29 -> x55, local copies, waits for them, and re-layouts: 5.38 us -> 2.86 us
    ppermute x34 -> x44, starting transfers between devices: 47 us -> 49.3 us  [swap(): lax.ppermute(array, axis, [(i, i ^ bit) for i in range(lax.axis_size(axis...]
  transfers between devices with their start and end apart: 36 -> 44, of which waited for: 19 -> 25; matrix products, arithmetic and copies ran while one was open for 3% -> 5% of each run, Pallas kernels for 30% -> 17%
where the time goes in v2:
time: 156 us; the launch traced here: 155 us
  starting transfers between devices  49.3 us (32%)
  Pallas kernels  48.7 us (31%)
  waiting for transfers between devices  43.3 us (28%)
  local copies, waits for them, and re-layouts  7.21 us (5%)
  other arithmetic  5.71 us (4%)
    ppermute x44, starting transfers between devices, swap(): lax.ppermute(array, axis, [(i, i ^ bit) for i in range(lax.axis_size(axis...  49.3 us
    pallas_call x3, Pallas kernels, run_kernel(): pl.pallas_call(body, out_shape=out_shape, in_specs=[SMEM] + specs, out_sp...  48.7 us
    ppermute x44, waiting for transfers between devices, swap(): lax.ppermute(array, axis, [(i, i ^ bit) for i in range(lax.axis_size(axis...  43.3 us
  transfers between devices with their start and end apart: 44, of which 25 were waited for; matrix products, arithmetic and copies ran while one was open for 5% of the time, Pallas kernels for 17%

profile of v2, /device:TPU:0, one launch (start us, length us, event | category | flops | bytes accessed | tf_op | source)
XLA Modules:
  0.0 155.3 jit_solution(10115491859601257481)
XLA Ops:
  2.2 3.9 %collective-permute-start.5 = (bf16[144,512]{1,0:T(8,128)(2,1)S(1)}, bf16[144,512]{1,0:T(8,128)(2,1)S(1)}, u32[]{:S(2)}, u32[]{:S(2)}) collective-permute-start(bf16[144,512]{1,0:T(8,128)(2,1)S(1)} %get-tuple-element.77), channel_id=1, source_target_pairs={{0,24},{4,28},{8,16},{12,20},{16,8},{20,12},{24,0},{28,4},{1,25},{... | collective-permute-start | bytes 442376 | tf_op jit(solution)/shard_map/ppermute | solution.py:486
  8.3 3.1 %collective-permute-start.1 = (bf16[16,1664]{1,0:T(8,128)(2,1)S(1)}, bf16[16,1664]{1,0:T(8,128)(2,1)S(1)}, u32[]{:S(2)}, u32[]{:S(2)}) collective-permute-start(bf16[16,1664]{1,0:T(8,128)(2,1)S(1)} %get-tuple-element.172), channel_id=1, source_target_pairs={{0,2},{1,3},{2,0},{3,1},{4,6},{5,7},{6,4},{7,5},{8,10},{9,11},{10,... | collective-permute-start | bytes 159752 | tf_op jit(solution)/shard_map/ppermute | solution.py:486
  14.5 2.5 %collective-permute-start = (bf16[16,3712]{1,0:T(8,128)(2,1)S(1)}, bf16[16,3712]{1,0:T(8,128)(2,1)S(1)}, u32[]{:S(2)}, u32[]{:S(2)}) collective-permute-start(bf16[16,3712]{1,0:T(8,128)(2,1)S(1)} %get-tuple-element.174), channel_id=1, source_target_pairs={{0,1},{1,0},{2,3},{3,2},{4,5},{5,4},{6,7},{7,6},{8,9},{9,8},{10,11... | collective-permute-start | bytes 356360 | tf_op jit(solution)/shard_map/ppermute | solution.py:486
  17.0 3.3 %collective-permute-done.2.far = bf16[16,3712]{1,0:T(8,128)(2,1)S(1)} collective-permute-done((bf16[16,3712]{1,0:T(8,128)(2,1)S(1)}, bf16[16,3712]{1,0:T(8,128)(2,1)S(1)}, u32[]{:S(2)}, u32[]{:S(2)}) %collective-permute-start.2) | collective-permute-done | bytes 118816 | tf_op jit(solution)/shard_map/ppermute | solution.py:486
  21.2 3.6 %collective-permute-start.11 = (bf16[144,512]{1,0:T(8,128)(2,1)S(1)}, bf16[144,512]{1,0:T(8,128)(2,1)S(1)}, u32[]{:S(2)}, u32[]{:S(2)}) collective-permute-start(bf16[144,512]{1,0:T(8,128)(2,1)S(1)} %get-tuple-element.77), channel_id=1, source_target_pairs={{0,3},{1,2},{2,1},{3,0},{4,7},{5,6},{6,5},{7,4},{8,11},{9,10},{10,... | collective-permute-start | bytes 442376 | tf_op jit(solution)/shard_map/ppermute | solution.py:486
  25.7 2.5 %collective-permute-start.8 = (bf16[4,16,1664]{2,1,0:T(8,128)(2,1)S(1)}, bf16[4,16,1664]{2,1,0:T(8,128)(2,1)S(1)}, u32[]{:S(2)}, u32[]{:S(2)}) collective-permute-start(bf16[4,16,1664]{2,1,0:T(8,128)(2,1)S(1)} %pad_maximum_fusion.1.refs_0_), channel_id=1, source_target_pairs={{0,24},{4,28},{8,16},{12,20},{16,8},{20,12},{24,0},{28,4},{1,25},{... | collective-permute-start | bytes 638984 | tf_op jit(solution)/shard_map/ppermute | solution.py:486
  28.2 1.7 %collective-permute-done.11 = bf16[144,512]{1,0:T(8,128)(2,1)S(1)} collective-permute-done((bf16[144,512]{1,0:T(8,128)(2,1)S(1)}, bf16[144,512]{1,0:T(8,128)(2,1)S(1)}, u32[]{:S(2)}, u32[]{:S(2)}) %collective-permute-start.11) | collective-permute-done | bytes 147488 | tf_op jit(solution)/shard_map/ppermute | solution.py:486
  31.4 5.1 %collective-permute-done.10 = bf16[144,512]{1,0:T(8,128)(2,1)S(1)} collective-permute-done((bf16[144,512]{1,0:T(8,128)(2,1)S(1)}, bf16[144,512]{1,0:T(8,128)(2,1)S(1)}, u32[]{:S(2)}, u32[]{:S(2)}) %collective-permute-start.10) | collective-permute-done | bytes 147488 | tf_op jit(solution)/shard_map/ppermute | solution.py:486
  39.6 3.0 %collective-permute-done.6.refs_1_ = bf16[4,16,1664]{2,1,0:T(8,128)(2,1)S(1)} collective-permute-done((bf16[4,16,1664]{2,1,0:T(8,128)(2,1)S(1)}, bf16[4,16,1664]{2,1,0:T(8,128)(2,1)S(1)}, u32[]{:S(2)}, u32[]{:S(2)}) %collective-permute-start.6) | collective-permute-done | bytes 213024 | tf_op jit(solution)/shard_map/ppermute | solution.py:486
  43.4 2.5 %collective-permute-start.22 = (bf16[3,144,512]{2,1,0:T(8,128)(2,1)S(1)}, bf16[3,144,512]{2,1,0:T(8,128)(2,1)S(1)}, u32[]{:S(2)}, u32[]{:S(2)}) collective-permute-start(bf16[3,144,512]{2,1,0:T(8,128)(2,1)S(1)} %pad_maximum_fusion.refs_8_), channel_id=1, source_target_pairs={{0,24},{4,28},{8,16},{12,20},{16,8},{20,12},{24,0},{28,4},{1,25},{... | collective-permute-start | bytes 1327112 | tf_op jit(solution)/shard_map/ppermute | solution.py:486
  49.1 12.6 %shard_map.195 = (bf16[768,512]{1,0:T(8,128)(2,1)S(1)}, bf16[768,1536]{1,0:T(8,128)(2,1)S(1)}, bf16[768,512]{1,0:T(8,128)(2,1)S(1)}, bf16[768,512]{1,0:T(8,128)(...) custom-call(s32[11]{0:T(128)S(1)} %pad_add_fusion.info, bf16[704,512]{1,0:T(8,128)(2,1)} %rows.2, ...), custom_call_target="tpu_custom_call" | custom-call | flops 2415919104 | bytes 2662400 | tf_op jit(solution)/shard_map/pallas_call | solution.py:472
  61.7 4.2 %collective-permute-done.21.refs_10_ = bf16[3,144,512]{2,1,0:T(8,128)(2,1)S(1)} collective-permute-done((bf16[3,144,512]{2,1,0:T(8,128)(2,1)S(1)}, bf16[3,144,512]{2,1,0:T(8,128)(2,1)S(1)}, u32[]{:S(2)}, u32[]{:S(2)}) %collective-permute-start.21) | collective-permute-done | bytes 442400 | tf_op jit(solution)/shard_map/ppermute | solution.py:486
  69.9 22.7 %shard_map.196 = (bf16[704,512]{1,0:T(8,128)(2,1)S(1)}, f32[768,512]{1,0:T(8,128)S(1)}, bf16[768,512]{1,0:T(8,128)(2,1)S(1)}, f32[8,512]{1,0:T(8,128)S(1)}, bf16...) custom-call(s32[11]{0:T(128)S(1)} %pad_add_fusion.info, bf16[704,512]{1,0:T(8,128)(2,1)} %rows.3, ...), custom_call_target="tpu_custom_call" | custom-call | flops 10871635968 | bytes 7266304 | tf_op jit(solution)/shard_map/pallas_call | solution.py:472
  92.8 4.4 %collective-permute-done.27 = bf16[4,4,144,512]{3,2,1,0:T(8,128)(2,1)S(1)} collective-permute-done((bf16[4,4,144,512]{3,2,1,0:T(8,128)(2,1)S(1)}, bf16[4,4,144,512]{3,2,1,0:T(8,128)(2,1)S(1)}, u32[]{:S(2)}, u32[]{:S(2)}) %collective-permute-start.27) | collective-permute-done | bytes 2359328 | tf_op jit(solution)/shard_map/ppermute | solution.py:486
  98.5 1.8 %collective-permute-start.30 = (bf16[3,144,512]{2,1,0:T(8,128)(2,1)S(1)}, bf16[3,144,512]{2,1,0:T(8,128)(2,1)S(1)}, u32[]{:S(2)}, u32[]{:S(2)}) collective-permute-start(bf16[3,144,512]{2,1,0:T(8,128)(2,1)S(1)} %get-tuple-element.142), channel_id=1, source_target_pairs={{0,24},{4,28},{8,16},{12,20},{16,8},{20,12},{24,0},{28,4},{1,25},{... | collective-permute-start | bytes 1327112 | tf_op jit(solution)/shard_map/ppermute | solution.py:486
  102.0 13.3 %shard_map.197 = (bf16[704,512]{1,0:T(8,128)(2,1)S(1)}, bf16[4,4,16,1664]{3,2,1,0:T(8,128)(2,1)S(1)}, bf16[4,4,16,1664]{3,2,1,0:T(8,128)(2,1)S(1)}) custom-call(s32[11]{0:T(128)S(1)} %pad_add_fusion.info, bf16[768,512]{1,0:T(8,128)(2,1)S(1)} %get-tuple-element.91.x_in, bf16[768,1536]{1,0:T(8,128)(2,1)S(1)} %get-tuple-element.104.qkv, ...), custom_call_target="tpu_custom_call" | custom-call | flops 3623878656 | bytes 8028160 | tf_op jit(solution)/shard_map/pallas_call | solution.py:472
  115.4 5.7 %collective-permute-done.29 = bf16[3,144,512]{2,1,0:T(8,128)(2,1)S(1)} collective-permute-done((bf16[3,144,512]{2,1,0:T(8,128)(2,1)S(1)}, bf16[3,144,512]{2,1,0:T(8,128)(2,1)S(1)}, u32[]{:S(2)}, u32[]{:S(2)}) %collective-permute-start.29) | collective-permute-done | bytes 442400 | tf_op jit(solution)/shard_map/ppermute | solution.py:486
  121.5 2.1 %collective-permute-done.31 = bf16[4,4,16,1664]{3,2,1,0:T(8,128)(2,1)S(1)} collective-permute-done((bf16[4,4,16,1664]{3,2,1,0:T(8,128)(2,1)S(1)}, bf16[4,4,16,1664]{3,2,1,0:T(8,128)(2,1)S(1)}, u32[]{:S(2)}, u32[]{:S(2)}) %collective-permute-start.31) | collective-permute-done | bytes 852000 | tf_op jit(solution)/shard_map/ppermute | solution.py:486
  123.9 2.9 %collective-permute-start.37 = (bf16[144,512]{1,0:T(8,128)(2,1)S(1)}, bf16[144,512]{1,0:T(8,128)(2,1)S(1)}, u32[]{:S(2)}, u32[]{:S(2)}) collective-permute-start(bf16[144,512]{1,0:T(8,128)(2,1)S(1)} %get-tuple-element.159), channel_id=1, source_target_pairs={{0,3},{1,2},{2,1},{3,0},{4,7},{5,6},{6,5},{7,4},{8,11},{9,10},{10,... | collective-permute-start | bytes 442376 | tf_op jit(solution)/shard_map/ppermute | solution.py:486
  126.9 1.7 %collective-permute-start.34 = (bf16[4,16,1664]{2,1,0:T(8,128)(2,1)S(1)}, bf16[4,16,1664]{2,1,0:T(8,128)(2,1)S(1)}, u32[]{:S(2)}, u32[]{:S(2)}) collective-permute-start(bf16[4,16,1664]{2,1,0:T(8,128)(2,1)S(1)} %get-tuple-element.153), channel_id=1, source_target_pairs={{0,24},{4,28},{8,16},{12,20},{16,8},{20,12},{24,0},{28,4},{1,25},{... | collective-permute-start | bytes 638984 | tf_op jit(solution)/shard_map/ppermute | solution.py:486
  130.4 1.7 %collective-permute-done.37 = bf16[144,512]{1,0:T(8,128)(2,1)S(1)} collective-permute-done((bf16[144,512]{1,0:T(8,128)(2,1)S(1)}, bf16[144,512]{1,0:T(8,128)(2,1)S(1)}, u32[]{:S(2)}, u32[]{:S(2)}) %collective-permute-start.37) | collective-permute-done | bytes 147488 | tf_op jit(solution)/shard_map/ppermute | solution.py:486
  132.2 4.7 %collective-permute-start.35 = (bf16[144,512]{1,0:T(8,128)(2,1)S(1)}, bf16[144,512]{1,0:T(8,128)(2,1)S(1)}, u32[]{:S(2)}, u32[]{:S(2)}) collective-permute-start(bf16[144,512]{1,0:T(8,128)(2,1)S(1)} %get-tuple-element.161), channel_id=1, source_target_pairs={{0,1},{1,0},{2,3},{3,2},{4,5},{5,4},{6,7},{7,6},{8,9},{9,8},{10,11... | collective-permute-start | bytes 442376 | tf_op jit(solution)/shard_map/ppermute | solution.py:486
  140.6 1.7 %collective-permute-start.38 = (bf16[16,1664]{1,0:T(8,128)(2,1)S(1)}, bf16[16,1664]{1,0:T(8,128)(2,1)S(1)}, u32[]{:S(2)}, u32[]{:S(2)}) collective-permute-start(bf16[16,1664]{1,0:T(8,128)(2,1)S(1)} %get-tuple-element.164), channel_id=1, source_target_pairs={{0,1},{1,0},{2,3},{3,2},{4,5},{5,4},{6,7},{7,6},{8,9},{9,8},{10,11... | collective-permute-start | bytes 159752 | tf_op jit(solution)/shard_map/ppermute | solution.py:486
  150.6 1.8 %collective-permute-done.43 = bf16[144,512]{1,0:T(8,128)(2,1)S(1)} collective-permute-done((bf16[144,512]{1,0:T(8,128)(2,1)S(1)}, bf16[144,512]{1,0:T(8,128)(2,1)S(1)}, u32[]{:S(2)}, u32[]{:S(2)}) %collective-permute-start.43) | collective-permute-done | bytes 147488 | tf_op jit(solution)/shard_map/ppermute | solution.py:486
  (158 shorter events, 41.5 us)
Async XLA Ops:
  2.2 18.9 %collective-permute-start.5 = (bf16[144,512]{1,0:T(8,128)(2,1)S(1)}, bf16[144,512]{1,0:T(8,128)(2,1)S(1)}, u32[]{:S(2)}, u32[]{:S(2)}) collective-permute-start(bf16[144,512]{1,0:T(8,128)(2,1)S(1)} %get-tuple-element.77), channel_id=1, source_target_pairs={{0,24},{4,28},{8,16},{12,20},{16,8},{20,12},{24,0},{28,4},{1,25},{... | collective-permute-start | bytes 442376 | tf_op jit(solution)/shard_map/ppermute | solution.py:486
  6.1 15.0 %collective-permute-start.4 = (bf16[144,512]{1,0:T(8,128)(2,1)S(1)}, bf16[144,512]{1,0:T(8,128)(2,1)S(1)}, u32[]{:S(2)}, u32[]{:S(2)}) collective-permute-start(bf16[144,512]{1,0:T(8,128)(2,1)S(1)} %get-tuple-element.77), channel_id=1, source_target_pairs={{0,16},{4,20},{8,24},{12,28},{16,0},{20,4},{24,8},{28,12},{1,17},{... | collective-permute-start | bytes 442376 | tf_op jit(solution)/shard_map/ppermute | solution.py:486
  6.6 14.5 %collective-permute-start.3 = (bf16[144,512]{1,0:T(8,128)(2,1)S(1)}, bf16[144,512]{1,0:T(8,128)(2,1)S(1)}, u32[]{:S(2)}, u32[]{:S(2)}) collective-permute-start(bf16[144,512]{1,0:T(8,128)(2,1)S(1)} %get-tuple-element.77), channel_id=1, source_target_pairs={{0,8},{4,12},{8,0},{12,4},{16,24},{20,28},{24,16},{28,20},{1,9},{5... | collective-permute-start | bytes 442376 | tf_op jit(solution)/shard_map/ppermute | solution.py:486
  13.1 7.2 %collective-permute-start.2 = (bf16[16,3712]{1,0:T(8,128)(2,1)S(1)}, bf16[16,3712]{1,0:T(8,128)(2,1)S(1)}, u32[]{:S(2)}, u32[]{:S(2)}) collective-permute-start(bf16[16,3712]{1,0:T(8,128)(2,1)S(1)} %get-tuple-element.173), channel_id=1, source_target_pairs={{0,3},{1,2},{2,1},{3,0},{4,7},{5,6},{6,5},{7,4},{8,11},{9,10},{10,... | collective-permute-start | bytes 356360 | tf_op jit(solution)/shard_map/ppermute | solution.py:486
  21.2 8.7 %collective-permute-start.11 = (bf16[144,512]{1,0:T(8,128)(2,1)S(1)}, bf16[144,512]{1,0:T(8,128)(2,1)S(1)}, u32[]{:S(2)}, u32[]{:S(2)}) collective-permute-start(bf16[144,512]{1,0:T(8,128)(2,1)S(1)} %get-tuple-element.77), channel_id=1, source_target_pairs={{0,3},{1,2},{2,1},{3,0},{4,7},{5,6},{6,5},{7,4},{8,11},{9,10},{10,... | collective-permute-start | bytes 442376 | tf_op jit(solution)/shard_map/ppermute | solution.py:486
  24.9 11.7 %collective-permute-start.10 = (bf16[144,512]{1,0:T(8,128)(2,1)S(1)}, bf16[144,512]{1,0:T(8,128)(2,1)S(1)}, u32[]{:S(2)}, u32[]{:S(2)}) collective-permute-start(bf16[144,512]{1,0:T(8,128)(2,1)S(1)} %get-tuple-element.77), channel_id=1, source_target_pairs={{0,2},{1,3},{2,0},{3,1},{4,6},{5,7},{6,4},{7,5},{8,10},{9,11},{10,... | collective-permute-start | bytes 442376 | tf_op jit(solution)/shard_map/ppermute | solution.py:486
  24.9 13.2 %collective-permute-start.9 = (bf16[144,512]{1,0:T(8,128)(2,1)S(1)}, bf16[144,512]{1,0:T(8,128)(2,1)S(1)}, u32[]{:S(2)}, u32[]{:S(2)}) collective-permute-start(bf16[144,512]{1,0:T(8,128)(2,1)S(1)} %get-tuple-element.77), channel_id=1, source_target_pairs={{0,1},{1,0},{2,3},{3,2},{4,5},{5,4},{6,7},{7,6},{8,9},{9,8},{10,11... | collective-permute-start | bytes 442376 | tf_op jit(solution)/shard_map/ppermute | solution.py:486
  25.7 12.4 %collective-permute-start.13 = (bf16[144,512]{1,0:T(8,128)(2,1)S(1)}, bf16[144,512]{1,0:T(8,128)(2,1)S(1)}, u32[]{:S(2)}, u32[]{:S(2)}) collective-permute-start(bf16[144,512]{1,0:T(8,128)(2,1)S(1)} %collective-permute-done.3), channel_id=1, source_target_pairs={{0,4},{4,0},{8,12},{12,8},{16,20},{20,16},{24,28},{28,24},{1,5},{5... | collective-permute-start | bytes 442376 | tf_op jit(solution)/shard_map/ppermute | solution.py:486
  25.7 13.9 %collective-permute-start.8 = (bf16[4,16,1664]{2,1,0:T(8,128)(2,1)S(1)}, bf16[4,16,1664]{2,1,0:T(8,128)(2,1)S(1)}, u32[]{:S(2)}, u32[]{:S(2)}) collective-permute-start(bf16[4,16,1664]{2,1,0:T(8,128)(2,1)S(1)} %pad_maximum_fusion.1.refs_0_), channel_id=1, source_target_pairs={{0,24},{4,28},{8,16},{12,20},{16,8},{20,12},{24,0},{28,4},{1,25},{... | collective-permute-start | bytes 638984 | tf_op jit(solution)/shard_map/ppermute | solution.py:486
  29.9 9.7 %collective-permute-start.7 = (bf16[4,16,1664]{2,1,0:T(8,128)(2,1)S(1)}, bf16[4,16,1664]{2,1,0:T(8,128)(2,1)S(1)}, u32[]{:S(2)}, u32[]{:S(2)}) collective-permute-start(bf16[4,16,1664]{2,1,0:T(8,128)(2,1)S(1)} %pad_maximum_fusion.1.refs_0_), channel_id=1, source_target_pairs={{0,16},{4,20},{8,24},{12,28},{16,0},{20,4},{24,8},{28,12},{1,17},{... | collective-permute-start | bytes 638984 | tf_op jit(solution)/shard_map/ppermute | solution.py:486
  43.4 18.3 %collective-permute-start.22 = (bf16[3,144,512]{2,1,0:T(8,128)(2,1)S(1)}, bf16[3,144,512]{2,1,0:T(8,128)(2,1)S(1)}, u32[]{:S(2)}, u32[]{:S(2)}) collective-permute-start(bf16[3,144,512]{2,1,0:T(8,128)(2,1)S(1)} %pad_maximum_fusion.refs_8_), channel_id=1, source_target_pairs={{0,24},{4,28},{8,16},{12,20},{16,8},{20,12},{24,0},{28,4},{1,25},{... | collective-permute-start | bytes 1327112 | tf_op jit(solution)/shard_map/ppermute | solution.py:486
  45.9 20.0 %collective-permute-start.21 = (bf16[3,144,512]{2,1,0:T(8,128)(2,1)S(1)}, bf16[3,144,512]{2,1,0:T(8,128)(2,1)S(1)}, u32[]{:S(2)}, u32[]{:S(2)}) collective-permute-start(bf16[3,144,512]{2,1,0:T(8,128)(2,1)S(1)} %pad_maximum_fusion.refs_8_), channel_id=1, source_target_pairs={{0,16},{4,20},{8,24},{12,28},{16,0},{20,4},{24,8},{28,12},{1,17},{... | collective-permute-start | bytes 1327112 | tf_op jit(solution)/shard_map/ppermute | solution.py:486
  46.4 19.6 %collective-permute-start.20 = (bf16[3,144,512]{2,1,0:T(8,128)(2,1)S(1)}, bf16[3,144,512]{2,1,0:T(8,128)(2,1)S(1)}, u32[]{:S(2)}, u32[]{:S(2)}) collective-permute-start(bf16[3,144,512]{2,1,0:T(8,128)(2,1)S(1)} %pad_maximum_fusion.refs_8_), channel_id=1, source_target_pairs={{0,8},{4,12},{8,0},{12,4},{16,24},{20,28},{24,16},{28,20},{1,9},{5... | collective-permute-start | bytes 1327112 | tf_op jit(solution)/shard_map/ppermute | solution.py:486
  48.4 18.2 %collective-permute-start.23 = (bf16[3,144,512]{2,1,0:T(8,128)(2,1)S(1)}, bf16[3,144,512]{2,1,0:T(8,128)(2,1)S(1)}, u32[]{:S(2)}, u32[]{:S(2)}) collective-permute-start(bf16[3,144,512]{2,1,0:T(8,128)(2,1)S(1)} %pad_maximum_fusion.refs_8_), channel_id=1, source_target_pairs={{0,4},{4,0},{8,12},{12,8},{16,20},{20,16},{24,28},{28,24},{1,5},{5... | collective-permute-start | bytes 1327112 | tf_op jit(solution)/shard_map/ppermute | solution.py:486
  98.5 16.9 %collective-permute-start.30 = (bf16[3,144,512]{2,1,0:T(8,128)(2,1)S(1)}, bf16[3,144,512]{2,1,0:T(8,128)(2,1)S(1)}, u32[]{:S(2)}, u32[]{:S(2)}) collective-permute-start(bf16[3,144,512]{2,1,0:T(8,128)(2,1)S(1)} %get-tuple-element.142), channel_id=1, source_target_pairs={{0,24},{4,28},{8,16},{12,20},{16,8},{20,12},{24,0},{28,4},{1,25},{... | collective-permute-start | bytes 1327112 | tf_op jit(solution)/shard_map/ppermute | solution.py:486
  100.3 20.9 %collective-permute-start.29 = (bf16[3,144,512]{2,1,0:T(8,128)(2,1)S(1)}, bf16[3,144,512]{2,1,0:T(8,128)(2,1)S(1)}, u32[]{:S(2)}, u32[]{:S(2)}) collective-permute-start(bf16[3,144,512]{2,1,0:T(8,128)(2,1)S(1)} %get-tuple-element.143), channel_id=1, source_target_pairs={{0,16},{4,20},{8,24},{12,28},{16,0},{20,4},{24,8},{28,12},{1,17},{... | collective-permute-start | bytes 1327112 | tf_op jit(solution)/shard_map/ppermute | solution.py:486
  101.5 19.7 %collective-permute-start.28 = (bf16[3,144,512]{2,1,0:T(8,128)(2,1)S(1)}, bf16[3,144,512]{2,1,0:T(8,128)(2,1)S(1)}, u32[]{:S(2)}, u32[]{:S(2)}) collective-permute-start(bf16[3,144,512]{2,1,0:T(8,128)(2,1)S(1)} %get-tuple-element.144), channel_id=1, source_target_pairs={{0,8},{4,12},{8,0},{12,4},{16,24},{20,28},{24,16},{28,20},{1,9},{5... | collective-permute-start | bytes 1327112 | tf_op jit(solution)/shard_map/ppermute | solution.py:486
  123.9 8.2 %collective-permute-start.37 = (bf16[144,512]{1,0:T(8,128)(2,1)S(1)}, bf16[144,512]{1,0:T(8,128)(2,1)S(1)}, u32[]{:S(2)}, u32[]{:S(2)}) collective-permute-start(bf16[144,512]{1,0:T(8,128)(2,1)S(1)} %get-tuple-element.159), channel_id=1, source_target_pairs={{0,3},{1,2},{2,1},{3,0},{4,7},{5,6},{6,5},{7,4},{8,11},{9,10},{10,... | collective-permute-start | bytes 442376 | tf_op jit(solution)/shard_map/ppermute | solution.py:486
  126.9 13.5 %collective-permute-start.34 = (bf16[4,16,1664]{2,1,0:T(8,128)(2,1)S(1)}, bf16[4,16,1664]{2,1,0:T(8,128)(2,1)S(1)}, u32[]{:S(2)}, u32[]{:S(2)}) collective-permute-start(bf16[4,16,1664]{2,1,0:T(8,128)(2,1)S(1)} %get-tuple-element.153), channel_id=1, source_target_pairs={{0,24},{4,28},{8,16},{12,20},{16,8},{20,12},{24,0},{28,4},{1,25},{... | collective-permute-start | bytes 638984 | tf_op jit(solution)/shard_map/ppermute | solution.py:486
  128.6 11.8 %collective-permute-start.33 = (bf16[4,16,1664]{2,1,0:T(8,128)(2,1)S(1)}, bf16[4,16,1664]{2,1,0:T(8,128)(2,1)S(1)}, u32[]{:S(2)}, u32[]{:S(2)}) collective-permute-start(bf16[4,16,1664]{2,1,0:T(8,128)(2,1)S(1)} %get-tuple-element.154), channel_id=1, source_target_pairs={{0,16},{4,20},{8,24},{12,28},{16,0},{20,4},{24,8},{28,12},{1,17},{... | collective-permute-start | bytes 638984 | tf_op jit(solution)/shard_map/ppermute | solution.py:486
  129.8 10.6 %collective-permute-start.32 = (bf16[4,16,1664]{2,1,0:T(8,128)(2,1)S(1)}, bf16[4,16,1664]{2,1,0:T(8,128)(2,1)S(1)}, u32[]{:S(2)}, u32[]{:S(2)}) collective-permute-start(bf16[4,16,1664]{2,1,0:T(8,128)(2,1)S(1)} %get-tuple-element.155), channel_id=1, source_target_pairs={{0,8},{4,12},{8,0},{12,4},{16,24},{20,28},{24,16},{28,20},{1,9},{5... | collective-permute-start | bytes 638984 | tf_op jit(solution)/shard_map/ppermute | solution.py:486
  130.4 8.4 %collective-permute-start.36 = (bf16[144,512]{1,0:T(8,128)(2,1)S(1)}, bf16[144,512]{1,0:T(8,128)(2,1)S(1)}, u32[]{:S(2)}, u32[]{:S(2)}) collective-permute-start(bf16[144,512]{1,0:T(8,128)(2,1)S(1)} %get-tuple-element.160), channel_id=1, source_target_pairs={{0,2},{1,3},{2,0},{3,1},{4,6},{5,7},{6,4},{7,5},{8,10},{9,11},{10,... | collective-permute-start | bytes 442376 | tf_op jit(solution)/shard_map/ppermute | solution.py:486
  132.2 8.3 %collective-permute-start.35 = (bf16[144,512]{1,0:T(8,128)(2,1)S(1)}, bf16[144,512]{1,0:T(8,128)(2,1)S(1)}, u32[]{:S(2)}, u32[]{:S(2)}) collective-permute-start(bf16[144,512]{1,0:T(8,128)(2,1)S(1)} %get-tuple-element.161), channel_id=1, source_target_pairs={{0,1},{1,0},{2,3},{3,2},{4,5},{5,4},{6,7},{7,6},{8,9},{9,8},{10,11... | collective-permute-start | bytes 442376 | tf_op jit(solution)/shard_map/ppermute | solution.py:486
  147.1 6.7 %collective-permute-start.42 = (bf16[144,512]{1,0:T(8,128)(2,1)S(1)}, bf16[144,512]{1,0:T(8,128)(2,1)S(1)}, u32[]{:S(2)}, u32[]{:S(2)}) collective-permute-start(bf16[144,512]{1,0:T(8,128)(2,1)S(1)} %get-tuple-element.158), channel_id=1, source_target_pairs={{0,16},{4,20},{8,24},{12,28},{16,0},{20,4},{24,8},{28,12},{1,17},{... | collective-permute-start | bytes 442376 | tf_op jit(solution)/shard_map/ppermute | solution.py:486
  (46 other events, 424.3 us)

commit v3 on v2

--- a/solution.py
+++ b/solution.py
@@ -100,12 +100,14 @@
         copy.wait()
 
 
-def row_copies(rows, near, far, column, stage, halos):
-    return [
-        (rows, stage),
-        (near.at[:, column : column + 2 * D], halos.at[0]),
-        (far.at[:, column : column + 2 * D], halos.at[1]),
-    ]
+def row_copies(rows, near, far, stage, halos):
+    pairs = [(rows, stage)]
+    for i, parts in enumerate((near, far)):
+        size = HALO // len(parts)
+        pairs += [
+            (part, halos.at[i, j * size : (j + 1) * size, :]) for j, part in enumerate(parts)
+        ]
+    return pairs
 
 
 def pad_rows(info, ext, stage, halos):
@@ -113,8 +115,7 @@
     odd = info[10] % 2 == 1
     for i, is_left in enumerate((odd, jnp.logical_not(odd))):
         at = pl.multiple_of(jnp.where(is_left, 0, HALO + ROWS), HALO)
-        ext[pl.ds(at, HALO // 2), :] = halos[i, :, 0:D].astype(F32)
-        ext[pl.ds(at + HALO // 2, HALO // 2), :] = halos[i, :, D : 2 * D].astype(F32)
+        ext[pl.ds(at, HALO), :] = halos[i].astype(F32)
 
 
 def normalized(values):
@@ -147,18 +148,144 @@
     )
 
 
+def sum_kernel(plan, *refs):
+    ins, outs = refs[: -len(plan)], refs[-len(plan) :]
+    for out, pieces in zip(outs, plan):
+        for target, source in pieces:
+            value = ins[0][source].astype(F32)
+            for part in ins[1:]:
+                value = value + part[source].astype(F32)
+            out[target] = value.astype(out.dtype)
+
+
+def add(plan, shapes, *operands):
+    return pl.pallas_call(
+        functools.partial(sum_kernel, plan),
+        out_shape=[jax.ShapeDtypeStruct(*s) for s in shapes],
+        in_specs=[VMEM] * len(operands),
+        out_specs=[VMEM] * len(shapes),
+        compiler_params=pltpu.CompilerParams(vmem_limit_bytes=SMALL),
+    )(*[near_core(a) for a in operands])
+
+
+def tail_kernel(row, own, *refs):
+    parts, out = refs[:-1], refs[-1]
+    total = own[...]
+    for part in parts:
+        total = total + part[row : row + out.shape[0], :].astype(F32)
+    out[...] = total
+
+
+def add_tail(own, parts, row):
+    return pl.pallas_call(
+        functools.partial(tail_kernel, row),
+        out_shape=[jax.ShapeDtypeStruct(own.shape, F32)],
+        in_specs=[VMEM] * (1 + len(parts)),
+        out_specs=[VMEM],
+        compiler_params=pltpu.CompilerParams(vmem_limit_bytes=SMALL),
+    )(*[near_core(a) for a in (own, *parts)])
+
+
+def pair_kernel(keep, *refs):
+    for m, (part, out) in enumerate(zip(refs[:4], refs[4:])):
+        out[...] = (keep[m].astype(F32) + part[...].astype(F32)).astype(out.dtype)
+
+
+def add_pairs(keep, parts):
+    slot = keep.shape[1:]
+    return pl.pallas_call(
+        pair_kernel,
+        out_shape=[jax.ShapeDtypeStruct(slot, kind) for kind in (F32, BF16, BF16, BF16)],
+        in_specs=[VMEM] * 5,
+        out_specs=[VMEM] * 4,
+        compiler_params=pltpu.CompilerParams(vmem_limit_bytes=SMALL),
+    )(*[near_core(a) for a in (keep, *parts)])
+
+
+def finish_kernel(own, one, two, three, grad, *norm_grads):
+    total = own[...] + (one[...].astype(F32) + two[...].astype(F32) + three[...].astype(F32))
+    grad[...] = total[:, : 3 * D]
+    rows = jnp.transpose(total[:, 3 * D :])
+    for i, norm_grad in enumerate(norm_grads):
+        norm_grad[...] = rows[i : i + 1]
+
+
+def finish_first(own, parts):
+    share = own.shape[0]
+    shapes = [(share, 3 * D)] + [(1, share)] * 4
+    return pl.pallas_call(
+        finish_kernel,
+        out_shape=[jax.ShapeDtypeStruct(dims, F32) for dims in shapes],
+        in_specs=[VMEM] * (1 + len(parts)),
+        out_specs=[VMEM] * len(shapes),
+        compiler_params=pltpu.CompilerParams(vmem_limit_bytes=SMALL),
+    )(*[near_core(a) for a in (own, *parts)])
+
+
+def add_slots(*operands):
+    slot = operands[0].shape[1:]
+    plan = [[(slice(None), i)] for i in range(4)]
+    return add(plan, [(slot, F32)] + [(slot, BF16)] * 3, *operands)
+
+
+def prepare_kernel(tokens, cotangent, w_qkv, w_out, w_up, w_down, *refs):
+    norms, (with_near, first, with_far, second, up_near, up_far, vectors, sems) = refs[:4], refs[4:]
+    share, width = first.shape
+    block = w_up.shape[0]
+    odd = lax.axis_index("seq") % 2
+    pairs = [(norm, vectors.at[i]) for i, norm in enumerate(norms)]
+    for target in (with_near, first, with_far):
+        pairs += [(w_qkv, target.at[:, : 3 * D]), (w_out, target.at[:, 3 * D : 4 * D])]
+    for target, up_target, is_head in ((with_near, up_near, odd), (with_far, up_far, 1 - odd)):
+        start = pl.multiple_of((1 - is_head) * (ROWS - HALO), HALO)
+        for j in range(2):
+            at = width + j * D
+            rows = pl.ds(start + j * (HALO // 2), HALO // 2)
+            pairs.append((tokens.at[rows, :], target.at[:, at : at + D]))
+        pairs.append((cotangent.at[pl.ds(start, HALO), :], up_target.at[2 * block :, :]))
+    for target in (second, up_near, up_far):
+        pairs += [(w_up, target.at[0:block]), (w_down, target.at[block : 2 * block])]
+    first_row = 2 * block
+    for i, source in enumerate([w_qkv.at[:, j * D : (j + 1) * D] for j in range(3)] + [w_out]):
+        pairs.append((source, second.at[first_row + share * i : first_row + share * (i + 1), :]))
+    copies = copy_all(pairs, sems)
+    wait_all(copies[: len(norms)])
+    columns = jnp.concatenate(
+        [vectors[i].astype(F32) for i in range(4)] + [jnp.zeros((NORMS - 4, share), F32)], axis=0
+    )
+    columns = jnp.transpose(columns).astype(BF16)
+    for target in (with_near, first, with_far):
+        target[:, 4 * D : width] = columns
+    second[first_row + 4 * share :, :] = jnp.concatenate([columns] * (D // NORMS), axis=1)
+    wait_all(copies[len(norms) :])
+
+
 def attention_kernel(direct, info, rows, near, far, *refs):
-    pieces, refs = (refs[:8], refs[8:]) if direct else (refs[:1], refs[1:])
+    pieces, refs = (refs[:4], refs[4:]) if direct else (refs[:1], refs[1:])
     x_out, qkv_out, mixed_out, probs_out, w_out, norms_out, ext, stage, halos, sems = refs
-    column = w_out.shape[1] if direct else 0
-    row_copy = copy_all(row_copies(rows, near, far, column, stage, halos), sems)
-    if direct:
-        share, pairs = pieces[0].shape[1], []
-        for piece, partner in zip(pieces, ORDER):
-            for k in range(piece.shape[0]):
-                owner = (info[9] ^ partner) * piece.shape[0] + (info[10] ^ k)
-                at = pl.multiple_of(owner * share, share)
-                pairs.append((piece.at[k], w_out.at[pl.ds(at, share), :]))
+    width = w_out.shape[1]
+    near, far = [
+        [a.at[:, width + j * D : width + (j + 1) * D] for j in range(2)] if direct else [a]
+        for a in (near, far)
+    ]
+    row_copy = copy_all(row_copies(rows, near, far, stage, halos), sems)
+    if direct:
+        count, share, pairs = pieces[0].shape[1] + 1, pieces[0].shape[2], []
+        for core, piece in enumerate(pieces[:2]):
+            for chip in range(4):
+                for k in range(1, count):
+                    owner = (2 * chip + (info[9] % 2 ^ core)) * count + (info[10] ^ k)
+                    at = pl.multiple_of(owner * share, share)
+                    pairs.append((piece.at[chip, k - 1], w_out.at[pl.ds(at, share), :]))
+        own = [piece.at[m] for piece in pieces[2:] for m in range(4)]
+        for piece, partner in zip(own, ORDER):
+            owner = (info[9] ^ partner) * count + info[10]
+            at = pl.ds(pl.multiple_of(owner * share, share), share)
+            for i in range(5):
+                cols = min(D, w_out.shape[1] - i * D)
+                row = D // 4 + i * share
+                source = piece.at[row : row + share, 0:cols]
+                pairs.append((source, w_out.at[at, i * D : i * D + cols]))
     else:
         pairs = [(pieces[0], w_out)]
     w_copy = copy_all(pairs, sems, len(row_copy))
@@ -173,7 +300,7 @@
 
     lax.fori_loop(0, WINDOWS, place, 0, unroll=4)
     wait_all(w_copy)
-    norms_out[...] = jnp.transpose(w_out[:, 3 * D :].astype(F32))[:8]
+    norms_out[...] = jnp.transpose(w_out[:, 4 * D :].astype(F32))[:8]
     gain, shift = norms_out[0:1], norms_out[1:2]
 
     def project(i, carry):
@@ -235,47 +362,61 @@
     return jnp.where(values >= 0, 1.0 - tail, tail), half_exp * 0.3989422804014327
 
 
-def feed_kernel(direct, info, rows, near, far, x_in, mixed_in, norms, *refs):
-    pieces, refs = (refs[:16], refs[16:]) if direct else (refs[:3], refs[3:])
-    out, grad_middle, grad_mixed, grad_norms = refs[:4]
-    if direct:
-        (keep, send), refs = refs[4:6], refs[6:]
-    else:
-        (grad_up_out, grad_down_out, grad_w_out), refs = refs[4:7], refs[7:]
-    up, down, w_out, ext, cot, cot_own, own, middle, total, normed, normed_own, hidden, pre, grad = refs[:14]
-    stage, halos, sems = refs[14:]
-    column = near.shape[1] - 2 * D
-    row_copy = copy_all(row_copies(rows, near, far, column, stage, halos), sems)
-    if direct:
-        count = CHUNKS
-        block = D // 8
-        out_pairs, pairs = [], [[], []]
-        for piece, partner, base in zip(pieces, ORDER * 2, (0,) * 8 + (1,) * 8):
-            dp = info[9] ^ partner
-            at = pl.ds(pl.multiple_of(dp * block, block), block)
-            ks = slice(base, base + piece.shape[0])
-            pairs[base].append((piece.at[:, 0:block, :], up.at[ks, at, :]))
-            pairs[base].append((piece.at[:, block : 2 * block, :], down.at[ks, at, :]))
-            for k in range(base, base + piece.shape[0]):
-                row = pl.multiple_of((dp * count + (info[10] ^ k)) * 16, 16)
-                out_pairs.append(
-                    (piece.at[k - base, 2 * block : 2 * block + 16, :], w_out.at[pl.ds(row, 16), :])
-                )
-    else:
-        pairs = [[(pieces[0], up), (pieces[1], down)], []]
-        out_pairs = [(pieces[2], w_out)]
-    at = len(row_copy)
-    out_copy = copy_all(out_pairs, sems, at)
-    at += len(out_pairs)
-    first_copy = copy_all(pairs[0], sems, at)
-    rest_copy = copy_all(pairs[1], sems, at + len(pairs[0]))
+def feed_pieces(info, pieces, up, down):
+    block, pairs = D // 8, []
+    for piece, partner in zip(pieces, ORDER):
+        at = pl.ds(pl.multiple_of((info[9] ^ partner) * block, block), block)
+        pairs.append((piece.at[:, 0:block, :], up.at[:, at, :]))
+        pairs.append((piece.at[:, block : 2 * block, :], down.at[:, at, :]))
+    return pairs
+
+
+def feed_rows(at, up, down, normed, cot, hidden, pre):
+    values = mm(normed[at, :], up)
+    grad_hidden = mm(cot[at, :], down)
+    below, density = gelu_parts(values)
+    hidden_low = (values * below).astype(BF16)
+    grad_low = (grad_hidden * (below + values * density)).astype(BF16)
+    hidden[at, :] = hidden_low
+    pre[at, :] = grad_low
+    return mm_right(hidden_low, down), mm_right(grad_low, up)
+
+
+def feed_grads(direct, info, row, normed_own, cot_own, hidden, pre, space, refs):
+    block = D // 8
+    for i, product in enumerate(((normed_own, pre), (cot_own, hidden))):
+        grad = mm_left(product[0][...], product[1][...])
+        if not direct:
+            refs[i][row // (2 * block)] = grad
+            continue
+        space[0:D, :] = grad
+        for partner in range(8):
+            at = pl.multiple_of((info[9] ^ partner) * block, block)
+            first = row + i * block
+            refs[partner & 1][partner >> 1, first : first + block, :] = space[
+                pl.ds(at, block), :
+            ].astype(BF16)
+
+
+def feed_first_kernel(direct, info, rows, near, far, x_in, mixed_in, norms, w_all, *refs):
+    pieces, refs = refs[:2], refs[2:]
+    middle, total, grad, normed, normed_own, cot, cot_own, own = refs[:8]
+    grads, (up, down, ext, hidden, pre, stage, halos, sems) = refs[8:10], refs[10:]
+    near, far = [[a.at[a.shape[0] - HALO :, :]] for a in (near, far)]
+    row_copy = copy_all(row_copies(rows, near, far, stage, halos), sems)
+    if direct:
+        own_pieces = [piece.at[m : m + 1] for piece in pieces for m in range(4)]
+        pairs = feed_pieces(info, own_pieces, up, down)
+    else:
+        pairs = [(pieces[0].at[0:1], up), (pieces[1].at[0:1], down)]
+    first_copy = copy_all(pairs, sems, len(row_copy))
     wait_all(row_copy)
     pad_rows(info, ext, stage, halos)
 
     def place(w, carry):
         row, low, high, own_low, own_high, _ = window_place(info, w)
         values = ext[pl.ds(row, WIN), :]
-        at = pl.ds(pl.multiple_of(w * WIN, WIN), WIN)
+        at = window_at(w)
         cot[at, :] = jnp.where(row_mask(low, high), values, 0.0).astype(BF16)
         cot_own[at, :] = jnp.where(row_mask(own_low, own_high), values, 0.0).astype(BF16)
         own[at, :] = jnp.where(row_mask(own_low, own_high), jnp.ones((WIN, QUAD), F32), 0.0)
@@ -283,57 +424,48 @@
 
     lax.fori_loop(0, WINDOWS, place, 0, unroll=4)
     gain, shift = norms[2:3], norms[3:4]
-    wait_all(out_copy)
 
     def before(i, carry):
         at = tile_at(i)
-        values = x_in[at, :].astype(F32) + mm(mixed_in[at, :], w_out[...])
+        values = x_in[at, :].astype(F32) + mm(mixed_in[at, :], w_all[:, 3 * D : 4 * D])
         middle[at, :] = values
-        total[at, :] = values
         unit, _ = normalized(values)
         low = unit * gain + shift
         normed[at, :] = low.astype(BF16)
         normed_own[at, :] = (low * own[at, 0:1]).astype(BF16)
-        grad[at, :] = jnp.zeros((TILE, D), F32)
         return carry
 
     lax.fori_loop(0, WROWS // TILE, before, 0)
-
-    def row_step(c, i):
-        at = tile_at(i)
-        values = mm(normed[at, :], up[c])
-        grad_hidden = mm(cot[at, :], down[c])
-        below, density = gelu_parts(values)
-        hidden_low = (values * below).astype(BF16)
-        grad_low = (grad_hidden * (below + values * density)).astype(BF16)
-        hidden[at, :] = hidden_low
-        pre[at, :] = grad_low
-        total[at, :] += mm_right(hidden_low, down[c])
-        grad[at, :] += mm_right(grad_low, up[c])
-
-    for c in range(CHUNKS):
-        if c < 2:
-            wait_all((first_copy, rest_copy)[c])
+    wait_all(first_copy)
+    for i in range(WROWS // TILE):
+        at = slice(i * TILE, (i + 1) * TILE)
+        branch, back = feed_rows(at, up[0], down[0], normed, cot, hidden, pre)
+        total[at, :] = middle[at, :] + branch
+        grad[at, :] = back
+    feed_grads(direct, info, 0, normed_own, cot_own, hidden, pre, ext, grads)
+
+
+def feed_rest_kernel(direct, info, *refs):
+    middle, total_in, grad_in, normed, normed_own, cot, cot_own, own = refs[:8]
+    mixed_in, norms, w_all = refs[8:11]
+    pieces, refs = (refs[11:19], refs[19:]) if direct else (refs[11:13], refs[13:])
+    out, grad_middle, grad_mixed, grad_norms = refs[:4]
+    grads, refs = (refs[4:6], refs[6:]) if direct else (refs[4:7], refs[7:])
+    up, down, ext, total, grad, grad_own, hidden, pre, sems = refs
+    if direct:
+        pairs = feed_pieces(info, pieces, up, down)
+    else:
+        pairs = [(pieces[0].at[1:CHUNKS], up), (pieces[1].at[1:CHUNKS], down)]
+    wait_all(copy_all(pairs, sems))
+    block = D // 8
+    gain = norms[2:3]
+    for c in range(CHUNKS - 1):
         for i in range(WROWS // TILE):
-            row_step(c, i)
-        grad_up = mm_left(normed_own[...], pre[...])
-        grad_down = mm_left(cot_own[...], hidden[...])
-        if direct:
-            ext[0:D, :] = grad_up
-            for partner in range(8):
-                target = send if partner & 1 else keep
-                row = pl.multiple_of((info[9] ^ partner) * block, block)
-                target[partner >> 1, c, 0:block, :] = ext[pl.ds(row, block), :].astype(BF16)
-            ext[0:D, :] = grad_down
-            for partner in range(8):
-                target = send if partner & 1 else keep
-                row = pl.multiple_of((info[9] ^ partner) * block, block)
-                target[partner >> 1, c, block : 2 * block, :] = ext[pl.ds(row, block), :].astype(
-                    BF16
-                )
-        else:
-            grad_up_out[c] = grad_up
-            grad_down_out[c] = grad_down
+            at = slice(i * TILE, (i + 1) * TILE)
+            branch, back = feed_rows(at, up[c], down[c], normed, cot, hidden, pre)
+            total[at, :] = (total if c else total_in)[at, :] + branch
+            grad[at, :] = (grad if c else grad_in)[at, :] + back
+        feed_grads(direct, info, c * 2 * block, normed_own, cot_own, hidden, pre, ext, grads)
     grad_norms[...] = jnp.zeros(grad_norms.shape, F32)
 
     def after(i, carry):
@@ -346,21 +478,23 @@
         result = cot[at, :].astype(F32) + norm_back(part * gain, unit, scale)
         grad_middle[at, :] = result
         low = result.astype(BF16)
-        grad_mixed[at, :] = mm_right(low, w_out[...]).astype(BF16)
-        normed_own[at, :] = (result * own[at, 0:1]).astype(BF16)
+        grad_mixed[at, :] = mm_right(low, w_all[:, 3 * D : 4 * D]).astype(BF16)
+        grad_own[at, :] = (result * own[at, 0:1]).astype(BF16)
         return carry
 
     lax.fori_loop(0, WROWS // TILE, after, 0)
-    grad_out = mm_left(mixed_in[...], normed_own[...])
+    grad_out = mm_left(mixed_in[...], grad_own[...])
     if direct:
         ext[0:D, :] = grad_out
+        first = (CHUNKS - 1) * 2 * block
         for partner in range(8):
-            target = send if partner & 1 else keep
-            for k in range(count):
-                row = pl.multiple_of(((info[9] ^ partner) * count + (info[10] ^ k)) * 16, 16)
-                target[partner >> 1, k, 2 * block :, :] = ext[pl.ds(row, 16), :].astype(BF16)
-    else:
-        grad_w_out[...] = grad_out
+            for k in range(CHUNKS):
+                row = pl.multiple_of(((info[9] ^ partner) * CHUNKS + (info[10] ^ k)) * 16, 16)
+                grads[partner & 1][partner >> 1, first + 16 * k : first + 16 * (k + 1), :] = ext[
+                    pl.ds(row, 16), :
+                ].astype(BF16)
+    else:
+        grads[2][...] = grad_out
     unplace(info, total, ext, out)
 
 
@@ -450,7 +584,9 @@
 
 
 ORDER = (0, 2, 4, 6, 1, 3, 5, 7)
-LIMIT = 36 * 1024 * 1024
+CHIPS = [[0, 2, 4, 6], [1, 3, 5, 7]]
+LIMIT = 20 * 1024 * 1024
+SMALL = 8 * 1024 * 1024
 SMEM = pl.BlockSpec(memory_space=pltpu.SMEM)
 VMEM = pl.BlockSpec(memory_space=pltpu.VMEM)
 ANY = pl.BlockSpec(memory_space=pl.ANY)
@@ -464,10 +600,9 @@
     return pltpu.with_memory_space_constraint(array, pltpu.HBM)
 
 
-def run_kernel(body, out_shape, scratch, flops, info, vmem, hbm):
-    operands = (*hbm[:3], *vmem, *hbm[3:])
-    specs = [ANY] * len(hbm[:3]) + [VMEM] * len(vmem) + [ANY] * len(hbm[3:])
-    placed = [near_core(a) if s is VMEM else far_core(a) for a, s in zip(operands, specs)]
+def run_kernel(body, out_shape, scratch, flops, info, *operands):
+    specs = [ANY if isinstance(a, list) else VMEM for a in operands]
+    operands = [a[0] if isinstance(a, list) else near_core(a) for a in operands]
     moved = sum(a.size * a.dtype.itemsize for a in operands)
     return pl.pallas_call(
         body,
@@ -479,7 +614,7 @@
             flops=flops, bytes_accessed=moved, transcendentals=flops // 1024
         ),
         compiler_params=pltpu.CompilerParams(vmem_limit_bytes=LIMIT),
-    )(info, *placed)
+    )(info, *operands)
 
 
 def swap(array, axis, bit):
@@ -535,43 +670,78 @@
             lax.axis_index("seq").reshape(1).astype(jnp.int32),
         ]
     )
-    norms = jnp.stack([norm1_gain, norm1_shift, norm2_gain, norm2_shift], axis=1)
-    first = jnp.concatenate([w_qkv, jnp.pad(norms, ((0, 0), (0, NORMS - 4)))], axis=1)
-    width = first.shape[1]
-    head = [a[i : i + HALO // 2] for a in (tokens, cotangent) for i in (0, HALO // 2)]
-    tail = [a[i : i + HALO // 2] for a in (tokens, cotangent) for i in (ROWS - HALO, ROWS - HALO // 2)]
-    head, tail = jnp.concatenate(head, axis=1), jnp.concatenate(tail, axis=1)
-    odd = lax.axis_index("seq") % 2 == 1
-    to_near, to_far = jnp.where(odd, head, tail), jnp.where(odd, tail, head)
-    if direct:
-        second = jnp.concatenate([w_up, w_down.T, w_out], axis=0)
-        with_near = jnp.concatenate([first, to_near], axis=1)
-        with_far = jnp.concatenate([first, to_far], axis=1)
-        near, middle, far, *second_own = together(
+    width = 4 * D + NORMS
+    vectors = (norm1_gain, norm1_shift, norm2_gain, norm2_shift)
+    if direct:
+        with_near, first, with_far, second, up_near, up_far = pl.pallas_call(
+            prepare_kernel,
+            out_shape=[
+                jax.ShapeDtypeStruct((share, width + 2 * D), BF16),
+                jax.ShapeDtypeStruct((share, width), BF16),
+                jax.ShapeDtypeStruct((share, width + 2 * D), BF16),
+                jax.ShapeDtypeStruct((2 * w_up.shape[0] + 5 * share, D), BF16),
+                jax.ShapeDtypeStruct((2 * w_up.shape[0] + HALO, D), BF16),
+                jax.ShapeDtypeStruct((2 * w_up.shape[0] + HALO, D), BF16),
+            ],
+            in_specs=[ANY] * 10,
+            out_specs=[VMEM] * 6,
+            scratch_shapes=[
+                pltpu.VMEM((4, 1, share), BF16),
+                pltpu.SemaphoreType.DMA((26,)),
+            ],
+            compiler_params=pltpu.CompilerParams(vmem_limit_bytes=LIMIT),
+        )(
+            *[
+                far_core(a)
+                for a in (tokens, cotangent, w_qkv, w_out, w_up, w_down.T)
+                + tuple(v.reshape(1, -1) for v in vectors)
+            ]
+        )
+        block = w_up.shape[0]
+        own_x, own_y, near, middle, far = together(
+            swap(second, "dp", 2),
+            swap(second, "dp", 4),
             swap(with_near, "seq", 1),
             swap(first, "seq", 2),
             swap(with_far, "seq", 3),
-            *along_plane(second),
         )
-        column = jnp.stack([first, near[:, :width], middle, far[:, :width]])
-        second_own = [second] + second_own
+        column = jnp.stack([near[:, :width], middle, far[:, :width]])
         column, second = together(column, second)
-        results = together(*along_plane(column), *along_seq(second), *along_core(second_own))
-        first_plane, rest, second_own = [column, *results[:3]], results[3:6], second_own + [*results[6:]]
+        first_half = lax.all_gather(column, "dp", axis_index_groups=CHIPS)
+        first_half, own_d, *rest = together(
+            first_half,
+            swap(second, "dp", 6),
+            swap(up_near, "seq", 1),
+            swap(second[: 2 * block], "seq", 2),
+            swap(up_far, "seq", 3),
+        )
+        second_own = jnp.stack([second, own_x, own_y, own_d])
+        near_cot, far_cot = rest[0], rest[2]
+        rest = [rest[0][: 2 * block], rest[1], rest[2][: 2 * block]]
         rest = jnp.stack(rest)
-        *first_plane, rest = together(*first_plane, rest)
-        first_all = first_plane + along_core(first_plane)
+        first_half, rest, second_own = together(first_half, rest, second_own)
+        second_own = [second_own, *along_core([second_own])]
+        first_all = [first_half, *along_core([first_half]), *second_own]
         second_plane = along_plane(rest)
     else:
+        norms = jnp.pad(jnp.stack(vectors, axis=1), ((0, 0), (0, NORMS - 4)))
+        first = jnp.concatenate([w_qkv, w_out, norms], axis=1)
+        both = jnp.stack([tokens, cotangent])
+        head, tail = both[:, :HALO], both[:, ROWS - HALO :]
+        odd = lax.axis_index("seq") % 2 == 1
         first_all = [lax.all_gather(first, ("dp", "seq"), axis=0, tiled=True)]
         up_all = lax.all_gather(lax.all_gather(w_up, "dp", axis=0, tiled=True), "seq", axis=0)
         down_all = lax.all_gather(lax.all_gather(w_down.T, "dp", axis=0, tiled=True), "seq", axis=0)
-        second_all = [up_all, down_all, lax.all_gather(w_out, ("dp", "seq"), axis=0, tiled=True)]
+        second_own = second_all = [up_all, down_all]
         from_left = lax.ppermute(tail, "seq", [(i, i + 1) for i in range(n_seq - 1)])
         from_right = lax.ppermute(head, "seq", [(i + 1, i) for i in range(n_seq - 1)])
-        near, far = jnp.where(odd, from_left, from_right), jnp.where(odd, from_right, from_left)
-
-    x, qkv, mixed, probs, w_qkv_all, norms_all = run_kernel(
+        near, near_cot = jnp.where(odd, from_left, from_right)
+        far, far_cot = jnp.where(odd, from_right, from_left)
+
+    def in_hbm(arrays):
+        return [[a] for a in arrays]
+
+    x, qkv, mixed, probs, w_all, norms_all = run_kernel(
         functools.partial(attention_kernel, direct),
         [
             shape((WROWS, D), BF16),
@@ -584,122 +754,165 @@
         [
             pltpu.VMEM((ROWS + 2 * HALO, D), F32),
             pltpu.VMEM((ROWS, D), BF16),
-            pltpu.VMEM((2, HALO // 2, 2 * D), BF16),
-            pltpu.SemaphoreType.DMA((35,)),
+            pltpu.VMEM((2, HALO, D), BF16),
+            pltpu.SemaphoreType.DMA((69,)),
         ],
         2 * WROWS * D * 3 * D * 2,
         info,
-        (),
-        (tokens, near, far, *first_all),
-    )
-    if direct:
-        *second_plane, mixed = together(*second_plane, mixed)
+        *in_hbm((tokens, near, far, *first_all)),
+    )
+    if direct:
+        grads_shape = [shape((4, 2 * block, D), BF16)] * 2
+    else:
+        grads_shape = [shape((1, D, CHUNK), F32)] * 2
+    *state, keep, send = run_kernel(
+        functools.partial(feed_first_kernel, direct),
+        [shape((WROWS, D), F32)] * 3
+        + [shape((WROWS, D), BF16)] * 4
+        + [shape((WROWS, QUAD), F32), *grads_shape],
+        [
+            pltpu.VMEM((1, D, CHUNK), BF16),
+            pltpu.VMEM((1, D, CHUNK), BF16),
+            pltpu.VMEM((ROWS + 2 * HALO, D), F32),
+            pltpu.VMEM((WROWS, CHUNK), BF16),
+            pltpu.VMEM((WROWS, CHUNK), BF16),
+            pltpu.VMEM((ROWS, D), BF16),
+            pltpu.VMEM((2, HALO, D), BF16),
+            pltpu.SemaphoreType.DMA((19,)),
+        ],
+        2 * WROWS * D * (6 * CHUNK + D),
+        info,
+        *in_hbm((cotangent, near_cot, far_cot)),
+        x,
+        mixed,
+        norms_all,
+        w_all,
+        *in_hbm(second_own),
+    )
+    if direct:
+        *second_plane, total = together(*second_plane, state[1])
+        state[1] = total
         second_plane = [rest, *second_plane]
-        second_all = second_own + second_plane + along_core(second_plane)
-        second_all = [a.reshape(-1, *second.shape) for a in second_all]
-        block = (4, n_seq, *second.shape)
-        grads_shape = [shape(block, BF16)] * 2
-    else:
-        grads_shape = [shape((CHUNKS, D, CHUNK), F32)] * 2 + [shape((D, D), F32)]
+        second_all = second_plane + along_core(second_plane)
+        own_pair, *low = add_slots(keep, *along_core([send]))
+        *low, state[1] = together(*low, state[1])
+        own_parts = [swap(part, "dp", 2 * m + 2) for m, part in enumerate(low)]
+        extra = (CHUNKS - 1) * 2 * block
+        grads_shape = [shape((4, extra + n_seq * share, D), BF16)] * 2
+    else:
+        first_grads = [keep, send]
+        grads_shape = [shape((CHUNKS - 1, D, CHUNK), F32)] * 2 + [shape((D, D), F32)]
     out, grad_middle, grad_mixed, grad_norms, *grads = run_kernel(
-        functools.partial(feed_kernel, direct),
+        functools.partial(feed_rest_kernel, direct),
         [
-            shape((ROWS, D), BF16),
+            jax.ShapeDtypeStruct((ROWS, D), BF16),
             shape((WROWS, D), F32),
             shape((WROWS, D), BF16),
             shape((8, D), F32),
             *grads_shape,
         ],
         [
-            pltpu.VMEM((CHUNKS, D, CHUNK), BF16),
-            pltpu.VMEM((CHUNKS, D, CHUNK), BF16),
-            pltpu.VMEM((D, D), BF16),
+            pltpu.VMEM((CHUNKS - 1, D, CHUNK), BF16),
+            pltpu.VMEM((CHUNKS - 1, D, CHUNK), BF16),
             pltpu.VMEM((ROWS + 2 * HALO, D), F32),
-            pltpu.VMEM((WROWS, D), BF16),
-            pltpu.VMEM((WROWS, D), BF16),
-            pltpu.VMEM((WROWS, QUAD), F32),
             pltpu.VMEM((WROWS, D), F32),
             pltpu.VMEM((WROWS, D), F32),
             pltpu.VMEM((WROWS, D), BF16),
-            pltpu.VMEM((WROWS, D), BF16),
             pltpu.VMEM((WROWS, CHUNK), BF16),
             pltpu.VMEM((WROWS, CHUNK), BF16),
-            pltpu.VMEM((WROWS, D), F32),
-            pltpu.VMEM((ROWS, D), BF16),
-            pltpu.VMEM((2, HALO // 2, 2 * D), BF16),
-            pltpu.SemaphoreType.DMA((67,)),
+            pltpu.SemaphoreType.DMA((16,)),
         ],
-        2 * WROWS * D * (6 * FF + 3 * D),
+        2 * WROWS * D * (18 * CHUNK + 2 * D),
         info,
-        (x, mixed, norms_all),
-        (cotangent, near, far, *second_all),
-    )
-    if direct:
-        pair = add_parts(grads[0], along_core(grads[1:]))
-        second_pair, low_own, low_rest, grad_mixed = together(
-            pair[0], pair[1:, 0].astype(BF16), pair[1:, 1:].astype(BF16), grad_mixed
-        )
-        second_parts = [swap(low_rest[m], "dp", 2 * m + 2) for m in range(3)]
-        grads_shape = [shape((4, n_seq, share, width), BF16)] * 2
-    else:
-        grad_up = lax.psum_scatter(grads[0], "seq", scatter_dimension=0)
+        *state,
+        mixed,
+        norms_all,
+        w_all,
+        *in_hbm(second_all),
+    )
+    if direct:
+        keep, send, *own_parts = together(*grads, *own_parts)
+        pair, *low = add_slots(keep, *along_core([send]))
+        *low, grad_mixed = together(*low, grad_mixed)
+        parts = [swap(part, "dp", 2 * m + 2) for m, part in enumerate(low)]
+        grads_shape = [shape((4, n_seq, share, 3 * D + NORMS), BF16)] * 2
+    else:
+        grads_up, grads_down = [
+            jnp.concatenate([a, b], axis=0) for a, b in zip(first_grads, grads[:2])
+        ]
+        grad_up = lax.psum_scatter(grads_up, "seq", scatter_dimension=0)
         grad_up = lax.psum_scatter(grad_up, "dp", scatter_dimension=0, tiled=True)
-        grad_down = lax.psum_scatter(grads[1], "seq", scatter_dimension=0)
+        grad_down = lax.psum_scatter(grads_down, "seq", scatter_dimension=0)
         grad_down = lax.psum_scatter(grad_down, "dp", scatter_dimension=0, tiled=True).T
         grad_out = lax.psum_scatter(grads[2], ("dp", "seq"), scatter_dimension=0, tiled=True)
-        grads_shape = [shape((D, width), F32)]
+        grads_shape = [shape((D, 3 * D + NORMS), F32)]
     tokens_grad, *grads = run_kernel(
         functools.partial(back_kernel, direct),
-        [shape((ROWS, D), BF16), *grads_shape],
+        [jax.ShapeDtypeStruct((ROWS, D), BF16), *grads_shape],
         [
             pltpu.VMEM((ROWS + 2 * HALO, D), F32),
             pltpu.VMEM((WROWS, D), BF16),
             pltpu.VMEM((WROWS, 3 * D), BF16),
             pltpu.VMEM((WROWS, D), F32),
             pltpu.VMEM((NORMS, D), F32),
-            pltpu.VMEM((D, width), F32),
+            pltpu.VMEM((D, 3 * D + NORMS), F32),
             pltpu.VMEM((WROWS, QUAD), F32),
         ],
         2 * WROWS * D * (6 * D + 3 * D),
         info,
-        (x, qkv, probs, grad_mixed, grad_middle, w_qkv_all, norms_all, grad_norms),
-        (),
-    )
-    if direct:
-        keep, send, *second_parts = together(*grads, *second_parts)
-        pair = add_parts(keep, along_core([send]))
-        low, first_own, second_rest = together(
-            pair[1:].astype(BF16), pair[0], add_parts(second_pair[1:], second_parts)
+        x,
+        qkv,
+        probs,
+        grad_mixed,
+        grad_middle,
+        w_all,
+        norms_all,
+        grad_norms,
+    )
+    if direct:
+        sends = [grads[1][m] for m in range(4)]
+        from_core = along_core(sends)
+        keep, *parts = together(grads[0], *from_core, *parts)
+        from_core, parts = parts[:4], parts[4:]
+        first_pair, *first_low = add_pairs(keep, from_core)
+        rows = [(slice(2 * block * k, 2 * block * (k + 1)),) for k in range(CHUNKS - 1)]
+        out_rows = [(slice(extra + share * k, extra + share * (k + 1)),) for k in range(n_seq)]
+        top, bottom = (slice(0, 2 * block),), (slice(2 * block, 2 * block + share),)
+        plan = [[(slice(None), out_rows[0])]]
+        plan += [[(top, r), (bottom, o)] for r, o in zip(rows, out_rows[1:])]
+        sizes = [((share, D), F32)] + [((2 * block + share, D), BF16)] * (n_seq - 1)
+        out_own, *low = add(plan, sizes, pair, *parts)
+        first = [swap(part, "dp", 2 * m + 2) for m, part in enumerate(first_low)]
+        second = [swap(low[1], "seq", 2), swap(low[2], "seq", 3)]
+        near_low, x0, x1, x2 = together(low[0], *first)
+        first_own, *first_low = add_slots(first_pair, x0, x1, x2)
+        first_parts = [swap(part, "seq", k + 1) for k, part in enumerate(first_low)]
+        second.append(swap(near_low, "seq", 1))
+        top, bottom = (slice(0, block),), (slice(block, 2 * block),)
+        everything = slice(None)
+        grad_up, grad_down = add(
+            [[(everything, top)], [(everything, bottom)]],
+            [((block, D), F32)] * 2,
+            own_pair,
+            *own_parts,
+            *second,
         )
-        second_low = second_rest.astype(BF16)
-        parts = together(
-            *[swap(low[m], "dp", 2 * m + 2) for m in range(3)],
-            *[swap(second_low[k], "seq", k + 1) for k in range(3)],
-        )
-        first_column = add_parts(first_own, parts[:3])
-        low, low_own, first_own = together(
-            first_column[1:].astype(BF16), low_own, first_column[0]
-        )
-        first_parts = [swap(low[k], "seq", k + 1) for k in range(3)]
-        own_parts = [swap(low_own[m], "dp", 2 * m + 2) for m in range(3)]
-        second_sum = add_parts(second_pair[0], [*parts[3:], *own_parts])
-        first_sum = add_parts(first_own, first_parts)
-        grad_up = second_sum[: D // 8]
-        grad_down = second_sum[D // 8 : D // 4].T
-        grad_out = second_sum[D // 4 :]
+        grad_down = grad_down.T
+        (grad_out,) = add_tail(out_own, second, 2 * block)
+        w_qkv_grad, *norm_grads = finish_first(first_own, first_parts)
+        norm_grads = [grad.reshape(share) for grad in norm_grads]
     else:
         first_sum = lax.psum_scatter(grads[0], ("dp", "seq"), scatter_dimension=0, tiled=True)
+        w_qkv_grad = first_sum[:, : 3 * D]
+        norm_grads = [first_sum[:, 3 * D + i] for i in range(4)]
     return (
         out,
         tokens_grad,
-        first_sum[:, : 3 * D],
+        w_qkv_grad,
         grad_out,
         grad_up,
         grad_down,
-        first_sum[:, 3 * D],
-        first_sum[:, 3 * D + 1],
-        first_sum[:, 3 * D + 2],
-        first_sum[:, 3 * D + 3],
+        *norm_grads,
     )
 
 

time: 156 us -> 140 us (0.90)
  waiting for transfers between devices: 43.3 us -> 28.4 us
  blocking collectives: 0 us -> 12.2 us
  starting transfers between devices: 49.3 us -> 39.9 us
  Pallas kernels: 48.7 us -> 58 us
  local copies, waits for them, and re-layouts: 7.21 us -> 0.3 us
  other arithmetic: 5.71 us -> 0.27 us
    ppermute x44 -> x39, waiting for transfers between devices: 43.3 us -> 28.4 us  [swap(): lax.ppermute(array, axis, [(i, i ^ bit) for i in range(lax.axis_size(axis...]
    all_gather x0 -> x1, blocking collectives: none -> 12.2 us  [per_device(): first_half = lax.all_gather(column, 'dp', axis_index_groups=CHIPS)]
    ppermute x44 -> x39, starting transfers between devices: 49.3 us -> 39.9 us  [swap(): lax.ppermute(array, axis, [(i, i ^ bit) for i in range(lax.axis_size(axis...]
    pallas_call x3 -> x4, Pallas kernels: 48.7 us -> 53.4 us  [run_kernel(): pl.pallas_call(body, out_shape=out_shape, in_specs=[SMEM] + specs, out_sp...]
    pallas_call x0 -> x9, Pallas kernels: none -> 4.57 us  [the longest x5 1.57 us: add(): pl.pallas_call(functools.partial(sum_kernel, plan), out_shape=[jax.ShapeD...]
    slice x7 -> x1, local copies, waits for them, and re-layouts: 3.05 us -> 0.01 us  [per_device(): second[:2 * block]]
    unnamed x55 -> x9, local copies, waits for them, and re-layouts: 2.86 us -> 0.11 us
    another operation x4 -> x2, other arithmetic: 2.47 us -> 0.14 us  [the longest x1 0.11 us: per_device(): second_own = jnp.stack([second, own_x, own_y, own_d])]
  transfers between devices with their start and end apart: 44 -> 39, of which waited for: 25 -> 12; matrix products, arithmetic and copies ran while one was open for 5% -> 0% of each run, Pallas kernels for 17% -> 39%
where the time goes in v3:
time: 140 us
  Pallas kernels  58 us (41%)
  starting transfers between devices  39.9 us (28%)
  waiting for transfers between devices  28.4 us (20%)
  blocking collectives  12.2 us (9%)
    pallas_call x4, Pallas kernels, run_kernel(): pl.pallas_call(body, out_shape=out_shape, in_specs=[SMEM] + specs, out_sp...  53.4 us
    ppermute x39, starting transfers between devices, swap(): lax.ppermute(array, axis, [(i, i ^ bit) for i in range(lax.axis_size(axis...  39.9 us
    ppermute x39, waiting for transfers between devices, swap(): lax.ppermute(array, axis, [(i, i ^ bit) for i in range(lax.axis_size(axis...  28.4 us
    all_gather x1, blocking collectives, per_device(): first_half = lax.all_gather(column, 'dp', axis_index_groups=CHIPS)  12.2 us
  transfers between devices with their start and end apart: 39, of which 12 were waited for; matrix products, arithmetic and copies ran while one was open for 0% of the time, Pallas kernels for 39%

profile of v3, /device:TPU:0, one launch (start us, length us, event | category | flops | bytes accessed | tf_op | source)
XLA Modules:
  0.0 140.0 jit_solution(7544750511959631100)
XLA Ops:
  0.6 1.5 %shard_map.195 = (bf16[16,3200]{1,0:T(8,128)(2,1)S(1)}, bf16[16,2176]{1,0:T(8,128)(2,1)S(1)}, bf16[16,3200]{1,0:T(8,128)(2,1)S(1)}, bf16[208,512]{1,0:T(8,128)(2...) custom-call(bf16[704,512]{1,0:T(8,128)(2,1)} %rows.2, bf16[704,512]{1,0:T(8,128)(2,1)} %rows.3, ...), custom_call_target="tpu_custom_call" | custom-call | tf_op jit(solution)/shard_map/pallas_call | solution.py:676
  2.2 3.0 %collective-permute-start.1 = (bf16[208,512]{1,0:T(8,128)(2,1)S(1)}, bf16[208,512]{1,0:T(8,128)(2,1)S(1)}, u32[]{:S(2)}, u32[]{:S(2)}) collective-permute-start(bf16[208,512]{1,0:T(8,128)(2,1)S(1)} %get-tuple-element.120), channel_id=1, source_target_pairs={{0,16},{4,20},{8,24},{12,28},{16,0},{20,4},{24,8},{28,12},{1,17},{... | collective-permute-start | bytes 638984 | tf_op jit(solution)/shard_map/ppermute | solution.py:621
  6.7 1.6 %collective-permute-start.2 = (bf16[16,3200]{1,0:T(8,128)(2,1)S(1)}, bf16[16,3200]{1,0:T(8,128)(2,1)S(1)}, u32[]{:S(2)}, u32[]{:S(2)}) collective-permute-start(bf16[16,3200]{1,0:T(8,128)(2,1)S(1)} %get-tuple-element.113), channel_id=1, source_target_pairs={{0,1},{1,0},{2,3},{3,2},{4,5},{5,4},{6,7},{7,6},{8,9},{9,8},{10,11... | collective-permute-start | bytes 307208 | tf_op jit(solution)/shard_map/ppermute | solution.py:621
  8.3 2.5 %collective-permute-start.4 = (bf16[16,3200]{1,0:T(8,128)(2,1)S(1)}, bf16[16,3200]{1,0:T(8,128)(2,1)S(1)}, u32[]{:S(2)}, u32[]{:S(2)}) collective-permute-start(bf16[16,3200]{1,0:T(8,128)(2,1)S(1)} %get-tuple-element.115), channel_id=1, source_target_pairs={{0,3},{1,2},{2,1},{3,0},{4,7},{5,6},{6,5},{7,4},{8,11},{9,10},{10,... | collective-permute-start | bytes 307208 | tf_op jit(solution)/shard_map/ppermute | solution.py:621
  10.9 7.2 %collective-permute-done.3 = bf16[16,2176]{1,0:T(8,128)(2,1)S(1)} collective-permute-done((bf16[16,2176]{1,0:T(8,128)(2,1)S(1)}, bf16[16,2176]{1,0:T(8,128)(2,1)S(1)}, u32[]{:S(2)}, u32[]{:S(2)}) %collective-permute-start.3) | collective-permute-done | bytes 69664 | tf_op jit(solution)/shard_map/ppermute | solution.py:621
  18.7 2.6 %collective-permute-start.8 = (bf16[160,512]{1,0:T(8,128)(2,1)S(1)}, bf16[160,512]{1,0:T(8,128)(2,1)S(1)}, u32[]{:S(2)}, u32[]{:S(2)}) collective-permute-start(bf16[160,512]{1,0:T(8,128)(2,1)S(1)} %get-tuple-element.122), channel_id=1, source_target_pairs={{0,3},{1,2},{2,1},{3,0},{4,7},{5,6},{6,5},{7,4},{8,11},{9,10},{10,... | collective-permute-start | bytes 491528 | tf_op jit(solution)/shard_map/ppermute | solution.py:621
  22.3 12.2 %all-gather = bf16[12,16,2176]{2,1,0:T(8,128)(2,1)S(1)} all-gather(bf16[3,16,2176]{2,1,0:T(8,128)(2,1)S(1)} %pad_maximum_fusion.2), channel_id=2, replica_groups={{0,8,16,24},{4,12,20,28},{1,9,17,25},{5,13,21,29},{2,10,18,26},{6,14,22..., dimensions={0}, use_global_device_ids=true | all-gather | bytes 1044480 | tf_op jit(solution)/shard_map/all_gather | solution.py:710
  35.6 1.7 %collective-permute-start.14 = (bf16[3,128,512]{2,1,0:T(8,128)(2,1)S(1)}, bf16[3,128,512]{2,1,0:T(8,128)(2,1)S(1)}, u32[]{:S(2)}, u32[]{:S(2)}) collective-permute-start(bf16[3,128,512]{2,1,0:T(8,128)(2,1)S(1)} %pad_maximum_fusion.1.refs_11_), channel_id=1, source_target_pairs={{0,24},{4,28},{8,16},{12,20},{16,8},{20,12},{24,0},{28,4},{1,25},{... | collective-permute-start | bytes 1179656 | tf_op jit(solution)/shard_map/ppermute | solution.py:621
  37.2 1.5 %collective-permute-start.13 = (bf16[3,128,512]{2,1,0:T(8,128)(2,1)S(1)}, bf16[3,128,512]{2,1,0:T(8,128)(2,1)S(1)}, u32[]{:S(2)}, u32[]{:S(2)}) collective-permute-start(bf16[3,128,512]{2,1,0:T(8,128)(2,1)S(1)} %pad_maximum_fusion.1.refs_11_), channel_id=1, source_target_pairs={{0,16},{4,20},{8,24},{12,28},{16,0},{20,4},{24,8},{28,12},{1,17},{... | collective-permute-start | bytes 1179656 | tf_op jit(solution)/shard_map/ppermute | solution.py:621
  39.1 13.9 %shard_map.196 = (bf16[768,512]{1,0:T(8,128)(2,1)S(1)}, bf16[768,1536]{1,0:T(8,128)(2,1)S(1)}, bf16[768,512]{1,0:T(8,128)(2,1)S(1)}, bf16[768,512]{1,0:T(8,128)(...) custom-call(s32[11]{0:T(128)S(1)} %pad_add_fusion.info, bf16[704,512]{1,0:T(8,128)(2,1)S(1)} %copy-done, ...), custom_call_target="tpu_custom_call" | custom-call | flops 2415919104 | bytes 4300800 | tf_op jit(solution)/shard_map/pallas_call | solution.py:607
  53.0 7.9 %shard_map.197 = (f32[768,512]{1,0:T(8,128)S(1)}, f32[768,512]{1,0:T(8,128)S(1)}, f32[768,512]{1,0:T(8,128)S(1)}, bf16[768,512]{1,0:T(8,128)(2,1)S(1)}, bf16[768...) custom-call(s32[11]{0:T(128)S(1)} %pad_add_fusion.info, ...), custom_call_target="tpu_custom_call" | custom-call | flops 2818572288 | bytes 6569984 | tf_op jit(solution)/shard_map/pallas_call | solution.py:607
  63.0 1.8 %collective-permute-start.19 = (bf16[128,512]{1,0:T(8,128)(2,1)S(1)}, bf16[128,512]{1,0:T(8,128)(2,1)S(1)}, u32[]{:S(2)}, u32[]{:S(2)}) collective-permute-start(bf16[128,512]{1,0:T(8,128)(2,1)S(1)} %get-tuple-element.160), channel_id=1, source_target_pairs={{0,8},{4,12},{8,0},{12,4},{16,24},{20,28},{24,16},{28,20},{1,9},{5... | collective-permute-start | bytes 393224 | tf_op jit(solution)/shard_map/ppermute | solution.py:621
  66.7 17.2 %shard_map.199 = (bf16[704,512]{1,0:T(8,128)(2,1)}, f32[768,512]{1,0:T(8,128)S(1)}, bf16[768,512]{1,0:T(8,128)(2,1)S(1)}, f32[8,512]{1,0:T(8,128)S(1)}, bf16[4,4...) custom-call(s32[11]{0:T(128)S(1)} %pad_add_fusion.info, f32[768,512]{1,0:T(8,128)S(1)} %get-tuple-element.136.refs_0_, ...), custom_call_target="tpu_custom_call" | custom-call | flops 8053063680 | bytes 14434304 | tf_op jit(solution)/shard_map/pallas_call | solution.py:607
  84.0 3.8 %collective-permute-done.22.refs_1_ = bf16[4,448,512]{2,1,0:T(8,128)(2,1)S(1)} collective-permute-done((bf16[4,448,512]{2,1,0:T(8,128)(2,1)S(1)}, bf16[4,448,512]{2,1,0:T(8,128)(2,1)S(1)}, u32[]{:S(2)}, u32[]{:S(2)}) %collective-permute-start.22) | collective-permute-done | bytes 1835040 | tf_op jit(solution)/shard_map/ppermute | solution.py:621
  88.2 1.7 %collective-permute-start.27 = (bf16[448,512]{1,0:T(8,128)(2,1)S(1)}, bf16[448,512]{1,0:T(8,128)(2,1)S(1)}, u32[]{:S(2)}, u32[]{:S(2)}) collective-permute-start(bf16[448,512]{1,0:T(8,128)(2,1)S(1)} %get-tuple-element.175), channel_id=1, source_target_pairs={{0,8},{4,12},{8,0},{12,4},{16,24},{20,28},{24,16},{28,20},{1,9},{5... | collective-permute-start | bytes 1376264 | tf_op jit(solution)/shard_map/ppermute | solution.py:621
  91.7 14.4 %shard_map.201 = (bf16[704,512]{1,0:T(8,128)(2,1)}, bf16[4,4,16,1664]{3,2,1,0:T(8,128)(2,1)S(1)}, bf16[4,4,16,1664]{3,2,1,0:T(8,128)(2,1)S(1)}) custom-call(s32[11]{0:T(128)S(1)} %pad_add_fusion.info, bf16[768,512]{1,0:T(8,128)(2,1)S(1)} %get-tuple-element.132.x_in, bf16[768,1536]{1,0:T(8,128)(2,1)S(1)} %get-tuple-element.156.qkv, ...), custom_call_target="tpu_custom_call" | custom-call | flops 3623878656 | bytes 8552448 | tf_op jit(solution)/shard_map/pallas_call | solution.py:607
  109.5 2.5 %collective-permute-done.28.refs_2_ = bf16[448,512]{1,0:T(8,128)(2,1)S(1)} collective-permute-done((bf16[448,512]{1,0:T(8,128)(2,1)S(1)}, bf16[448,512]{1,0:T(8,128)(2,1)S(1)}, u32[]{:S(2)}, u32[]{:S(2)}) %collective-permute-start.28) | collective-permute-done | bytes 458784 | tf_op jit(solution)/shard_map/ppermute | solution.py:621
  112.6 1.7 %collective-permute-start.31 = (bf16[4,16,1664]{2,1,0:T(8,128)(2,1)S(1)}, bf16[4,16,1664]{2,1,0:T(8,128)(2,1)S(1)}, u32[]{:S(2)}, u32[]{:S(2)}) collective-permute-start(bf16[4,16,1664]{2,1,0:T(8,128)(2,1)S(1)} %get-tuple-element.190), channel_id=1, source_target_pairs={{0,16},{4,20},{8,24},{12,28},{16,0},{20,4},{24,8},{28,12},{1,17},{... | collective-permute-start | bytes 638984 | tf_op jit(solution)/shard_map/ppermute | solution.py:621
  116.0 2.2 %collective-permute-start.36 = (bf16[144,512]{1,0:T(8,128)(2,1)S(1)}, bf16[144,512]{1,0:T(8,128)(2,1)S(1)}, u32[]{:S(2)}, u32[]{:S(2)}) collective-permute-start(bf16[144,512]{1,0:T(8,128)(2,1)S(1)} %get-tuple-element.201), channel_id=1, source_target_pairs={{0,2},{1,3},{2,0},{3,1},{4,6},{5,7},{6,4},{7,5},{8,10},{9,11},{10,... | collective-permute-start | bytes 442376 | tf_op jit(solution)/shard_map/ppermute | solution.py:621
  120.5 2.8 %collective-permute-done.31.refs_2_ = bf16[4,16,1664]{2,1,0:T(8,128)(2,1)S(1)} collective-permute-done((bf16[4,16,1664]{2,1,0:T(8,128)(2,1)S(1)}, bf16[4,16,1664]{2,1,0:T(8,128)(2,1)S(1)}, u32[]{:S(2)}, u32[]{:S(2)}) %collective-permute-start.31) | collective-permute-done | bytes 213024 | tf_op jit(solution)/shard_map/ppermute | solution.py:621
  125.5 2.0 %collective-permute-start.34 = (bf16[16,1664]{1,0:T(8,128)(2,1)S(1)}, bf16[16,1664]{1,0:T(8,128)(2,1)S(1)}, u32[]{:S(2)}, u32[]{:S(2)}) collective-permute-start(bf16[16,1664]{1,0:T(8,128)(2,1)S(1)} %get-tuple-element.197), channel_id=1, source_target_pairs={{0,2},{1,3},{2,0},{3,1},{4,6},{5,7},{6,4},{7,5},{8,10},{9,11},{10,... | collective-permute-start | bytes 159752 | tf_op jit(solution)/shard_map/ppermute | solution.py:621
  127.5 4.5 %collective-permute-done.33.one = bf16[16,1664]{1,0:T(8,128)(2,1)S(1)} collective-permute-done((bf16[16,1664]{1,0:T(8,128)(2,1)S(1)}, bf16[16,1664]{1,0:T(8,128)(2,1)S(1)}, u32[]{:S(2)}, u32[]{:S(2)}) %collective-permute-start.33) | collective-permute-done | bytes 53280 | tf_op jit(solution)/shard_map/ppermute | solution.py:621
  132.0 2.6 %collective-permute-start.35 = (bf16[16,1664]{1,0:T(8,128)(2,1)S(1)}, bf16[16,1664]{1,0:T(8,128)(2,1)S(1)}, u32[]{:S(2)}, u32[]{:S(2)}) collective-permute-start(bf16[16,1664]{1,0:T(8,128)(2,1)S(1)} %get-tuple-element.198), channel_id=1, source_target_pairs={{0,3},{1,2},{2,1},{3,0},{4,7},{5,6},{6,5},{7,4},{8,11},{9,10},{10,... | collective-permute-start | bytes 159752 | tf_op jit(solution)/shard_map/ppermute | solution.py:621
  134.6 3.3 %collective-permute-done.35.three = bf16[16,1664]{1,0:T(8,128)(2,1)S(1)} collective-permute-done((bf16[16,1664]{1,0:T(8,128)(2,1)S(1)}, bf16[16,1664]{1,0:T(8,128)(2,1)S(1)}, u32[]{:S(2)}, u32[]{:S(2)}) %collective-permute-start.35) | collective-permute-done | bytes 53280 | tf_op jit(solution)/shard_map/ppermute | solution.py:621
  (87 shorter events, 22.9 us)
Async XLA Ops:
  2.2 15.9 %collective-permute-start.1 = (bf16[208,512]{1,0:T(8,128)(2,1)S(1)}, bf16[208,512]{1,0:T(8,128)(2,1)S(1)}, u32[]{:S(2)}, u32[]{:S(2)}) collective-permute-start(bf16[208,512]{1,0:T(8,128)(2,1)S(1)} %get-tuple-element.120), channel_id=1, source_target_pairs={{0,16},{4,20},{8,24},{12,28},{16,0},{20,4},{24,8},{28,12},{1,17},{... | collective-permute-start | bytes 638984 | tf_op jit(solution)/shard_map/ppermute | solution.py:621
  5.2 12.9 %collective-permute-start = (bf16[208,512]{1,0:T(8,128)(2,1)S(1)}, bf16[208,512]{1,0:T(8,128)(2,1)S(1)}, u32[]{:S(2)}, u32[]{:S(2)}) collective-permute-start(bf16[208,512]{1,0:T(8,128)(2,1)S(1)} %get-tuple-element.120), channel_id=1, source_target_pairs={{0,8},{4,12},{8,0},{12,4},{16,24},{20,28},{24,16},{28,20},{1,9},{5... | collective-permute-start | bytes 638984 | tf_op jit(solution)/shard_map/ppermute | solution.py:621
  6.7 11.4 %collective-permute-start.2 = (bf16[16,3200]{1,0:T(8,128)(2,1)S(1)}, bf16[16,3200]{1,0:T(8,128)(2,1)S(1)}, u32[]{:S(2)}, u32[]{:S(2)}) collective-permute-start(bf16[16,3200]{1,0:T(8,128)(2,1)S(1)} %get-tuple-element.113), channel_id=1, source_target_pairs={{0,1},{1,0},{2,3},{3,2},{4,5},{5,4},{6,7},{7,6},{8,9},{9,8},{10,11... | collective-permute-start | bytes 307208 | tf_op jit(solution)/shard_map/ppermute | solution.py:621
  8.3 9.8 %collective-permute-start.4 = (bf16[16,3200]{1,0:T(8,128)(2,1)S(1)}, bf16[16,3200]{1,0:T(8,128)(2,1)S(1)}, u32[]{:S(2)}, u32[]{:S(2)}) collective-permute-start(bf16[16,3200]{1,0:T(8,128)(2,1)S(1)} %get-tuple-element.115), channel_id=1, source_target_pairs={{0,3},{1,2},{2,1},{3,0},{4,7},{5,6},{6,5},{7,4},{8,11},{9,10},{10,... | collective-permute-start | bytes 307208 | tf_op jit(solution)/shard_map/ppermute | solution.py:621
  18.2 16.3 %collective-permute-start.5 = (bf16[208,512]{1,0:T(8,128)(2,1)S(1)}, bf16[208,512]{1,0:T(8,128)(2,1)S(1)}, u32[]{:S(2)}, u32[]{:S(2)}) collective-permute-start(bf16[208,512]{1,0:T(8,128)(2,1)S(1)} %get-tuple-element.120), channel_id=1, source_target_pairs={{0,24},{4,28},{8,16},{12,20},{16,8},{20,12},{24,0},{28,4},{1,25},{... | collective-permute-start | bytes 638984 | tf_op jit(solution)/shard_map/ppermute | solution.py:621
  18.7 15.8 %collective-permute-start.6 = (bf16[160,512]{1,0:T(8,128)(2,1)S(1)}, bf16[160,512]{1,0:T(8,128)(2,1)S(1)}, u32[]{:S(2)}, u32[]{:S(2)}) collective-permute-start(bf16[160,512]{1,0:T(8,128)(2,1)S(1)} %get-tuple-element.121), channel_id=1, source_target_pairs={{0,1},{1,0},{2,3},{3,2},{4,5},{5,4},{6,7},{7,6},{8,9},{9,8},{10,11... | collective-permute-start | bytes 491528 | tf_op jit(solution)/shard_map/ppermute | solution.py:621
  18.7 15.8 %collective-permute-start.8 = (bf16[160,512]{1,0:T(8,128)(2,1)S(1)}, bf16[160,512]{1,0:T(8,128)(2,1)S(1)}, u32[]{:S(2)}, u32[]{:S(2)}) collective-permute-start(bf16[160,512]{1,0:T(8,128)(2,1)S(1)} %get-tuple-element.122), channel_id=1, source_target_pairs={{0,3},{1,2},{2,1},{3,0},{4,7},{5,6},{6,5},{7,4},{8,11},{9,10},{10,... | collective-permute-start | bytes 491528 | tf_op jit(solution)/shard_map/ppermute | solution.py:621
  21.4 13.1 %collective-permute-start.7 = (bf16[128,512]{1,0:T(8,128)(2,1)S(1)}, bf16[128,512]{1,0:T(8,128)(2,1)S(1)}, u32[]{:S(2)}, u32[]{:S(2)}) collective-permute-start(bf16[128,512]{1,0:T(8,128)(2,1)S(1)} %slice.29), channel_id=1, source_target_pairs={{0,2},{1,3},{2,0},{3,1},{4,6},{5,7},{6,4},{7,5},{8,10},{9,11},{10,... | collective-permute-start | bytes 393224 | tf_op jit(solution)/shard_map/ppermute | solution.py:621
  35.6 25.9 %collective-permute-start.14 = (bf16[3,128,512]{2,1,0:T(8,128)(2,1)S(1)}, bf16[3,128,512]{2,1,0:T(8,128)(2,1)S(1)}, u32[]{:S(2)}, u32[]{:S(2)}) collective-permute-start(bf16[3,128,512]{2,1,0:T(8,128)(2,1)S(1)} %pad_maximum_fusion.1.refs_11_), channel_id=1, source_target_pairs={{0,24},{4,28},{8,16},{12,20},{16,8},{20,12},{24,0},{28,4},{1,25},{... | collective-permute-start | bytes 1179656 | tf_op jit(solution)/shard_map/ppermute | solution.py:621
  37.2 24.2 %collective-permute-start.13 = (bf16[3,128,512]{2,1,0:T(8,128)(2,1)S(1)}, bf16[3,128,512]{2,1,0:T(8,128)(2,1)S(1)}, u32[]{:S(2)}, u32[]{:S(2)}) collective-permute-start(bf16[3,128,512]{2,1,0:T(8,128)(2,1)S(1)} %pad_maximum_fusion.1.refs_11_), channel_id=1, source_target_pairs={{0,16},{4,20},{8,24},{12,28},{16,0},{20,4},{24,8},{28,12},{1,17},{... | collective-permute-start | bytes 1179656 | tf_op jit(solution)/shard_map/ppermute | solution.py:621
  38.8 22.7 %collective-permute-start.12 = (bf16[3,128,512]{2,1,0:T(8,128)(2,1)S(1)}, bf16[3,128,512]{2,1,0:T(8,128)(2,1)S(1)}, u32[]{:S(2)}, u32[]{:S(2)}) collective-permute-start(bf16[3,128,512]{2,1,0:T(8,128)(2,1)S(1)} %pad_maximum_fusion.1.refs_11_), channel_id=1, source_target_pairs={{0,8},{4,12},{8,0},{12,4},{16,24},{20,28},{24,16},{28,20},{1,9},{5... | collective-permute-start | bytes 1179656 | tf_op jit(solution)/shard_map/ppermute | solution.py:621
  63.0 20.9 %collective-permute-start.19 = (bf16[128,512]{1,0:T(8,128)(2,1)S(1)}, bf16[128,512]{1,0:T(8,128)(2,1)S(1)}, u32[]{:S(2)}, u32[]{:S(2)}) collective-permute-start(bf16[128,512]{1,0:T(8,128)(2,1)S(1)} %get-tuple-element.160), channel_id=1, source_target_pairs={{0,8},{4,12},{8,0},{12,4},{16,24},{20,28},{24,16},{28,20},{1,9},{5... | collective-permute-start | bytes 393224 | tf_op jit(solution)/shard_map/ppermute | solution.py:621
  64.8 19.1 %collective-permute-start.20 = (bf16[128,512]{1,0:T(8,128)(2,1)S(1)}, bf16[128,512]{1,0:T(8,128)(2,1)S(1)}, u32[]{:S(2)}, u32[]{:S(2)}) collective-permute-start(bf16[128,512]{1,0:T(8,128)(2,1)S(1)} %get-tuple-element.161), channel_id=1, source_target_pairs={{0,16},{4,20},{8,24},{12,28},{16,0},{20,4},{24,8},{28,12},{1,17},{... | collective-permute-start | bytes 393224 | tf_op jit(solution)/shard_map/ppermute | solution.py:621
  65.3 18.6 %collective-permute-start.21 = (bf16[128,512]{1,0:T(8,128)(2,1)S(1)}, bf16[128,512]{1,0:T(8,128)(2,1)S(1)}, u32[]{:S(2)}, u32[]{:S(2)}) collective-permute-start(bf16[128,512]{1,0:T(8,128)(2,1)S(1)} %get-tuple-element.162), channel_id=1, source_target_pairs={{0,24},{4,28},{8,16},{12,20},{16,8},{20,12},{24,0},{28,4},{1,25},{... | collective-permute-start | bytes 393224 | tf_op jit(solution)/shard_map/ppermute | solution.py:621
  88.2 21.3 %collective-permute-start.27 = (bf16[448,512]{1,0:T(8,128)(2,1)S(1)}, bf16[448,512]{1,0:T(8,128)(2,1)S(1)}, u32[]{:S(2)}, u32[]{:S(2)}) collective-permute-start(bf16[448,512]{1,0:T(8,128)(2,1)S(1)} %get-tuple-element.175), channel_id=1, source_target_pairs={{0,8},{4,12},{8,0},{12,4},{16,24},{20,28},{24,16},{28,20},{1,9},{5... | collective-permute-start | bytes 1376264 | tf_op jit(solution)/shard_map/ppermute | solution.py:621
  89.9 22.1 %collective-permute-start.28 = (bf16[448,512]{1,0:T(8,128)(2,1)S(1)}, bf16[448,512]{1,0:T(8,128)(2,1)S(1)}, u32[]{:S(2)}, u32[]{:S(2)}) collective-permute-start(bf16[448,512]{1,0:T(8,128)(2,1)S(1)} %get-tuple-element.176), channel_id=1, source_target_pairs={{0,16},{4,20},{8,24},{12,28},{16,0},{20,4},{24,8},{28,12},{1,17},{... | collective-permute-start | bytes 1376264 | tf_op jit(solution)/shard_map/ppermute | solution.py:621
  90.4 21.6 %collective-permute-start.29 = (bf16[448,512]{1,0:T(8,128)(2,1)S(1)}, bf16[448,512]{1,0:T(8,128)(2,1)S(1)}, u32[]{:S(2)}, u32[]{:S(2)}) collective-permute-start(bf16[448,512]{1,0:T(8,128)(2,1)S(1)} %get-tuple-element.177), channel_id=1, source_target_pairs={{0,24},{4,28},{8,16},{12,20},{16,8},{20,12},{24,0},{28,4},{1,25},{... | collective-permute-start | bytes 1376264 | tf_op jit(solution)/shard_map/ppermute | solution.py:621
  112.2 8.3 %collective-permute-start.30 = (bf16[4,16,1664]{2,1,0:T(8,128)(2,1)S(1)}, bf16[4,16,1664]{2,1,0:T(8,128)(2,1)S(1)}, u32[]{:S(2)}, u32[]{:S(2)}) collective-permute-start(bf16[4,16,1664]{2,1,0:T(8,128)(2,1)S(1)} %get-tuple-element.189), channel_id=1, source_target_pairs={{0,8},{4,12},{8,0},{12,4},{16,24},{20,28},{24,16},{28,20},{1,9},{5... | collective-permute-start | bytes 638984 | tf_op jit(solution)/shard_map/ppermute | solution.py:621
  112.6 10.6 %collective-permute-start.31 = (bf16[4,16,1664]{2,1,0:T(8,128)(2,1)S(1)}, bf16[4,16,1664]{2,1,0:T(8,128)(2,1)S(1)}, u32[]{:S(2)}, u32[]{:S(2)}) collective-permute-start(bf16[4,16,1664]{2,1,0:T(8,128)(2,1)S(1)} %get-tuple-element.190), channel_id=1, source_target_pairs={{0,16},{4,20},{8,24},{12,28},{16,0},{20,4},{24,8},{28,12},{1,17},{... | collective-permute-start | bytes 638984 | tf_op jit(solution)/shard_map/ppermute | solution.py:621
  114.3 8.9 %collective-permute-start.32 = (bf16[4,16,1664]{2,1,0:T(8,128)(2,1)S(1)}, bf16[4,16,1664]{2,1,0:T(8,128)(2,1)S(1)}, u32[]{:S(2)}, u32[]{:S(2)}) collective-permute-start(bf16[4,16,1664]{2,1,0:T(8,128)(2,1)S(1)} %get-tuple-element.191), channel_id=1, source_target_pairs={{0,24},{4,28},{8,16},{12,20},{16,8},{20,12},{24,0},{28,4},{1,25},{... | collective-permute-start | bytes 638984 | tf_op jit(solution)/shard_map/ppermute | solution.py:621
  116.0 22.6 %collective-permute-start.36 = (bf16[144,512]{1,0:T(8,128)(2,1)S(1)}, bf16[144,512]{1,0:T(8,128)(2,1)S(1)}, u32[]{:S(2)}, u32[]{:S(2)}) collective-permute-start(bf16[144,512]{1,0:T(8,128)(2,1)S(1)} %get-tuple-element.201), channel_id=1, source_target_pairs={{0,2},{1,3},{2,0},{3,1},{4,6},{5,7},{6,4},{7,5},{8,10},{9,11},{10,... | collective-permute-start | bytes 442376 | tf_op jit(solution)/shard_map/ppermute | solution.py:621
  118.1 20.5 %collective-permute-start.37 = (bf16[144,512]{1,0:T(8,128)(2,1)S(1)}, bf16[144,512]{1,0:T(8,128)(2,1)S(1)}, u32[]{:S(2)}, u32[]{:S(2)}) collective-permute-start(bf16[144,512]{1,0:T(8,128)(2,1)S(1)} %get-tuple-element.202), channel_id=1, source_target_pairs={{0,3},{1,2},{2,1},{3,0},{4,7},{5,6},{6,5},{7,4},{8,11},{9,10},{10,... | collective-permute-start | bytes 442376 | tf_op jit(solution)/shard_map/ppermute | solution.py:621
  123.3 15.3 %collective-permute-start.38 = (bf16[144,512]{1,0:T(8,128)(2,1)S(1)}, bf16[144,512]{1,0:T(8,128)(2,1)S(1)}, u32[]{:S(2)}, u32[]{:S(2)}) collective-permute-start(bf16[144,512]{1,0:T(8,128)(2,1)S(1)} %get-tuple-element.203), channel_id=1, source_target_pairs={{0,1},{1,0},{2,3},{3,2},{4,5},{5,4},{6,7},{7,6},{8,9},{9,8},{10,11... | collective-permute-start | bytes 442376 | tf_op jit(solution)/shard_map/ppermute | solution.py:621
  125.5 9.2 %collective-permute-start.34 = (bf16[16,1664]{1,0:T(8,128)(2,1)S(1)}, bf16[16,1664]{1,0:T(8,128)(2,1)S(1)}, u32[]{:S(2)}, u32[]{:S(2)}) collective-permute-start(bf16[16,1664]{1,0:T(8,128)(2,1)S(1)} %get-tuple-element.197), channel_id=1, source_target_pairs={{0,2},{1,3},{2,0},{3,1},{4,6},{5,7},{6,4},{7,5},{8,10},{9,11},{10,... | collective-permute-start | bytes 159752 | tf_op jit(solution)/shard_map/ppermute | solution.py:621
  (19 other events, 122.1 us)

commit v4 on v3

--- a/solution.py
+++ b/solution.py
@@ -18,7 +18,7 @@
 WIN = 4 * FREQ
 WINDOWS = STEPS_DEV // 4 + 2
 WROWS = WINDOWS * WIN
-TILE = 256
+TILE = 768
 QUAD = 128
 NORMS = 128
 CHUNK = 512
@@ -100,8 +100,11 @@
         copy.wait()
 
 
-def row_copies(rows, near, far, stage, halos):
-    pairs = [(rows, stage)]
+def edge_copies(rows, near, far, ext_low, halos):
+    pairs = [
+        (rows.at[0:HALO, :], ext_low.at[0:HALO, :]),
+        (rows.at[ROWS - 2 * HALO :, :], ext_low.at[HALO:, :]),
+    ]
     for i, parts in enumerate((near, far)):
         size = HALO // len(parts)
         pairs += [
@@ -110,12 +113,53 @@
     return pairs
 
 
-def pad_rows(info, ext, stage, halos):
-    ext[HALO : HALO + ROWS] = stage[...].astype(F32)
+def pad_edges(info, ext, ext_low, halos):
+    ext[HALO : 2 * HALO] = ext_low[0:HALO].astype(F32)
+    ext[ROWS - HALO : ROWS + HALO] = ext_low[HALO:].astype(F32)
     odd = info[10] % 2 == 1
     for i, is_left in enumerate((odd, jnp.logical_not(odd))):
         at = pl.multiple_of(jnp.where(is_left, 0, HALO + ROWS), HALO)
         ext[pl.ds(at, HALO), :] = halos[i].astype(F32)
+
+
+EDGES = (0, WINDOWS - 2, WINDOWS - 1)
+
+
+def place_rows(info, w, ext, out):
+    row, low, high, _, _, _ = window_place(info, w)
+    values = jnp.where(row_mask(low, high), ext[pl.ds(row, WIN), :], 0.0)
+    out[window_at(w), :] = values.astype(BF16)
+
+
+def place_cotangent(info, w, ext, cot, cot_own):
+    row, low, high, own_low, own_high, _ = window_place(info, w)
+    values = ext[pl.ds(row, WIN), :]
+    cot[window_at(w), :] = jnp.where(row_mask(low, high), values, 0.0).astype(BF16)
+    cot_own[window_at(w), :] = jnp.where(row_mask(own_low, own_high), values, 0.0).astype(BF16)
+
+
+def layout_kernel(info, tokens, cotangent, x_out, cot, cot_own, own, ext, stage, sems):
+    copies = copy_all([(tokens, stage.at[0]), (cotangent, stage.at[1])], sems)
+    for edge in (slice(0, HALO), slice(HALO + ROWS, 2 * HALO + ROWS)):
+        ext[edge, :] = jnp.zeros((HALO, D), F32)
+    copies[0].wait()
+    ext[HALO : HALO + ROWS] = stage[0].astype(F32)
+
+    def tokens_step(w, carry):
+        place_rows(info, w, ext, x_out)
+        return carry
+
+    lax.fori_loop(0, WINDOWS, tokens_step, 0, unroll=4)
+    copies[1].wait()
+    ext[HALO : HALO + ROWS] = stage[1].astype(F32)
+
+    def cotangent_step(w, carry):
+        place_cotangent(info, w, ext, cot, cot_own)
+        mask = row_mask(*window_place(info, w)[3:5])
+        own[window_at(w), :] = jnp.where(mask, jnp.ones((WIN, QUAD), F32), 0.0)
+        return carry
+
+    lax.fori_loop(0, WINDOWS, cotangent_step, 0, unroll=4)
 
 
 def normalized(values):
@@ -166,24 +210,6 @@
         out_specs=[VMEM] * len(shapes),
         compiler_params=pltpu.CompilerParams(vmem_limit_bytes=SMALL),
     )(*[near_core(a) for a in operands])
-
-
-def tail_kernel(row, own, *refs):
-    parts, out = refs[:-1], refs[-1]
-    total = own[...]
-    for part in parts:
-        total = total + part[row : row + out.shape[0], :].astype(F32)
-    out[...] = total
-
-
-def add_tail(own, parts, row):
-    return pl.pallas_call(
-        functools.partial(tail_kernel, row),
-        out_shape=[jax.ShapeDtypeStruct(own.shape, F32)],
-        in_specs=[VMEM] * (1 + len(parts)),
-        out_specs=[VMEM],
-        compiler_params=pltpu.CompilerParams(vmem_limit_bytes=SMALL),
-    )(*[near_core(a) for a in (own, *parts)])
 
 
 def pair_kernel(keep, *refs):
@@ -200,6 +226,42 @@
         out_specs=[VMEM] * 4,
         compiler_params=pltpu.CompilerParams(vmem_limit_bytes=SMALL),
     )(*[near_core(a) for a in (keep, *parts)])
+
+
+def chunks_kernel(keep_first, keep_rest, keep_out, first, rest, out, *refs):
+    own, near, pair, *low = refs
+    block, share = keep_first.shape[1], keep_out.shape[1] // CHUNKS
+
+    def sums(slot, k):
+        a, b, row = (keep_first, first, 0) if k == 0 else (keep_rest, rest, (k - 1) * block)
+        rows, out_rows = slice(row, row + block), slice(share * k, share * (k + 1))
+        return (
+            a[slot, rows].astype(F32) + b[slot, rows].astype(F32),
+            keep_out[slot, out_rows].astype(F32) + out[slot, out_rows].astype(F32),
+        )
+
+    for slot in range(4):
+        for k in range(CHUNKS):
+            if k < 2:
+                target, row = (own, near)[k].at[slot], 0
+            else:
+                target, row = ([pair] + low)[slot], (k - 2) * (block + share)
+            one, two = sums(slot, k)
+            target[row : row + block, :] = one.astype(target.dtype)
+            target[row + block : row + block + share, :] = two.astype(target.dtype)
+
+
+def add_chunks(keeps, parts):
+    rows = keeps[0].shape[1] + keeps[2].shape[1] // CHUNKS
+    shapes = [((4, rows, D), F32), ((4, rows, D), BF16), ((2 * rows, D), F32)]
+    shapes += [((2 * rows, D), BF16)] * 3
+    return pl.pallas_call(
+        chunks_kernel,
+        out_shape=[jax.ShapeDtypeStruct(*s) for s in shapes],
+        in_specs=[VMEM] * 6,
+        out_specs=[VMEM] * 6,
+        compiler_params=pltpu.CompilerParams(vmem_limit_bytes=SMALL),
+    )(*[near_core(a) for a in (*keeps, *parts)])
 
 
 def finish_kernel(own, one, two, three, grad, *norm_grads):
@@ -260,46 +322,38 @@
     wait_all(copies[len(norms) :])
 
 
-def attention_kernel(direct, info, rows, near, far, *refs):
+def attention_kernel(direct, info, rows, near, far, x_in, *refs):
     pieces, refs = (refs[:4], refs[4:]) if direct else (refs[:1], refs[1:])
-    x_out, qkv_out, mixed_out, probs_out, w_out, norms_out, ext, stage, halos, sems = refs
+    x_out, qkv_out, mixed_out, probs_out, w_out, norms_out, ext, edges, halos, sems = refs
     width = w_out.shape[1]
     near, far = [
         [a.at[:, width + j * D : width + (j + 1) * D] for j in range(2)] if direct else [a]
         for a in (near, far)
     ]
-    row_copy = copy_all(row_copies(rows, near, far, stage, halos), sems)
-    if direct:
-        count, share, pairs = pieces[0].shape[1] + 1, pieces[0].shape[2], []
+    edge_copy = copy_all(edge_copies(rows, near, far, edges, halos), sems)
+    x_out[...] = x_in[...]
+    if direct:
+        count, share = pieces[0].shape[1] + 1, pieces[0].shape[2]
         for core, piece in enumerate(pieces[:2]):
             for chip in range(4):
                 for k in range(1, count):
                     owner = (2 * chip + (info[9] % 2 ^ core)) * count + (info[10] ^ k)
                     at = pl.multiple_of(owner * share, share)
-                    pairs.append((piece.at[chip, k - 1], w_out.at[pl.ds(at, share), :]))
-        own = [piece.at[m] for piece in pieces[2:] for m in range(4)]
-        for piece, partner in zip(own, ORDER):
+                    w_out[pl.ds(at, share), :] = piece[chip, k - 1]
+        for i, partner in enumerate(ORDER):
             owner = (info[9] ^ partner) * count + info[10]
             at = pl.ds(pl.multiple_of(owner * share, share), share)
-            for i in range(5):
-                cols = min(D, w_out.shape[1] - i * D)
-                row = D // 4 + i * share
-                source = piece.at[row : row + share, 0:cols]
-                pairs.append((source, w_out.at[at, i * D : i * D + cols]))
+            for j in range(5):
+                cols = min(D, width - j * D)
+                row = D // 4 + j * share
+                part = pieces[2 + i // 4][i % 4, row : row + share, 0:cols]
+                w_out[at, j * D : j * D + cols] = part
     else:
-        pairs = [(pieces[0], w_out)]
-    w_copy = copy_all(pairs, sems, len(row_copy))
-    wait_all(row_copy)
-    pad_rows(info, ext, stage, halos)
-
-    def place(w, carry):
-        row, low, high, _, _, _ = window_place(info, w)
-        values = jnp.where(row_mask(low, high), ext[pl.ds(row, WIN), :], 0.0)
-        x_out[window_at(w), :] = values.astype(BF16)
-        return carry
-
-    lax.fori_loop(0, WINDOWS, place, 0, unroll=4)
-    wait_all(w_copy)
+        w_out[...] = pieces[0][...]
+    wait_all(edge_copy)
+    pad_edges(info, ext, edges, halos)
+    for w in EDGES:
+        place_rows(info, w, ext, x_out)
     norms_out[...] = jnp.transpose(w_out[:, 4 * D :].astype(F32))[:8]
     gain, shift = norms_out[0:1], norms_out[1:2]
 
@@ -344,7 +398,7 @@
             mixed_out[at, quad * QUAD : (quad + 1) * QUAD] = mixed
         return carry
 
-    lax.fori_loop(0, WINDOWS, attend, 0, unroll=4)
+    lax.fori_loop(0, WINDOWS, attend, 0, unroll=12)
 
 
 def gelu_parts(values):
@@ -362,13 +416,13 @@
     return jnp.where(values >= 0, 1.0 - tail, tail), half_exp * 0.3989422804014327
 
 
-def feed_pieces(info, pieces, up, down):
-    block, pairs = D // 8, []
+def place_feed(info, pieces, up, down):
+    block = D // 8
     for piece, partner in zip(pieces, ORDER):
         at = pl.ds(pl.multiple_of((info[9] ^ partner) * block, block), block)
-        pairs.append((piece.at[:, 0:block, :], up.at[:, at, :]))
-        pairs.append((piece.at[:, block : 2 * block, :], down.at[:, at, :]))
-    return pairs
+        for c in range(up.shape[0]):
+            up[c, at, :] = piece[c, 0:block, :]
+            down[c, at, :] = piece[c, block : 2 * block, :]
 
 
 def feed_rows(at, up, down, normed, cot, hidden, pre):
@@ -398,31 +452,24 @@
             ].astype(BF16)
 
 
-def feed_first_kernel(direct, info, rows, near, far, x_in, mixed_in, norms, w_all, *refs):
+def feed_first_kernel(
+    direct, info, rows, near, far, cot_in, cot_own_in, own, x_in, mixed_in, norms, w_all, *refs
+):
     pieces, refs = refs[:2], refs[2:]
-    middle, total, grad, normed, normed_own, cot, cot_own, own = refs[:8]
-    grads, (up, down, ext, hidden, pre, stage, halos, sems) = refs[8:10], refs[10:]
+    middle, total, grad, normed, normed_own, cot, cot_own = refs[:7]
+    grads, (up, down, ext, hidden, pre, edges, halos, sems) = refs[7:9], refs[9:]
     near, far = [[a.at[a.shape[0] - HALO :, :]] for a in (near, far)]
-    row_copy = copy_all(row_copies(rows, near, far, stage, halos), sems)
+    edge_copy = copy_all(edge_copies(rows, near, far, edges, halos), sems)
+    cot[...], cot_own[...] = cot_in[...], cot_own_in[...]
     if direct:
         own_pieces = [piece.at[m : m + 1] for piece in pieces for m in range(4)]
-        pairs = feed_pieces(info, own_pieces, up, down)
+        place_feed(info, own_pieces, up, down)
     else:
-        pairs = [(pieces[0].at[0:1], up), (pieces[1].at[0:1], down)]
-    first_copy = copy_all(pairs, sems, len(row_copy))
-    wait_all(row_copy)
-    pad_rows(info, ext, stage, halos)
-
-    def place(w, carry):
-        row, low, high, own_low, own_high, _ = window_place(info, w)
-        values = ext[pl.ds(row, WIN), :]
-        at = window_at(w)
-        cot[at, :] = jnp.where(row_mask(low, high), values, 0.0).astype(BF16)
-        cot_own[at, :] = jnp.where(row_mask(own_low, own_high), values, 0.0).astype(BF16)
-        own[at, :] = jnp.where(row_mask(own_low, own_high), jnp.ones((WIN, QUAD), F32), 0.0)
-        return carry
-
-    lax.fori_loop(0, WINDOWS, place, 0, unroll=4)
+        up[...], down[...] = pieces[0][0:1], pieces[1][0:1]
+    wait_all(edge_copy)
+    pad_edges(info, ext, edges, halos)
+    for w in EDGES:
+        place_cotangent(info, w, ext, cot, cot_own)
     gain, shift = norms[2:3], norms[3:4]
 
     def before(i, carry):
@@ -436,7 +483,6 @@
         return carry
 
     lax.fori_loop(0, WROWS // TILE, before, 0)
-    wait_all(first_copy)
     for i in range(WROWS // TILE):
         at = slice(i * TILE, (i + 1) * TILE)
         branch, back = feed_rows(at, up[0], down[0], normed, cot, hidden, pre)
@@ -445,31 +491,28 @@
     feed_grads(direct, info, 0, normed_own, cot_own, hidden, pre, ext, grads)
 
 
-def feed_rest_kernel(direct, info, *refs):
-    middle, total_in, grad_in, normed, normed_own, cot, cot_own, own = refs[:8]
-    mixed_in, norms, w_all = refs[8:11]
-    pieces, refs = (refs[11:19], refs[19:]) if direct else (refs[11:13], refs[13:])
-    out, grad_middle, grad_mixed, grad_norms = refs[:4]
-    grads, refs = (refs[4:6], refs[6:]) if direct else (refs[4:7], refs[7:])
-    up, down, ext, total, grad, grad_own, hidden, pre, sems = refs
-    if direct:
-        pairs = feed_pieces(info, pieces, up, down)
+def feed_rest_kernel(direct, info, total_in, grad_in, normed, normed_own, cot, cot_own, *refs):
+    pieces, refs = (refs[:8], refs[8:]) if direct else (refs[:2], refs[2:])
+    total, grad, *grads, up, down, ext, hidden, pre = refs
+    if direct:
+        place_feed(info, pieces, up, down)
     else:
-        pairs = [(pieces[0].at[1:CHUNKS], up), (pieces[1].at[1:CHUNKS], down)]
-    wait_all(copy_all(pairs, sems))
-    block = D // 8
-    gain = norms[2:3]
+        up[...], down[...] = pieces[0][1:CHUNKS], pieces[1][1:CHUNKS]
     for c in range(CHUNKS - 1):
         for i in range(WROWS // TILE):
             at = slice(i * TILE, (i + 1) * TILE)
             branch, back = feed_rows(at, up[c], down[c], normed, cot, hidden, pre)
             total[at, :] = (total if c else total_in)[at, :] + branch
             grad[at, :] = (grad if c else grad_in)[at, :] + back
-        feed_grads(direct, info, c * 2 * block, normed_own, cot_own, hidden, pre, ext, grads)
+        feed_grads(direct, info, c * (D // 4), normed_own, cot_own, hidden, pre, ext, grads)
+
+
+def feed_last_kernel(direct, info, middle, grad, cot, own, mixed_in, norms, w_all, *refs):
+    grad_middle, grad_mixed, grad_norms, *grads, ext, grad_own = refs
+    gain = norms[2:3]
     grad_norms[...] = jnp.zeros(grad_norms.shape, F32)
-
-    def after(i, carry):
-        at = tile_at(i)
+    for i in range(WROWS // TILE):
+        at = slice(i * TILE, (i + 1) * TILE)
         unit, scale = normalized(middle[at, :])
         part = grad[at, :]
         masked = part * own[at, 0:1]
@@ -477,25 +520,28 @@
         grad_norms[1:2] += jnp.sum(masked, axis=0, keepdims=True)
         result = cot[at, :].astype(F32) + norm_back(part * gain, unit, scale)
         grad_middle[at, :] = result
-        low = result.astype(BF16)
-        grad_mixed[at, :] = mm_right(low, w_all[:, 3 * D : 4 * D]).astype(BF16)
+        grad_mixed[at, :] = mm_right(result.astype(BF16), w_all[:, 3 * D : 4 * D]).astype(BF16)
         grad_own[at, :] = (result * own[at, 0:1]).astype(BF16)
-        return carry
-
-    lax.fori_loop(0, WROWS // TILE, after, 0)
     grad_out = mm_left(mixed_in[...], grad_own[...])
     if direct:
         ext[0:D, :] = grad_out
-        first = (CHUNKS - 1) * 2 * block
+        share = grads[0].shape[1] // CHUNKS
         for partner in range(8):
             for k in range(CHUNKS):
-                row = pl.multiple_of(((info[9] ^ partner) * CHUNKS + (info[10] ^ k)) * 16, 16)
-                grads[partner & 1][partner >> 1, first + 16 * k : first + 16 * (k + 1), :] = ext[
-                    pl.ds(row, 16), :
+                owner = (info[9] ^ partner) * CHUNKS + (info[10] ^ k)
+                row = pl.multiple_of(owner * share, share)
+                grads[partner & 1][partner >> 1, share * k : share * (k + 1), :] = ext[
+                    pl.ds(row, share), :
                 ].astype(BF16)
     else:
-        grads[2][...] = grad_out
+        grads[0][...] = grad_out
+
+
+def finish_rows_kernel(info, total, x_in, grad_normed, grad_middle, norms, out, tokens_grad, ext):
     unplace(info, total, ext, out)
+    unit, scale = normalized(x_in[...].astype(F32))
+    grad_normed[...] = grad_middle[...] + norm_back(grad_normed[...] * norms[0:1], unit, scale)
+    unplace(info, grad_normed, ext, tokens_grad)
 
 
 def unplace(info, values, ext, out):
@@ -511,22 +557,19 @@
 
 
 def back_kernel(
-    direct, info, x_in, qkv, probs_in, grad_mixed, grad_middle, w_qkv, norms, grad_norms, *refs
+    direct, info, x_in, own, qkv, probs_in, grad_mixed, w_qkv, norms, grad_norms, *refs
 ):
-    out, refs = refs[0], refs[1:]
+    grad_normed, refs = refs[0], refs[1:]
     if direct:
         (keep, send), refs = refs[:2], refs[2:]
     else:
         w_grad, refs = refs[0], refs[1:]
-    ext, normed, grad_qkv, result, gains, grad_w, own = refs
+    normed, grad_qkv, gains, grad_w = refs
     masks = head_masks()
     lane = lax.broadcasted_iota(jnp.int32, (1, QUAD), 1) // HEAD_DIM
 
     def attend_back(w, carry):
         at = window_at(w)
-        own[at, :] = jnp.where(
-            row_mask(*window_place(info, w)[3:5]), jnp.ones((WIN, QUAD), F32), 0.0
-        )
         quads = range(D // QUAD)
         cols = [slice(quad * QUAD, (quad + 1) * QUAD) for quad in quads]
         cols_key = [slice(D + quad * QUAD, D + (quad + 1) * QUAD) for quad in quads]
@@ -549,20 +592,20 @@
             grad_qkv[at, cols[quad]] = gathered(grad_query[quad], lane).astype(BF16)
         return carry
 
-    lax.fori_loop(0, WINDOWS, attend_back, 0, unroll=4)
+    lax.fori_loop(0, WINDOWS, attend_back, 0, unroll=12)
     gain, shift = norms[0:1], norms[1:2]
     gains[...] = jnp.zeros(gains.shape, F32)
 
     def after(i, carry):
         at = tile_at(i)
-        unit, scale = normalized(x_in[at, :].astype(F32))
+        unit, _ = normalized(x_in[at, :].astype(F32))
         mask = own[at, 0:1]
         normed[at, :] = ((unit * gain + shift) * mask).astype(BF16)
         part = mm_right(grad_qkv[at, :], w_qkv[:, : 3 * D])
         masked = part * mask
         gains[0:1] += jnp.sum(masked * unit, axis=0, keepdims=True)
         gains[1:2] += jnp.sum(masked, axis=0, keepdims=True)
-        result[at, :] = grad_middle[at, :] + norm_back(part * gain, unit, scale)
+        grad_normed[at, :] = part
         return carry
 
     lax.fori_loop(0, WROWS // TILE, after, 0)
@@ -580,7 +623,6 @@
                 target[partner >> 1, k] = grad_w[pl.ds(row, 16), :].astype(BF16)
     else:
         w_grad[...] = grad_w[...]
-    unplace(info, result, ext, out)
 
 
 ORDER = (0, 2, 4, 6, 1, 3, 5, 7)
@@ -672,6 +714,22 @@
     )
     width = 4 * D + NORMS
     vectors = (norm1_gain, norm1_shift, norm2_gain, norm2_shift)
+
+    def in_hbm(arrays):
+        return [[a] for a in arrays]
+
+    x, cot, cot_own, own = run_kernel(
+        layout_kernel,
+        [shape((WROWS, D), BF16)] * 3 + [shape((WROWS, QUAD), F32)],
+        [
+            pltpu.VMEM((ROWS + 2 * HALO, D), F32),
+            pltpu.VMEM((2, ROWS, D), BF16),
+            pltpu.SemaphoreType.DMA((2,)),
+        ],
+        2 * WROWS * D * D,
+        info,
+        *in_hbm((tokens, cotangent)),
+    )
     if direct:
         with_near, first, with_far, second, up_near, up_far = pl.pallas_call(
             prepare_kernel,
@@ -698,12 +756,16 @@
             ]
         )
         block = w_up.shape[0]
-        own_x, own_y, near, middle, far = together(
+        own_x, own_y, near, middle, far, x, cot, cot_own, own = together(
             swap(second, "dp", 2),
             swap(second, "dp", 4),
             swap(with_near, "seq", 1),
             swap(first, "seq", 2),
             swap(with_far, "seq", 3),
+            x,
+            cot,
+            cot_own,
+            own,
         )
         column = jnp.stack([near[:, :width], middle, far[:, :width]])
         column, second = together(column, second)
@@ -738,9 +800,6 @@
         near, near_cot = jnp.where(odd, from_left, from_right)
         far, far_cot = jnp.where(odd, from_right, from_left)
 
-    def in_hbm(arrays):
-        return [[a] for a in arrays]
-
     x, qkv, mixed, probs, w_all, norms_all = run_kernel(
         functools.partial(attention_kernel, direct),
         [
@@ -753,13 +812,15 @@
         ],
         [
             pltpu.VMEM((ROWS + 2 * HALO, D), F32),
-            pltpu.VMEM((ROWS, D), BF16),
+            pltpu.VMEM((3 * HALO, D), BF16),
             pltpu.VMEM((2, HALO, D), BF16),
-            pltpu.SemaphoreType.DMA((69,)),
+            pltpu.SemaphoreType.DMA((6,)),
         ],
         2 * WROWS * D * 3 * D * 2,
         info,
-        *in_hbm((tokens, near, far, *first_all)),
+        *in_hbm((tokens, near, far)),
+        x,
+        *first_all,
     )
     if direct:
         grads_shape = [shape((4, 2 * block, D), BF16)] * 2
@@ -769,136 +830,161 @@
         functools.partial(feed_first_kernel, direct),
         [shape((WROWS, D), F32)] * 3
         + [shape((WROWS, D), BF16)] * 4
-        + [shape((WROWS, QUAD), F32), *grads_shape],
+        + grads_shape,
         [
             pltpu.VMEM((1, D, CHUNK), BF16),
             pltpu.VMEM((1, D, CHUNK), BF16),
             pltpu.VMEM((ROWS + 2 * HALO, D), F32),
             pltpu.VMEM((WROWS, CHUNK), BF16),
             pltpu.VMEM((WROWS, CHUNK), BF16),
-            pltpu.VMEM((ROWS, D), BF16),
+            pltpu.VMEM((3 * HALO, D), BF16),
             pltpu.VMEM((2, HALO, D), BF16),
-            pltpu.SemaphoreType.DMA((19,)),
+            pltpu.SemaphoreType.DMA((4,)),
         ],
         2 * WROWS * D * (6 * CHUNK + D),
         info,
         *in_hbm((cotangent, near_cot, far_cot)),
+        cot,
+        cot_own,
+        own,
         x,
         mixed,
         norms_all,
         w_all,
-        *in_hbm(second_own),
+        *second_own,
     )
     if direct:
         *second_plane, total = together(*second_plane, state[1])
         state[1] = total
         second_plane = [rest, *second_plane]
         second_all = second_plane + along_core(second_plane)
-        own_pair, *low = add_slots(keep, *along_core([send]))
-        *low, state[1] = together(*low, state[1])
-        own_parts = [swap(part, "dp", 2 * m + 2) for m, part in enumerate(low)]
+        first_grads = [keep, send]
         extra = (CHUNKS - 1) * 2 * block
-        grads_shape = [shape((4, extra + n_seq * share, D), BF16)] * 2
+        grads_shape = [shape((4, extra, D), BF16)] * 2
+        out_shape = [shape((4, n_seq * share, D), BF16)] * 2
     else:
         first_grads = [keep, send]
-        grads_shape = [shape((CHUNKS - 1, D, CHUNK), F32)] * 2 + [shape((D, D), F32)]
-    out, grad_middle, grad_mixed, grad_norms, *grads = run_kernel(
+        grads_shape = [shape((CHUNKS - 1, D, CHUNK), F32)] * 2
+        out_shape = [shape((D, D), F32)]
+    middle, total, grad, normed, normed_own, cot, cot_own = state
+    total, grad, *grads = run_kernel(
         functools.partial(feed_rest_kernel, direct),
+        [shape((WROWS, D), F32)] * 2 + grads_shape,
         [
-            jax.ShapeDtypeStruct((ROWS, D), BF16),
+            pltpu.VMEM((CHUNKS - 1, D, CHUNK), BF16),
+            pltpu.VMEM((CHUNKS - 1, D, CHUNK), BF16),
+            pltpu.VMEM((D, D), F32),
+            pltpu.VMEM((WROWS, CHUNK), BF16),
+            pltpu.VMEM((WROWS, CHUNK), BF16),
+        ],
+        2 * WROWS * D * 18 * CHUNK,
+        info,
+        total,
+        grad,
+        normed,
+        normed_own,
+        cot,
+        cot_own,
+        *second_all,
+    )
+    if direct:
+        from_core = along_core([first_grads[1], grads[1]])
+    grad_middle, grad_mixed, grad_norms, *out_grads = run_kernel(
+        functools.partial(feed_last_kernel, direct),
+        [
             shape((WROWS, D), F32),
             shape((WROWS, D), BF16),
             shape((8, D), F32),
-            *grads_shape,
+            *out_shape,
         ],
-        [
-            pltpu.VMEM((CHUNKS - 1, D, CHUNK), BF16),
-            pltpu.VMEM((CHUNKS - 1, D, CHUNK), BF16),
-            pltpu.VMEM((ROWS + 2 * HALO, D), F32),
-            pltpu.VMEM((WROWS, D), F32),
-            pltpu.VMEM((WROWS, D), F32),
-            pltpu.VMEM((WROWS, D), BF16),
-            pltpu.VMEM((WROWS, CHUNK), BF16),
-            pltpu.VMEM((WROWS, CHUNK), BF16),
-            pltpu.SemaphoreType.DMA((16,)),
-        ],
-        2 * WROWS * D * (18 * CHUNK + 2 * D),
+        [pltpu.VMEM((D, D), F32), pltpu.VMEM((WROWS, D), BF16)],
+        2 * WROWS * D * 2 * D,
         info,
-        *state,
+        middle,
+        grad,
+        cot,
+        own,
         mixed,
         norms_all,
         w_all,
-        *in_hbm(second_all),
-    )
-    if direct:
-        keep, send, *own_parts = together(*grads, *own_parts)
-        pair, *low = add_slots(keep, *along_core([send]))
-        *low, grad_mixed = together(*low, grad_mixed)
+    )
+    if direct:
+        from_core = [*from_core, *along_core(out_grads[1:])]
+        keeps, from_core = [first_grads[0], grads[0], out_grads[0]], together(*from_core)
+        own_pair, to_near, pair, *low = add_chunks(keeps, from_core)
+        to_near, *low, grad_mixed = together(to_near, *low, grad_mixed)
         parts = [swap(part, "dp", 2 * m + 2) for m, part in enumerate(low)]
+        parts.append(swap(to_near, "seq", 1))
         grads_shape = [shape((4, n_seq, share, 3 * D + NORMS), BF16)] * 2
     else:
         grads_up, grads_down = [
-            jnp.concatenate([a, b], axis=0) for a, b in zip(first_grads, grads[:2])
+            jnp.concatenate([a, b], axis=0) for a, b in zip(first_grads, grads)
         ]
         grad_up = lax.psum_scatter(grads_up, "seq", scatter_dimension=0)
         grad_up = lax.psum_scatter(grad_up, "dp", scatter_dimension=0, tiled=True)
         grad_down = lax.psum_scatter(grads_down, "seq", scatter_dimension=0)
         grad_down = lax.psum_scatter(grad_down, "dp", scatter_dimension=0, tiled=True).T
-        grad_out = lax.psum_scatter(grads[2], ("dp", "seq"), scatter_dimension=0, tiled=True)
+        grad_out = lax.psum_scatter(out_grads[0], ("dp", "seq"), scatter_dimension=0, tiled=True)
         grads_shape = [shape((D, 3 * D + NORMS), F32)]
-    tokens_grad, *grads = run_kernel(
+    grad_normed, *grads = run_kernel(
         functools.partial(back_kernel, direct),
-        [jax.ShapeDtypeStruct((ROWS, D), BF16), *grads_shape],
+        [shape((WROWS, D), F32), *grads_shape],
         [
-            pltpu.VMEM((ROWS + 2 * HALO, D), F32),
             pltpu.VMEM((WROWS, D), BF16),
             pltpu.VMEM((WROWS, 3 * D), BF16),
-            pltpu.VMEM((WROWS, D), F32),
             pltpu.VMEM((NORMS, D), F32),
             pltpu.VMEM((D, 3 * D + NORMS), F32),
-            pltpu.VMEM((WROWS, QUAD), F32),
         ],
         2 * WROWS * D * (6 * D + 3 * D),
         info,
         x,
+        own,
         qkv,
         probs,
         grad_mixed,
-        grad_middle,
         w_all,
         norms_all,
         grad_norms,
     )
     if direct:
-        sends = [grads[1][m] for m in range(4)]
-        from_core = along_core(sends)
-        keep, *parts = together(grads[0], *from_core, *parts)
-        from_core, parts = parts[:4], parts[4:]
-        first_pair, *first_low = add_pairs(keep, from_core)
-        rows = [(slice(2 * block * k, 2 * block * (k + 1)),) for k in range(CHUNKS - 1)]
-        out_rows = [(slice(extra + share * k, extra + share * (k + 1)),) for k in range(n_seq)]
-        top, bottom = (slice(0, 2 * block),), (slice(2 * block, 2 * block + share),)
-        plan = [[(slice(None), out_rows[0])]]
-        plan += [[(top, r), (bottom, o)] for r, o in zip(rows, out_rows[1:])]
-        sizes = [((share, D), F32)] + [((2 * block + share, D), BF16)] * (n_seq - 1)
-        out_own, *low = add(plan, sizes, pair, *parts)
+        grad_normed, *grads = together(grad_normed, *grads)
+    out, tokens_grad = run_kernel(
+        finish_rows_kernel,
+        [jax.ShapeDtypeStruct((ROWS, D), BF16)] * 2,
+        [pltpu.VMEM((ROWS + 2 * HALO, D), F32)],
+        2 * WROWS * D * D,
+        info,
+        total,
+        x,
+        grad_normed,
+        grad_middle,
+        norms_all,
+    )
+    if direct:
+        keep, send, *parts, from_near = together(*grads, *parts)
+        rows = 2 * block + share
+        plan = [[(slice(None), (slice(k * rows, (k + 1) * rows),))] for k in range(2)]
+        low = add(plan, [((rows, D), BF16)] * 2, pair, *parts)
+        second = [swap(low[0], "seq", 2), swap(low[1], "seq", 3)]
+        first_pair, *first_low = add_slots(keep, *along_core([send]))
         first = [swap(part, "dp", 2 * m + 2) for m, part in enumerate(first_low)]
-        second = [swap(low[1], "seq", 2), swap(low[2], "seq", 3)]
-        near_low, x0, x1, x2 = together(low[0], *first)
-        first_own, *first_low = add_slots(first_pair, x0, x1, x2)
+        own_pair, *own_low = add_slots(own_pair, from_near)
+        *first, own0, own1, own2 = together(*first, *own_low)
+        first_own, *first_low = add_slots(first_pair, *first)
         first_parts = [swap(part, "seq", k + 1) for k, part in enumerate(first_low)]
-        second.append(swap(near_low, "seq", 1))
-        top, bottom = (slice(0, block),), (slice(block, 2 * block),)
-        everything = slice(None)
-        grad_up, grad_down = add(
-            [[(everything, top)], [(everything, bottom)]],
-            [((block, D), F32)] * 2,
+        own_parts = [swap(part, "dp", 2 * m + 2) for m, part in enumerate((own0, own1, own2))]
+        everything, bounds = slice(None), (0, block, 2 * block, rows)
+        grad_up, grad_down, grad_out = add(
+            [[(everything, (slice(a, b),))] for a, b in zip(bounds, bounds[1:])],
+            [((b - a, D), F32) for a, b in zip(bounds, bounds[1:])],
             own_pair,
             *own_parts,
             *second,
         )
+        first_own, grad_up, grad_down, grad_out = together(
+            first_own, grad_up, grad_down, grad_out
+        )
         grad_down = grad_down.T
-        (grad_out,) = add_tail(out_own, second, 2 * block)
         w_qkv_grad, *norm_grads = finish_first(first_own, first_parts)
         norm_grads = [grad.reshape(share) for grad in norm_grads]
     else:

time: 140 us -> 123 us (0.88)
  waiting for transfers between devices: 28.4 us -> 17.3 us
  Pallas kernels: 58 us -> 51.5 us
    ppermute x39 -> x37, waiting for transfers between devices: 28.4 us -> 17.3 us  [swap(): lax.ppermute(array, axis, [(i, i ^ bit) for i in range(lax.axis_size(axis...]
    pallas_call x4 -> x7, Pallas kernels: 53.4 us -> 47.5 us  [run_kernel(): pl.pallas_call(body, out_shape=out_shape, in_specs=[SMEM] + specs, out_sp...]
    ppermute x39 -> x37, starting transfers between devices: 39.9 us -> 40.5 us  [swap(): lax.ppermute(array, axis, [(i, i ^ bit) for i in range(lax.axis_size(axis...]
  transfers between devices with their start and end apart: 39 -> 37, of which waited for: 12 -> 13; matrix products, arithmetic and copies ran while one was open for 0% -> 0% of each run, Pallas kernels for 39% -> 30%
where the time goes in v4:
time: 123 us
  Pallas kernels  51.5 us (42%)
  starting transfers between devices  40.5 us (33%)
  waiting for transfers between devices  17.3 us (14%)
  blocking collectives  12.4 us (10%)
    pallas_call x7, Pallas kernels, run_kernel(): pl.pallas_call(body, out_shape=out_shape, in_specs=[SMEM] + specs, out_sp...  47.5 us
    ppermute x37, starting transfers between devices, swap(): lax.ppermute(array, axis, [(i, i ^ bit) for i in range(lax.axis_size(axis...  40.5 us
    ppermute x37, waiting for transfers between devices, swap(): lax.ppermute(array, axis, [(i, i ^ bit) for i in range(lax.axis_size(axis...  17.3 us
    all_gather x1, blocking collectives, per_device(): first_half = lax.all_gather(column, 'dp', axis_index_groups=CHIPS)  12.4 us
  transfers between devices with their start and end apart: 37, of which 13 were waited for; matrix products, arithmetic and copies ran while one was open for 0% of the time, Pallas kernels for 30%

profile of v4, /device:TPU:0, one launch (start us, length us, event | category | flops | bytes accessed | tf_op | source)
XLA Modules:
  0.0 123.1 jit_solution(17595742472945407880)
XLA Ops:
  0.7 1.6 %shard_map.195 = (bf16[16,3200]{1,0:T(8,128)(2,1)S(1)}, bf16[16,2176]{1,0:T(8,128)(2,1)S(1)}, bf16[16,3200]{1,0:T(8,128)(2,1)S(1)}, bf16[208,512]{1,0:T(8,128)(2...) custom-call(bf16[704,512]{1,0:T(8,128)(2,1)} %rows.2, bf16[704,512]{1,0:T(8,128)(2,1)} %rows.3, ...), custom_call_target="tpu_custom_call" | custom-call | tf_op jit(solution)/shard_map/pallas_call | solution.py:734
  2.3 3.0 %collective-permute-start.1 = (bf16[208,512]{1,0:T(8,128)(2,1)S(1)}, bf16[208,512]{1,0:T(8,128)(2,1)S(1)}, u32[]{:S(2)}, u32[]{:S(2)}) collective-permute-start(bf16[208,512]{1,0:T(8,128)(2,1)S(1)} %get-tuple-element.136), channel_id=1, source_target_pairs={{0,16},{4,20},{8,24},{12,28},{16,0},{20,4},{24,8},{28,12},{1,17},{... | collective-permute-start | bytes 638984 | tf_op jit(solution)/shard_map/ppermute | solution.py:663
  6.8 2.6 %collective-permute-start.3 = (bf16[16,2176]{1,0:T(8,128)(2,1)S(1)}, bf16[16,2176]{1,0:T(8,128)(2,1)S(1)}, u32[]{:S(2)}, u32[]{:S(2)}) collective-permute-start(bf16[16,2176]{1,0:T(8,128)(2,1)S(1)} %get-tuple-element.126), channel_id=1, source_target_pairs={{0,2},{1,3},{2,0},{3,1},{4,6},{5,7},{6,4},{7,5},{8,10},{9,11},{10,... | collective-permute-start | bytes 208904 | tf_op jit(solution)/shard_map/ppermute | solution.py:663
  9.4 1.6 %collective-permute-start.2 = (bf16[16,3200]{1,0:T(8,128)(2,1)S(1)}, bf16[16,3200]{1,0:T(8,128)(2,1)S(1)}, u32[]{:S(2)}, u32[]{:S(2)}) collective-permute-start(bf16[16,3200]{1,0:T(8,128)(2,1)S(1)} %get-tuple-element.125), channel_id=1, source_target_pairs={{0,1},{1,0},{2,3},{3,2},{4,5},{5,4},{6,7},{7,6},{8,9},{9,8},{10,11... | collective-permute-start | bytes 307208 | tf_op jit(solution)/shard_map/ppermute | solution.py:663
  11.5 2.9 %shard_map.196 = (bf16[768,512]{1,0:T(8,128)(2,1)S(1)}, bf16[768,512]{1,0:T(8,128)(2,1)S(1)}, bf16[768,512]{1,0:T(8,128)(2,1)S(1)}, f32[768,128]{1,0:T(8,128)S(1)}) custom-call(s32[11]{0:T(128)S(1)} %pad_add_fusion.info, bf16[704,512]{1,0:T(8,128)(2,1)S(1)} %copy-done, bf16[704,512]{1,0:T(8,128)(2,1)S(1)} %copy-done.1), custom_call_target="tpu_custom_call" | custom-call | flops 402653184 | bytes 1441792 | tf_op jit(solution)/shard_map/pallas_call | solution.py:649
  14.4 3.1 %collective-permute-done.4.far = bf16[16,3200]{1,0:T(8,128)(2,1)S(1)} collective-permute-done((bf16[16,3200]{1,0:T(8,128)(2,1)S(1)}, bf16[16,3200]{1,0:T(8,128)(2,1)S(1)}, u32[]{:S(2)}, u32[]{:S(2)}) %collective-permute-start.4) | collective-permute-done | bytes 102432 | tf_op jit(solution)/shard_map/ppermute | solution.py:663
  18.7 2.9 %collective-permute-start.8 = (bf16[160,512]{1,0:T(8,128)(2,1)S(1)}, bf16[160,512]{1,0:T(8,128)(2,1)S(1)}, u32[]{:S(2)}, u32[]{:S(2)}) collective-permute-start(bf16[160,512]{1,0:T(8,128)(2,1)S(1)} %get-tuple-element.138), channel_id=1, source_target_pairs={{0,3},{1,2},{2,1},{3,0},{4,7},{5,6},{6,5},{7,4},{8,11},{9,10},{10,... | collective-permute-start | bytes 491528 | tf_op jit(solution)/shard_map/ppermute | solution.py:663
  21.7 12.4 %all-gather = bf16[12,16,2176]{2,1,0:T(8,128)(2,1)S(1)} all-gather(bf16[3,16,2176]{2,1,0:T(8,128)(2,1)S(1)} %pad_maximum_fusion.2), channel_id=2, replica_groups={{0,8,16,24},{4,12,20,28},{1,9,17,25},{5,13,21,29},{2,10,18,26},{6,14,22..., dimensions={0}, use_global_device_ids=true | all-gather | bytes 1044480 | tf_op jit(solution)/shard_map/all_gather | solution.py:772
  36.4 1.6 %collective-permute-start.10 = (bf16[3,128,512]{2,1,0:T(8,128)(2,1)S(1)}, bf16[3,128,512]{2,1,0:T(8,128)(2,1)S(1)}, u32[]{:S(2)}, u32[]{:S(2)}) collective-permute-start(bf16[3,128,512]{2,1,0:T(8,128)(2,1)S(1)} %pad_maximum_fusion.1.refs_0_), channel_id=1, source_target_pairs={{0,16},{4,20},{8,24},{12,28},{16,0},{20,4},{24,8},{28,12},{1,17},{... | collective-permute-start | bytes 1179656 | tf_op jit(solution)/shard_map/ppermute | solution.py:663
  38.0 1.5 %collective-permute-start.9 = (bf16[3,128,512]{2,1,0:T(8,128)(2,1)S(1)}, bf16[3,128,512]{2,1,0:T(8,128)(2,1)S(1)}, u32[]{:S(2)}, u32[]{:S(2)}) collective-permute-start(bf16[3,128,512]{2,1,0:T(8,128)(2,1)S(1)} %pad_maximum_fusion.1.refs_0_), channel_id=1, source_target_pairs={{0,8},{4,12},{8,0},{12,4},{16,24},{20,28},{24,16},{28,20},{1,9},{5... | collective-permute-start | bytes 1179656 | tf_op jit(solution)/shard_map/ppermute | solution.py:663
  39.5 9.9 %shard_map.197 = (bf16[768,512]{1,0:T(8,128)(2,1)S(1)}, bf16[768,1536]{1,0:T(8,128)(2,1)S(1)}, bf16[768,512]{1,0:T(8,128)(2,1)S(1)}, bf16[768,512]{1,0:T(8,128)(...) custom-call(s32[11]{0:T(128)S(1)} %pad_add_fusion.info, bf16[704,512]{1,0:T(8,128)(2,1)S(1)} %copy-done, ...), custom_call_target="tpu_custom_call" | custom-call | flops 2415919104 | bytes 5087232 | tf_op jit(solution)/shard_map/pallas_call | solution.py:649
  49.4 5.8 %shard_map.198 = (f32[768,512]{1,0:T(8,128)S(1)}, f32[768,512]{1,0:T(8,128)S(1)}, f32[768,512]{1,0:T(8,128)S(1)}, bf16[768,512]{1,0:T(8,128)(2,1)S(1)}, bf16[768...) custom-call(s32[11]{0:T(128)S(1)} %pad_add_fusion.info, ...), custom_call_target="tpu_custom_call" | custom-call | flops 2818572288 | bytes 8536064 | tf_op jit(solution)/shard_map/pallas_call | solution.py:649
  58.7 11.4 %shard_map.199 = (f32[768,512]{1,0:T(8,128)S(1)}, f32[768,512]{1,0:T(8,128)S(1)}, bf16[4,384,512]{2,1,0:T(8,128)(2,1)S(1)}, bf16[4,384,512]{2,1,0:T(8,128)(2,1)S(1)}) custom-call(s32[11]{0:T(128)S(1)} %pad_add_fusion.info, f32[768,512]{1,0:T(8,128)S(1)} %get-tuple-element.158.total_in, f32[768,512]{1,0:T(8,128)S(1)} %get-tuple-element.159.grad_in, ...), custom_call_target="tpu_custom_call" | custom-call | flops 7247757312 | bytes 9437184 | tf_op jit(solution)/shard_map/pallas_call | solution.py:649
  70.7 2.5 %shard_map.200 = (f32[768,512]{1,0:T(8,128)S(1)}, bf16[768,512]{1,0:T(8,128)(2,1)S(1)}, f32[8,512]{1,0:T(8,128)S(1)}, bf16[4,64,512]{2,1,0:T(8,128)(2,1)S(1)}, bf16[4,64,512]{2,1,0:T(8,128)(2,1)S(1)}) custom-call(s32[11]{0:T(128)S(1)} %pad_add_fusion.info, f32[768,512]{1,0:T(8,128)S(1)} %get-tuple-element.172.middle, ...), custom_call_target="tpu_custom_call" | custom-call | flops 805306368 | bytes 7356416 | tf_op jit(solution)/shard_map/pallas_call | solution.py:649
  75.4 1.6 %collective-permute-start.24 = (bf16[4,144,512]{2,1,0:T(8,128)(2,1)S(1)}, bf16[4,144,512]{2,1,0:T(8,128)(2,1)S(1)}, u32[]{:S(2)}, u32[]{:S(2)}) collective-permute-start(bf16[4,144,512]{2,1,0:T(8,128)(2,1)S(1)} %get-tuple-element.197), channel_id=1, source_target_pairs={{0,1},{1,0},{2,3},{3,2},{4,5},{5,4},{6,7},{7,6},{8,9},{9,8},{10,11... | collective-permute-start | bytes 1769480 | tf_op jit(solution)/shard_map/ppermute | solution.py:663
  78.9 1.5 %collective-permute-start.23 = (bf16[288,512]{1,0:T(8,128)(2,1)S(1)}, bf16[288,512]{1,0:T(8,128)(2,1)S(1)}, u32[]{:S(2)}, u32[]{:S(2)}) collective-permute-start(bf16[288,512]{1,0:T(8,128)(2,1)S(1)} %get-tuple-element.196), channel_id=1, source_target_pairs={{0,24},{4,28},{8,16},{12,20},{16,8},{20,12},{24,0},{28,4},{1,25},{... | collective-permute-start | bytes 884744 | tf_op jit(solution)/shard_map/ppermute | solution.py:663
  80.4 10.9 %shard_map.202 = (f32[768,512]{1,0:T(8,128)S(1)}, bf16[4,4,16,1664]{3,2,1,0:T(8,128)(2,1)S(1)}, bf16[4,4,16,1664]{3,2,1,0:T(8,128)(2,1)S(1)}) custom-call(s32[11]{0:T(128)S(1)} %pad_add_fusion.info, bf16[768,512]{1,0:T(8,128)(2,1)S(1)} %get-tuple-element.153.x_in, f32[768,128]{1,0:T(8,128)S(1)} %get-tuple-element.149.own, ...), custom_call_target="tpu_custom_call" | custom-call | flops 3623878656 | bytes 7372800 | tf_op jit(solution)/shard_map/pallas_call | solution.py:649
  91.4 1.5 %collective-permute-done.22.refs_2_ = bf16[288,512]{1,0:T(8,128)(2,1)S(1)} collective-permute-done((bf16[288,512]{1,0:T(8,128)(2,1)S(1)}, bf16[288,512]{1,0:T(8,128)(2,1)S(1)}, u32[]{:S(2)}, u32[]{:S(2)}) %collective-permute-start.22) | collective-permute-done | bytes 294944 | tf_op jit(solution)/shard_map/ppermute | solution.py:663
  92.9 2.4 %collective-permute-done.25.refs_1_ = bf16[4,4,16,1664]{3,2,1,0:T(8,128)(2,1)S(1)} collective-permute-done((bf16[4,4,16,1664]{3,2,1,0:T(8,128)(2,1)S(1)}, bf16[4,4,16,1664]{3,2,1,0:T(8,128)(2,1)S(1)}, u32[]{:S(2)}, u32[]{:S(2)}) %collective-permute-start.25) | collective-permute-done | bytes 852000 | tf_op jit(solution)/shard_map/ppermute | solution.py:663
  99.2 1.8 %collective-permute-start.32 = (bf16[144,512]{1,0:T(8,128)(2,1)S(1)}, bf16[144,512]{1,0:T(8,128)(2,1)S(1)}, u32[]{:S(2)}, u32[]{:S(2)}) collective-permute-start(bf16[144,512]{1,0:T(8,128)(2,1)S(1)} %get-tuple-element.221), channel_id=1, source_target_pairs={{0,2},{1,3},{2,0},{3,1},{4,6},{5,7},{6,4},{7,5},{8,10},{9,11},{10,... | collective-permute-start | bytes 442376 | tf_op jit(solution)/shard_map/ppermute | solution.py:663
  103.7 4.3 %collective-permute-done.27.refs_2_ = bf16[4,16,1664]{2,1,0:T(8,128)(2,1)S(1)} collective-permute-done((bf16[4,16,1664]{2,1,0:T(8,128)(2,1)S(1)}, bf16[4,16,1664]{2,1,0:T(8,128)(2,1)S(1)}, u32[]{:S(2)}, u32[]{:S(2)}) %collective-permute-start.27) | collective-permute-done | bytes 213024 | tf_op jit(solution)/shard_map/ppermute | solution.py:663
  110.0 1.5 %collective-permute-start.31 = (bf16[144,512]{1,0:T(8,128)(2,1)S(1)}, bf16[144,512]{1,0:T(8,128)(2,1)S(1)}, u32[]{:S(2)}, u32[]{:S(2)}) collective-permute-start(bf16[144,512]{1,0:T(8,128)(2,1)S(1)} %get-tuple-element.216), channel_id=1, source_target_pairs={{0,24},{4,28},{8,16},{12,20},{16,8},{20,12},{24,0},{28,4},{1,25},{... | collective-permute-start | bytes 442376 | tf_op jit(solution)/shard_map/ppermute | solution.py:663
  112.2 4.2 %collective-permute-start.35 = (bf16[16,1664]{1,0:T(8,128)(2,1)S(1)}, bf16[16,1664]{1,0:T(8,128)(2,1)S(1)}, u32[]{:S(2)}, u32[]{:S(2)}) collective-permute-start(bf16[16,1664]{1,0:T(8,128)(2,1)S(1)} %get-tuple-element.228), channel_id=1, source_target_pairs={{0,2},{1,3},{2,0},{3,1},{4,6},{5,7},{6,4},{7,5},{8,10},{9,11},{10,... | collective-permute-start | bytes 159752 | tf_op jit(solution)/shard_map/ppermute | solution.py:663
  117.6 4.0 %shard_map.203 = (bf16[704,512]{1,0:T(8,128)(2,1)}, bf16[704,512]{1,0:T(8,128)(2,1)}) custom-call(s32[11]{0:T(128)S(1)} %pad_add_fusion.info, f32[768,512]{1,0:T(8,128)S(1)} %get-tuple-element.167.total, bf16[768,512]{1,0:T(8,128)(2,1)S(1)} %get-tuple-element.153.x_in, f32[768,512]{1,0:T(8,128)S(1)} %get-tuple-element.188.grad_normed, ...), custom_call_target="tpu_custom_call" | custom-call | flops 402653184 | bytes 5521408 | tf_op jit(solution)/shard_map/pallas_call | solution.py:649
  (84 shorter events, 25.5 us)
Async XLA Ops:
  2.3 15.3 %collective-permute-start.1 = (bf16[208,512]{1,0:T(8,128)(2,1)S(1)}, bf16[208,512]{1,0:T(8,128)(2,1)S(1)}, u32[]{:S(2)}, u32[]{:S(2)}) collective-permute-start(bf16[208,512]{1,0:T(8,128)(2,1)S(1)} %get-tuple-element.136), channel_id=1, source_target_pairs={{0,16},{4,20},{8,24},{12,28},{16,0},{20,4},{24,8},{28,12},{1,17},{... | collective-permute-start | bytes 638984 | tf_op jit(solution)/shard_map/ppermute | solution.py:663
  5.3 12.2 %collective-permute-start = (bf16[208,512]{1,0:T(8,128)(2,1)S(1)}, bf16[208,512]{1,0:T(8,128)(2,1)S(1)}, u32[]{:S(2)}, u32[]{:S(2)}) collective-permute-start(bf16[208,512]{1,0:T(8,128)(2,1)S(1)} %get-tuple-element.136), channel_id=1, source_target_pairs={{0,8},{4,12},{8,0},{12,4},{16,24},{20,28},{24,16},{28,20},{1,9},{5... | collective-permute-start | bytes 638984 | tf_op jit(solution)/shard_map/ppermute | solution.py:663
  17.6 16.6 %collective-permute-start.5 = (bf16[208,512]{1,0:T(8,128)(2,1)S(1)}, bf16[208,512]{1,0:T(8,128)(2,1)S(1)}, u32[]{:S(2)}, u32[]{:S(2)}) collective-permute-start(bf16[208,512]{1,0:T(8,128)(2,1)S(1)} %get-tuple-element.136), channel_id=1, source_target_pairs={{0,24},{4,28},{8,16},{12,20},{16,8},{20,12},{24,0},{28,4},{1,25},{... | collective-permute-start | bytes 638984 | tf_op jit(solution)/shard_map/ppermute | solution.py:663
  18.1 16.0 %collective-permute-start.6 = (bf16[160,512]{1,0:T(8,128)(2,1)S(1)}, bf16[160,512]{1,0:T(8,128)(2,1)S(1)}, u32[]{:S(2)}, u32[]{:S(2)}) collective-permute-start(bf16[160,512]{1,0:T(8,128)(2,1)S(1)} %get-tuple-element.137), channel_id=1, source_target_pairs={{0,1},{1,0},{2,3},{3,2},{4,5},{5,4},{6,7},{7,6},{8,9},{9,8},{10,11... | collective-permute-start | bytes 491528 | tf_op jit(solution)/shard_map/ppermute | solution.py:663
  18.7 15.4 %collective-permute-start.8 = (bf16[160,512]{1,0:T(8,128)(2,1)S(1)}, bf16[160,512]{1,0:T(8,128)(2,1)S(1)}, u32[]{:S(2)}, u32[]{:S(2)}) collective-permute-start(bf16[160,512]{1,0:T(8,128)(2,1)S(1)} %get-tuple-element.138), channel_id=1, source_target_pairs={{0,3},{1,2},{2,1},{3,0},{4,7},{5,6},{6,5},{7,4},{8,11},{9,10},{10,... | collective-permute-start | bytes 491528 | tf_op jit(solution)/shard_map/ppermute | solution.py:663
  21.6 12.5 %collective-permute-start.7 = (bf16[128,512]{1,0:T(8,128)(2,1)S(1)}, bf16[128,512]{1,0:T(8,128)(2,1)S(1)}, u32[]{:S(2)}, u32[]{:S(2)}) collective-permute-start(bf16[128,512]{1,0:T(8,128)(2,1)S(1)} %slice.17), channel_id=1, source_target_pairs={{0,2},{1,3},{2,0},{3,1},{4,6},{5,7},{6,4},{7,5},{8,10},{9,11},{10,... | collective-permute-start | bytes 393224 | tf_op jit(solution)/shard_map/ppermute | solution.py:663
  34.9 21.5 %collective-permute-start.14 = (bf16[3,128,512]{2,1,0:T(8,128)(2,1)S(1)}, bf16[3,128,512]{2,1,0:T(8,128)(2,1)S(1)}, u32[]{:S(2)}, u32[]{:S(2)}) collective-permute-start(bf16[3,128,512]{2,1,0:T(8,128)(2,1)S(1)} %pad_maximum_fusion.1.refs_0_), channel_id=1, source_target_pairs={{0,4},{4,0},{8,12},{12,8},{16,20},{20,16},{24,28},{28,24},{1,5},{5... | collective-permute-start | bytes 1179656 | tf_op jit(solution)/shard_map/ppermute | solution.py:663
  35.0 20.2 %collective-permute-start.11 = (bf16[3,128,512]{2,1,0:T(8,128)(2,1)S(1)}, bf16[3,128,512]{2,1,0:T(8,128)(2,1)S(1)}, u32[]{:S(2)}, u32[]{:S(2)}) collective-permute-start(bf16[3,128,512]{2,1,0:T(8,128)(2,1)S(1)} %pad_maximum_fusion.1.refs_0_), channel_id=1, source_target_pairs={{0,24},{4,28},{8,16},{12,20},{16,8},{20,12},{24,0},{28,4},{1,25},{... | collective-permute-start | bytes 1179656 | tf_op jit(solution)/shard_map/ppermute | solution.py:663
  36.4 19.4 %collective-permute-start.10 = (bf16[3,128,512]{2,1,0:T(8,128)(2,1)S(1)}, bf16[3,128,512]{2,1,0:T(8,128)(2,1)S(1)}, u32[]{:S(2)}, u32[]{:S(2)}) collective-permute-start(bf16[3,128,512]{2,1,0:T(8,128)(2,1)S(1)} %pad_maximum_fusion.1.refs_0_), channel_id=1, source_target_pairs={{0,16},{4,20},{8,24},{12,28},{16,0},{20,4},{24,8},{28,12},{1,17},{... | collective-permute-start | bytes 1179656 | tf_op jit(solution)/shard_map/ppermute | solution.py:663
  38.0 17.9 %collective-permute-start.9 = (bf16[3,128,512]{2,1,0:T(8,128)(2,1)S(1)}, bf16[3,128,512]{2,1,0:T(8,128)(2,1)S(1)}, u32[]{:S(2)}, u32[]{:S(2)}) collective-permute-start(bf16[3,128,512]{2,1,0:T(8,128)(2,1)S(1)} %pad_maximum_fusion.1.refs_0_), channel_id=1, source_target_pairs={{0,8},{4,12},{8,0},{12,4},{16,24},{20,28},{24,16},{28,20},{1,9},{5... | collective-permute-start | bytes 1179656 | tf_op jit(solution)/shard_map/ppermute | solution.py:663
  75.4 17.6 %collective-permute-start.24 = (bf16[4,144,512]{2,1,0:T(8,128)(2,1)S(1)}, bf16[4,144,512]{2,1,0:T(8,128)(2,1)S(1)}, u32[]{:S(2)}, u32[]{:S(2)}) collective-permute-start(bf16[4,144,512]{2,1,0:T(8,128)(2,1)S(1)} %get-tuple-element.197), channel_id=1, source_target_pairs={{0,1},{1,0},{2,3},{3,2},{4,5},{5,4},{6,7},{7,6},{8,9},{9,8},{10,11... | collective-permute-start | bytes 1769480 | tf_op jit(solution)/shard_map/ppermute | solution.py:663
  76.9 14.4 %collective-permute-start.21 = (bf16[288,512]{1,0:T(8,128)(2,1)S(1)}, bf16[288,512]{1,0:T(8,128)(2,1)S(1)}, u32[]{:S(2)}, u32[]{:S(2)}) collective-permute-start(bf16[288,512]{1,0:T(8,128)(2,1)S(1)} %get-tuple-element.194), channel_id=1, source_target_pairs={{0,8},{4,12},{8,0},{12,4},{16,24},{20,28},{24,16},{28,20},{1,9},{5... | collective-permute-start | bytes 884744 | tf_op jit(solution)/shard_map/ppermute | solution.py:663
  78.1 14.8 %collective-permute-start.22 = (bf16[288,512]{1,0:T(8,128)(2,1)S(1)}, bf16[288,512]{1,0:T(8,128)(2,1)S(1)}, u32[]{:S(2)}, u32[]{:S(2)}) collective-permute-start(bf16[288,512]{1,0:T(8,128)(2,1)S(1)} %get-tuple-element.195), channel_id=1, source_target_pairs={{0,16},{4,20},{8,24},{12,28},{16,0},{20,4},{24,8},{28,12},{1,17},{... | collective-permute-start | bytes 884744 | tf_op jit(solution)/shard_map/ppermute | solution.py:663
  78.9 14.0 %collective-permute-start.23 = (bf16[288,512]{1,0:T(8,128)(2,1)S(1)}, bf16[288,512]{1,0:T(8,128)(2,1)S(1)}, u32[]{:S(2)}, u32[]{:S(2)}) collective-permute-start(bf16[288,512]{1,0:T(8,128)(2,1)S(1)} %get-tuple-element.196), channel_id=1, source_target_pairs={{0,24},{4,28},{8,16},{12,20},{16,8},{20,12},{24,0},{28,4},{1,25},{... | collective-permute-start | bytes 884744 | tf_op jit(solution)/shard_map/ppermute | solution.py:663
  95.5 8.2 %collective-permute-start.26 = (bf16[4,16,1664]{2,1,0:T(8,128)(2,1)S(1)}, bf16[4,16,1664]{2,1,0:T(8,128)(2,1)S(1)}, u32[]{:S(2)}, u32[]{:S(2)}) collective-permute-start(bf16[4,16,1664]{2,1,0:T(8,128)(2,1)S(1)} %get-tuple-element.201), channel_id=1, source_target_pairs={{0,8},{4,12},{8,0},{12,4},{16,24},{20,28},{24,16},{28,20},{1,9},{5... | collective-permute-start | bytes 638984 | tf_op jit(solution)/shard_map/ppermute | solution.py:663
  96.4 11.6 %collective-permute-start.27 = (bf16[4,16,1664]{2,1,0:T(8,128)(2,1)S(1)}, bf16[4,16,1664]{2,1,0:T(8,128)(2,1)S(1)}, u32[]{:S(2)}, u32[]{:S(2)}) collective-permute-start(bf16[4,16,1664]{2,1,0:T(8,128)(2,1)S(1)} %get-tuple-element.202), channel_id=1, source_target_pairs={{0,16},{4,20},{8,24},{12,28},{16,0},{20,4},{24,8},{28,12},{1,17},{... | collective-permute-start | bytes 638984 | tf_op jit(solution)/shard_map/ppermute | solution.py:663
  97.6 10.4 %collective-permute-start.28 = (bf16[4,16,1664]{2,1,0:T(8,128)(2,1)S(1)}, bf16[4,16,1664]{2,1,0:T(8,128)(2,1)S(1)}, u32[]{:S(2)}, u32[]{:S(2)}) collective-permute-start(bf16[4,16,1664]{2,1,0:T(8,128)(2,1)S(1)} %get-tuple-element.203), channel_id=1, source_target_pairs={{0,24},{4,28},{8,16},{12,20},{16,8},{20,12},{24,0},{28,4},{1,25},{... | collective-permute-start | bytes 638984 | tf_op jit(solution)/shard_map/ppermute | solution.py:663
  99.2 12.7 %collective-permute-start.32 = (bf16[144,512]{1,0:T(8,128)(2,1)S(1)}, bf16[144,512]{1,0:T(8,128)(2,1)S(1)}, u32[]{:S(2)}, u32[]{:S(2)}) collective-permute-start(bf16[144,512]{1,0:T(8,128)(2,1)S(1)} %get-tuple-element.221), channel_id=1, source_target_pairs={{0,2},{1,3},{2,0},{3,1},{4,6},{5,7},{6,4},{7,5},{8,10},{9,11},{10,... | collective-permute-start | bytes 442376 | tf_op jit(solution)/shard_map/ppermute | solution.py:663
  101.0 11.2 %collective-permute-start.33 = (bf16[144,512]{1,0:T(8,128)(2,1)S(1)}, bf16[144,512]{1,0:T(8,128)(2,1)S(1)}, u32[]{:S(2)}, u32[]{:S(2)}) collective-permute-start(bf16[144,512]{1,0:T(8,128)(2,1)S(1)} %get-tuple-element.222), channel_id=1, source_target_pairs={{0,3},{1,2},{2,1},{3,0},{4,7},{5,6},{6,5},{7,4},{8,11},{9,10},{10,... | collective-permute-start | bytes 442376 | tf_op jit(solution)/shard_map/ppermute | solution.py:663
  108.0 8.4 %collective-permute-start.29 = (bf16[144,512]{1,0:T(8,128)(2,1)S(1)}, bf16[144,512]{1,0:T(8,128)(2,1)S(1)}, u32[]{:S(2)}, u32[]{:S(2)}) collective-permute-start(bf16[144,512]{1,0:T(8,128)(2,1)S(1)} %get-tuple-element.214), channel_id=1, source_target_pairs={{0,8},{4,12},{8,0},{12,4},{16,24},{20,28},{24,16},{28,20},{1,9},{5... | collective-permute-start | bytes 442376 | tf_op jit(solution)/shard_map/ppermute | solution.py:663
  109.2 12.4 %collective-permute-start.30 = (bf16[144,512]{1,0:T(8,128)(2,1)S(1)}, bf16[144,512]{1,0:T(8,128)(2,1)S(1)}, u32[]{:S(2)}, u32[]{:S(2)}) collective-permute-start(bf16[144,512]{1,0:T(8,128)(2,1)S(1)} %get-tuple-element.215), channel_id=1, source_target_pairs={{0,16},{4,20},{8,24},{12,28},{16,0},{20,4},{24,8},{28,12},{1,17},{... | collective-permute-start | bytes 442376 | tf_op jit(solution)/shard_map/ppermute | solution.py:663
  110.0 11.7 %collective-permute-start.31 = (bf16[144,512]{1,0:T(8,128)(2,1)S(1)}, bf16[144,512]{1,0:T(8,128)(2,1)S(1)}, u32[]{:S(2)}, u32[]{:S(2)}) collective-permute-start(bf16[144,512]{1,0:T(8,128)(2,1)S(1)} %get-tuple-element.216), channel_id=1, source_target_pairs={{0,24},{4,28},{8,16},{12,20},{16,8},{20,12},{24,0},{28,4},{1,25},{... | collective-permute-start | bytes 442376 | tf_op jit(solution)/shard_map/ppermute | solution.py:663
  111.8 10.5 %collective-permute-start.34 = (bf16[16,1664]{1,0:T(8,128)(2,1)S(1)}, bf16[16,1664]{1,0:T(8,128)(2,1)S(1)}, u32[]{:S(2)}, u32[]{:S(2)}) collective-permute-start(bf16[16,1664]{1,0:T(8,128)(2,1)S(1)} %get-tuple-element.227), channel_id=1, source_target_pairs={{0,1},{1,0},{2,3},{3,2},{4,5},{5,4},{6,7},{7,6},{8,9},{9,8},{10,11... | collective-permute-start | bytes 159752 | tf_op jit(solution)/shard_map/ppermute | solution.py:663
  112.2 10.2 %collective-permute-start.35 = (bf16[16,1664]{1,0:T(8,128)(2,1)S(1)}, bf16[16,1664]{1,0:T(8,128)(2,1)S(1)}, u32[]{:S(2)}, u32[]{:S(2)}) collective-permute-start(bf16[16,1664]{1,0:T(8,128)(2,1)S(1)} %get-tuple-element.228), channel_id=1, source_target_pairs={{0,2},{1,3},{2,0},{3,1},{4,6},{5,7},{6,4},{7,5},{8,10},{9,11},{10,... | collective-permute-start | bytes 159752 | tf_op jit(solution)/shard_map/ppermute | solution.py:663
  (17 other events, 95.7 us)

commit v5 on v4

--- a/solution.py
+++ b/solution.py
@@ -537,11 +537,8 @@
         grads[0][...] = grad_out
 
 
-def finish_rows_kernel(info, total, x_in, grad_normed, grad_middle, norms, out, tokens_grad, ext):
-    unplace(info, total, ext, out)
-    unit, scale = normalized(x_in[...].astype(F32))
-    grad_normed[...] = grad_middle[...] + norm_back(grad_normed[...] * norms[0:1], unit, scale)
-    unplace(info, grad_normed, ext, tokens_grad)
+def finish_rows_kernel(info, values, out, ext):
+    unplace(info, values, ext, out)
 
 
 def unplace(info, values, ext, out):
@@ -557,9 +554,9 @@
 
 
 def back_kernel(
-    direct, info, x_in, own, qkv, probs_in, grad_mixed, w_qkv, norms, grad_norms, *refs
+    direct, info, x_in, own, qkv, probs_in, grad_mixed, grad_middle, w_qkv, norms, grad_norms, *refs
 ):
-    grad_normed, refs = refs[0], refs[1:]
+    grad_tokens, refs = refs[0], refs[1:]
     if direct:
         (keep, send), refs = refs[:2], refs[2:]
     else:
@@ -598,14 +595,14 @@
 
     def after(i, carry):
         at = tile_at(i)
-        unit, _ = normalized(x_in[at, :].astype(F32))
+        unit, scale = normalized(x_in[at, :].astype(F32))
         mask = own[at, 0:1]
         normed[at, :] = ((unit * gain + shift) * mask).astype(BF16)
         part = mm_right(grad_qkv[at, :], w_qkv[:, : 3 * D])
         masked = part * mask
         gains[0:1] += jnp.sum(masked * unit, axis=0, keepdims=True)
         gains[1:2] += jnp.sum(masked, axis=0, keepdims=True)
-        grad_normed[at, :] = part
+        grad_tokens[at, :] = grad_middle[at, :] + norm_back(part * gain, unit, scale)
         return carry
 
     lax.fori_loop(0, WROWS // TILE, after, 0)
@@ -926,7 +923,7 @@
         grad_down = lax.psum_scatter(grad_down, "dp", scatter_dimension=0, tiled=True).T
         grad_out = lax.psum_scatter(out_grads[0], ("dp", "seq"), scatter_dimension=0, tiled=True)
         grads_shape = [shape((D, 3 * D + NORMS), F32)]
-    grad_normed, *grads = run_kernel(
+    grad_tokens, *grads = run_kernel(
         functools.partial(back_kernel, direct),
         [shape((WROWS, D), F32), *grads_shape],
         [
@@ -942,31 +939,34 @@
         qkv,
         probs,
         grad_mixed,
+        grad_middle,
         w_all,
         norms_all,
         grad_norms,
     )
     if direct:
-        grad_normed, *grads = together(grad_normed, *grads)
-    out, tokens_grad = run_kernel(
-        finish_rows_kernel,
-        [jax.ShapeDtypeStruct((ROWS, D), BF16)] * 2,
-        [pltpu.VMEM((ROWS + 2 * HALO, D), F32)],
-        2 * WROWS * D * D,
-        info,
-        total,
-        x,
-        grad_normed,
-        grad_middle,
-        norms_all,
-    )
+        grad_tokens, *grads = together(grad_tokens, *grads)
+    out, tokens_grad = [
+        run_kernel(
+            finish_rows_kernel,
+            [jax.ShapeDtypeStruct((ROWS, D), BF16)],
+            [pltpu.VMEM((ROWS + 2 * HALO, D), F32)],
+            2 * WROWS * D * D,
+            info,
+            values,
+        )[0]
+        for values in (total, grad_tokens)
+    ]
     if direct:
         keep, send, *parts, from_near = together(*grads, *parts)
         rows = 2 * block + share
         plan = [[(slice(None), (slice(k * rows, (k + 1) * rows),))] for k in range(2)]
         low = add(plan, [((rows, D), BF16)] * 2, pair, *parts)
-        second = [swap(low[0], "seq", 2), swap(low[1], "seq", 3)]
-        first_pair, *first_low = add_slots(keep, *along_core([send]))
+        second_far, from_near_far = together(low[1], swap(low[0], "seq", 1))
+        (second_far,) = add([[(slice(None), slice(None))]], [(low[1].shape, BF16)], second_far, from_near_far)
+        second = [swap(second_far, "seq", 3)]
+        from_core, tokens_grad = together(*along_core([send]), tokens_grad)
+        first_pair, *first_low = add_slots(keep, from_core)
         first = [swap(part, "dp", 2 * m + 2) for m, part in enumerate(first_low)]
         own_pair, *own_low = add_slots(own_pair, from_near)
         *first, own0, own1, own2 = together(*first, *own_low)

time: 123 us -> 122 us (level)
  waiting for transfers between devices: 17.3 us -> 14.9 us
    ppermute x37, waiting for transfers between devices: 17.3 us -> 14.9 us  [swap(): lax.ppermute(array, axis, [(i, i ^ bit) for i in range(lax.axis_size(axis...]
    pallas_call x7 -> x8, Pallas kernels: 47.5 us -> 48 us  [run_kernel(): pl.pallas_call(body, out_shape=out_shape, in_specs=[SMEM] + specs, out_sp...]
  transfers between devices with their start and end apart: 37 -> 37, of which waited for: 13 -> 13; matrix products, arithmetic and copies ran while one was open for 0% -> 0% of each run, Pallas kernels for 30% -> 31%
where the time goes in v5:
time: 122 us
  Pallas kernels  52.1 us (43%)
  starting transfers between devices  41 us (34%)
  waiting for transfers between devices  14.9 us (12%)
  blocking collectives  12.4 us (10%)
    pallas_call x8, Pallas kernels, run_kernel(): pl.pallas_call(body, out_shape=out_shape, in_specs=[SMEM] + specs, out_sp...  48 us
    ppermute x37, starting transfers between devices, swap(): lax.ppermute(array, axis, [(i, i ^ bit) for i in range(lax.axis_size(axis...  41 us
    ppermute x37, waiting for transfers between devices, swap(): lax.ppermute(array, axis, [(i, i ^ bit) for i in range(lax.axis_size(axis...  14.9 us
    all_gather x1, blocking collectives, per_device(): first_half = lax.all_gather(column, 'dp', axis_index_groups=CHIPS)  12.4 us
  transfers between devices with their start and end apart: 37, of which 13 were waited for; matrix products, arithmetic and copies ran while one was open for 0% of the time, Pallas kernels for 31%

profile of v5, /device:TPU:0, one launch (start us, length us, event | category | flops | bytes accessed | tf_op | source)
XLA Modules:
  0.0 121.8 jit_solution(17954420564652542452)
XLA Ops:
  0.7 1.6 %shard_map.195 = (bf16[16,3200]{1,0:T(8,128)(2,1)S(1)}, bf16[16,2176]{1,0:T(8,128)(2,1)S(1)}, bf16[16,3200]{1,0:T(8,128)(2,1)S(1)}, bf16[208,512]{1,0:T(8,128)(2...) custom-call(bf16[704,512]{1,0:T(8,128)(2,1)} %rows.2, bf16[704,512]{1,0:T(8,128)(2,1)} %rows.3, ...), custom_call_target="tpu_custom_call" | custom-call | tf_op jit(solution)/shard_map/pallas_call | solution.py:731
  2.3 3.0 %collective-permute-start.1 = (bf16[208,512]{1,0:T(8,128)(2,1)S(1)}, bf16[208,512]{1,0:T(8,128)(2,1)S(1)}, u32[]{:S(2)}, u32[]{:S(2)}) collective-permute-start(bf16[208,512]{1,0:T(8,128)(2,1)S(1)} %get-tuple-element.138), channel_id=1, source_target_pairs={{0,16},{4,20},{8,24},{12,28},{16,0},{20,4},{24,8},{28,12},{1,17},{... | collective-permute-start | bytes 638984 | tf_op jit(solution)/shard_map/ppermute | solution.py:660
  6.8 2.6 %collective-permute-start.3 = (bf16[16,2176]{1,0:T(8,128)(2,1)S(1)}, bf16[16,2176]{1,0:T(8,128)(2,1)S(1)}, u32[]{:S(2)}, u32[]{:S(2)}) collective-permute-start(bf16[16,2176]{1,0:T(8,128)(2,1)S(1)} %get-tuple-element.128), channel_id=1, source_target_pairs={{0,2},{1,3},{2,0},{3,1},{4,6},{5,7},{6,4},{7,5},{8,10},{9,11},{10,... | collective-permute-start | bytes 208904 | tf_op jit(solution)/shard_map/ppermute | solution.py:660
  9.4 1.6 %collective-permute-start.2 = (bf16[16,3200]{1,0:T(8,128)(2,1)S(1)}, bf16[16,3200]{1,0:T(8,128)(2,1)S(1)}, u32[]{:S(2)}, u32[]{:S(2)}) collective-permute-start(bf16[16,3200]{1,0:T(8,128)(2,1)S(1)} %get-tuple-element.127), channel_id=1, source_target_pairs={{0,1},{1,0},{2,3},{3,2},{4,5},{5,4},{6,7},{7,6},{8,9},{9,8},{10,11... | collective-permute-start | bytes 307208 | tf_op jit(solution)/shard_map/ppermute | solution.py:660
  11.5 2.9 %shard_map.196 = (bf16[768,512]{1,0:T(8,128)(2,1)S(1)}, bf16[768,512]{1,0:T(8,128)(2,1)S(1)}, bf16[768,512]{1,0:T(8,128)(2,1)S(1)}, f32[768,128]{1,0:T(8,128)S(1)}) custom-call(s32[11]{0:T(128)S(1)} %pad_add_fusion.info, bf16[704,512]{1,0:T(8,128)(2,1)S(1)} %copy-done, bf16[704,512]{1,0:T(8,128)(2,1)S(1)} %copy-done.1), custom_call_target="tpu_custom_call" | custom-call | flops 402653184 | bytes 1441792 | tf_op jit(solution)/shard_map/pallas_call | solution.py:646
  14.4 3.1 %collective-permute-done.4.far = bf16[16,3200]{1,0:T(8,128)(2,1)S(1)} collective-permute-done((bf16[16,3200]{1,0:T(8,128)(2,1)S(1)}, bf16[16,3200]{1,0:T(8,128)(2,1)S(1)}, u32[]{:S(2)}, u32[]{:S(2)}) %collective-permute-start.4) | collective-permute-done | bytes 102432 | tf_op jit(solution)/shard_map/ppermute | solution.py:660
  18.7 2.9 %collective-permute-start.8 = (bf16[160,512]{1,0:T(8,128)(2,1)S(1)}, bf16[160,512]{1,0:T(8,128)(2,1)S(1)}, u32[]{:S(2)}, u32[]{:S(2)}) collective-permute-start(bf16[160,512]{1,0:T(8,128)(2,1)S(1)} %get-tuple-element.140), channel_id=1, source_target_pairs={{0,3},{1,2},{2,1},{3,0},{4,7},{5,6},{6,5},{7,4},{8,11},{9,10},{10,... | collective-permute-start | bytes 491528 | tf_op jit(solution)/shard_map/ppermute | solution.py:660
  21.7 12.4 %all-gather = bf16[12,16,2176]{2,1,0:T(8,128)(2,1)S(1)} all-gather(bf16[3,16,2176]{2,1,0:T(8,128)(2,1)S(1)} %pad_maximum_fusion.2), channel_id=2, replica_groups={{0,8,16,24},{4,12,20,28},{1,9,17,25},{5,13,21,29},{2,10,18,26},{6,14,22..., dimensions={0}, use_global_device_ids=true | all-gather | bytes 1044480 | tf_op jit(solution)/shard_map/all_gather | solution.py:769
  36.4 1.6 %collective-permute-start.10 = (bf16[3,128,512]{2,1,0:T(8,128)(2,1)S(1)}, bf16[3,128,512]{2,1,0:T(8,128)(2,1)S(1)}, u32[]{:S(2)}, u32[]{:S(2)}) collective-permute-start(bf16[3,128,512]{2,1,0:T(8,128)(2,1)S(1)} %pad_maximum_fusion.1.refs_0_), channel_id=1, source_target_pairs={{0,16},{4,20},{8,24},{12,28},{16,0},{20,4},{24,8},{28,12},{1,17},{... | collective-permute-start | bytes 1179656 | tf_op jit(solution)/shard_map/ppermute | solution.py:660
  38.0 1.5 %collective-permute-start.9 = (bf16[3,128,512]{2,1,0:T(8,128)(2,1)S(1)}, bf16[3,128,512]{2,1,0:T(8,128)(2,1)S(1)}, u32[]{:S(2)}, u32[]{:S(2)}) collective-permute-start(bf16[3,128,512]{2,1,0:T(8,128)(2,1)S(1)} %pad_maximum_fusion.1.refs_0_), channel_id=1, source_target_pairs={{0,8},{4,12},{8,0},{12,4},{16,24},{20,28},{24,16},{28,20},{1,9},{5... | collective-permute-start | bytes 1179656 | tf_op jit(solution)/shard_map/ppermute | solution.py:660
  39.5 9.9 %shard_map.197 = (bf16[768,512]{1,0:T(8,128)(2,1)S(1)}, bf16[768,1536]{1,0:T(8,128)(2,1)S(1)}, bf16[768,512]{1,0:T(8,128)(2,1)S(1)}, bf16[768,512]{1,0:T(8,128)(...) custom-call(s32[11]{0:T(128)S(1)} %pad_add_fusion.info, bf16[704,512]{1,0:T(8,128)(2,1)S(1)} %copy-done, ...), custom_call_target="tpu_custom_call" | custom-call | flops 2415919104 | bytes 5087232 | tf_op jit(solution)/shard_map/pallas_call | solution.py:646
  49.4 5.8 %shard_map.198 = (f32[768,512]{1,0:T(8,128)S(1)}, f32[768,512]{1,0:T(8,128)S(1)}, f32[768,512]{1,0:T(8,128)S(1)}, bf16[768,512]{1,0:T(8,128)(2,1)S(1)}, bf16[768...) custom-call(s32[11]{0:T(128)S(1)} %pad_add_fusion.info, ...), custom_call_target="tpu_custom_call" | custom-call | flops 2818572288 | bytes 8536064 | tf_op jit(solution)/shard_map/pallas_call | solution.py:646
  58.7 11.4 %shard_map.199 = (f32[768,512]{1,0:T(8,128)S(1)}, f32[768,512]{1,0:T(8,128)S(1)}, bf16[4,384,512]{2,1,0:T(8,128)(2,1)S(1)}, bf16[4,384,512]{2,1,0:T(8,128)(2,1)S(1)}) custom-call(s32[11]{0:T(128)S(1)} %pad_add_fusion.info, f32[768,512]{1,0:T(8,128)S(1)} %get-tuple-element.160.total_in, f32[768,512]{1,0:T(8,128)S(1)} %get-tuple-element.161.grad_in, ...), custom_call_target="tpu_custom_call" | custom-call | flops 7247757312 | bytes 9437184 | tf_op jit(solution)/shard_map/pallas_call | solution.py:646
  70.7 2.5 %shard_map.201 = (f32[768,512]{1,0:T(8,128)S(1)}, bf16[768,512]{1,0:T(8,128)(2,1)S(1)}, f32[8,512]{1,0:T(8,128)S(1)}, bf16[4,64,512]{2,1,0:T(8,128)(2,1)S(1)}, bf16[4,64,512]{2,1,0:T(8,128)(2,1)S(1)}) custom-call(s32[11]{0:T(128)S(1)} %pad_add_fusion.info, f32[768,512]{1,0:T(8,128)S(1)} %get-tuple-element.174.middle, ...), custom_call_target="tpu_custom_call" | custom-call | flops 805306368 | bytes 7356416 | tf_op jit(solution)/shard_map/pallas_call | solution.py:646
  75.4 1.6 %collective-permute-start.24 = (bf16[4,144,512]{2,1,0:T(8,128)(2,1)S(1)}, bf16[4,144,512]{2,1,0:T(8,128)(2,1)S(1)}, u32[]{:S(2)}, u32[]{:S(2)}) collective-permute-start(bf16[4,144,512]{2,1,0:T(8,128)(2,1)S(1)} %get-tuple-element.196), channel_id=1, source_target_pairs={{0,1},{1,0},{2,3},{3,2},{4,5},{5,4},{6,7},{7,6},{8,9},{9,8},{10,11... | collective-permute-start | bytes 1769480 | tf_op jit(solution)/shard_map/ppermute | solution.py:660
  78.9 1.5 %collective-permute-start.23 = (bf16[288,512]{1,0:T(8,128)(2,1)S(1)}, bf16[288,512]{1,0:T(8,128)(2,1)S(1)}, u32[]{:S(2)}, u32[]{:S(2)}) collective-permute-start(bf16[288,512]{1,0:T(8,128)(2,1)S(1)} %get-tuple-element.195), channel_id=1, source_target_pairs={{0,24},{4,28},{8,16},{12,20},{16,8},{20,12},{24,0},{28,4},{1,25},{... | collective-permute-start | bytes 884744 | tf_op jit(solution)/shard_map/ppermute | solution.py:660
  80.4 11.3 %shard_map.203 = (f32[768,512]{1,0:T(8,128)S(1)}, bf16[4,4,16,1664]{3,2,1,0:T(8,128)(2,1)S(1)}, bf16[4,4,16,1664]{3,2,1,0:T(8,128)(2,1)S(1)}) custom-call(s32[11]{0:T(128)S(1)} %pad_add_fusion.info, bf16[768,512]{1,0:T(8,128)(2,1)S(1)} %get-tuple-element.155.x_in, f32[768,128]{1,0:T(8,128)S(1)} %get-tuple-element.151.own, ...), custom_call_target="tpu_custom_call" | custom-call | flops 3623878656 | bytes 8945664 | tf_op jit(solution)/shard_map/pallas_call | solution.py:646
  93.0 2.1 %shard_map.204 = bf16[704,512]{1,0:T(8,128)(2,1)} custom-call(s32[11]{0:T(128)S(1)} %pad_add_fusion.info, f32[768,512]{1,0:T(8,128)S(1)} %get-tuple-element.198.values), custom_call_target="tpu_custom_call" | custom-call | flops 402653184 | bytes 1572864 | tf_op jit(solution)/shard_map/pallas_call | solution.py:646
  100.2 4.3 %collective-permute-done.32.refs_1_ = bf16[144,512]{1,0:T(8,128)(2,1)S(1)} collective-permute-done((bf16[144,512]{1,0:T(8,128)(2,1)S(1)}, bf16[144,512]{1,0:T(8,128)(2,1)S(1)}, u32[]{:S(2)}, u32[]{:S(2)}) %collective-permute-start.32) | collective-permute-done | bytes 147488 | tf_op jit(solution)/shard_map/ppermute | solution.py:660
  104.5 2.9 %collective-permute-start.33 = (bf16[144,512]{1,0:T(8,128)(2,1)S(1)}, bf16[144,512]{1,0:T(8,128)(2,1)S(1)}, u32[]{:S(2)}, u32[]{:S(2)}) collective-permute-start(bf16[144,512]{1,0:T(8,128)(2,1)S(1)} %shard_map.209), channel_id=1, source_target_pairs={{0,3},{1,2},{2,1},{3,0},{4,7},{5,6},{6,5},{7,4},{8,11},{9,10},{10,... | collective-permute-start | bytes 442376 | tf_op jit(solution)/shard_map/ppermute | solution.py:660
  110.0 1.5 %collective-permute-start.31 = (bf16[144,512]{1,0:T(8,128)(2,1)S(1)}, bf16[144,512]{1,0:T(8,128)(2,1)S(1)}, u32[]{:S(2)}, u32[]{:S(2)}) collective-permute-start(bf16[144,512]{1,0:T(8,128)(2,1)S(1)} %get-tuple-element.218), channel_id=1, source_target_pairs={{0,24},{4,28},{8,16},{12,20},{16,8},{20,12},{24,0},{28,4},{1,25},{... | collective-permute-start | bytes 442376 | tf_op jit(solution)/shard_map/ppermute | solution.py:660
  112.3 2.9 %collective-permute-start.35 = (bf16[16,1664]{1,0:T(8,128)(2,1)S(1)}, bf16[16,1664]{1,0:T(8,128)(2,1)S(1)}, u32[]{:S(2)}, u32[]{:S(2)}) collective-permute-start(bf16[16,1664]{1,0:T(8,128)(2,1)S(1)} %get-tuple-element.232), channel_id=1, source_target_pairs={{0,2},{1,3},{2,0},{3,1},{4,6},{5,7},{6,4},{7,5},{8,10},{9,11},{10,... | collective-permute-start | bytes 159752 | tf_op jit(solution)/shard_map/ppermute | solution.py:660
  115.2 2.2 %collective-permute-start.36 = (bf16[16,1664]{1,0:T(8,128)(2,1)S(1)}, bf16[16,1664]{1,0:T(8,128)(2,1)S(1)}, u32[]{:S(2)}, u32[]{:S(2)}) collective-permute-start(bf16[16,1664]{1,0:T(8,128)(2,1)S(1)} %get-tuple-element.233), channel_id=1, source_target_pairs={{0,3},{1,2},{2,1},{3,0},{4,7},{5,6},{6,5},{7,4},{8,11},{9,10},{10,... | collective-permute-start | bytes 159752 | tf_op jit(solution)/shard_map/ppermute | solution.py:660
  117.4 2.1 %shard_map.200 = bf16[704,512]{1,0:T(8,128)(2,1)} custom-call(s32[11]{0:T(128)S(1)} %pad_add_fusion.info, f32[768,512]{1,0:T(8,128)S(1)} %get-tuple-element.169.values), custom_call_target="tpu_custom_call" | custom-call | flops 402653184 | bytes 1572864 | tf_op jit(solution)/shard_map/pallas_call | solution.py:646
  (86 shorter events, 25.6 us)
Async XLA Ops:
  2.3 15.3 %collective-permute-start.1 = (bf16[208,512]{1,0:T(8,128)(2,1)S(1)}, bf16[208,512]{1,0:T(8,128)(2,1)S(1)}, u32[]{:S(2)}, u32[]{:S(2)}) collective-permute-start(bf16[208,512]{1,0:T(8,128)(2,1)S(1)} %get-tuple-element.138), channel_id=1, source_target_pairs={{0,16},{4,20},{8,24},{12,28},{16,0},{20,4},{24,8},{28,12},{1,17},{... | collective-permute-start | bytes 638984 | tf_op jit(solution)/shard_map/ppermute | solution.py:660
  5.3 12.2 %collective-permute-start = (bf16[208,512]{1,0:T(8,128)(2,1)S(1)}, bf16[208,512]{1,0:T(8,128)(2,1)S(1)}, u32[]{:S(2)}, u32[]{:S(2)}) collective-permute-start(bf16[208,512]{1,0:T(8,128)(2,1)S(1)} %get-tuple-element.138), channel_id=1, source_target_pairs={{0,8},{4,12},{8,0},{12,4},{16,24},{20,28},{24,16},{28,20},{1,9},{5... | collective-permute-start | bytes 638984 | tf_op jit(solution)/shard_map/ppermute | solution.py:660
  6.8 7.6 %collective-permute-start.3 = (bf16[16,2176]{1,0:T(8,128)(2,1)S(1)}, bf16[16,2176]{1,0:T(8,128)(2,1)S(1)}, u32[]{:S(2)}, u32[]{:S(2)}) collective-permute-start(bf16[16,2176]{1,0:T(8,128)(2,1)S(1)} %get-tuple-element.128), channel_id=1, source_target_pairs={{0,2},{1,3},{2,0},{3,1},{4,6},{5,7},{6,4},{7,5},{8,10},{9,11},{10,... | collective-permute-start | bytes 208904 | tf_op jit(solution)/shard_map/ppermute | solution.py:660
  17.6 16.6 %collective-permute-start.5 = (bf16[208,512]{1,0:T(8,128)(2,1)S(1)}, bf16[208,512]{1,0:T(8,128)(2,1)S(1)}, u32[]{:S(2)}, u32[]{:S(2)}) collective-permute-start(bf16[208,512]{1,0:T(8,128)(2,1)S(1)} %get-tuple-element.138), channel_id=1, source_target_pairs={{0,24},{4,28},{8,16},{12,20},{16,8},{20,12},{24,0},{28,4},{1,25},{... | collective-permute-start | bytes 638984 | tf_op jit(solution)/shard_map/ppermute | solution.py:660
  18.1 16.0 %collective-permute-start.6 = (bf16[160,512]{1,0:T(8,128)(2,1)S(1)}, bf16[160,512]{1,0:T(8,128)(2,1)S(1)}, u32[]{:S(2)}, u32[]{:S(2)}) collective-permute-start(bf16[160,512]{1,0:T(8,128)(2,1)S(1)} %get-tuple-element.139), channel_id=1, source_target_pairs={{0,1},{1,0},{2,3},{3,2},{4,5},{5,4},{6,7},{7,6},{8,9},{9,8},{10,11... | collective-permute-start | bytes 491528 | tf_op jit(solution)/shard_map/ppermute | solution.py:660
  18.7 15.4 %collective-permute-start.8 = (bf16[160,512]{1,0:T(8,128)(2,1)S(1)}, bf16[160,512]{1,0:T(8,128)(2,1)S(1)}, u32[]{:S(2)}, u32[]{:S(2)}) collective-permute-start(bf16[160,512]{1,0:T(8,128)(2,1)S(1)} %get-tuple-element.140), channel_id=1, source_target_pairs={{0,3},{1,2},{2,1},{3,0},{4,7},{5,6},{6,5},{7,4},{8,11},{9,10},{10,... | collective-permute-start | bytes 491528 | tf_op jit(solution)/shard_map/ppermute | solution.py:660
  21.6 12.5 %collective-permute-start.7 = (bf16[128,512]{1,0:T(8,128)(2,1)S(1)}, bf16[128,512]{1,0:T(8,128)(2,1)S(1)}, u32[]{:S(2)}, u32[]{:S(2)}) collective-permute-start(bf16[128,512]{1,0:T(8,128)(2,1)S(1)} %slice.17), channel_id=1, source_target_pairs={{0,2},{1,3},{2,0},{3,1},{4,6},{5,7},{6,4},{7,5},{8,10},{9,11},{10,... | collective-permute-start | bytes 393224 | tf_op jit(solution)/shard_map/ppermute | solution.py:660
  34.9 21.5 %collective-permute-start.14 = (bf16[3,128,512]{2,1,0:T(8,128)(2,1)S(1)}, bf16[3,128,512]{2,1,0:T(8,128)(2,1)S(1)}, u32[]{:S(2)}, u32[]{:S(2)}) collective-permute-start(bf16[3,128,512]{2,1,0:T(8,128)(2,1)S(1)} %pad_maximum_fusion.1.refs_0_), channel_id=1, source_target_pairs={{0,4},{4,0},{8,12},{12,8},{16,20},{20,16},{24,28},{28,24},{1,5},{5... | collective-permute-start | bytes 1179656 | tf_op jit(solution)/shard_map/ppermute | solution.py:660
  35.0 20.2 %collective-permute-start.11 = (bf16[3,128,512]{2,1,0:T(8,128)(2,1)S(1)}, bf16[3,128,512]{2,1,0:T(8,128)(2,1)S(1)}, u32[]{:S(2)}, u32[]{:S(2)}) collective-permute-start(bf16[3,128,512]{2,1,0:T(8,128)(2,1)S(1)} %pad_maximum_fusion.1.refs_0_), channel_id=1, source_target_pairs={{0,24},{4,28},{8,16},{12,20},{16,8},{20,12},{24,0},{28,4},{1,25},{... | collective-permute-start | bytes 1179656 | tf_op jit(solution)/shard_map/ppermute | solution.py:660
  36.4 19.4 %collective-permute-start.10 = (bf16[3,128,512]{2,1,0:T(8,128)(2,1)S(1)}, bf16[3,128,512]{2,1,0:T(8,128)(2,1)S(1)}, u32[]{:S(2)}, u32[]{:S(2)}) collective-permute-start(bf16[3,128,512]{2,1,0:T(8,128)(2,1)S(1)} %pad_maximum_fusion.1.refs_0_), channel_id=1, source_target_pairs={{0,16},{4,20},{8,24},{12,28},{16,0},{20,4},{24,8},{28,12},{1,17},{... | collective-permute-start | bytes 1179656 | tf_op jit(solution)/shard_map/ppermute | solution.py:660
  38.0 17.9 %collective-permute-start.9 = (bf16[3,128,512]{2,1,0:T(8,128)(2,1)S(1)}, bf16[3,128,512]{2,1,0:T(8,128)(2,1)S(1)}, u32[]{:S(2)}, u32[]{:S(2)}) collective-permute-start(bf16[3,128,512]{2,1,0:T(8,128)(2,1)S(1)} %pad_maximum_fusion.1.refs_0_), channel_id=1, source_target_pairs={{0,8},{4,12},{8,0},{12,4},{16,24},{20,28},{24,16},{28,20},{1,9},{5... | collective-permute-start | bytes 1179656 | tf_op jit(solution)/shard_map/ppermute | solution.py:660
  75.4 17.6 %collective-permute-start.24 = (bf16[4,144,512]{2,1,0:T(8,128)(2,1)S(1)}, bf16[4,144,512]{2,1,0:T(8,128)(2,1)S(1)}, u32[]{:S(2)}, u32[]{:S(2)}) collective-permute-start(bf16[4,144,512]{2,1,0:T(8,128)(2,1)S(1)} %get-tuple-element.196), channel_id=1, source_target_pairs={{0,1},{1,0},{2,3},{3,2},{4,5},{5,4},{6,7},{7,6},{8,9},{9,8},{10,11... | collective-permute-start | bytes 1769480 | tf_op jit(solution)/shard_map/ppermute | solution.py:660
  77.0 14.8 %collective-permute-start.21 = (bf16[288,512]{1,0:T(8,128)(2,1)S(1)}, bf16[288,512]{1,0:T(8,128)(2,1)S(1)}, u32[]{:S(2)}, u32[]{:S(2)}) collective-permute-start(bf16[288,512]{1,0:T(8,128)(2,1)S(1)} %get-tuple-element.193), channel_id=1, source_target_pairs={{0,8},{4,12},{8,0},{12,4},{16,24},{20,28},{24,16},{28,20},{1,9},{5... | collective-permute-start | bytes 884744 | tf_op jit(solution)/shard_map/ppermute | solution.py:660
  78.1 14.8 %collective-permute-start.22 = (bf16[288,512]{1,0:T(8,128)(2,1)S(1)}, bf16[288,512]{1,0:T(8,128)(2,1)S(1)}, u32[]{:S(2)}, u32[]{:S(2)}) collective-permute-start(bf16[288,512]{1,0:T(8,128)(2,1)S(1)} %get-tuple-element.194), channel_id=1, source_target_pairs={{0,16},{4,20},{8,24},{12,28},{16,0},{20,4},{24,8},{28,12},{1,17},{... | collective-permute-start | bytes 884744 | tf_op jit(solution)/shard_map/ppermute | solution.py:660
  78.9 14.1 %collective-permute-start.23 = (bf16[288,512]{1,0:T(8,128)(2,1)S(1)}, bf16[288,512]{1,0:T(8,128)(2,1)S(1)}, u32[]{:S(2)}, u32[]{:S(2)}) collective-permute-start(bf16[288,512]{1,0:T(8,128)(2,1)S(1)} %get-tuple-element.195), channel_id=1, source_target_pairs={{0,24},{4,28},{8,16},{12,20},{16,8},{20,12},{24,0},{28,4},{1,25},{... | collective-permute-start | bytes 884744 | tf_op jit(solution)/shard_map/ppermute | solution.py:660
  95.5 11.9 %collective-permute-start.26 = (bf16[4,16,1664]{2,1,0:T(8,128)(2,1)S(1)}, bf16[4,16,1664]{2,1,0:T(8,128)(2,1)S(1)}, u32[]{:S(2)}, u32[]{:S(2)}) collective-permute-start(bf16[4,16,1664]{2,1,0:T(8,128)(2,1)S(1)} %get-tuple-element.203), channel_id=1, source_target_pairs={{0,8},{4,12},{8,0},{12,4},{16,24},{20,28},{24,16},{28,20},{1,9},{5... | collective-permute-start | bytes 638984 | tf_op jit(solution)/shard_map/ppermute | solution.py:660
  96.4 11.6 %collective-permute-start.27 = (bf16[4,16,1664]{2,1,0:T(8,128)(2,1)S(1)}, bf16[4,16,1664]{2,1,0:T(8,128)(2,1)S(1)}, u32[]{:S(2)}, u32[]{:S(2)}) collective-permute-start(bf16[4,16,1664]{2,1,0:T(8,128)(2,1)S(1)} %get-tuple-element.204), channel_id=1, source_target_pairs={{0,16},{4,20},{8,24},{12,28},{16,0},{20,4},{24,8},{28,12},{1,17},{... | collective-permute-start | bytes 638984 | tf_op jit(solution)/shard_map/ppermute | solution.py:660
  97.6 10.5 %collective-permute-start.28 = (bf16[4,16,1664]{2,1,0:T(8,128)(2,1)S(1)}, bf16[4,16,1664]{2,1,0:T(8,128)(2,1)S(1)}, u32[]{:S(2)}, u32[]{:S(2)}) collective-permute-start(bf16[4,16,1664]{2,1,0:T(8,128)(2,1)S(1)} %get-tuple-element.205), channel_id=1, source_target_pairs={{0,24},{4,28},{8,16},{12,20},{16,8},{20,12},{24,0},{28,4},{1,25},{... | collective-permute-start | bytes 638984 | tf_op jit(solution)/shard_map/ppermute | solution.py:660
  104.5 7.8 %collective-permute-start.33 = (bf16[144,512]{1,0:T(8,128)(2,1)S(1)}, bf16[144,512]{1,0:T(8,128)(2,1)S(1)}, u32[]{:S(2)}, u32[]{:S(2)}) collective-permute-start(bf16[144,512]{1,0:T(8,128)(2,1)S(1)} %shard_map.209), channel_id=1, source_target_pairs={{0,3},{1,2},{2,1},{3,0},{4,7},{5,6},{6,5},{7,4},{8,11},{9,10},{10,... | collective-permute-start | bytes 442376 | tf_op jit(solution)/shard_map/ppermute | solution.py:660
  108.1 7.1 %collective-permute-start.29 = (bf16[144,512]{1,0:T(8,128)(2,1)S(1)}, bf16[144,512]{1,0:T(8,128)(2,1)S(1)}, u32[]{:S(2)}, u32[]{:S(2)}) collective-permute-start(bf16[144,512]{1,0:T(8,128)(2,1)S(1)} %get-tuple-element.216), channel_id=1, source_target_pairs={{0,8},{4,12},{8,0},{12,4},{16,24},{20,28},{24,16},{28,20},{1,9},{5... | collective-permute-start | bytes 442376 | tf_op jit(solution)/shard_map/ppermute | solution.py:660
  109.3 10.2 %collective-permute-start.30 = (bf16[144,512]{1,0:T(8,128)(2,1)S(1)}, bf16[144,512]{1,0:T(8,128)(2,1)S(1)}, u32[]{:S(2)}, u32[]{:S(2)}) collective-permute-start(bf16[144,512]{1,0:T(8,128)(2,1)S(1)} %get-tuple-element.217), channel_id=1, source_target_pairs={{0,16},{4,20},{8,24},{12,28},{16,0},{20,4},{24,8},{28,12},{1,17},{... | collective-permute-start | bytes 442376 | tf_op jit(solution)/shard_map/ppermute | solution.py:660
  110.0 9.5 %collective-permute-start.31 = (bf16[144,512]{1,0:T(8,128)(2,1)S(1)}, bf16[144,512]{1,0:T(8,128)(2,1)S(1)}, u32[]{:S(2)}, u32[]{:S(2)}) collective-permute-start(bf16[144,512]{1,0:T(8,128)(2,1)S(1)} %get-tuple-element.218), channel_id=1, source_target_pairs={{0,24},{4,28},{8,16},{12,20},{16,8},{20,12},{24,0},{28,4},{1,25},{... | collective-permute-start | bytes 442376 | tf_op jit(solution)/shard_map/ppermute | solution.py:660
  111.7 8.6 %collective-permute-start.34 = (bf16[16,1664]{1,0:T(8,128)(2,1)S(1)}, bf16[16,1664]{1,0:T(8,128)(2,1)S(1)}, u32[]{:S(2)}, u32[]{:S(2)}) collective-permute-start(bf16[16,1664]{1,0:T(8,128)(2,1)S(1)} %get-tuple-element.231), channel_id=1, source_target_pairs={{0,1},{1,0},{2,3},{3,2},{4,5},{5,4},{6,7},{7,6},{8,9},{9,8},{10,11... | collective-permute-start | bytes 159752 | tf_op jit(solution)/shard_map/ppermute | solution.py:660
  112.3 8.0 %collective-permute-start.35 = (bf16[16,1664]{1,0:T(8,128)(2,1)S(1)}, bf16[16,1664]{1,0:T(8,128)(2,1)S(1)}, u32[]{:S(2)}, u32[]{:S(2)}) collective-permute-start(bf16[16,1664]{1,0:T(8,128)(2,1)S(1)} %get-tuple-element.232), channel_id=1, source_target_pairs={{0,2},{1,3},{2,0},{3,1},{4,6},{5,7},{6,4},{7,5},{8,10},{9,11},{10,... | collective-permute-start | bytes 159752 | tf_op jit(solution)/shard_map/ppermute | solution.py:660
  (17 other events, 93.3 us)

commit v6 on v5

--- a/solution.py
+++ b/solution.py
@@ -264,8 +264,22 @@
     )(*[near_core(a) for a in (*keeps, *parts)])
 
 
-def finish_kernel(own, one, two, three, grad, *norm_grads):
-    total = own[...] + (one[...].astype(F32) + two[...].astype(F32) + three[...].astype(F32))
+def far_kernel(own, pair, out):
+    out[...] = (own[...] + pair[1].astype(F32)).astype(BF16)
+
+
+def add_far(own, pair):
+    return pl.pallas_call(
+        far_kernel,
+        out_shape=[jax.ShapeDtypeStruct(own.shape, BF16)],
+        in_specs=[VMEM] * 2,
+        out_specs=[VMEM],
+        compiler_params=pltpu.CompilerParams(vmem_limit_bytes=SMALL),
+    )(near_core(own), near_core(pair))[0]
+
+
+def finish_kernel(own, pair, far, grad, *norm_grads):
+    total = own[...] + (pair[0].astype(F32) + far[...].astype(F32))
     grad[...] = total[:, : 3 * D]
     rows = jnp.transpose(total[:, 3 * D :])
     for i, norm_grad in enumerate(norm_grads):
@@ -969,9 +983,17 @@
         first_pair, *first_low = add_slots(keep, from_core)
         first = [swap(part, "dp", 2 * m + 2) for m, part in enumerate(first_low)]
         own_pair, *own_low = add_slots(own_pair, from_near)
-        *first, own0, own1, own2 = together(*first, *own_low)
-        first_own, *first_low = add_slots(first_pair, *first)
-        first_parts = [swap(part, "seq", k + 1) for k, part in enumerate(first_low)]
+        *first, second[0], own0, own1, own2, out = together(*first, *second, *own_low, out)
+        everything = slice(None)
+        slot = first_pair.shape[1:]
+        first_own, to_near, to_far = add(
+            [[(everything, 0)], [(0, 1), (1, 2)], [(everything, 3)]],
+            [(slot, F32), ((2, *slot), BF16), (slot, F32)],
+            first_pair,
+            *first,
+        )
+        near_part = swap(to_near, "seq", 1)
+        first_parts = [near_part, swap(add_far(to_far, near_part), "seq", 3)]
         own_parts = [swap(part, "dp", 2 * m + 2) for m, part in enumerate((own0, own1, own2))]
         everything, bounds = slice(None), (0, block, 2 * block, rows)
         grad_up, grad_down, grad_out = add(

time: 122 us -> 121 us (level)
  starting transfers between devices: 41 us -> 39.4 us
    ppermute x37 -> x36, starting transfers between devices: 41 us -> 39.4 us  [swap(): lax.ppermute(array, axis, [(i, i ^ bit) for i in range(lax.axis_size(axis...]
    ppermute x37 -> x36, waiting for transfers between devices: 14.9 us -> 15.2 us  [swap(): lax.ppermute(array, axis, [(i, i ^ bit) for i in range(lax.axis_size(axis...]
  transfers between devices with their start and end apart: 37 -> 36, of which waited for: 13 -> 13; matrix products, arithmetic and copies ran while one was open for 0% -> 0% of each run, Pallas kernels for 31% -> 31%
where the time goes in v6:
time: 121 us; the launch traced here: 120 us
  Pallas kernels  52.1 us (43%)
  starting transfers between devices  39.4 us (33%)
  waiting for transfers between devices  15.2 us (13%)
  blocking collectives  12.4 us (10%)
    pallas_call x8, Pallas kernels, run_kernel(): pl.pallas_call(body, out_shape=out_shape, in_specs=[SMEM] + specs, out_sp...  48 us
    ppermute x36, starting transfers between devices, swap(): lax.ppermute(array, axis, [(i, i ^ bit) for i in range(lax.axis_size(axis...  39.4 us
    ppermute x36, waiting for transfers between devices, swap(): lax.ppermute(array, axis, [(i, i ^ bit) for i in range(lax.axis_size(axis...  15.2 us
    all_gather x1, blocking collectives, per_device(): first_half = lax.all_gather(column, 'dp', axis_index_groups=CHIPS)  12.4 us
  transfers between devices with their start and end apart: 36, of which 13 were waited for; matrix products, arithmetic and copies ran while one was open for 0% of the time, Pallas kernels for 31%

profile of v6, /device:TPU:0, one launch (start us, length us, event | category | flops | bytes accessed | tf_op | source)
XLA Modules:
  0.0 120.5 jit_solution(232160753716550406)
XLA Ops:
  0.7 1.6 %shard_map.195 = (bf16[16,3200]{1,0:T(8,128)(2,1)S(1)}, bf16[16,2176]{1,0:T(8,128)(2,1)S(1)}, bf16[16,3200]{1,0:T(8,128)(2,1)S(1)}, bf16[208,512]{1,0:T(8,128)(2...) custom-call(bf16[704,512]{1,0:T(8,128)(2,1)} %rows.2, bf16[704,512]{1,0:T(8,128)(2,1)} %rows.3, ...), custom_call_target="tpu_custom_call" | custom-call | tf_op jit(solution)/shard_map/pallas_call | solution.py:745
  2.3 3.0 %collective-permute-start.1 = (bf16[208,512]{1,0:T(8,128)(2,1)S(1)}, bf16[208,512]{1,0:T(8,128)(2,1)S(1)}, u32[]{:S(2)}, u32[]{:S(2)}) collective-permute-start(bf16[208,512]{1,0:T(8,128)(2,1)S(1)} %get-tuple-element.140), channel_id=1, source_target_pairs={{0,16},{4,20},{8,24},{12,28},{16,0},{20,4},{24,8},{28,12},{1,17},{... | collective-permute-start | bytes 638984 | tf_op jit(solution)/shard_map/ppermute | solution.py:674
  6.8 2.6 %collective-permute-start.3 = (bf16[16,2176]{1,0:T(8,128)(2,1)S(1)}, bf16[16,2176]{1,0:T(8,128)(2,1)S(1)}, u32[]{:S(2)}, u32[]{:S(2)}) collective-permute-start(bf16[16,2176]{1,0:T(8,128)(2,1)S(1)} %get-tuple-element.129), channel_id=1, source_target_pairs={{0,2},{1,3},{2,0},{3,1},{4,6},{5,7},{6,4},{7,5},{8,10},{9,11},{10,... | collective-permute-start | bytes 208904 | tf_op jit(solution)/shard_map/ppermute | solution.py:674
  9.4 1.6 %collective-permute-start.2 = (bf16[16,3200]{1,0:T(8,128)(2,1)S(1)}, bf16[16,3200]{1,0:T(8,128)(2,1)S(1)}, u32[]{:S(2)}, u32[]{:S(2)}) collective-permute-start(bf16[16,3200]{1,0:T(8,128)(2,1)S(1)} %get-tuple-element.128), channel_id=1, source_target_pairs={{0,1},{1,0},{2,3},{3,2},{4,5},{5,4},{6,7},{7,6},{8,9},{9,8},{10,11... | collective-permute-start | bytes 307208 | tf_op jit(solution)/shard_map/ppermute | solution.py:674
  11.5 2.9 %shard_map.196 = (bf16[768,512]{1,0:T(8,128)(2,1)S(1)}, bf16[768,512]{1,0:T(8,128)(2,1)S(1)}, bf16[768,512]{1,0:T(8,128)(2,1)S(1)}, f32[768,128]{1,0:T(8,128)S(1)}) custom-call(s32[11]{0:T(128)S(1)} %pad_add_fusion.info, bf16[704,512]{1,0:T(8,128)(2,1)S(1)} %copy-done, bf16[704,512]{1,0:T(8,128)(2,1)S(1)} %copy-done.1), custom_call_target="tpu_custom_call" | custom-call | flops 402653184 | bytes 1441792 | tf_op jit(solution)/shard_map/pallas_call | solution.py:660
  14.4 3.1 %collective-permute-done.4.far = bf16[16,3200]{1,0:T(8,128)(2,1)S(1)} collective-permute-done((bf16[16,3200]{1,0:T(8,128)(2,1)S(1)}, bf16[16,3200]{1,0:T(8,128)(2,1)S(1)}, u32[]{:S(2)}, u32[]{:S(2)}) %collective-permute-start.4) | collective-permute-done | bytes 102432 | tf_op jit(solution)/shard_map/ppermute | solution.py:674
  18.7 2.9 %collective-permute-start.8 = (bf16[160,512]{1,0:T(8,128)(2,1)S(1)}, bf16[160,512]{1,0:T(8,128)(2,1)S(1)}, u32[]{:S(2)}, u32[]{:S(2)}) collective-permute-start(bf16[160,512]{1,0:T(8,128)(2,1)S(1)} %get-tuple-element.142), channel_id=1, source_target_pairs={{0,3},{1,2},{2,1},{3,0},{4,7},{5,6},{6,5},{7,4},{8,11},{9,10},{10,... | collective-permute-start | bytes 491528 | tf_op jit(solution)/shard_map/ppermute | solution.py:674
  21.7 12.4 %all-gather = bf16[12,16,2176]{2,1,0:T(8,128)(2,1)S(1)} all-gather(bf16[3,16,2176]{2,1,0:T(8,128)(2,1)S(1)} %pad_maximum_fusion.2), channel_id=2, replica_groups={{0,8,16,24},{4,12,20,28},{1,9,17,25},{5,13,21,29},{2,10,18,26},{6,14,22..., dimensions={0}, use_global_device_ids=true | all-gather | bytes 1044480 | tf_op jit(solution)/shard_map/all_gather | solution.py:783
  36.4 1.6 %collective-permute-start.12 = (bf16[3,128,512]{2,1,0:T(8,128)(2,1)S(1)}, bf16[3,128,512]{2,1,0:T(8,128)(2,1)S(1)}, u32[]{:S(2)}, u32[]{:S(2)}) collective-permute-start(bf16[3,128,512]{2,1,0:T(8,128)(2,1)S(1)} %pad_maximum_fusion.1.refs_0_), channel_id=1, source_target_pairs={{0,16},{4,20},{8,24},{12,28},{16,0},{20,4},{24,8},{28,12},{1,17},{... | collective-permute-start | bytes 1179656 | tf_op jit(solution)/shard_map/ppermute | solution.py:674
  39.5 9.9 %shard_map.197 = (bf16[768,512]{1,0:T(8,128)(2,1)S(1)}, bf16[768,1536]{1,0:T(8,128)(2,1)S(1)}, bf16[768,512]{1,0:T(8,128)(2,1)S(1)}, bf16[768,512]{1,0:T(8,128)(...) custom-call(s32[11]{0:T(128)S(1)} %pad_add_fusion.info, bf16[704,512]{1,0:T(8,128)(2,1)S(1)} %copy-done, ...), custom_call_target="tpu_custom_call" | custom-call | flops 2415919104 | bytes 5087232 | tf_op jit(solution)/shard_map/pallas_call | solution.py:660
  49.4 5.8 %shard_map.198 = (f32[768,512]{1,0:T(8,128)S(1)}, f32[768,512]{1,0:T(8,128)S(1)}, f32[768,512]{1,0:T(8,128)S(1)}, bf16[768,512]{1,0:T(8,128)(2,1)S(1)}, bf16[768...) custom-call(s32[11]{0:T(128)S(1)} %pad_add_fusion.info, ...), custom_call_target="tpu_custom_call" | custom-call | flops 2818572288 | bytes 8536064 | tf_op jit(solution)/shard_map/pallas_call | solution.py:660
  58.7 11.4 %shard_map.199 = (f32[768,512]{1,0:T(8,128)S(1)}, f32[768,512]{1,0:T(8,128)S(1)}, bf16[4,384,512]{2,1,0:T(8,128)(2,1)S(1)}, bf16[4,384,512]{2,1,0:T(8,128)(2,1)S(1)}) custom-call(s32[11]{0:T(128)S(1)} %pad_add_fusion.info, f32[768,512]{1,0:T(8,128)S(1)} %get-tuple-element.164.total_in, f32[768,512]{1,0:T(8,128)S(1)} %get-tuple-element.165.grad_in, ...), custom_call_target="tpu_custom_call" | custom-call | flops 7247757312 | bytes 9437184 | tf_op jit(solution)/shard_map/pallas_call | solution.py:660
  70.7 2.5 %shard_map.200 = (f32[768,512]{1,0:T(8,128)S(1)}, bf16[768,512]{1,0:T(8,128)(2,1)S(1)}, f32[8,512]{1,0:T(8,128)S(1)}, bf16[4,64,512]{2,1,0:T(8,128)(2,1)S(1)}, bf16[4,64,512]{2,1,0:T(8,128)(2,1)S(1)}) custom-call(s32[11]{0:T(128)S(1)} %pad_add_fusion.info, f32[768,512]{1,0:T(8,128)S(1)} %get-tuple-element.174.middle, ...), custom_call_target="tpu_custom_call" | custom-call | flops 805306368 | bytes 7356416 | tf_op jit(solution)/shard_map/pallas_call | solution.py:660
  75.4 1.6 %collective-permute-start.24 = (bf16[4,144,512]{2,1,0:T(8,128)(2,1)S(1)}, bf16[4,144,512]{2,1,0:T(8,128)(2,1)S(1)}, u32[]{:S(2)}, u32[]{:S(2)}) collective-permute-start(bf16[4,144,512]{2,1,0:T(8,128)(2,1)S(1)} %get-tuple-element.196), channel_id=1, source_target_pairs={{0,1},{1,0},{2,3},{3,2},{4,5},{5,4},{6,7},{7,6},{8,9},{9,8},{10,11... | collective-permute-start | bytes 1769480 | tf_op jit(solution)/shard_map/ppermute | solution.py:674
  80.4 11.3 %shard_map.202 = (f32[768,512]{1,0:T(8,128)S(1)}, bf16[4,4,16,1664]{3,2,1,0:T(8,128)(2,1)S(1)}, bf16[4,4,16,1664]{3,2,1,0:T(8,128)(2,1)S(1)}) custom-call(s32[11]{0:T(128)S(1)} %pad_add_fusion.info, bf16[768,512]{1,0:T(8,128)(2,1)S(1)} %get-tuple-element.152.x_in, f32[768,128]{1,0:T(8,128)S(1)} %get-tuple-element.153.own, ...), custom_call_target="tpu_custom_call" | custom-call | flops 3623878656 | bytes 8945664 | tf_op jit(solution)/shard_map/pallas_call | solution.py:660
  94.0 2.1 %shard_map.203 = bf16[704,512]{1,0:T(8,128)(2,1)} custom-call(s32[11]{0:T(128)S(1)} %pad_add_fusion.info, f32[768,512]{1,0:T(8,128)S(1)} %get-tuple-element.199.values), custom_call_target="tpu_custom_call" | custom-call | flops 402653184 | bytes 1572864 | tf_op jit(solution)/shard_map/pallas_call | solution.py:660
  99.8 2.6 %collective-permute-start.30 = (bf16[144,512]{1,0:T(8,128)(2,1)S(1)}, bf16[144,512]{1,0:T(8,128)(2,1)S(1)}, u32[]{:S(2)}, u32[]{:S(2)}) collective-permute-start(bf16[144,512]{1,0:T(8,128)(2,1)S(1)} %shard_map.206), channel_id=1, source_target_pairs={{0,3},{1,2},{2,1},{3,0},{4,7},{5,6},{6,5},{7,4},{8,11},{9,10},{10,... | collective-permute-start | bytes 442376 | tf_op jit(solution)/shard_map/ppermute | solution.py:674
  102.4 2.1 %shard_map.208 = bf16[704,512]{1,0:T(8,128)(2,1)} custom-call(s32[11]{0:T(128)S(1)} %pad_add_fusion.info, f32[768,512]{1,0:T(8,128)S(1)} %get-tuple-element.217.values), custom_call_target="tpu_custom_call" | custom-call | flops 402653184 | bytes 1572864 | tf_op jit(solution)/shard_map/pallas_call | solution.py:660
  104.6 2.4 %collective-permute-done.30.refs_4_ = bf16[144,512]{1,0:T(8,128)(2,1)S(1)} collective-permute-done((bf16[144,512]{1,0:T(8,128)(2,1)S(1)}, bf16[144,512]{1,0:T(8,128)(2,1)S(1)}, u32[]{:S(2)}, u32[]{:S(2)}) %collective-permute-start.30) | collective-permute-done | bytes 147488 | tf_op jit(solution)/shard_map/ppermute | solution.py:674
  106.9 1.6 %collective-permute-done.27.refs_2_ = bf16[4,16,1664]{2,1,0:T(8,128)(2,1)S(1)} collective-permute-done((bf16[4,16,1664]{2,1,0:T(8,128)(2,1)S(1)}, bf16[4,16,1664]{2,1,0:T(8,128)(2,1)S(1)}, u32[]{:S(2)}, u32[]{:S(2)}) %collective-permute-start.27) | collective-permute-done | bytes 213024 | tf_op jit(solution)/shard_map/ppermute | solution.py:674
  108.6 1.6 %collective-permute-start.34 = (bf16[2,16,1664]{2,1,0:T(8,128)(2,1)S(1)}, bf16[2,16,1664]{2,1,0:T(8,128)(2,1)S(1)}, u32[]{:S(2)}, u32[]{:S(2)}) collective-permute-start(bf16[2,16,1664]{2,1,0:T(8,128)(2,1)S(1)} %get-tuple-element.234), channel_id=1, source_target_pairs={{0,1},{1,0},{2,3},{3,2},{4,5},{5,4},{6,7},{7,6},{8,9},{9,8},{10,11... | collective-permute-start | bytes 319496 | tf_op jit(solution)/shard_map/ppermute | solution.py:674
  112.1 1.6 %collective-permute-start.33 = (bf16[144,512]{1,0:T(8,128)(2,1)S(1)}, bf16[144,512]{1,0:T(8,128)(2,1)S(1)}, u32[]{:S(2)}, u32[]{:S(2)}) collective-permute-start(bf16[144,512]{1,0:T(8,128)(2,1)S(1)} %get-tuple-element.228), channel_id=1, source_target_pairs={{0,24},{4,28},{8,16},{12,20},{16,8},{20,12},{24,0},{28,4},{1,25},{... | collective-permute-start | bytes 442376 | tf_op jit(solution)/shard_map/ppermute | solution.py:674
  113.7 2.9 %collective-permute-start.35 = (bf16[16,1664]{1,0:T(8,128)(2,1)S(1)}, bf16[16,1664]{1,0:T(8,128)(2,1)S(1)}, u32[]{:S(2)}, u32[]{:S(2)}) collective-permute-start(bf16[16,1664]{1,0:T(8,128)(2,1)S(1)} %shard_map.211), channel_id=1, source_target_pairs={{0,3},{1,2},{2,1},{3,0},{4,7},{5,6},{6,5},{7,4},{8,11},{9,10},{10,... | collective-permute-start | bytes 159752 | tf_op jit(solution)/shard_map/ppermute | solution.py:674
  116.9 2.2 %collective-permute-done.32.refs_2_ = bf16[144,512]{1,0:T(8,128)(2,1)S(1)} collective-permute-done((bf16[144,512]{1,0:T(8,128)(2,1)S(1)}, bf16[144,512]{1,0:T(8,128)(2,1)S(1)}, u32[]{:S(2)}, u32[]{:S(2)}) %collective-permute-start.32) | collective-permute-done | bytes 147488 | tf_op jit(solution)/shard_map/ppermute | solution.py:674
  (85 shorter events, 26.4 us)
Async XLA Ops:
  2.3 15.3 %collective-permute-start.1 = (bf16[208,512]{1,0:T(8,128)(2,1)S(1)}, bf16[208,512]{1,0:T(8,128)(2,1)S(1)}, u32[]{:S(2)}, u32[]{:S(2)}) collective-permute-start(bf16[208,512]{1,0:T(8,128)(2,1)S(1)} %get-tuple-element.140), channel_id=1, source_target_pairs={{0,16},{4,20},{8,24},{12,28},{16,0},{20,4},{24,8},{28,12},{1,17},{... | collective-permute-start | bytes 638984 | tf_op jit(solution)/shard_map/ppermute | solution.py:674
  5.3 12.2 %collective-permute-start = (bf16[208,512]{1,0:T(8,128)(2,1)S(1)}, bf16[208,512]{1,0:T(8,128)(2,1)S(1)}, u32[]{:S(2)}, u32[]{:S(2)}) collective-permute-start(bf16[208,512]{1,0:T(8,128)(2,1)S(1)} %get-tuple-element.140), channel_id=1, source_target_pairs={{0,8},{4,12},{8,0},{12,4},{16,24},{20,28},{24,16},{28,20},{1,9},{5... | collective-permute-start | bytes 638984 | tf_op jit(solution)/shard_map/ppermute | solution.py:674
  6.8 7.6 %collective-permute-start.3 = (bf16[16,2176]{1,0:T(8,128)(2,1)S(1)}, bf16[16,2176]{1,0:T(8,128)(2,1)S(1)}, u32[]{:S(2)}, u32[]{:S(2)}) collective-permute-start(bf16[16,2176]{1,0:T(8,128)(2,1)S(1)} %get-tuple-element.129), channel_id=1, source_target_pairs={{0,2},{1,3},{2,0},{3,1},{4,6},{5,7},{6,4},{7,5},{8,10},{9,11},{10,... | collective-permute-start | bytes 208904 | tf_op jit(solution)/shard_map/ppermute | solution.py:674
  11.0 6.6 %collective-permute-start.4 = (bf16[16,3200]{1,0:T(8,128)(2,1)S(1)}, bf16[16,3200]{1,0:T(8,128)(2,1)S(1)}, u32[]{:S(2)}, u32[]{:S(2)}) collective-permute-start(bf16[16,3200]{1,0:T(8,128)(2,1)S(1)} %get-tuple-element.130), channel_id=1, source_target_pairs={{0,3},{1,2},{2,1},{3,0},{4,7},{5,6},{6,5},{7,4},{8,11},{9,10},{10,... | collective-permute-start | bytes 307208 | tf_op jit(solution)/shard_map/ppermute | solution.py:674
  17.6 16.6 %collective-permute-start.5 = (bf16[208,512]{1,0:T(8,128)(2,1)S(1)}, bf16[208,512]{1,0:T(8,128)(2,1)S(1)}, u32[]{:S(2)}, u32[]{:S(2)}) collective-permute-start(bf16[208,512]{1,0:T(8,128)(2,1)S(1)} %get-tuple-element.140), channel_id=1, source_target_pairs={{0,24},{4,28},{8,16},{12,20},{16,8},{20,12},{24,0},{28,4},{1,25},{... | collective-permute-start | bytes 638984 | tf_op jit(solution)/shard_map/ppermute | solution.py:674
  18.1 16.0 %collective-permute-start.6 = (bf16[160,512]{1,0:T(8,128)(2,1)S(1)}, bf16[160,512]{1,0:T(8,128)(2,1)S(1)}, u32[]{:S(2)}, u32[]{:S(2)}) collective-permute-start(bf16[160,512]{1,0:T(8,128)(2,1)S(1)} %get-tuple-element.141), channel_id=1, source_target_pairs={{0,1},{1,0},{2,3},{3,2},{4,5},{5,4},{6,7},{7,6},{8,9},{9,8},{10,11... | collective-permute-start | bytes 491528 | tf_op jit(solution)/shard_map/ppermute | solution.py:674
  18.7 15.4 %collective-permute-start.8 = (bf16[160,512]{1,0:T(8,128)(2,1)S(1)}, bf16[160,512]{1,0:T(8,128)(2,1)S(1)}, u32[]{:S(2)}, u32[]{:S(2)}) collective-permute-start(bf16[160,512]{1,0:T(8,128)(2,1)S(1)} %get-tuple-element.142), channel_id=1, source_target_pairs={{0,3},{1,2},{2,1},{3,0},{4,7},{5,6},{6,5},{7,4},{8,11},{9,10},{10,... | collective-permute-start | bytes 491528 | tf_op jit(solution)/shard_map/ppermute | solution.py:674
  21.6 12.5 %collective-permute-start.7 = (bf16[128,512]{1,0:T(8,128)(2,1)S(1)}, bf16[128,512]{1,0:T(8,128)(2,1)S(1)}, u32[]{:S(2)}, u32[]{:S(2)}) collective-permute-start(bf16[128,512]{1,0:T(8,128)(2,1)S(1)} %slice.17), channel_id=1, source_target_pairs={{0,2},{1,3},{2,0},{3,1},{4,6},{5,7},{6,4},{7,5},{8,10},{9,11},{10,... | collective-permute-start | bytes 393224 | tf_op jit(solution)/shard_map/ppermute | solution.py:674
  34.9 21.5 %collective-permute-start.14 = (bf16[3,128,512]{2,1,0:T(8,128)(2,1)S(1)}, bf16[3,128,512]{2,1,0:T(8,128)(2,1)S(1)}, u32[]{:S(2)}, u32[]{:S(2)}) collective-permute-start(bf16[3,128,512]{2,1,0:T(8,128)(2,1)S(1)} %pad_maximum_fusion.1.refs_0_), channel_id=1, source_target_pairs={{0,4},{4,0},{8,12},{12,8},{16,20},{20,16},{24,28},{28,24},{1,5},{5... | collective-permute-start | bytes 1179656 | tf_op jit(solution)/shard_map/ppermute | solution.py:674
  35.0 20.2 %collective-permute-start.13 = (bf16[3,128,512]{2,1,0:T(8,128)(2,1)S(1)}, bf16[3,128,512]{2,1,0:T(8,128)(2,1)S(1)}, u32[]{:S(2)}, u32[]{:S(2)}) collective-permute-start(bf16[3,128,512]{2,1,0:T(8,128)(2,1)S(1)} %pad_maximum_fusion.1.refs_0_), channel_id=1, source_target_pairs={{0,24},{4,28},{8,16},{12,20},{16,8},{20,12},{24,0},{28,4},{1,25},{... | collective-permute-start | bytes 1179656 | tf_op jit(solution)/shard_map/ppermute | solution.py:674
  36.4 19.4 %collective-permute-start.12 = (bf16[3,128,512]{2,1,0:T(8,128)(2,1)S(1)}, bf16[3,128,512]{2,1,0:T(8,128)(2,1)S(1)}, u32[]{:S(2)}, u32[]{:S(2)}) collective-permute-start(bf16[3,128,512]{2,1,0:T(8,128)(2,1)S(1)} %pad_maximum_fusion.1.refs_0_), channel_id=1, source_target_pairs={{0,16},{4,20},{8,24},{12,28},{16,0},{20,4},{24,8},{28,12},{1,17},{... | collective-permute-start | bytes 1179656 | tf_op jit(solution)/shard_map/ppermute | solution.py:674
  38.0 17.9 %collective-permute-start.11 = (bf16[3,128,512]{2,1,0:T(8,128)(2,1)S(1)}, bf16[3,128,512]{2,1,0:T(8,128)(2,1)S(1)}, u32[]{:S(2)}, u32[]{:S(2)}) collective-permute-start(bf16[3,128,512]{2,1,0:T(8,128)(2,1)S(1)} %pad_maximum_fusion.1.refs_0_), channel_id=1, source_target_pairs={{0,8},{4,12},{8,0},{12,4},{16,24},{20,28},{24,16},{28,20},{1,9},{5... | collective-permute-start | bytes 1179656 | tf_op jit(solution)/shard_map/ppermute | solution.py:674
  75.4 17.6 %collective-permute-start.24 = (bf16[4,144,512]{2,1,0:T(8,128)(2,1)S(1)}, bf16[4,144,512]{2,1,0:T(8,128)(2,1)S(1)}, u32[]{:S(2)}, u32[]{:S(2)}) collective-permute-start(bf16[4,144,512]{2,1,0:T(8,128)(2,1)S(1)} %get-tuple-element.196), channel_id=1, source_target_pairs={{0,1},{1,0},{2,3},{3,2},{4,5},{5,4},{6,7},{7,6},{8,9},{9,8},{10,11... | collective-permute-start | bytes 1769480 | tf_op jit(solution)/shard_map/ppermute | solution.py:674
  77.0 14.8 %collective-permute-start.21 = (bf16[288,512]{1,0:T(8,128)(2,1)S(1)}, bf16[288,512]{1,0:T(8,128)(2,1)S(1)}, u32[]{:S(2)}, u32[]{:S(2)}) collective-permute-start(bf16[288,512]{1,0:T(8,128)(2,1)S(1)} %get-tuple-element.193), channel_id=1, source_target_pairs={{0,8},{4,12},{8,0},{12,4},{16,24},{20,28},{24,16},{28,20},{1,9},{5... | collective-permute-start | bytes 884744 | tf_op jit(solution)/shard_map/ppermute | solution.py:674
  78.1 14.8 %collective-permute-start.22 = (bf16[288,512]{1,0:T(8,128)(2,1)S(1)}, bf16[288,512]{1,0:T(8,128)(2,1)S(1)}, u32[]{:S(2)}, u32[]{:S(2)}) collective-permute-start(bf16[288,512]{1,0:T(8,128)(2,1)S(1)} %get-tuple-element.194), channel_id=1, source_target_pairs={{0,16},{4,20},{8,24},{12,28},{16,0},{20,4},{24,8},{28,12},{1,17},{... | collective-permute-start | bytes 884744 | tf_op jit(solution)/shard_map/ppermute | solution.py:674
  78.9 14.1 %collective-permute-start.23 = (bf16[288,512]{1,0:T(8,128)(2,1)S(1)}, bf16[288,512]{1,0:T(8,128)(2,1)S(1)}, u32[]{:S(2)}, u32[]{:S(2)}) collective-permute-start(bf16[288,512]{1,0:T(8,128)(2,1)S(1)} %get-tuple-element.195), channel_id=1, source_target_pairs={{0,24},{4,28},{8,16},{12,20},{16,8},{20,12},{24,0},{28,4},{1,25},{... | collective-permute-start | bytes 884744 | tf_op jit(solution)/shard_map/ppermute | solution.py:674
  93.1 6.7 %collective-permute-start.29 = (bf16[144,512]{1,0:T(8,128)(2,1)S(1)}, bf16[144,512]{1,0:T(8,128)(2,1)S(1)}, u32[]{:S(2)}, u32[]{:S(2)}) collective-permute-start(bf16[144,512]{1,0:T(8,128)(2,1)S(1)} %get-tuple-element.209), channel_id=1, source_target_pairs={{0,1},{1,0},{2,3},{3,2},{4,5},{5,4},{6,7},{7,6},{8,9},{9,8},{10,11... | collective-permute-start | bytes 442376 | tf_op jit(solution)/shard_map/ppermute | solution.py:674
  96.2 10.7 %collective-permute-start.26 = (bf16[4,16,1664]{2,1,0:T(8,128)(2,1)S(1)}, bf16[4,16,1664]{2,1,0:T(8,128)(2,1)S(1)}, u32[]{:S(2)}, u32[]{:S(2)}) collective-permute-start(bf16[4,16,1664]{2,1,0:T(8,128)(2,1)S(1)} %get-tuple-element.201), channel_id=1, source_target_pairs={{0,8},{4,12},{8,0},{12,4},{16,24},{20,28},{24,16},{28,20},{1,9},{5... | collective-permute-start | bytes 638984 | tf_op jit(solution)/shard_map/ppermute | solution.py:674
  96.9 11.7 %collective-permute-start.27 = (bf16[4,16,1664]{2,1,0:T(8,128)(2,1)S(1)}, bf16[4,16,1664]{2,1,0:T(8,128)(2,1)S(1)}, u32[]{:S(2)}, u32[]{:S(2)}) collective-permute-start(bf16[4,16,1664]{2,1,0:T(8,128)(2,1)S(1)} %get-tuple-element.202), channel_id=1, source_target_pairs={{0,16},{4,20},{8,24},{12,28},{16,0},{20,4},{24,8},{28,12},{1,17},{... | collective-permute-start | bytes 638984 | tf_op jit(solution)/shard_map/ppermute | solution.py:674
  98.3 10.2 %collective-permute-start.28 = (bf16[4,16,1664]{2,1,0:T(8,128)(2,1)S(1)}, bf16[4,16,1664]{2,1,0:T(8,128)(2,1)S(1)}, u32[]{:S(2)}, u32[]{:S(2)}) collective-permute-start(bf16[4,16,1664]{2,1,0:T(8,128)(2,1)S(1)} %get-tuple-element.203), channel_id=1, source_target_pairs={{0,24},{4,28},{8,16},{12,20},{16,8},{20,12},{24,0},{28,4},{1,25},{... | collective-permute-start | bytes 638984 | tf_op jit(solution)/shard_map/ppermute | solution.py:674
  99.8 7.1 %collective-permute-start.30 = (bf16[144,512]{1,0:T(8,128)(2,1)S(1)}, bf16[144,512]{1,0:T(8,128)(2,1)S(1)}, u32[]{:S(2)}, u32[]{:S(2)}) collective-permute-start(bf16[144,512]{1,0:T(8,128)(2,1)S(1)} %shard_map.206), channel_id=1, source_target_pairs={{0,3},{1,2},{2,1},{3,0},{4,7},{5,6},{6,5},{7,4},{8,11},{9,10},{10,... | collective-permute-start | bytes 442376 | tf_op jit(solution)/shard_map/ppermute | solution.py:674
  110.2 6.7 %collective-permute-start.31 = (bf16[144,512]{1,0:T(8,128)(2,1)S(1)}, bf16[144,512]{1,0:T(8,128)(2,1)S(1)}, u32[]{:S(2)}, u32[]{:S(2)}) collective-permute-start(bf16[144,512]{1,0:T(8,128)(2,1)S(1)} %get-tuple-element.226), channel_id=1, source_target_pairs={{0,8},{4,12},{8,0},{12,4},{16,24},{20,28},{24,16},{28,20},{1,9},{5... | collective-permute-start | bytes 442376 | tf_op jit(solution)/shard_map/ppermute | solution.py:674
  111.4 7.7 %collective-permute-start.32 = (bf16[144,512]{1,0:T(8,128)(2,1)S(1)}, bf16[144,512]{1,0:T(8,128)(2,1)S(1)}, u32[]{:S(2)}, u32[]{:S(2)}) collective-permute-start(bf16[144,512]{1,0:T(8,128)(2,1)S(1)} %get-tuple-element.227), channel_id=1, source_target_pairs={{0,16},{4,20},{8,24},{12,28},{16,0},{20,4},{24,8},{28,12},{1,17},{... | collective-permute-start | bytes 442376 | tf_op jit(solution)/shard_map/ppermute | solution.py:674
  112.1 7.0 %collective-permute-start.33 = (bf16[144,512]{1,0:T(8,128)(2,1)S(1)}, bf16[144,512]{1,0:T(8,128)(2,1)S(1)}, u32[]{:S(2)}, u32[]{:S(2)}) collective-permute-start(bf16[144,512]{1,0:T(8,128)(2,1)S(1)} %get-tuple-element.228), channel_id=1, source_target_pairs={{0,24},{4,28},{8,16},{12,20},{16,8},{20,12},{24,0},{28,4},{1,25},{... | collective-permute-start | bytes 442376 | tf_op jit(solution)/shard_map/ppermute | solution.py:674
  (16 other events, 87.5 us)

commit v7 on v6

--- a/solution.py
+++ b/solution.py
@@ -212,20 +212,22 @@
     )(*[near_core(a) for a in operands])
 
 
-def pair_kernel(keep, *refs):
-    for m, (part, out) in enumerate(zip(refs[:4], refs[4:])):
-        out[...] = (keep[m].astype(F32) + part[...].astype(F32)).astype(out.dtype)
-
-
-def add_pairs(keep, parts):
-    slot = keep.shape[1:]
+def small_call(body, shapes, *operands, flops=0):
+    moved = sum(a.size * a.dtype.itemsize for a in operands)
     return pl.pallas_call(
-        pair_kernel,
-        out_shape=[jax.ShapeDtypeStruct(slot, kind) for kind in (F32, BF16, BF16, BF16)],
-        in_specs=[VMEM] * 5,
-        out_specs=[VMEM] * 4,
+        body,
+        out_shape=[jax.ShapeDtypeStruct(*s) for s in shapes],
+        in_specs=[VMEM] * len(operands),
+        out_specs=[VMEM] * len(shapes),
+        cost_estimate=pl.CostEstimate(flops=flops, bytes_accessed=moved, transcendentals=0),
         compiler_params=pltpu.CompilerParams(vmem_limit_bytes=SMALL),
-    )(*[near_core(a) for a in (keep, *parts)])
+    )(*[near_core(a) for a in operands])
+
+
+def stack_kernel(*refs):
+    *parts, out = refs
+    for i, part in enumerate(parts):
+        out[i] = part[:, 0 : out.shape[2]]
 
 
 def chunks_kernel(keep_first, keep_rest, keep_out, first, rest, out, *refs):
@@ -268,34 +270,19 @@
     out[...] = (own[...] + pair[1].astype(F32)).astype(BF16)
 
 
-def add_far(own, pair):
-    return pl.pallas_call(
-        far_kernel,
-        out_shape=[jax.ShapeDtypeStruct(own.shape, BF16)],
-        in_specs=[VMEM] * 2,
-        out_specs=[VMEM],
-        compiler_params=pltpu.CompilerParams(vmem_limit_bytes=SMALL),
-    )(near_core(own), near_core(pair))[0]
-
-
-def finish_kernel(own, pair, far, grad, *norm_grads):
-    total = own[...] + (pair[0].astype(F32) + far[...].astype(F32))
-    grad[...] = total[:, : 3 * D]
+def finish_kernel(chunk, first, one, two, three, second, pair, far, *outs):
+    total = chunk[...] + second[...].astype(F32)
+    for part in (one, two, three):
+        total = total + part[...].astype(F32)
+    row = 0
+    for out in outs[:3]:
+        out[...] = total[row : row + out.shape[0]]
+        row += out.shape[0]
+    total = first[...] + (pair[0].astype(F32) + far[...].astype(F32))
+    outs[3][...] = total[:, : 3 * D]
     rows = jnp.transpose(total[:, 3 * D :])
-    for i, norm_grad in enumerate(norm_grads):
-        norm_grad[...] = rows[i : i + 1]
-
-
-def finish_first(own, parts):
-    share = own.shape[0]
-    shapes = [(share, 3 * D)] + [(1, share)] * 4
-    return pl.pallas_call(
-        finish_kernel,
-        out_shape=[jax.ShapeDtypeStruct(dims, F32) for dims in shapes],
-        in_specs=[VMEM] * (1 + len(parts)),
-        out_specs=[VMEM] * len(shapes),
-        compiler_params=pltpu.CompilerParams(vmem_limit_bytes=SMALL),
-    )(*[near_core(a) for a in (own, *parts)])
+    for i, out in enumerate(outs[4:]):
+        out[...] = rows[i : i + 1]
 
 
 def add_slots(*operands):
@@ -640,6 +627,7 @@
 CHIPS = [[0, 2, 4, 6], [1, 3, 5, 7]]
 LIMIT = 20 * 1024 * 1024
 SMALL = 8 * 1024 * 1024
+EARLY = 4 * 10**9
 SMEM = pl.BlockSpec(memory_space=pltpu.SMEM)
 VMEM = pl.BlockSpec(memory_space=pltpu.VMEM)
 ANY = pl.BlockSpec(memory_space=pl.ANY)
@@ -979,11 +967,13 @@
         second_far, from_near_far = together(low[1], swap(low[0], "seq", 1))
         (second_far,) = add([[(slice(None), slice(None))]], [(low[1].shape, BF16)], second_far, from_near_far)
         second = [swap(second_far, "seq", 3)]
-        from_core, tokens_grad = together(*along_core([send]), tokens_grad)
+        (from_core,) = along_core([send])
         first_pair, *first_low = add_slots(keep, from_core)
         first = [swap(part, "dp", 2 * m + 2) for m, part in enumerate(first_low)]
         own_pair, *own_low = add_slots(own_pair, from_near)
-        *first, second[0], own0, own1, own2, out = together(*first, *second, *own_low, out)
+        *first, second, own0, own1, own2, out, tokens_grad = together(
+            *first, *second, *own_low, out, tokens_grad
+        )
         everything = slice(None)
         slot = first_pair.shape[1:]
         first_own, to_near, to_far = add(
@@ -993,21 +983,22 @@
             *first,
         )
         near_part = swap(to_near, "seq", 1)
-        first_parts = [near_part, swap(add_far(to_far, near_part), "seq", 3)]
+        (far_low,) = small_call(far_kernel, [(slot, BF16)], to_far, near_part, flops=EARLY)
+        far_part = swap(far_low, "seq", 3)
         own_parts = [swap(part, "dp", 2 * m + 2) for m, part in enumerate((own0, own1, own2))]
-        everything, bounds = slice(None), (0, block, 2 * block, rows)
-        grad_up, grad_down, grad_out = add(
-            [[(everything, (slice(a, b),))] for a, b in zip(bounds, bounds[1:])],
-            [((b - a, D), F32) for a, b in zip(bounds, bounds[1:])],
+        shapes = [((block, D), F32)] * 2 + [((share, D), F32), ((share, 3 * D), F32)]
+        shapes += [((1, share), F32)] * 4
+        grad_up, grad_down, grad_out, w_qkv_grad, *norm_grads = small_call(
+            finish_kernel,
+            shapes,
             own_pair,
+            first_own,
             *own_parts,
-            *second,
-        )
-        first_own, grad_up, grad_down, grad_out = together(
-            first_own, grad_up, grad_down, grad_out
+            second,
+            near_part,
+            far_part,
         )
         grad_down = grad_down.T
-        w_qkv_grad, *norm_grads = finish_first(first_own, first_parts)
         norm_grads = [grad.reshape(share) for grad in norm_grads]
     else:
         first_sum = lax.psum_scatter(grads[0], ("dp", "seq"), scatter_dimension=0, tiled=True)

time: 121 us -> 120 us (level)
  transfers between devices with their start and end apart: 36 -> 36, of which waited for: 13 -> 16; matrix products, arithmetic and copies ran while one was open for 0% -> 0% of each run, Pallas kernels for 31% -> 31%
where the time goes in v7:
time: 120 us
  Pallas kernels  51.5 us (43%)
  starting transfers between devices  39.2 us (33%)
  waiting for transfers between devices  15.2 us (13%)
  blocking collectives  12.4 us (10%)
    pallas_call x8, Pallas kernels, run_kernel(): pl.pallas_call(body, out_shape=out_shape, in_specs=[SMEM] + specs, out_sp...  48 us
    ppermute x36, starting transfers between devices, swap(): lax.ppermute(array, axis, [(i, i ^ bit) for i in range(lax.axis_size(axis...  39.2 us
    ppermute x36, waiting for transfers between devices, swap(): lax.ppermute(array, axis, [(i, i ^ bit) for i in range(lax.axis_size(axis...  15.2 us
    all_gather x1, blocking collectives, per_device(): first_half = lax.all_gather(column, 'dp', axis_index_groups=CHIPS)  12.4 us
  transfers between devices with their start and end apart: 36, of which 16 were waited for; matrix products, arithmetic and copies ran while one was open for 0% of the time, Pallas kernels for 31%

profile of v7, /device:TPU:0, one launch (start us, length us, event | category | flops | bytes accessed | tf_op | source)
XLA Modules:
  0.0 119.7 jit_solution(15605450794635168864)
XLA Ops:
  0.7 1.6 %shard_map.195 = (bf16[16,3200]{1,0:T(8,128)(2,1)S(1)}, bf16[16,2176]{1,0:T(8,128)(2,1)S(1)}, bf16[16,3200]{1,0:T(8,128)(2,1)S(1)}, bf16[208,512]{1,0:T(8,128)(2...) custom-call(bf16[704,512]{1,0:T(8,128)(2,1)} %rows.2, bf16[704,512]{1,0:T(8,128)(2,1)} %rows.3, ...), custom_call_target="tpu_custom_call" | custom-call | tf_op jit(solution)/shard_map/pallas_call | solution.py:733
  2.3 3.0 %collective-permute-start.1 = (bf16[208,512]{1,0:T(8,128)(2,1)S(1)}, bf16[208,512]{1,0:T(8,128)(2,1)S(1)}, u32[]{:S(2)}, u32[]{:S(2)}) collective-permute-start(bf16[208,512]{1,0:T(8,128)(2,1)S(1)} %get-tuple-element.135), channel_id=1, source_target_pairs={{0,16},{4,20},{8,24},{12,28},{16,0},{20,4},{24,8},{28,12},{1,17},{... | collective-permute-start | bytes 638984 | tf_op jit(solution)/shard_map/ppermute | solution.py:662
  5.3 1.5 %collective-permute-start = (bf16[208,512]{1,0:T(8,128)(2,1)S(1)}, bf16[208,512]{1,0:T(8,128)(2,1)S(1)}, u32[]{:S(2)}, u32[]{:S(2)}) collective-permute-start(bf16[208,512]{1,0:T(8,128)(2,1)S(1)} %get-tuple-element.135), channel_id=1, source_target_pairs={{0,8},{4,12},{8,0},{12,4},{16,24},{20,28},{24,16},{28,20},{1,9},{5... | collective-permute-start | bytes 638984 | tf_op jit(solution)/shard_map/ppermute | solution.py:662
  6.8 2.6 %collective-permute-start.3 = (bf16[16,2176]{1,0:T(8,128)(2,1)S(1)}, bf16[16,2176]{1,0:T(8,128)(2,1)S(1)}, u32[]{:S(2)}, u32[]{:S(2)}) collective-permute-start(bf16[16,2176]{1,0:T(8,128)(2,1)S(1)} %get-tuple-element.124), channel_id=1, source_target_pairs={{0,2},{1,3},{2,0},{3,1},{4,6},{5,7},{6,4},{7,5},{8,10},{9,11},{10,... | collective-permute-start | bytes 208904 | tf_op jit(solution)/shard_map/ppermute | solution.py:662
  9.4 1.6 %collective-permute-start.2 = (bf16[16,3200]{1,0:T(8,128)(2,1)S(1)}, bf16[16,3200]{1,0:T(8,128)(2,1)S(1)}, u32[]{:S(2)}, u32[]{:S(2)}) collective-permute-start(bf16[16,3200]{1,0:T(8,128)(2,1)S(1)} %get-tuple-element.123), channel_id=1, source_target_pairs={{0,1},{1,0},{2,3},{3,2},{4,5},{5,4},{6,7},{7,6},{8,9},{9,8},{10,11... | collective-permute-start | bytes 307208 | tf_op jit(solution)/shard_map/ppermute | solution.py:662
  11.5 2.9 %shard_map.196 = (bf16[768,512]{1,0:T(8,128)(2,1)S(1)}, bf16[768,512]{1,0:T(8,128)(2,1)S(1)}, bf16[768,512]{1,0:T(8,128)(2,1)S(1)}, f32[768,128]{1,0:T(8,128)S(1)}) custom-call(s32[11]{0:T(128)S(1)} %pad_add_fusion.info, bf16[704,512]{1,0:T(8,128)(2,1)S(1)} %copy-done, bf16[704,512]{1,0:T(8,128)(2,1)S(1)} %copy-done.1), custom_call_target="tpu_custom_call" | custom-call | flops 402653184 | bytes 1441792 | tf_op jit(solution)/shard_map/pallas_call | solution.py:648
  14.4 3.1 %collective-permute-done.4.far = bf16[16,3200]{1,0:T(8,128)(2,1)S(1)} collective-permute-done((bf16[16,3200]{1,0:T(8,128)(2,1)S(1)}, bf16[16,3200]{1,0:T(8,128)(2,1)S(1)}, u32[]{:S(2)}, u32[]{:S(2)}) %collective-permute-start.4) | collective-permute-done | bytes 102432 | tf_op jit(solution)/shard_map/ppermute | solution.py:662
  18.7 2.9 %collective-permute-start.8 = (bf16[160,512]{1,0:T(8,128)(2,1)S(1)}, bf16[160,512]{1,0:T(8,128)(2,1)S(1)}, u32[]{:S(2)}, u32[]{:S(2)}) collective-permute-start(bf16[160,512]{1,0:T(8,128)(2,1)S(1)} %get-tuple-element.137), channel_id=1, source_target_pairs={{0,3},{1,2},{2,1},{3,0},{4,7},{5,6},{6,5},{7,4},{8,11},{9,10},{10,... | collective-permute-start | bytes 491528 | tf_op jit(solution)/shard_map/ppermute | solution.py:662
  21.7 12.4 %all-gather = bf16[12,16,2176]{2,1,0:T(8,128)(2,1)S(1)} all-gather(bf16[3,16,2176]{2,1,0:T(8,128)(2,1)S(1)} %pad_maximum_fusion.2), channel_id=2, replica_groups={{0,8,16,24},{4,12,20,28},{1,9,17,25},{5,13,21,29},{2,10,18,26},{6,14,22..., dimensions={0}, use_global_device_ids=true | all-gather | bytes 1044480 | tf_op jit(solution)/shard_map/all_gather | solution.py:771
  36.4 1.6 %collective-permute-start.12 = (bf16[3,128,512]{2,1,0:T(8,128)(2,1)S(1)}, bf16[3,128,512]{2,1,0:T(8,128)(2,1)S(1)}, u32[]{:S(2)}, u32[]{:S(2)}) collective-permute-start(bf16[3,128,512]{2,1,0:T(8,128)(2,1)S(1)} %pad_maximum_fusion.1.refs_0_), channel_id=1, source_target_pairs={{0,16},{4,20},{8,24},{12,28},{16,0},{20,4},{24,8},{28,12},{1,17},{... | collective-permute-start | bytes 1179656 | tf_op jit(solution)/shard_map/ppermute | solution.py:662
  38.0 1.5 %collective-permute-start.11 = (bf16[3,128,512]{2,1,0:T(8,128)(2,1)S(1)}, bf16[3,128,512]{2,1,0:T(8,128)(2,1)S(1)}, u32[]{:S(2)}, u32[]{:S(2)}) collective-permute-start(bf16[3,128,512]{2,1,0:T(8,128)(2,1)S(1)} %pad_maximum_fusion.1.refs_0_), channel_id=1, source_target_pairs={{0,8},{4,12},{8,0},{12,4},{16,24},{20,28},{24,16},{28,20},{1,9},{5... | collective-permute-start | bytes 1179656 | tf_op jit(solution)/shard_map/ppermute | solution.py:662
  39.5 9.9 %shard_map.197 = (bf16[768,512]{1,0:T(8,128)(2,1)S(1)}, bf16[768,1536]{1,0:T(8,128)(2,1)S(1)}, bf16[768,512]{1,0:T(8,128)(2,1)S(1)}, bf16[768,512]{1,0:T(8,128)(...) custom-call(s32[11]{0:T(128)S(1)} %pad_add_fusion.info, bf16[704,512]{1,0:T(8,128)(2,1)S(1)} %copy-done, ...), custom_call_target="tpu_custom_call" | custom-call | flops 2415919104 | bytes 5087232 | tf_op jit(solution)/shard_map/pallas_call | solution.py:648
  49.4 5.8 %shard_map.198 = (f32[768,512]{1,0:T(8,128)S(1)}, f32[768,512]{1,0:T(8,128)S(1)}, f32[768,512]{1,0:T(8,128)S(1)}, bf16[768,512]{1,0:T(8,128)(2,1)S(1)}, bf16[768...) custom-call(s32[11]{0:T(128)S(1)} %pad_add_fusion.info, ...), custom_call_target="tpu_custom_call" | custom-call | flops 2818572288 | bytes 8536064 | tf_op jit(solution)/shard_map/pallas_call | solution.py:648
  58.7 11.4 %shard_map.199 = (f32[768,512]{1,0:T(8,128)S(1)}, f32[768,512]{1,0:T(8,128)S(1)}, bf16[4,384,512]{2,1,0:T(8,128)(2,1)S(1)}, bf16[4,384,512]{2,1,0:T(8,128)(2,1)S(1)}) custom-call(s32[11]{0:T(128)S(1)} %pad_add_fusion.info, f32[768,512]{1,0:T(8,128)S(1)} %get-tuple-element.159.total_in, f32[768,512]{1,0:T(8,128)S(1)} %get-tuple-element.160.grad_in, ...), custom_call_target="tpu_custom_call" | custom-call | flops 7247757312 | bytes 9437184 | tf_op jit(solution)/shard_map/pallas_call | solution.py:648
  70.7 2.5 %shard_map.200 = (f32[768,512]{1,0:T(8,128)S(1)}, bf16[768,512]{1,0:T(8,128)(2,1)S(1)}, f32[8,512]{1,0:T(8,128)S(1)}, bf16[4,64,512]{2,1,0:T(8,128)(2,1)S(1)}, bf16[4,64,512]{2,1,0:T(8,128)(2,1)S(1)}) custom-call(s32[11]{0:T(128)S(1)} %pad_add_fusion.info, f32[768,512]{1,0:T(8,128)S(1)} %get-tuple-element.169.middle, ...), custom_call_target="tpu_custom_call" | custom-call | flops 805306368 | bytes 7356416 | tf_op jit(solution)/shard_map/pallas_call | solution.py:648
  75.4 1.6 %collective-permute-start.24 = (bf16[4,144,512]{2,1,0:T(8,128)(2,1)S(1)}, bf16[4,144,512]{2,1,0:T(8,128)(2,1)S(1)}, u32[]{:S(2)}, u32[]{:S(2)}) collective-permute-start(bf16[4,144,512]{2,1,0:T(8,128)(2,1)S(1)} %get-tuple-element.191), channel_id=1, source_target_pairs={{0,1},{1,0},{2,3},{3,2},{4,5},{5,4},{6,7},{7,6},{8,9},{9,8},{10,11... | collective-permute-start | bytes 1769480 | tf_op jit(solution)/shard_map/ppermute | solution.py:662
  78.9 1.5 %collective-permute-start.23 = (bf16[288,512]{1,0:T(8,128)(2,1)S(1)}, bf16[288,512]{1,0:T(8,128)(2,1)S(1)}, u32[]{:S(2)}, u32[]{:S(2)}) collective-permute-start(bf16[288,512]{1,0:T(8,128)(2,1)S(1)} %get-tuple-element.190), channel_id=1, source_target_pairs={{0,24},{4,28},{8,16},{12,20},{16,8},{20,12},{24,0},{28,4},{1,25},{... | collective-permute-start | bytes 884744 | tf_op jit(solution)/shard_map/ppermute | solution.py:662
  80.4 11.3 %shard_map.202 = (f32[768,512]{1,0:T(8,128)S(1)}, bf16[4,4,16,1664]{3,2,1,0:T(8,128)(2,1)S(1)}, bf16[4,4,16,1664]{3,2,1,0:T(8,128)(2,1)S(1)}) custom-call(s32[11]{0:T(128)S(1)} %pad_add_fusion.info, bf16[768,512]{1,0:T(8,128)(2,1)S(1)} %get-tuple-element.147.x_in, f32[768,128]{1,0:T(8,128)S(1)} %get-tuple-element.148.own, ...), custom_call_target="tpu_custom_call" | custom-call | flops 3623878656 | bytes 8945664 | tf_op jit(solution)/shard_map/pallas_call | solution.py:648
  97.6 1.5 %collective-permute-start.28 = (bf16[4,16,1664]{2,1,0:T(8,128)(2,1)S(1)}, bf16[4,16,1664]{2,1,0:T(8,128)(2,1)S(1)}, u32[]{:S(2)}, u32[]{:S(2)}) collective-permute-start(bf16[4,16,1664]{2,1,0:T(8,128)(2,1)S(1)} %get-tuple-element.196), channel_id=1, source_target_pairs={{0,24},{4,28},{8,16},{12,20},{16,8},{20,12},{24,0},{28,4},{1,25},{... | collective-permute-start | bytes 638984 | tf_op jit(solution)/shard_map/ppermute | solution.py:662
  99.5 2.9 %collective-permute-start.30 = (bf16[144,512]{1,0:T(8,128)(2,1)S(1)}, bf16[144,512]{1,0:T(8,128)(2,1)S(1)}, u32[]{:S(2)}, u32[]{:S(2)}) collective-permute-start(bf16[144,512]{1,0:T(8,128)(2,1)S(1)} %shard_map.205), channel_id=1, source_target_pairs={{0,3},{1,2},{2,1},{3,0},{4,7},{5,6},{6,5},{7,4},{8,11},{9,10},{10,... | collective-permute-start | bytes 442376 | tf_op jit(solution)/shard_map/ppermute | solution.py:662
  102.4 2.1 %shard_map.207 = bf16[704,512]{1,0:T(8,128)(2,1)} custom-call(s32[11]{0:T(128)S(1)} %pad_add_fusion.info, f32[768,512]{1,0:T(8,128)S(1)} %get-tuple-element.210.values), custom_call_target="tpu_custom_call" | custom-call | flops 402653184 | bytes 1572864 | tf_op jit(solution)/shard_map/pallas_call | solution.py:648
  104.5 2.1 %shard_map.208 = bf16[704,512]{1,0:T(8,128)(2,1)} custom-call(s32[11]{0:T(128)S(1)} %pad_add_fusion.info, f32[768,512]{1,0:T(8,128)S(1)} %get-tuple-element.211.values), custom_call_target="tpu_custom_call" | custom-call | flops 402653184 | bytes 1572864 | tf_op jit(solution)/shard_map/pallas_call | solution.py:648
  112.9 2.9 %collective-permute-start.35 = (bf16[16,1664]{1,0:T(8,128)(2,1)S(1)}, bf16[16,1664]{1,0:T(8,128)(2,1)S(1)}, u32[]{:S(2)}, u32[]{:S(2)}) collective-permute-start(bf16[16,1664]{1,0:T(8,128)(2,1)S(1)} %shard_map.210), channel_id=1, source_target_pairs={{0,3},{1,2},{2,1},{3,0},{4,7},{5,6},{6,5},{7,4},{8,11},{9,10},{10,... | collective-permute-start | bytes 159752 | tf_op jit(solution)/shard_map/ppermute | solution.py:662
  115.8 1.8 %collective-permute-done.32.two = bf16[144,512]{1,0:T(8,128)(2,1)S(1)} collective-permute-done((bf16[144,512]{1,0:T(8,128)(2,1)S(1)}, bf16[144,512]{1,0:T(8,128)(2,1)S(1)}, u32[]{:S(2)}, u32[]{:S(2)}) %collective-permute-start.32) | collective-permute-done | bytes 147488 | tf_op jit(solution)/shard_map/ppermute | solution.py:662
  (84 shorter events, 26.7 us)
Async XLA Ops:
  2.3 15.3 %collective-permute-start.1 = (bf16[208,512]{1,0:T(8,128)(2,1)S(1)}, bf16[208,512]{1,0:T(8,128)(2,1)S(1)}, u32[]{:S(2)}, u32[]{:S(2)}) collective-permute-start(bf16[208,512]{1,0:T(8,128)(2,1)S(1)} %get-tuple-element.135), channel_id=1, source_target_pairs={{0,16},{4,20},{8,24},{12,28},{16,0},{20,4},{24,8},{28,12},{1,17},{... | collective-permute-start | bytes 638984 | tf_op jit(solution)/shard_map/ppermute | solution.py:662
  5.3 12.2 %collective-permute-start = (bf16[208,512]{1,0:T(8,128)(2,1)S(1)}, bf16[208,512]{1,0:T(8,128)(2,1)S(1)}, u32[]{:S(2)}, u32[]{:S(2)}) collective-permute-start(bf16[208,512]{1,0:T(8,128)(2,1)S(1)} %get-tuple-element.135), channel_id=1, source_target_pairs={{0,8},{4,12},{8,0},{12,4},{16,24},{20,28},{24,16},{28,20},{1,9},{5... | collective-permute-start | bytes 638984 | tf_op jit(solution)/shard_map/ppermute | solution.py:662
  6.8 7.6 %collective-permute-start.3 = (bf16[16,2176]{1,0:T(8,128)(2,1)S(1)}, bf16[16,2176]{1,0:T(8,128)(2,1)S(1)}, u32[]{:S(2)}, u32[]{:S(2)}) collective-permute-start(bf16[16,2176]{1,0:T(8,128)(2,1)S(1)} %get-tuple-element.124), channel_id=1, source_target_pairs={{0,2},{1,3},{2,0},{3,1},{4,6},{5,7},{6,4},{7,5},{8,10},{9,11},{10,... | collective-permute-start | bytes 208904 | tf_op jit(solution)/shard_map/ppermute | solution.py:662
  11.0 6.6 %collective-permute-start.4 = (bf16[16,3200]{1,0:T(8,128)(2,1)S(1)}, bf16[16,3200]{1,0:T(8,128)(2,1)S(1)}, u32[]{:S(2)}, u32[]{:S(2)}) collective-permute-start(bf16[16,3200]{1,0:T(8,128)(2,1)S(1)} %get-tuple-element.125), channel_id=1, source_target_pairs={{0,3},{1,2},{2,1},{3,0},{4,7},{5,6},{6,5},{7,4},{8,11},{9,10},{10,... | collective-permute-start | bytes 307208 | tf_op jit(solution)/shard_map/ppermute | solution.py:662
  17.6 16.6 %collective-permute-start.5 = (bf16[208,512]{1,0:T(8,128)(2,1)S(1)}, bf16[208,512]{1,0:T(8,128)(2,1)S(1)}, u32[]{:S(2)}, u32[]{:S(2)}) collective-permute-start(bf16[208,512]{1,0:T(8,128)(2,1)S(1)} %get-tuple-element.135), channel_id=1, source_target_pairs={{0,24},{4,28},{8,16},{12,20},{16,8},{20,12},{24,0},{28,4},{1,25},{... | collective-permute-start | bytes 638984 | tf_op jit(solution)/shard_map/ppermute | solution.py:662
  18.1 16.0 %collective-permute-start.6 = (bf16[160,512]{1,0:T(8,128)(2,1)S(1)}, bf16[160,512]{1,0:T(8,128)(2,1)S(1)}, u32[]{:S(2)}, u32[]{:S(2)}) collective-permute-start(bf16[160,512]{1,0:T(8,128)(2,1)S(1)} %get-tuple-element.136), channel_id=1, source_target_pairs={{0,1},{1,0},{2,3},{3,2},{4,5},{5,4},{6,7},{7,6},{8,9},{9,8},{10,11... | collective-permute-start | bytes 491528 | tf_op jit(solution)/shard_map/ppermute | solution.py:662
  18.7 15.4 %collective-permute-start.8 = (bf16[160,512]{1,0:T(8,128)(2,1)S(1)}, bf16[160,512]{1,0:T(8,128)(2,1)S(1)}, u32[]{:S(2)}, u32[]{:S(2)}) collective-permute-start(bf16[160,512]{1,0:T(8,128)(2,1)S(1)} %get-tuple-element.137), channel_id=1, source_target_pairs={{0,3},{1,2},{2,1},{3,0},{4,7},{5,6},{6,5},{7,4},{8,11},{9,10},{10,... | collective-permute-start | bytes 491528 | tf_op jit(solution)/shard_map/ppermute | solution.py:662
  21.6 12.5 %collective-permute-start.7 = (bf16[128,512]{1,0:T(8,128)(2,1)S(1)}, bf16[128,512]{1,0:T(8,128)(2,1)S(1)}, u32[]{:S(2)}, u32[]{:S(2)}) collective-permute-start(bf16[128,512]{1,0:T(8,128)(2,1)S(1)} %slice.17), channel_id=1, source_target_pairs={{0,2},{1,3},{2,0},{3,1},{4,6},{5,7},{6,4},{7,5},{8,10},{9,11},{10,... | collective-permute-start | bytes 393224 | tf_op jit(solution)/shard_map/ppermute | solution.py:662
  34.9 21.5 %collective-permute-start.14 = (bf16[3,128,512]{2,1,0:T(8,128)(2,1)S(1)}, bf16[3,128,512]{2,1,0:T(8,128)(2,1)S(1)}, u32[]{:S(2)}, u32[]{:S(2)}) collective-permute-start(bf16[3,128,512]{2,1,0:T(8,128)(2,1)S(1)} %pad_maximum_fusion.1.refs_0_), channel_id=1, source_target_pairs={{0,4},{4,0},{8,12},{12,8},{16,20},{20,16},{24,28},{28,24},{1,5},{5... | collective-permute-start | bytes 1179656 | tf_op jit(solution)/shard_map/ppermute | solution.py:662
  35.0 20.2 %collective-permute-start.13 = (bf16[3,128,512]{2,1,0:T(8,128)(2,1)S(1)}, bf16[3,128,512]{2,1,0:T(8,128)(2,1)S(1)}, u32[]{:S(2)}, u32[]{:S(2)}) collective-permute-start(bf16[3,128,512]{2,1,0:T(8,128)(2,1)S(1)} %pad_maximum_fusion.1.refs_0_), channel_id=1, source_target_pairs={{0,24},{4,28},{8,16},{12,20},{16,8},{20,12},{24,0},{28,4},{1,25},{... | collective-permute-start | bytes 1179656 | tf_op jit(solution)/shard_map/ppermute | solution.py:662
  36.4 19.4 %collective-permute-start.12 = (bf16[3,128,512]{2,1,0:T(8,128)(2,1)S(1)}, bf16[3,128,512]{2,1,0:T(8,128)(2,1)S(1)}, u32[]{:S(2)}, u32[]{:S(2)}) collective-permute-start(bf16[3,128,512]{2,1,0:T(8,128)(2,1)S(1)} %pad_maximum_fusion.1.refs_0_), channel_id=1, source_target_pairs={{0,16},{4,20},{8,24},{12,28},{16,0},{20,4},{24,8},{28,12},{1,17},{... | collective-permute-start | bytes 1179656 | tf_op jit(solution)/shard_map/ppermute | solution.py:662
  38.0 17.9 %collective-permute-start.11 = (bf16[3,128,512]{2,1,0:T(8,128)(2,1)S(1)}, bf16[3,128,512]{2,1,0:T(8,128)(2,1)S(1)}, u32[]{:S(2)}, u32[]{:S(2)}) collective-permute-start(bf16[3,128,512]{2,1,0:T(8,128)(2,1)S(1)} %pad_maximum_fusion.1.refs_0_), channel_id=1, source_target_pairs={{0,8},{4,12},{8,0},{12,4},{16,24},{20,28},{24,16},{28,20},{1,9},{5... | collective-permute-start | bytes 1179656 | tf_op jit(solution)/shard_map/ppermute | solution.py:662
  75.4 17.6 %collective-permute-start.24 = (bf16[4,144,512]{2,1,0:T(8,128)(2,1)S(1)}, bf16[4,144,512]{2,1,0:T(8,128)(2,1)S(1)}, u32[]{:S(2)}, u32[]{:S(2)}) collective-permute-start(bf16[4,144,512]{2,1,0:T(8,128)(2,1)S(1)} %get-tuple-element.191), channel_id=1, source_target_pairs={{0,1},{1,0},{2,3},{3,2},{4,5},{5,4},{6,7},{7,6},{8,9},{9,8},{10,11... | collective-permute-start | bytes 1769480 | tf_op jit(solution)/shard_map/ppermute | solution.py:662
  77.0 14.8 %collective-permute-start.21 = (bf16[288,512]{1,0:T(8,128)(2,1)S(1)}, bf16[288,512]{1,0:T(8,128)(2,1)S(1)}, u32[]{:S(2)}, u32[]{:S(2)}) collective-permute-start(bf16[288,512]{1,0:T(8,128)(2,1)S(1)} %get-tuple-element.188), channel_id=1, source_target_pairs={{0,8},{4,12},{8,0},{12,4},{16,24},{20,28},{24,16},{28,20},{1,9},{5... | collective-permute-start | bytes 884744 | tf_op jit(solution)/shard_map/ppermute | solution.py:662
  78.1 14.8 %collective-permute-start.22 = (bf16[288,512]{1,0:T(8,128)(2,1)S(1)}, bf16[288,512]{1,0:T(8,128)(2,1)S(1)}, u32[]{:S(2)}, u32[]{:S(2)}) collective-permute-start(bf16[288,512]{1,0:T(8,128)(2,1)S(1)} %get-tuple-element.189), channel_id=1, source_target_pairs={{0,16},{4,20},{8,24},{12,28},{16,0},{20,4},{24,8},{28,12},{1,17},{... | collective-permute-start | bytes 884744 | tf_op jit(solution)/shard_map/ppermute | solution.py:662
  78.9 14.1 %collective-permute-start.23 = (bf16[288,512]{1,0:T(8,128)(2,1)S(1)}, bf16[288,512]{1,0:T(8,128)(2,1)S(1)}, u32[]{:S(2)}, u32[]{:S(2)}) collective-permute-start(bf16[288,512]{1,0:T(8,128)(2,1)S(1)} %get-tuple-element.190), channel_id=1, source_target_pairs={{0,24},{4,28},{8,16},{12,20},{16,8},{20,12},{24,0},{28,4},{1,25},{... | collective-permute-start | bytes 884744 | tf_op jit(solution)/shard_map/ppermute | solution.py:662
  93.1 6.3 %collective-permute-start.29 = (bf16[144,512]{1,0:T(8,128)(2,1)S(1)}, bf16[144,512]{1,0:T(8,128)(2,1)S(1)}, u32[]{:S(2)}, u32[]{:S(2)}) collective-permute-start(bf16[144,512]{1,0:T(8,128)(2,1)S(1)} %get-tuple-element.202), channel_id=1, source_target_pairs={{0,1},{1,0},{2,3},{3,2},{4,5},{5,4},{6,7},{7,6},{8,9},{9,8},{10,11... | collective-permute-start | bytes 442376 | tf_op jit(solution)/shard_map/ppermute | solution.py:662
  95.5 11.4 %collective-permute-start.26 = (bf16[4,16,1664]{2,1,0:T(8,128)(2,1)S(1)}, bf16[4,16,1664]{2,1,0:T(8,128)(2,1)S(1)}, u32[]{:S(2)}, u32[]{:S(2)}) collective-permute-start(bf16[4,16,1664]{2,1,0:T(8,128)(2,1)S(1)} %get-tuple-element.194), channel_id=1, source_target_pairs={{0,8},{4,12},{8,0},{12,4},{16,24},{20,28},{24,16},{28,20},{1,9},{5... | collective-permute-start | bytes 638984 | tf_op jit(solution)/shard_map/ppermute | solution.py:662
  96.4 11.6 %collective-permute-start.27 = (bf16[4,16,1664]{2,1,0:T(8,128)(2,1)S(1)}, bf16[4,16,1664]{2,1,0:T(8,128)(2,1)S(1)}, u32[]{:S(2)}, u32[]{:S(2)}) collective-permute-start(bf16[4,16,1664]{2,1,0:T(8,128)(2,1)S(1)} %get-tuple-element.195), channel_id=1, source_target_pairs={{0,16},{4,20},{8,24},{12,28},{16,0},{20,4},{24,8},{28,12},{1,17},{... | collective-permute-start | bytes 638984 | tf_op jit(solution)/shard_map/ppermute | solution.py:662
  97.6 10.4 %collective-permute-start.28 = (bf16[4,16,1664]{2,1,0:T(8,128)(2,1)S(1)}, bf16[4,16,1664]{2,1,0:T(8,128)(2,1)S(1)}, u32[]{:S(2)}, u32[]{:S(2)}) collective-permute-start(bf16[4,16,1664]{2,1,0:T(8,128)(2,1)S(1)} %get-tuple-element.196), channel_id=1, source_target_pairs={{0,24},{4,28},{8,16},{12,20},{16,8},{20,12},{24,0},{28,4},{1,25},{... | collective-permute-start | bytes 638984 | tf_op jit(solution)/shard_map/ppermute | solution.py:662
  99.5 7.4 %collective-permute-start.30 = (bf16[144,512]{1,0:T(8,128)(2,1)S(1)}, bf16[144,512]{1,0:T(8,128)(2,1)S(1)}, u32[]{:S(2)}, u32[]{:S(2)}) collective-permute-start(bf16[144,512]{1,0:T(8,128)(2,1)S(1)} %shard_map.205), channel_id=1, source_target_pairs={{0,3},{1,2},{2,1},{3,0},{4,7},{5,6},{6,5},{7,4},{8,11},{9,10},{10,... | collective-permute-start | bytes 442376 | tf_op jit(solution)/shard_map/ppermute | solution.py:662
  109.1 6.7 %collective-permute-start.31 = (bf16[144,512]{1,0:T(8,128)(2,1)S(1)}, bf16[144,512]{1,0:T(8,128)(2,1)S(1)}, u32[]{:S(2)}, u32[]{:S(2)}) collective-permute-start(bf16[144,512]{1,0:T(8,128)(2,1)S(1)} %get-tuple-element.220), channel_id=1, source_target_pairs={{0,8},{4,12},{8,0},{12,4},{16,24},{20,28},{24,16},{28,20},{1,9},{5... | collective-permute-start | bytes 442376 | tf_op jit(solution)/shard_map/ppermute | solution.py:662
  110.2 7.5 %collective-permute-start.32 = (bf16[144,512]{1,0:T(8,128)(2,1)S(1)}, bf16[144,512]{1,0:T(8,128)(2,1)S(1)}, u32[]{:S(2)}, u32[]{:S(2)}) collective-permute-start(bf16[144,512]{1,0:T(8,128)(2,1)S(1)} %get-tuple-element.221), channel_id=1, source_target_pairs={{0,16},{4,20},{8,24},{12,28},{16,0},{20,4},{24,8},{28,12},{1,17},{... | collective-permute-start | bytes 442376 | tf_op jit(solution)/shard_map/ppermute | solution.py:662
  111.1 6.5 %collective-permute-start.33 = (bf16[144,512]{1,0:T(8,128)(2,1)S(1)}, bf16[144,512]{1,0:T(8,128)(2,1)S(1)}, u32[]{:S(2)}, u32[]{:S(2)}) collective-permute-start(bf16[144,512]{1,0:T(8,128)(2,1)S(1)} %get-tuple-element.222), channel_id=1, source_target_pairs={{0,24},{4,28},{8,16},{12,20},{16,8},{20,12},{24,0},{28,4},{1,25},{... | collective-permute-start | bytes 442376 | tf_op jit(solution)/shard_map/ppermute | solution.py:662
  (16 other events, 86.4 us)

commit v8 on v7

--- a/solution.py
+++ b/solution.py
@@ -887,7 +887,8 @@
         *second_all,
     )
     if direct:
-        from_core = along_core([first_grads[1], grads[1]])
+        total, *grads, from_first = together(total, *grads, *along_core([first_grads[1]]))
+        from_core = [from_first, *along_core([grads[1]])]
     grad_middle, grad_mixed, grad_norms, *out_grads = run_kernel(
         functools.partial(feed_last_kernel, direct),
         [

time: 120 us -> 120 us (level)
  transfers between devices with their start and end apart: 36 -> 36, of which waited for: 16 -> 15; matrix products, arithmetic and copies ran while one was open for 0% -> 0% of each run, Pallas kernels for 31% -> 41%
where the time goes in v8:
time: 120 us
  Pallas kernels  51.5 us (43%)
  starting transfers between devices  39.6 us (33%)
  waiting for transfers between devices  14.7 us (12%)
  blocking collectives  12.4 us (10%)
    pallas_call x8, Pallas kernels, run_kernel(): pl.pallas_call(body, out_shape=out_shape, in_specs=[SMEM] + specs, out_sp...  48 us
    ppermute x36, starting transfers between devices, swap(): lax.ppermute(array, axis, [(i, i ^ bit) for i in range(lax.axis_size(axis...  39.6 us
    ppermute x36, waiting for transfers between devices, swap(): lax.ppermute(array, axis, [(i, i ^ bit) for i in range(lax.axis_size(axis...  14.7 us
    all_gather x1, blocking collectives, per_device(): first_half = lax.all_gather(column, 'dp', axis_index_groups=CHIPS)  12.4 us
  transfers between devices with their start and end apart: 36, of which 15 were waited for; matrix products, arithmetic and copies ran while one was open for 0% of the time, Pallas kernels for 41%

profile of v8, /device:TPU:0, one launch (start us, length us, event | category | flops | bytes accessed | tf_op | source)
XLA Modules:
  0.0 119.6 jit_solution(14305246808124221580)
XLA Ops:
  0.7 1.6 %shard_map.195 = (bf16[16,3200]{1,0:T(8,128)(2,1)S(1)}, bf16[16,2176]{1,0:T(8,128)(2,1)S(1)}, bf16[16,3200]{1,0:T(8,128)(2,1)S(1)}, bf16[208,512]{1,0:T(8,128)(2...) custom-call(bf16[704,512]{1,0:T(8,128)(2,1)} %rows.2, bf16[704,512]{1,0:T(8,128)(2,1)} %rows.3, ...), custom_call_target="tpu_custom_call" | custom-call | tf_op jit(solution)/shard_map/pallas_call | solution.py:733
  2.3 3.0 %collective-permute-start.1 = (bf16[208,512]{1,0:T(8,128)(2,1)S(1)}, bf16[208,512]{1,0:T(8,128)(2,1)S(1)}, u32[]{:S(2)}, u32[]{:S(2)}) collective-permute-start(bf16[208,512]{1,0:T(8,128)(2,1)S(1)} %get-tuple-element.139), channel_id=1, source_target_pairs={{0,16},{4,20},{8,24},{12,28},{16,0},{20,4},{24,8},{28,12},{1,17},{... | collective-permute-start | bytes 638984 | tf_op jit(solution)/shard_map/ppermute | solution.py:662
  5.3 1.5 %collective-permute-start = (bf16[208,512]{1,0:T(8,128)(2,1)S(1)}, bf16[208,512]{1,0:T(8,128)(2,1)S(1)}, u32[]{:S(2)}, u32[]{:S(2)}) collective-permute-start(bf16[208,512]{1,0:T(8,128)(2,1)S(1)} %get-tuple-element.139), channel_id=1, source_target_pairs={{0,8},{4,12},{8,0},{12,4},{16,24},{20,28},{24,16},{28,20},{1,9},{5... | collective-permute-start | bytes 638984 | tf_op jit(solution)/shard_map/ppermute | solution.py:662
  6.8 2.6 %collective-permute-start.3 = (bf16[16,2176]{1,0:T(8,128)(2,1)S(1)}, bf16[16,2176]{1,0:T(8,128)(2,1)S(1)}, u32[]{:S(2)}, u32[]{:S(2)}) collective-permute-start(bf16[16,2176]{1,0:T(8,128)(2,1)S(1)} %get-tuple-element.128), channel_id=1, source_target_pairs={{0,2},{1,3},{2,0},{3,1},{4,6},{5,7},{6,4},{7,5},{8,10},{9,11},{10,... | collective-permute-start | bytes 208904 | tf_op jit(solution)/shard_map/ppermute | solution.py:662
  9.4 1.6 %collective-permute-start.2 = (bf16[16,3200]{1,0:T(8,128)(2,1)S(1)}, bf16[16,3200]{1,0:T(8,128)(2,1)S(1)}, u32[]{:S(2)}, u32[]{:S(2)}) collective-permute-start(bf16[16,3200]{1,0:T(8,128)(2,1)S(1)} %get-tuple-element.127), channel_id=1, source_target_pairs={{0,1},{1,0},{2,3},{3,2},{4,5},{5,4},{6,7},{7,6},{8,9},{9,8},{10,11... | collective-permute-start | bytes 307208 | tf_op jit(solution)/shard_map/ppermute | solution.py:662
  11.5 2.9 %shard_map.196 = (bf16[768,512]{1,0:T(8,128)(2,1)S(1)}, bf16[768,512]{1,0:T(8,128)(2,1)S(1)}, bf16[768,512]{1,0:T(8,128)(2,1)S(1)}, f32[768,128]{1,0:T(8,128)S(1)}) custom-call(s32[11]{0:T(128)S(1)} %pad_add_fusion.info, bf16[704,512]{1,0:T(8,128)(2,1)S(1)} %copy-done, bf16[704,512]{1,0:T(8,128)(2,1)S(1)} %copy-done.1), custom_call_target="tpu_custom_call" | custom-call | flops 402653184 | bytes 1441792 | tf_op jit(solution)/shard_map/pallas_call | solution.py:648
  14.4 3.1 %collective-permute-done.4.far = bf16[16,3200]{1,0:T(8,128)(2,1)S(1)} collective-permute-done((bf16[16,3200]{1,0:T(8,128)(2,1)S(1)}, bf16[16,3200]{1,0:T(8,128)(2,1)S(1)}, u32[]{:S(2)}, u32[]{:S(2)}) %collective-permute-start.4) | collective-permute-done | bytes 102432 | tf_op jit(solution)/shard_map/ppermute | solution.py:662
  18.7 2.9 %collective-permute-start.8 = (bf16[160,512]{1,0:T(8,128)(2,1)S(1)}, bf16[160,512]{1,0:T(8,128)(2,1)S(1)}, u32[]{:S(2)}, u32[]{:S(2)}) collective-permute-start(bf16[160,512]{1,0:T(8,128)(2,1)S(1)} %get-tuple-element.141), channel_id=1, source_target_pairs={{0,3},{1,2},{2,1},{3,0},{4,7},{5,6},{6,5},{7,4},{8,11},{9,10},{10,... | collective-permute-start | bytes 491528 | tf_op jit(solution)/shard_map/ppermute | solution.py:662
  21.7 12.4 %all-gather = bf16[12,16,2176]{2,1,0:T(8,128)(2,1)S(1)} all-gather(bf16[3,16,2176]{2,1,0:T(8,128)(2,1)S(1)} %pad_maximum_fusion.2), channel_id=2, replica_groups={{0,8,16,24},{4,12,20,28},{1,9,17,25},{5,13,21,29},{2,10,18,26},{6,14,22..., dimensions={0}, use_global_device_ids=true | all-gather | bytes 1044480 | tf_op jit(solution)/shard_map/all_gather | solution.py:771
  36.4 1.6 %collective-permute-start.12 = (bf16[3,128,512]{2,1,0:T(8,128)(2,1)S(1)}, bf16[3,128,512]{2,1,0:T(8,128)(2,1)S(1)}, u32[]{:S(2)}, u32[]{:S(2)}) collective-permute-start(bf16[3,128,512]{2,1,0:T(8,128)(2,1)S(1)} %pad_maximum_fusion.1.refs_0_), channel_id=1, source_target_pairs={{0,16},{4,20},{8,24},{12,28},{16,0},{20,4},{24,8},{28,12},{1,17},{... | collective-permute-start | bytes 1179656 | tf_op jit(solution)/shard_map/ppermute | solution.py:662
  38.0 1.5 %collective-permute-start.11 = (bf16[3,128,512]{2,1,0:T(8,128)(2,1)S(1)}, bf16[3,128,512]{2,1,0:T(8,128)(2,1)S(1)}, u32[]{:S(2)}, u32[]{:S(2)}) collective-permute-start(bf16[3,128,512]{2,1,0:T(8,128)(2,1)S(1)} %pad_maximum_fusion.1.refs_0_), channel_id=1, source_target_pairs={{0,8},{4,12},{8,0},{12,4},{16,24},{20,28},{24,16},{28,20},{1,9},{5... | collective-permute-start | bytes 1179656 | tf_op jit(solution)/shard_map/ppermute | solution.py:662
  39.5 9.9 %shard_map.197 = (bf16[768,512]{1,0:T(8,128)(2,1)S(1)}, bf16[768,1536]{1,0:T(8,128)(2,1)S(1)}, bf16[768,512]{1,0:T(8,128)(2,1)S(1)}, bf16[768,512]{1,0:T(8,128)(...) custom-call(s32[11]{0:T(128)S(1)} %pad_add_fusion.info, bf16[704,512]{1,0:T(8,128)(2,1)S(1)} %copy-done, ...), custom_call_target="tpu_custom_call" | custom-call | flops 2415919104 | bytes 5087232 | tf_op jit(solution)/shard_map/pallas_call | solution.py:648
  49.4 5.8 %shard_map.198 = (f32[768,512]{1,0:T(8,128)S(1)}, f32[768,512]{1,0:T(8,128)S(1)}, f32[768,512]{1,0:T(8,128)S(1)}, bf16[768,512]{1,0:T(8,128)(2,1)S(1)}, bf16[768...) custom-call(s32[11]{0:T(128)S(1)} %pad_add_fusion.info, ...), custom_call_target="tpu_custom_call" | custom-call | flops 2818572288 | bytes 8536064 | tf_op jit(solution)/shard_map/pallas_call | solution.py:648
  58.7 11.4 %shard_map.199 = (f32[768,512]{1,0:T(8,128)S(1)}, f32[768,512]{1,0:T(8,128)S(1)}, bf16[4,384,512]{2,1,0:T(8,128)(2,1)S(1)}, bf16[4,384,512]{2,1,0:T(8,128)(2,1)S(1)}) custom-call(s32[11]{0:T(128)S(1)} %pad_add_fusion.info, f32[768,512]{1,0:T(8,128)S(1)} %get-tuple-element.163.total_in, f32[768,512]{1,0:T(8,128)S(1)} %get-tuple-element.164.grad_in, ...), custom_call_target="tpu_custom_call" | custom-call | flops 7247757312 | bytes 9437184 | tf_op jit(solution)/shard_map/pallas_call | solution.py:648
  70.4 2.5 %shard_map.200 = (f32[768,512]{1,0:T(8,128)S(1)}, bf16[768,512]{1,0:T(8,128)(2,1)S(1)}, f32[8,512]{1,0:T(8,128)S(1)}, bf16[4,64,512]{2,1,0:T(8,128)(2,1)S(1)}, bf16[4,64,512]{2,1,0:T(8,128)(2,1)S(1)}) custom-call(s32[11]{0:T(128)S(1)} %pad_add_fusion.info, f32[768,512]{1,0:T(8,128)S(1)} %get-tuple-element.177.middle, ...), custom_call_target="tpu_custom_call" | custom-call | flops 805306368 | bytes 7356416 | tf_op jit(solution)/shard_map/pallas_call | solution.py:648
  75.0 1.6 %collective-permute-start.24 = (bf16[4,144,512]{2,1,0:T(8,128)(2,1)S(1)}, bf16[4,144,512]{2,1,0:T(8,128)(2,1)S(1)}, u32[]{:S(2)}, u32[]{:S(2)}) collective-permute-start(bf16[4,144,512]{2,1,0:T(8,128)(2,1)S(1)} %get-tuple-element.199), channel_id=1, source_target_pairs={{0,1},{1,0},{2,3},{3,2},{4,5},{5,4},{6,7},{7,6},{8,9},{9,8},{10,11... | collective-permute-start | bytes 1769480 | tf_op jit(solution)/shard_map/ppermute | solution.py:662
  78.6 1.5 %collective-permute-start.23 = (bf16[288,512]{1,0:T(8,128)(2,1)S(1)}, bf16[288,512]{1,0:T(8,128)(2,1)S(1)}, u32[]{:S(2)}, u32[]{:S(2)}) collective-permute-start(bf16[288,512]{1,0:T(8,128)(2,1)S(1)} %get-tuple-element.198), channel_id=1, source_target_pairs={{0,24},{4,28},{8,16},{12,20},{16,8},{20,12},{24,0},{28,4},{1,25},{... | collective-permute-start | bytes 884744 | tf_op jit(solution)/shard_map/ppermute | solution.py:662
  80.1 11.3 %shard_map.202 = (f32[768,512]{1,0:T(8,128)S(1)}, bf16[4,4,16,1664]{3,2,1,0:T(8,128)(2,1)S(1)}, bf16[4,4,16,1664]{3,2,1,0:T(8,128)(2,1)S(1)}) custom-call(s32[11]{0:T(128)S(1)} %pad_add_fusion.info, bf16[768,512]{1,0:T(8,128)(2,1)S(1)} %get-tuple-element.151.x_in, f32[768,128]{1,0:T(8,128)S(1)} %get-tuple-element.152.own, ...), custom_call_target="tpu_custom_call" | custom-call | flops 3623878656 | bytes 8945664 | tf_op jit(solution)/shard_map/pallas_call | solution.py:648
  97.5 1.5 %collective-permute-start.28 = (bf16[4,16,1664]{2,1,0:T(8,128)(2,1)S(1)}, bf16[4,16,1664]{2,1,0:T(8,128)(2,1)S(1)}, u32[]{:S(2)}, u32[]{:S(2)}) collective-permute-start(bf16[4,16,1664]{2,1,0:T(8,128)(2,1)S(1)} %get-tuple-element.204), channel_id=1, source_target_pairs={{0,24},{4,28},{8,16},{12,20},{16,8},{20,12},{24,0},{28,4},{1,25},{... | collective-permute-start | bytes 638984 | tf_op jit(solution)/shard_map/ppermute | solution.py:662
  99.3 2.9 %collective-permute-start.30 = (bf16[144,512]{1,0:T(8,128)(2,1)S(1)}, bf16[144,512]{1,0:T(8,128)(2,1)S(1)}, u32[]{:S(2)}, u32[]{:S(2)}) collective-permute-start(bf16[144,512]{1,0:T(8,128)(2,1)S(1)} %shard_map.205), channel_id=1, source_target_pairs={{0,3},{1,2},{2,1},{3,0},{4,7},{5,6},{6,5},{7,4},{8,11},{9,10},{10,... | collective-permute-start | bytes 442376 | tf_op jit(solution)/shard_map/ppermute | solution.py:662
  102.3 2.1 %shard_map.207 = bf16[704,512]{1,0:T(8,128)(2,1)} custom-call(s32[11]{0:T(128)S(1)} %pad_add_fusion.info, f32[768,512]{1,0:T(8,128)S(1)} %get-tuple-element.218.values), custom_call_target="tpu_custom_call" | custom-call | flops 402653184 | bytes 1572864 | tf_op jit(solution)/shard_map/pallas_call | solution.py:648
  104.3 2.1 %shard_map.208 = bf16[704,512]{1,0:T(8,128)(2,1)} custom-call(s32[11]{0:T(128)S(1)} %pad_add_fusion.info, f32[768,512]{1,0:T(8,128)S(1)} %get-tuple-element.219.values), custom_call_target="tpu_custom_call" | custom-call | flops 402653184 | bytes 1572864 | tf_op jit(solution)/shard_map/pallas_call | solution.py:648
  112.8 2.9 %collective-permute-start.35 = (bf16[16,1664]{1,0:T(8,128)(2,1)S(1)}, bf16[16,1664]{1,0:T(8,128)(2,1)S(1)}, u32[]{:S(2)}, u32[]{:S(2)}) collective-permute-start(bf16[16,1664]{1,0:T(8,128)(2,1)S(1)} %shard_map.210), channel_id=1, source_target_pairs={{0,3},{1,2},{2,1},{3,0},{4,7},{5,6},{6,5},{7,4},{8,11},{9,10},{10,... | collective-permute-start | bytes 159752 | tf_op jit(solution)/shard_map/ppermute | solution.py:662
  115.7 1.8 %collective-permute-done.32.two = bf16[144,512]{1,0:T(8,128)(2,1)S(1)} collective-permute-done((bf16[144,512]{1,0:T(8,128)(2,1)S(1)}, bf16[144,512]{1,0:T(8,128)(2,1)S(1)}, u32[]{:S(2)}, u32[]{:S(2)}) %collective-permute-start.32) | collective-permute-done | bytes 147488 | tf_op jit(solution)/shard_map/ppermute | solution.py:662
  (84 shorter events, 26.6 us)
Async XLA Ops:
  2.3 15.3 %collective-permute-start.1 = (bf16[208,512]{1,0:T(8,128)(2,1)S(1)}, bf16[208,512]{1,0:T(8,128)(2,1)S(1)}, u32[]{:S(2)}, u32[]{:S(2)}) collective-permute-start(bf16[208,512]{1,0:T(8,128)(2,1)S(1)} %get-tuple-element.139), channel_id=1, source_target_pairs={{0,16},{4,20},{8,24},{12,28},{16,0},{20,4},{24,8},{28,12},{1,17},{... | collective-permute-start | bytes 638984 | tf_op jit(solution)/shard_map/ppermute | solution.py:662
  5.3 12.2 %collective-permute-start = (bf16[208,512]{1,0:T(8,128)(2,1)S(1)}, bf16[208,512]{1,0:T(8,128)(2,1)S(1)}, u32[]{:S(2)}, u32[]{:S(2)}) collective-permute-start(bf16[208,512]{1,0:T(8,128)(2,1)S(1)} %get-tuple-element.139), channel_id=1, source_target_pairs={{0,8},{4,12},{8,0},{12,4},{16,24},{20,28},{24,16},{28,20},{1,9},{5... | collective-permute-start | bytes 638984 | tf_op jit(solution)/shard_map/ppermute | solution.py:662
  6.8 7.6 %collective-permute-start.3 = (bf16[16,2176]{1,0:T(8,128)(2,1)S(1)}, bf16[16,2176]{1,0:T(8,128)(2,1)S(1)}, u32[]{:S(2)}, u32[]{:S(2)}) collective-permute-start(bf16[16,2176]{1,0:T(8,128)(2,1)S(1)} %get-tuple-element.128), channel_id=1, source_target_pairs={{0,2},{1,3},{2,0},{3,1},{4,6},{5,7},{6,4},{7,5},{8,10},{9,11},{10,... | collective-permute-start | bytes 208904 | tf_op jit(solution)/shard_map/ppermute | solution.py:662
  11.0 6.6 %collective-permute-start.4 = (bf16[16,3200]{1,0:T(8,128)(2,1)S(1)}, bf16[16,3200]{1,0:T(8,128)(2,1)S(1)}, u32[]{:S(2)}, u32[]{:S(2)}) collective-permute-start(bf16[16,3200]{1,0:T(8,128)(2,1)S(1)} %get-tuple-element.129), channel_id=1, source_target_pairs={{0,3},{1,2},{2,1},{3,0},{4,7},{5,6},{6,5},{7,4},{8,11},{9,10},{10,... | collective-permute-start | bytes 307208 | tf_op jit(solution)/shard_map/ppermute | solution.py:662
  17.6 16.6 %collective-permute-start.5 = (bf16[208,512]{1,0:T(8,128)(2,1)S(1)}, bf16[208,512]{1,0:T(8,128)(2,1)S(1)}, u32[]{:S(2)}, u32[]{:S(2)}) collective-permute-start(bf16[208,512]{1,0:T(8,128)(2,1)S(1)} %get-tuple-element.139), channel_id=1, source_target_pairs={{0,24},{4,28},{8,16},{12,20},{16,8},{20,12},{24,0},{28,4},{1,25},{... | collective-permute-start | bytes 638984 | tf_op jit(solution)/shard_map/ppermute | solution.py:662
  18.1 16.0 %collective-permute-start.6 = (bf16[160,512]{1,0:T(8,128)(2,1)S(1)}, bf16[160,512]{1,0:T(8,128)(2,1)S(1)}, u32[]{:S(2)}, u32[]{:S(2)}) collective-permute-start(bf16[160,512]{1,0:T(8,128)(2,1)S(1)} %get-tuple-element.140), channel_id=1, source_target_pairs={{0,1},{1,0},{2,3},{3,2},{4,5},{5,4},{6,7},{7,6},{8,9},{9,8},{10,11... | collective-permute-start | bytes 491528 | tf_op jit(solution)/shard_map/ppermute | solution.py:662
  18.7 15.4 %collective-permute-start.8 = (bf16[160,512]{1,0:T(8,128)(2,1)S(1)}, bf16[160,512]{1,0:T(8,128)(2,1)S(1)}, u32[]{:S(2)}, u32[]{:S(2)}) collective-permute-start(bf16[160,512]{1,0:T(8,128)(2,1)S(1)} %get-tuple-element.141), channel_id=1, source_target_pairs={{0,3},{1,2},{2,1},{3,0},{4,7},{5,6},{6,5},{7,4},{8,11},{9,10},{10,... | collective-permute-start | bytes 491528 | tf_op jit(solution)/shard_map/ppermute | solution.py:662
  21.6 12.5 %collective-permute-start.7 = (bf16[128,512]{1,0:T(8,128)(2,1)S(1)}, bf16[128,512]{1,0:T(8,128)(2,1)S(1)}, u32[]{:S(2)}, u32[]{:S(2)}) collective-permute-start(bf16[128,512]{1,0:T(8,128)(2,1)S(1)} %slice.17), channel_id=1, source_target_pairs={{0,2},{1,3},{2,0},{3,1},{4,6},{5,7},{6,4},{7,5},{8,10},{9,11},{10,... | collective-permute-start | bytes 393224 | tf_op jit(solution)/shard_map/ppermute | solution.py:662
  34.9 22.0 %collective-permute-start.14 = (bf16[3,128,512]{2,1,0:T(8,128)(2,1)S(1)}, bf16[3,128,512]{2,1,0:T(8,128)(2,1)S(1)}, u32[]{:S(2)}, u32[]{:S(2)}) collective-permute-start(bf16[3,128,512]{2,1,0:T(8,128)(2,1)S(1)} %pad_maximum_fusion.1.refs_0_), channel_id=1, source_target_pairs={{0,4},{4,0},{8,12},{12,8},{16,20},{20,16},{24,28},{28,24},{1,5},{5... | collective-permute-start | bytes 1179656 | tf_op jit(solution)/shard_map/ppermute | solution.py:662
  35.0 20.2 %collective-permute-start.13 = (bf16[3,128,512]{2,1,0:T(8,128)(2,1)S(1)}, bf16[3,128,512]{2,1,0:T(8,128)(2,1)S(1)}, u32[]{:S(2)}, u32[]{:S(2)}) collective-permute-start(bf16[3,128,512]{2,1,0:T(8,128)(2,1)S(1)} %pad_maximum_fusion.1.refs_0_), channel_id=1, source_target_pairs={{0,24},{4,28},{8,16},{12,20},{16,8},{20,12},{24,0},{28,4},{1,25},{... | collective-permute-start | bytes 1179656 | tf_op jit(solution)/shard_map/ppermute | solution.py:662
  36.4 19.4 %collective-permute-start.12 = (bf16[3,128,512]{2,1,0:T(8,128)(2,1)S(1)}, bf16[3,128,512]{2,1,0:T(8,128)(2,1)S(1)}, u32[]{:S(2)}, u32[]{:S(2)}) collective-permute-start(bf16[3,128,512]{2,1,0:T(8,128)(2,1)S(1)} %pad_maximum_fusion.1.refs_0_), channel_id=1, source_target_pairs={{0,16},{4,20},{8,24},{12,28},{16,0},{20,4},{24,8},{28,12},{1,17},{... | collective-permute-start | bytes 1179656 | tf_op jit(solution)/shard_map/ppermute | solution.py:662
  38.0 17.9 %collective-permute-start.11 = (bf16[3,128,512]{2,1,0:T(8,128)(2,1)S(1)}, bf16[3,128,512]{2,1,0:T(8,128)(2,1)S(1)}, u32[]{:S(2)}, u32[]{:S(2)}) collective-permute-start(bf16[3,128,512]{2,1,0:T(8,128)(2,1)S(1)} %pad_maximum_fusion.1.refs_0_), channel_id=1, source_target_pairs={{0,8},{4,12},{8,0},{12,4},{16,24},{20,28},{24,16},{28,20},{1,9},{5... | collective-permute-start | bytes 1179656 | tf_op jit(solution)/shard_map/ppermute | solution.py:662
  56.4 13.8 %collective-permute-start.18 = (bf16[4,128,512]{2,1,0:T(8,128)(2,1)S(1)}, bf16[4,128,512]{2,1,0:T(8,128)(2,1)S(1)}, u32[]{:S(2)}, u32[]{:S(2)}) collective-permute-start(bf16[4,128,512]{2,1,0:T(8,128)(2,1)S(1)} %get-tuple-element.175), channel_id=1, source_target_pairs={{0,4},{4,0},{8,12},{12,8},{16,20},{20,16},{24,28},{28,24},{1,5},{5... | collective-permute-start | bytes 1572872 | tf_op jit(solution)/shard_map/ppermute | solution.py:662
  75.0 17.8 %collective-permute-start.24 = (bf16[4,144,512]{2,1,0:T(8,128)(2,1)S(1)}, bf16[4,144,512]{2,1,0:T(8,128)(2,1)S(1)}, u32[]{:S(2)}, u32[]{:S(2)}) collective-permute-start(bf16[4,144,512]{2,1,0:T(8,128)(2,1)S(1)} %get-tuple-element.199), channel_id=1, source_target_pairs={{0,1},{1,0},{2,3},{3,2},{4,5},{5,4},{6,7},{7,6},{8,9},{9,8},{10,11... | collective-permute-start | bytes 1769480 | tf_op jit(solution)/shard_map/ppermute | solution.py:662
  76.6 14.8 %collective-permute-start.21 = (bf16[288,512]{1,0:T(8,128)(2,1)S(1)}, bf16[288,512]{1,0:T(8,128)(2,1)S(1)}, u32[]{:S(2)}, u32[]{:S(2)}) collective-permute-start(bf16[288,512]{1,0:T(8,128)(2,1)S(1)} %get-tuple-element.196), channel_id=1, source_target_pairs={{0,8},{4,12},{8,0},{12,4},{16,24},{20,28},{24,16},{28,20},{1,9},{5... | collective-permute-start | bytes 884744 | tf_op jit(solution)/shard_map/ppermute | solution.py:662
  77.8 15.0 %collective-permute-start.22 = (bf16[288,512]{1,0:T(8,128)(2,1)S(1)}, bf16[288,512]{1,0:T(8,128)(2,1)S(1)}, u32[]{:S(2)}, u32[]{:S(2)}) collective-permute-start(bf16[288,512]{1,0:T(8,128)(2,1)S(1)} %get-tuple-element.197), channel_id=1, source_target_pairs={{0,16},{4,20},{8,24},{12,28},{16,0},{20,4},{24,8},{28,12},{1,17},{... | collective-permute-start | bytes 884744 | tf_op jit(solution)/shard_map/ppermute | solution.py:662
  78.6 14.3 %collective-permute-start.23 = (bf16[288,512]{1,0:T(8,128)(2,1)S(1)}, bf16[288,512]{1,0:T(8,128)(2,1)S(1)}, u32[]{:S(2)}, u32[]{:S(2)}) collective-permute-start(bf16[288,512]{1,0:T(8,128)(2,1)S(1)} %get-tuple-element.198), channel_id=1, source_target_pairs={{0,24},{4,28},{8,16},{12,20},{16,8},{20,12},{24,0},{28,4},{1,25},{... | collective-permute-start | bytes 884744 | tf_op jit(solution)/shard_map/ppermute | solution.py:662
  95.4 11.4 %collective-permute-start.26 = (bf16[4,16,1664]{2,1,0:T(8,128)(2,1)S(1)}, bf16[4,16,1664]{2,1,0:T(8,128)(2,1)S(1)}, u32[]{:S(2)}, u32[]{:S(2)}) collective-permute-start(bf16[4,16,1664]{2,1,0:T(8,128)(2,1)S(1)} %get-tuple-element.202), channel_id=1, source_target_pairs={{0,8},{4,12},{8,0},{12,4},{16,24},{20,28},{24,16},{28,20},{1,9},{5... | collective-permute-start | bytes 638984 | tf_op jit(solution)/shard_map/ppermute | solution.py:662
  96.3 11.6 %collective-permute-start.27 = (bf16[4,16,1664]{2,1,0:T(8,128)(2,1)S(1)}, bf16[4,16,1664]{2,1,0:T(8,128)(2,1)S(1)}, u32[]{:S(2)}, u32[]{:S(2)}) collective-permute-start(bf16[4,16,1664]{2,1,0:T(8,128)(2,1)S(1)} %get-tuple-element.203), channel_id=1, source_target_pairs={{0,16},{4,20},{8,24},{12,28},{16,0},{20,4},{24,8},{28,12},{1,17},{... | collective-permute-start | bytes 638984 | tf_op jit(solution)/shard_map/ppermute | solution.py:662
  97.5 10.4 %collective-permute-start.28 = (bf16[4,16,1664]{2,1,0:T(8,128)(2,1)S(1)}, bf16[4,16,1664]{2,1,0:T(8,128)(2,1)S(1)}, u32[]{:S(2)}, u32[]{:S(2)}) collective-permute-start(bf16[4,16,1664]{2,1,0:T(8,128)(2,1)S(1)} %get-tuple-element.204), channel_id=1, source_target_pairs={{0,24},{4,28},{8,16},{12,20},{16,8},{20,12},{24,0},{28,4},{1,25},{... | collective-permute-start | bytes 638984 | tf_op jit(solution)/shard_map/ppermute | solution.py:662
  99.3 7.4 %collective-permute-start.30 = (bf16[144,512]{1,0:T(8,128)(2,1)S(1)}, bf16[144,512]{1,0:T(8,128)(2,1)S(1)}, u32[]{:S(2)}, u32[]{:S(2)}) collective-permute-start(bf16[144,512]{1,0:T(8,128)(2,1)S(1)} %shard_map.205), channel_id=1, source_target_pairs={{0,3},{1,2},{2,1},{3,0},{4,7},{5,6},{6,5},{7,4},{8,11},{9,10},{10,... | collective-permute-start | bytes 442376 | tf_op jit(solution)/shard_map/ppermute | solution.py:662
  109.0 6.7 %collective-permute-start.31 = (bf16[144,512]{1,0:T(8,128)(2,1)S(1)}, bf16[144,512]{1,0:T(8,128)(2,1)S(1)}, u32[]{:S(2)}, u32[]{:S(2)}) collective-permute-start(bf16[144,512]{1,0:T(8,128)(2,1)S(1)} %get-tuple-element.228), channel_id=1, source_target_pairs={{0,8},{4,12},{8,0},{12,4},{16,24},{20,28},{24,16},{28,20},{1,9},{5... | collective-permute-start | bytes 442376 | tf_op jit(solution)/shard_map/ppermute | solution.py:662
  110.0 7.5 %collective-permute-start.32 = (bf16[144,512]{1,0:T(8,128)(2,1)S(1)}, bf16[144,512]{1,0:T(8,128)(2,1)S(1)}, u32[]{:S(2)}, u32[]{:S(2)}) collective-permute-start(bf16[144,512]{1,0:T(8,128)(2,1)S(1)} %get-tuple-element.229), channel_id=1, source_target_pairs={{0,16},{4,20},{8,24},{12,28},{16,0},{20,4},{24,8},{28,12},{1,17},{... | collective-permute-start | bytes 442376 | tf_op jit(solution)/shard_map/ppermute | solution.py:662
  111.0 6.5 %collective-permute-start.33 = (bf16[144,512]{1,0:T(8,128)(2,1)S(1)}, bf16[144,512]{1,0:T(8,128)(2,1)S(1)}, u32[]{:S(2)}, u32[]{:S(2)}) collective-permute-start(bf16[144,512]{1,0:T(8,128)(2,1)S(1)} %get-tuple-element.230), channel_id=1, source_target_pairs={{0,24},{4,28},{8,16},{12,20},{16,8},{20,12},{24,0},{28,4},{1,25},{... | collective-permute-start | bytes 442376 | tf_op jit(solution)/shard_map/ppermute | solution.py:662
  (16 other events, 88.3 us)

commit v9 on v8

--- a/solution.py
+++ b/solution.py
@@ -509,7 +509,7 @@
 
 
 def feed_last_kernel(direct, info, middle, grad, cot, own, mixed_in, norms, w_all, *refs):
-    grad_middle, grad_mixed, grad_norms, *grads, ext, grad_own = refs
+    grad_middle, grad_norms, *grads, ext, grad_own = refs
     gain = norms[2:3]
     grad_norms[...] = jnp.zeros(grad_norms.shape, F32)
     for i in range(WROWS // TILE):
@@ -521,7 +521,6 @@
         grad_norms[1:2] += jnp.sum(masked, axis=0, keepdims=True)
         result = cot[at, :].astype(F32) + norm_back(part * gain, unit, scale)
         grad_middle[at, :] = result
-        grad_mixed[at, :] = mm_right(result.astype(BF16), w_all[:, 3 * D : 4 * D]).astype(BF16)
         grad_own[at, :] = (result * own[at, 0:1]).astype(BF16)
     grad_out = mm_left(mixed_in[...], grad_own[...])
     if direct:
@@ -540,6 +539,11 @@
 
 def finish_rows_kernel(info, values, out, ext):
     unplace(info, values, ext, out)
+
+
+def mixed_kernel(info, grad_middle, w_all, grad_mixed):
+    low = grad_middle[...].astype(BF16)
+    grad_mixed[...] = mm_right(low, w_all[:, 3 * D : 4 * D]).astype(BF16)
 
 
 def unplace(info, values, ext, out):
@@ -889,11 +893,10 @@
     if direct:
         total, *grads, from_first = together(total, *grads, *along_core([first_grads[1]]))
         from_core = [from_first, *along_core([grads[1]])]
-    grad_middle, grad_mixed, grad_norms, *out_grads = run_kernel(
+    grad_middle, grad_norms, *out_grads = run_kernel(
         functools.partial(feed_last_kernel, direct),
         [
             shape((WROWS, D), F32),
-            shape((WROWS, D), BF16),
             shape((8, D), F32),
             *out_shape,
         ],
@@ -908,8 +911,18 @@
         norms_all,
         w_all,
     )
+    (grad_mixed,) = run_kernel(
+        mixed_kernel,
+        [shape((WROWS, D), BF16)],
+        [],
+        2 * WROWS * D * D,
+        info,
+        grad_middle,
+        w_all,
+    )
     if direct:
         from_core = [*from_core, *along_core(out_grads[1:])]
+        *from_core, grad_mixed = together(*from_core, grad_mixed)
         keeps, from_core = [first_grads[0], grads[0], out_grads[0]], together(*from_core)
         own_pair, to_near, pair, *low = add_chunks(keeps, from_core)
         to_near, *low, grad_mixed = together(to_near, *low, grad_mixed)

time: 120 us -> 120 us (level)
  Pallas kernels: 51.5 us -> 52.7 us
    pallas_call x8 -> x9, Pallas kernels: 48 us -> 49.2 us  [run_kernel(): pl.pallas_call(body, out_shape=out_shape, in_specs=[SMEM] + specs, out_sp...]
  transfers between devices with their start and end apart: 36 -> 36, of which waited for: 15 -> 14; matrix products, arithmetic and copies ran while one was open for 0% -> 0% of each run, Pallas kernels for 41% -> 42%
where the time goes in v9:
time: 120 us
  Pallas kernels  52.7 us (44%)
  starting transfers between devices  39.5 us (33%)
  waiting for transfers between devices  13.6 us (11%)
  blocking collectives  12.4 us (10%)
    pallas_call x9, Pallas kernels, run_kernel(): pl.pallas_call(body, out_shape=out_shape, in_specs=[SMEM] + specs, out_sp...  49.2 us
    ppermute x36, starting transfers between devices, swap(): lax.ppermute(array, axis, [(i, i ^ bit) for i in range(lax.axis_size(axis...  39.5 us
    ppermute x36, waiting for transfers between devices, swap(): lax.ppermute(array, axis, [(i, i ^ bit) for i in range(lax.axis_size(axis...  13.6 us
    all_gather x1, blocking collectives, per_device(): first_half = lax.all_gather(column, 'dp', axis_index_groups=CHIPS)  12.4 us
  transfers between devices with their start and end apart: 36, of which 14 were waited for; matrix products, arithmetic and copies ran while one was open for 0% of the time, Pallas kernels for 42%

profile of v9, /device:TPU:0, one launch (start us, length us, event | category | flops | bytes accessed | tf_op | source)
XLA Modules:
  0.0 119.6 jit_solution(8309785556758121355)
XLA Ops:
  0.7 1.6 %shard_map.195 = (bf16[16,3200]{1,0:T(8,128)(2,1)S(1)}, bf16[16,2176]{1,0:T(8,128)(2,1)S(1)}, bf16[16,3200]{1,0:T(8,128)(2,1)S(1)}, bf16[208,512]{1,0:T(8,128)(2...) custom-call(bf16[704,512]{1,0:T(8,128)(2,1)} %rows.2, bf16[704,512]{1,0:T(8,128)(2,1)} %rows.3, ...), custom_call_target="tpu_custom_call" | custom-call | tf_op jit(solution)/shard_map/pallas_call | solution.py:737
  2.3 3.0 %collective-permute-start.1 = (bf16[208,512]{1,0:T(8,128)(2,1)S(1)}, bf16[208,512]{1,0:T(8,128)(2,1)S(1)}, u32[]{:S(2)}, u32[]{:S(2)}) collective-permute-start(bf16[208,512]{1,0:T(8,128)(2,1)S(1)} %get-tuple-element.142), channel_id=1, source_target_pairs={{0,16},{4,20},{8,24},{12,28},{16,0},{20,4},{24,8},{28,12},{1,17},{... | collective-permute-start | bytes 638984 | tf_op jit(solution)/shard_map/ppermute | solution.py:666
  5.3 1.5 %collective-permute-start = (bf16[208,512]{1,0:T(8,128)(2,1)S(1)}, bf16[208,512]{1,0:T(8,128)(2,1)S(1)}, u32[]{:S(2)}, u32[]{:S(2)}) collective-permute-start(bf16[208,512]{1,0:T(8,128)(2,1)S(1)} %get-tuple-element.142), channel_id=1, source_target_pairs={{0,8},{4,12},{8,0},{12,4},{16,24},{20,28},{24,16},{28,20},{1,9},{5... | collective-permute-start | bytes 638984 | tf_op jit(solution)/shard_map/ppermute | solution.py:666
  6.8 2.6 %collective-permute-start.3 = (bf16[16,2176]{1,0:T(8,128)(2,1)S(1)}, bf16[16,2176]{1,0:T(8,128)(2,1)S(1)}, u32[]{:S(2)}, u32[]{:S(2)}) collective-permute-start(bf16[16,2176]{1,0:T(8,128)(2,1)S(1)} %get-tuple-element.131), channel_id=1, source_target_pairs={{0,2},{1,3},{2,0},{3,1},{4,6},{5,7},{6,4},{7,5},{8,10},{9,11},{10,... | collective-permute-start | bytes 208904 | tf_op jit(solution)/shard_map/ppermute | solution.py:666
  9.4 1.6 %collective-permute-start.2 = (bf16[16,3200]{1,0:T(8,128)(2,1)S(1)}, bf16[16,3200]{1,0:T(8,128)(2,1)S(1)}, u32[]{:S(2)}, u32[]{:S(2)}) collective-permute-start(bf16[16,3200]{1,0:T(8,128)(2,1)S(1)} %get-tuple-element.130), channel_id=1, source_target_pairs={{0,1},{1,0},{2,3},{3,2},{4,5},{5,4},{6,7},{7,6},{8,9},{9,8},{10,11... | collective-permute-start | bytes 307208 | tf_op jit(solution)/shard_map/ppermute | solution.py:666
  11.5 2.9 %shard_map.196 = (bf16[768,512]{1,0:T(8,128)(2,1)S(1)}, bf16[768,512]{1,0:T(8,128)(2,1)S(1)}, bf16[768,512]{1,0:T(8,128)(2,1)S(1)}, f32[768,128]{1,0:T(8,128)S(1)}) custom-call(s32[11]{0:T(128)S(1)} %pad_add_fusion.info, bf16[704,512]{1,0:T(8,128)(2,1)S(1)} %copy-done, bf16[704,512]{1,0:T(8,128)(2,1)S(1)} %copy-done.1), custom_call_target="tpu_custom_call" | custom-call | flops 402653184 | bytes 1441792 | tf_op jit(solution)/shard_map/pallas_call | solution.py:652
  14.4 3.1 %collective-permute-done.4.far = bf16[16,3200]{1,0:T(8,128)(2,1)S(1)} collective-permute-done((bf16[16,3200]{1,0:T(8,128)(2,1)S(1)}, bf16[16,3200]{1,0:T(8,128)(2,1)S(1)}, u32[]{:S(2)}, u32[]{:S(2)}) %collective-permute-start.4) | collective-permute-done | bytes 102432 | tf_op jit(solution)/shard_map/ppermute | solution.py:666
  18.7 2.9 %collective-permute-start.8 = (bf16[160,512]{1,0:T(8,128)(2,1)S(1)}, bf16[160,512]{1,0:T(8,128)(2,1)S(1)}, u32[]{:S(2)}, u32[]{:S(2)}) collective-permute-start(bf16[160,512]{1,0:T(8,128)(2,1)S(1)} %get-tuple-element.144), channel_id=1, source_target_pairs={{0,3},{1,2},{2,1},{3,0},{4,7},{5,6},{6,5},{7,4},{8,11},{9,10},{10,... | collective-permute-start | bytes 491528 | tf_op jit(solution)/shard_map/ppermute | solution.py:666
  21.7 12.4 %all-gather = bf16[12,16,2176]{2,1,0:T(8,128)(2,1)S(1)} all-gather(bf16[3,16,2176]{2,1,0:T(8,128)(2,1)S(1)} %pad_maximum_fusion.2), channel_id=2, replica_groups={{0,8,16,24},{4,12,20,28},{1,9,17,25},{5,13,21,29},{2,10,18,26},{6,14,22..., dimensions={0}, use_global_device_ids=true | all-gather | bytes 1044480 | tf_op jit(solution)/shard_map/all_gather | solution.py:775
  36.4 1.6 %collective-permute-start.12 = (bf16[3,128,512]{2,1,0:T(8,128)(2,1)S(1)}, bf16[3,128,512]{2,1,0:T(8,128)(2,1)S(1)}, u32[]{:S(2)}, u32[]{:S(2)}) collective-permute-start(bf16[3,128,512]{2,1,0:T(8,128)(2,1)S(1)} %pad_maximum_fusion.1.refs_0_), channel_id=1, source_target_pairs={{0,16},{4,20},{8,24},{12,28},{16,0},{20,4},{24,8},{28,12},{1,17},{... | collective-permute-start | bytes 1179656 | tf_op jit(solution)/shard_map/ppermute | solution.py:666
  38.0 1.5 %collective-permute-start.11 = (bf16[3,128,512]{2,1,0:T(8,128)(2,1)S(1)}, bf16[3,128,512]{2,1,0:T(8,128)(2,1)S(1)}, u32[]{:S(2)}, u32[]{:S(2)}) collective-permute-start(bf16[3,128,512]{2,1,0:T(8,128)(2,1)S(1)} %pad_maximum_fusion.1.refs_0_), channel_id=1, source_target_pairs={{0,8},{4,12},{8,0},{12,4},{16,24},{20,28},{24,16},{28,20},{1,9},{5... | collective-permute-start | bytes 1179656 | tf_op jit(solution)/shard_map/ppermute | solution.py:666
  39.5 9.9 %shard_map.197 = (bf16[768,512]{1,0:T(8,128)(2,1)S(1)}, bf16[768,1536]{1,0:T(8,128)(2,1)S(1)}, bf16[768,512]{1,0:T(8,128)(2,1)S(1)}, bf16[768,512]{1,0:T(8,128)(...) custom-call(s32[11]{0:T(128)S(1)} %pad_add_fusion.info, bf16[704,512]{1,0:T(8,128)(2,1)S(1)} %copy-done, ...), custom_call_target="tpu_custom_call" | custom-call | flops 2415919104 | bytes 5087232 | tf_op jit(solution)/shard_map/pallas_call | solution.py:652
  49.4 5.8 %shard_map.198 = (f32[768,512]{1,0:T(8,128)S(1)}, f32[768,512]{1,0:T(8,128)S(1)}, f32[768,512]{1,0:T(8,128)S(1)}, bf16[768,512]{1,0:T(8,128)(2,1)S(1)}, bf16[768...) custom-call(s32[11]{0:T(128)S(1)} %pad_add_fusion.info, ...), custom_call_target="tpu_custom_call" | custom-call | flops 2818572288 | bytes 8536064 | tf_op jit(solution)/shard_map/pallas_call | solution.py:652
  58.7 11.4 %shard_map.199 = (f32[768,512]{1,0:T(8,128)S(1)}, f32[768,512]{1,0:T(8,128)S(1)}, bf16[4,384,512]{2,1,0:T(8,128)(2,1)S(1)}, bf16[4,384,512]{2,1,0:T(8,128)(2,1)S(1)}) custom-call(s32[11]{0:T(128)S(1)} %pad_add_fusion.info, f32[768,512]{1,0:T(8,128)S(1)} %get-tuple-element.166.total_in, f32[768,512]{1,0:T(8,128)S(1)} %get-tuple-element.167.grad_in, ...), custom_call_target="tpu_custom_call" | custom-call | flops 7247757312 | bytes 9437184 | tf_op jit(solution)/shard_map/pallas_call | solution.py:652
  70.4 2.6 %shard_map.200 = (f32[768,512]{1,0:T(8,128)S(1)}, f32[8,512]{1,0:T(8,128)S(1)}, bf16[4,64,512]{2,1,0:T(8,128)(2,1)S(1)}, bf16[4,64,512]{2,1,0:T(8,128)(2,1)S(1)}) custom-call(s32[11]{0:T(128)S(1)} %pad_add_fusion.info, f32[768,512]{1,0:T(8,128)S(1)} %get-tuple-element.180.middle, f32[768,512]{1,0:T(8,128)S(1)} %get-tuple-element.181.grad, ...), custom_call_target="tpu_custom_call" | custom-call | flops 805306368 | bytes 7356416 | tf_op jit(solution)/shard_map/pallas_call | solution.py:652
  75.1 1.6 %collective-permute-start.24 = (bf16[4,144,512]{2,1,0:T(8,128)(2,1)S(1)}, bf16[4,144,512]{2,1,0:T(8,128)(2,1)S(1)}, u32[]{:S(2)}, u32[]{:S(2)}) collective-permute-start(bf16[4,144,512]{2,1,0:T(8,128)(2,1)S(1)} %get-tuple-element.205), channel_id=1, source_target_pairs={{0,1},{1,0},{2,3},{3,2},{4,5},{5,4},{6,7},{7,6},{8,9},{9,8},{10,11... | collective-permute-start | bytes 1769480 | tf_op jit(solution)/shard_map/ppermute | solution.py:666
  78.6 1.5 %collective-permute-start.23 = (bf16[288,512]{1,0:T(8,128)(2,1)S(1)}, bf16[288,512]{1,0:T(8,128)(2,1)S(1)}, u32[]{:S(2)}, u32[]{:S(2)}) collective-permute-start(bf16[288,512]{1,0:T(8,128)(2,1)S(1)} %get-tuple-element.204), channel_id=1, source_target_pairs={{0,24},{4,28},{8,16},{12,20},{16,8},{20,12},{24,0},{28,4},{1,25},{... | collective-permute-start | bytes 884744 | tf_op jit(solution)/shard_map/ppermute | solution.py:666
  80.2 11.3 %shard_map.203 = (f32[768,512]{1,0:T(8,128)S(1)}, bf16[4,4,16,1664]{3,2,1,0:T(8,128)(2,1)S(1)}, bf16[4,4,16,1664]{3,2,1,0:T(8,128)(2,1)S(1)}) custom-call(s32[11]{0:T(128)S(1)} %pad_add_fusion.info, bf16[768,512]{1,0:T(8,128)(2,1)S(1)} %get-tuple-element.154.x_in, f32[768,128]{1,0:T(8,128)S(1)} %get-tuple-element.155.own, ...), custom_call_target="tpu_custom_call" | custom-call | flops 3623878656 | bytes 8945664 | tf_op jit(solution)/shard_map/pallas_call | solution.py:652
  97.5 1.5 %collective-permute-start.28 = (bf16[4,16,1664]{2,1,0:T(8,128)(2,1)S(1)}, bf16[4,16,1664]{2,1,0:T(8,128)(2,1)S(1)}, u32[]{:S(2)}, u32[]{:S(2)}) collective-permute-start(bf16[4,16,1664]{2,1,0:T(8,128)(2,1)S(1)} %get-tuple-element.210), channel_id=1, source_target_pairs={{0,24},{4,28},{8,16},{12,20},{16,8},{20,12},{24,0},{28,4},{1,25},{... | collective-permute-start | bytes 638984 | tf_op jit(solution)/shard_map/ppermute | solution.py:666
  99.4 2.9 %collective-permute-start.30 = (bf16[144,512]{1,0:T(8,128)(2,1)S(1)}, bf16[144,512]{1,0:T(8,128)(2,1)S(1)}, u32[]{:S(2)}, u32[]{:S(2)}) collective-permute-start(bf16[144,512]{1,0:T(8,128)(2,1)S(1)} %shard_map.206), channel_id=1, source_target_pairs={{0,3},{1,2},{2,1},{3,0},{4,7},{5,6},{6,5},{7,4},{8,11},{9,10},{10,... | collective-permute-start | bytes 442376 | tf_op jit(solution)/shard_map/ppermute | solution.py:666
  102.3 2.1 %shard_map.208 = bf16[704,512]{1,0:T(8,128)(2,1)} custom-call(s32[11]{0:T(128)S(1)} %pad_add_fusion.info, f32[768,512]{1,0:T(8,128)S(1)} %get-tuple-element.224.values), custom_call_target="tpu_custom_call" | custom-call | flops 402653184 | bytes 1572864 | tf_op jit(solution)/shard_map/pallas_call | solution.py:652
  104.4 2.1 %shard_map.209 = bf16[704,512]{1,0:T(8,128)(2,1)} custom-call(s32[11]{0:T(128)S(1)} %pad_add_fusion.info, f32[768,512]{1,0:T(8,128)S(1)} %get-tuple-element.225.values), custom_call_target="tpu_custom_call" | custom-call | flops 402653184 | bytes 1572864 | tf_op jit(solution)/shard_map/pallas_call | solution.py:652
  112.8 2.9 %collective-permute-start.35 = (bf16[16,1664]{1,0:T(8,128)(2,1)S(1)}, bf16[16,1664]{1,0:T(8,128)(2,1)S(1)}, u32[]{:S(2)}, u32[]{:S(2)}) collective-permute-start(bf16[16,1664]{1,0:T(8,128)(2,1)S(1)} %shard_map.211), channel_id=1, source_target_pairs={{0,3},{1,2},{2,1},{3,0},{4,7},{5,6},{6,5},{7,4},{8,11},{9,10},{10,... | collective-permute-start | bytes 159752 | tf_op jit(solution)/shard_map/ppermute | solution.py:666
  115.8 1.8 %collective-permute-done.32.two = bf16[144,512]{1,0:T(8,128)(2,1)S(1)} collective-permute-done((bf16[144,512]{1,0:T(8,128)(2,1)S(1)}, bf16[144,512]{1,0:T(8,128)(2,1)S(1)}, u32[]{:S(2)}, u32[]{:S(2)}) %collective-permute-start.32) | collective-permute-done | bytes 147488 | tf_op jit(solution)/shard_map/ppermute | solution.py:666
  (85 shorter events, 26.6 us)
Async XLA Ops:
  2.3 15.3 %collective-permute-start.1 = (bf16[208,512]{1,0:T(8,128)(2,1)S(1)}, bf16[208,512]{1,0:T(8,128)(2,1)S(1)}, u32[]{:S(2)}, u32[]{:S(2)}) collective-permute-start(bf16[208,512]{1,0:T(8,128)(2,1)S(1)} %get-tuple-element.142), channel_id=1, source_target_pairs={{0,16},{4,20},{8,24},{12,28},{16,0},{20,4},{24,8},{28,12},{1,17},{... | collective-permute-start | bytes 638984 | tf_op jit(solution)/shard_map/ppermute | solution.py:666
  5.3 12.2 %collective-permute-start = (bf16[208,512]{1,0:T(8,128)(2,1)S(1)}, bf16[208,512]{1,0:T(8,128)(2,1)S(1)}, u32[]{:S(2)}, u32[]{:S(2)}) collective-permute-start(bf16[208,512]{1,0:T(8,128)(2,1)S(1)} %get-tuple-element.142), channel_id=1, source_target_pairs={{0,8},{4,12},{8,0},{12,4},{16,24},{20,28},{24,16},{28,20},{1,9},{5... | collective-permute-start | bytes 638984 | tf_op jit(solution)/shard_map/ppermute | solution.py:666
  6.8 7.6 %collective-permute-start.3 = (bf16[16,2176]{1,0:T(8,128)(2,1)S(1)}, bf16[16,2176]{1,0:T(8,128)(2,1)S(1)}, u32[]{:S(2)}, u32[]{:S(2)}) collective-permute-start(bf16[16,2176]{1,0:T(8,128)(2,1)S(1)} %get-tuple-element.131), channel_id=1, source_target_pairs={{0,2},{1,3},{2,0},{3,1},{4,6},{5,7},{6,4},{7,5},{8,10},{9,11},{10,... | collective-permute-start | bytes 208904 | tf_op jit(solution)/shard_map/ppermute | solution.py:666
  11.0 6.6 %collective-permute-start.4 = (bf16[16,3200]{1,0:T(8,128)(2,1)S(1)}, bf16[16,3200]{1,0:T(8,128)(2,1)S(1)}, u32[]{:S(2)}, u32[]{:S(2)}) collective-permute-start(bf16[16,3200]{1,0:T(8,128)(2,1)S(1)} %get-tuple-element.132), channel_id=1, source_target_pairs={{0,3},{1,2},{2,1},{3,0},{4,7},{5,6},{6,5},{7,4},{8,11},{9,10},{10,... | collective-permute-start | bytes 307208 | tf_op jit(solution)/shard_map/ppermute | solution.py:666
  17.6 16.6 %collective-permute-start.5 = (bf16[208,512]{1,0:T(8,128)(2,1)S(1)}, bf16[208,512]{1,0:T(8,128)(2,1)S(1)}, u32[]{:S(2)}, u32[]{:S(2)}) collective-permute-start(bf16[208,512]{1,0:T(8,128)(2,1)S(1)} %get-tuple-element.142), channel_id=1, source_target_pairs={{0,24},{4,28},{8,16},{12,20},{16,8},{20,12},{24,0},{28,4},{1,25},{... | collective-permute-start | bytes 638984 | tf_op jit(solution)/shard_map/ppermute | solution.py:666
  18.1 16.0 %collective-permute-start.6 = (bf16[160,512]{1,0:T(8,128)(2,1)S(1)}, bf16[160,512]{1,0:T(8,128)(2,1)S(1)}, u32[]{:S(2)}, u32[]{:S(2)}) collective-permute-start(bf16[160,512]{1,0:T(8,128)(2,1)S(1)} %get-tuple-element.143), channel_id=1, source_target_pairs={{0,1},{1,0},{2,3},{3,2},{4,5},{5,4},{6,7},{7,6},{8,9},{9,8},{10,11... | collective-permute-start | bytes 491528 | tf_op jit(solution)/shard_map/ppermute | solution.py:666
  18.7 15.4 %collective-permute-start.8 = (bf16[160,512]{1,0:T(8,128)(2,1)S(1)}, bf16[160,512]{1,0:T(8,128)(2,1)S(1)}, u32[]{:S(2)}, u32[]{:S(2)}) collective-permute-start(bf16[160,512]{1,0:T(8,128)(2,1)S(1)} %get-tuple-element.144), channel_id=1, source_target_pairs={{0,3},{1,2},{2,1},{3,0},{4,7},{5,6},{6,5},{7,4},{8,11},{9,10},{10,... | collective-permute-start | bytes 491528 | tf_op jit(solution)/shard_map/ppermute | solution.py:666
  21.6 12.5 %collective-permute-start.7 = (bf16[128,512]{1,0:T(8,128)(2,1)S(1)}, bf16[128,512]{1,0:T(8,128)(2,1)S(1)}, u32[]{:S(2)}, u32[]{:S(2)}) collective-permute-start(bf16[128,512]{1,0:T(8,128)(2,1)S(1)} %slice.17), channel_id=1, source_target_pairs={{0,2},{1,3},{2,0},{3,1},{4,6},{5,7},{6,4},{7,5},{8,10},{9,11},{10,... | collective-permute-start | bytes 393224 | tf_op jit(solution)/shard_map/ppermute | solution.py:666
  34.9 22.0 %collective-permute-start.14 = (bf16[3,128,512]{2,1,0:T(8,128)(2,1)S(1)}, bf16[3,128,512]{2,1,0:T(8,128)(2,1)S(1)}, u32[]{:S(2)}, u32[]{:S(2)}) collective-permute-start(bf16[3,128,512]{2,1,0:T(8,128)(2,1)S(1)} %pad_maximum_fusion.1.refs_0_), channel_id=1, source_target_pairs={{0,4},{4,0},{8,12},{12,8},{16,20},{20,16},{24,28},{28,24},{1,5},{5... | collective-permute-start | bytes 1179656 | tf_op jit(solution)/shard_map/ppermute | solution.py:666
  35.0 20.2 %collective-permute-start.13 = (bf16[3,128,512]{2,1,0:T(8,128)(2,1)S(1)}, bf16[3,128,512]{2,1,0:T(8,128)(2,1)S(1)}, u32[]{:S(2)}, u32[]{:S(2)}) collective-permute-start(bf16[3,128,512]{2,1,0:T(8,128)(2,1)S(1)} %pad_maximum_fusion.1.refs_0_), channel_id=1, source_target_pairs={{0,24},{4,28},{8,16},{12,20},{16,8},{20,12},{24,0},{28,4},{1,25},{... | collective-permute-start | bytes 1179656 | tf_op jit(solution)/shard_map/ppermute | solution.py:666
  36.4 19.4 %collective-permute-start.12 = (bf16[3,128,512]{2,1,0:T(8,128)(2,1)S(1)}, bf16[3,128,512]{2,1,0:T(8,128)(2,1)S(1)}, u32[]{:S(2)}, u32[]{:S(2)}) collective-permute-start(bf16[3,128,512]{2,1,0:T(8,128)(2,1)S(1)} %pad_maximum_fusion.1.refs_0_), channel_id=1, source_target_pairs={{0,16},{4,20},{8,24},{12,28},{16,0},{20,4},{24,8},{28,12},{1,17},{... | collective-permute-start | bytes 1179656 | tf_op jit(solution)/shard_map/ppermute | solution.py:666
  38.0 17.9 %collective-permute-start.11 = (bf16[3,128,512]{2,1,0:T(8,128)(2,1)S(1)}, bf16[3,128,512]{2,1,0:T(8,128)(2,1)S(1)}, u32[]{:S(2)}, u32[]{:S(2)}) collective-permute-start(bf16[3,128,512]{2,1,0:T(8,128)(2,1)S(1)} %pad_maximum_fusion.1.refs_0_), channel_id=1, source_target_pairs={{0,8},{4,12},{8,0},{12,4},{16,24},{20,28},{24,16},{28,20},{1,9},{5... | collective-permute-start | bytes 1179656 | tf_op jit(solution)/shard_map/ppermute | solution.py:666
  56.4 13.8 %collective-permute-start.18 = (bf16[4,128,512]{2,1,0:T(8,128)(2,1)S(1)}, bf16[4,128,512]{2,1,0:T(8,128)(2,1)S(1)}, u32[]{:S(2)}, u32[]{:S(2)}) collective-permute-start(bf16[4,128,512]{2,1,0:T(8,128)(2,1)S(1)} %get-tuple-element.178), channel_id=1, source_target_pairs={{0,4},{4,0},{8,12},{12,8},{16,20},{20,16},{24,28},{28,24},{1,5},{5... | collective-permute-start | bytes 1572872 | tf_op jit(solution)/shard_map/ppermute | solution.py:666
  75.1 17.8 %collective-permute-start.24 = (bf16[4,144,512]{2,1,0:T(8,128)(2,1)S(1)}, bf16[4,144,512]{2,1,0:T(8,128)(2,1)S(1)}, u32[]{:S(2)}, u32[]{:S(2)}) collective-permute-start(bf16[4,144,512]{2,1,0:T(8,128)(2,1)S(1)} %get-tuple-element.205), channel_id=1, source_target_pairs={{0,1},{1,0},{2,3},{3,2},{4,5},{5,4},{6,7},{7,6},{8,9},{9,8},{10,11... | collective-permute-start | bytes 1769480 | tf_op jit(solution)/shard_map/ppermute | solution.py:666
  76.7 14.8 %collective-permute-start.21 = (bf16[288,512]{1,0:T(8,128)(2,1)S(1)}, bf16[288,512]{1,0:T(8,128)(2,1)S(1)}, u32[]{:S(2)}, u32[]{:S(2)}) collective-permute-start(bf16[288,512]{1,0:T(8,128)(2,1)S(1)} %get-tuple-element.202), channel_id=1, source_target_pairs={{0,8},{4,12},{8,0},{12,4},{16,24},{20,28},{24,16},{28,20},{1,9},{5... | collective-permute-start | bytes 884744 | tf_op jit(solution)/shard_map/ppermute | solution.py:666
  77.9 15.0 %collective-permute-start.22 = (bf16[288,512]{1,0:T(8,128)(2,1)S(1)}, bf16[288,512]{1,0:T(8,128)(2,1)S(1)}, u32[]{:S(2)}, u32[]{:S(2)}) collective-permute-start(bf16[288,512]{1,0:T(8,128)(2,1)S(1)} %get-tuple-element.203), channel_id=1, source_target_pairs={{0,16},{4,20},{8,24},{12,28},{16,0},{20,4},{24,8},{28,12},{1,17},{... | collective-permute-start | bytes 884744 | tf_op jit(solution)/shard_map/ppermute | solution.py:666
  78.6 14.3 %collective-permute-start.23 = (bf16[288,512]{1,0:T(8,128)(2,1)S(1)}, bf16[288,512]{1,0:T(8,128)(2,1)S(1)}, u32[]{:S(2)}, u32[]{:S(2)}) collective-permute-start(bf16[288,512]{1,0:T(8,128)(2,1)S(1)} %get-tuple-element.204), channel_id=1, source_target_pairs={{0,24},{4,28},{8,16},{12,20},{16,8},{20,12},{24,0},{28,4},{1,25},{... | collective-permute-start | bytes 884744 | tf_op jit(solution)/shard_map/ppermute | solution.py:666
  95.5 11.4 %collective-permute-start.26 = (bf16[4,16,1664]{2,1,0:T(8,128)(2,1)S(1)}, bf16[4,16,1664]{2,1,0:T(8,128)(2,1)S(1)}, u32[]{:S(2)}, u32[]{:S(2)}) collective-permute-start(bf16[4,16,1664]{2,1,0:T(8,128)(2,1)S(1)} %get-tuple-element.208), channel_id=1, source_target_pairs={{0,8},{4,12},{8,0},{12,4},{16,24},{20,28},{24,16},{28,20},{1,9},{5... | collective-permute-start | bytes 638984 | tf_op jit(solution)/shard_map/ppermute | solution.py:666
  96.4 11.6 %collective-permute-start.27 = (bf16[4,16,1664]{2,1,0:T(8,128)(2,1)S(1)}, bf16[4,16,1664]{2,1,0:T(8,128)(2,1)S(1)}, u32[]{:S(2)}, u32[]{:S(2)}) collective-permute-start(bf16[4,16,1664]{2,1,0:T(8,128)(2,1)S(1)} %get-tuple-element.209), channel_id=1, source_target_pairs={{0,16},{4,20},{8,24},{12,28},{16,0},{20,4},{24,8},{28,12},{1,17},{... | collective-permute-start | bytes 638984 | tf_op jit(solution)/shard_map/ppermute | solution.py:666
  97.5 10.4 %collective-permute-start.28 = (bf16[4,16,1664]{2,1,0:T(8,128)(2,1)S(1)}, bf16[4,16,1664]{2,1,0:T(8,128)(2,1)S(1)}, u32[]{:S(2)}, u32[]{:S(2)}) collective-permute-start(bf16[4,16,1664]{2,1,0:T(8,128)(2,1)S(1)} %get-tuple-element.210), channel_id=1, source_target_pairs={{0,24},{4,28},{8,16},{12,20},{16,8},{20,12},{24,0},{28,4},{1,25},{... | collective-permute-start | bytes 638984 | tf_op jit(solution)/shard_map/ppermute | solution.py:666
  99.4 7.4 %collective-permute-start.30 = (bf16[144,512]{1,0:T(8,128)(2,1)S(1)}, bf16[144,512]{1,0:T(8,128)(2,1)S(1)}, u32[]{:S(2)}, u32[]{:S(2)}) collective-permute-start(bf16[144,512]{1,0:T(8,128)(2,1)S(1)} %shard_map.206), channel_id=1, source_target_pairs={{0,3},{1,2},{2,1},{3,0},{4,7},{5,6},{6,5},{7,4},{8,11},{9,10},{10,... | collective-permute-start | bytes 442376 | tf_op jit(solution)/shard_map/ppermute | solution.py:666
  109.0 6.7 %collective-permute-start.31 = (bf16[144,512]{1,0:T(8,128)(2,1)S(1)}, bf16[144,512]{1,0:T(8,128)(2,1)S(1)}, u32[]{:S(2)}, u32[]{:S(2)}) collective-permute-start(bf16[144,512]{1,0:T(8,128)(2,1)S(1)} %get-tuple-element.234), channel_id=1, source_target_pairs={{0,8},{4,12},{8,0},{12,4},{16,24},{20,28},{24,16},{28,20},{1,9},{5... | collective-permute-start | bytes 442376 | tf_op jit(solution)/shard_map/ppermute | solution.py:666
  110.1 7.5 %collective-permute-start.32 = (bf16[144,512]{1,0:T(8,128)(2,1)S(1)}, bf16[144,512]{1,0:T(8,128)(2,1)S(1)}, u32[]{:S(2)}, u32[]{:S(2)}) collective-permute-start(bf16[144,512]{1,0:T(8,128)(2,1)S(1)} %get-tuple-element.235), channel_id=1, source_target_pairs={{0,16},{4,20},{8,24},{12,28},{16,0},{20,4},{24,8},{28,12},{1,17},{... | collective-permute-start | bytes 442376 | tf_op jit(solution)/shard_map/ppermute | solution.py:666
  111.1 6.5 %collective-permute-start.33 = (bf16[144,512]{1,0:T(8,128)(2,1)S(1)}, bf16[144,512]{1,0:T(8,128)(2,1)S(1)}, u32[]{:S(2)}, u32[]{:S(2)}) collective-permute-start(bf16[144,512]{1,0:T(8,128)(2,1)S(1)} %get-tuple-element.236), channel_id=1, source_target_pairs={{0,24},{4,28},{8,16},{12,20},{16,8},{20,12},{24,0},{28,4},{1,25},{... | collective-permute-start | bytes 442376 | tf_op jit(solution)/shard_map/ppermute | solution.py:666
  (16 other events, 88.3 us)
